TPU v7x, 32 devices: a whole 2x2x4 slice. The times are simulated.
32 devices in a mesh: groups: 2 (over y), elem: 4 (over z), lag: 2 (over x), gust: 2 (over core).
Axes of the slice: x: 2, y: 2, z: 4, core: 2. Of those that a mesh axis runs over, the one named last changes fastest.
Arguments:
- history: float32 [16, 16, 512], P('lag', ('groups', 'gust'), 'elem'), parts along dimension 1, may hold values from -6 to 6
- forcing: float32 [5, 16, 512], P(None, ('groups', 'gust'), 'elem'), parts along dimension 1, may hold values from -6 to 6
- interaction: bfloat16 [16, 512, 512], P('lag', 'elem'), may hold values from -0.09375 to 0.09375
- block_mask: int32 [16, 4, 4], P('lag', 'elem'), may hold values from 0 to 1, as said below
- correction: float32 [512, 128], P('elem'), may hold values from -0.5 to 0.5
- neighbours: int32 [4, 512], P(None, 'elem'), may hold values from 0 to 511, as said below
- edge_coef: float32 [4, 512], P(None, 'elem'), may hold values from -2 to 2
Outputs:
- sources: float32 [5, 16, 512], P(None, ('groups', 'gust'), 'elem'), parts along dimension 1
There are 2 independent parts, one for each index of `groups`. A program takes and returns all parts, laid end to end along the dimension named above; an argument that names none is the same for every part. Nothing has to cross between parts.
Inputs may be any that keep to these rules, and one draw needn't show every extreme that they name: block_mask[l, i, j] is 1 where the elements of block i (the 128 elements of one index of elem) feel block j at lag l + 1, else 0. neighbours[k, e] - e, taken cyclically modulo 512, lies within -8 to 8, and both ends are taken.
All inputs are finite; a program needn't handle non-finite values.
Results may differ from a plain program's by a relative error of at most 0.002.
Values may be sent and summed in bfloat16 or wider, within the bound.
No kernel may reach another device: no remote copies, remote signals or barrier semaphores. Data moves between devices by JAX's collectives and lax.ppermute only.
A program may use at most 64 MiB of HBM per device.

v0:
```python
import jax
import jax.numpy as jnp
from jax import lax
from jax.sharding import PartitionSpec as P

RIM = 8
STEPS = 5


def with_halo(cells, sides, width):
    for axis, dim in sides:
        count = lax.axis_size(axis)
        head = lax.slice_in_dim(cells, 0, width, axis=dim)
        tail = lax.slice_in_dim(cells, cells.shape[dim] - width, cells.shape[dim], axis=dim)
        cells = jnp.concatenate(
            [
                lax.ppermute(tail, axis, [(i, (i + 1) % count) for i in range(count)]),
                cells,
                lax.ppermute(head, axis, [((i + 1) % count, i) for i in range(count)]),
            ],
            axis=dim,
        )
    return cells


def from_behind(value, axis, steps):
    count = lax.axis_size(axis)
    first, last = (max(0, -steps), min(count, count - steps))
    return lax.ppermute(value, axis, [(source, source + steps) for source in range(first, last)])


def on_device(history, forcing, interaction, block_mask, correction, neighbours, edge_coef):
    precise = lax.Precision.HIGHEST
    row_count = correction.shape[0]
    block_count = lax.axis_size("elem")
    total_count = row_count * block_count
    lag_place = lax.axis_index("lag")
    own_start = lax.axis_index("elem") * row_count
    first_flag = (lag_place == 0).astype(jnp.float32)
    mask_rows = block_mask[:, 0, :].astype(jnp.float32)
    results = []
    own_newest = history[0]
    history_now = history
    for step in range(STEPS):
        rounded = history_now.astype(jnp.bfloat16)
        piece = lax.all_gather(rounded, "elem", axis=2, tiled=True)
        count = piece.shape[2]
        columns = jnp.arange(count, dtype=jnp.int32)
        owner = columns // row_count
        select = (owner[:, None] == jnp.arange(block_count, dtype=jnp.int32)[None, :]).astype(
            jnp.float32
        )
        live = jnp.dot(mask_rows, select.T, precision=precise).astype(jnp.bfloat16)
        masked = piece * live[:, None, :]
        retarded = jnp.einsum(
            "lgc,lrc->gr", masked, interaction, preferred_element_type=jnp.float32
        )
        padded = with_halo(own_newest, (("elem", 1),), RIM)
        local_index = (neighbours - own_start + RIM) % total_count
        across = jnp.take(padded, local_index, axis=1)
        gradient = jnp.sum(edge_coef[None, :, :] * (across - own_newest[:, None, :]), axis=1)
        drive = lax.psum(first_flag * (forcing[step] + gradient) - retarded, "lag")
        fresh = drive + jnp.dot(drive, correction.T, precision=precise)
        results.append(fresh)
        if step + 1 < STEPS:
            moved = from_behind(history_now[-1], "lag", 1)
            incoming = jnp.where(lag_place == 0, fresh, moved)
            history_now = jnp.concatenate([incoming[None], history_now[:-1]], 0)
            own_newest = history_now[0]
    return jnp.stack(results, 0)


def solution(mesh):
    placed = (
        P("lag", ("groups", "gust"), "elem"),
        P(None, ("groups", "gust"), "elem"),
        P("lag", "elem", None),
        P("lag", "elem", None),
        P("elem", None),
        P(None, "elem"),
        P(None, "elem"),
    )
    return jax.shard_map(
        on_device,
        mesh=mesh,
        in_specs=placed,
        out_specs=P(None, ("groups", "gust"), "elem"),
        check_vma=False,
    )
```

profile of v0, /device:TPU:0, one launch (start us, length us, event | category | flops | bytes accessed | tf_op | source)
XLA Modules:
  0.0 114.0 jit_solution(1474697888466916771)
XLA Ops:
  0.0 0.8 slice_bitcast_fusion
  0.9 3.0 %collective-permute-start = (f32[4,8]{1,0:T(4,128)S(1)}, f32[4,8]{1,0:T(4,128)S(1)}, u32[]{:S(2)}, u32[]{:S(2)}) collective-permute-start(f32[4,8]{1,0:T(4,128)S(1)} %get-tuple-element.23), channel_id=1, source_target_pairs={{0,4},{4,8},{8,12},{12,0},{1,5},{5,9},{9,13},{13,1},{2,6},{6,10},{... | collective-permute-start | bytes 392 | tf_op jit(solution)/shard_map/ppermute | solution.py:17
  3.9 2.1 %collective-permute-start.1 = (f32[4,8]{1,0:T(4,128)S(1)}, f32[4,8]{1,0:T(4,128)S(1)}, u32[]{:S(2)}, u32[]{:S(2)}) collective-permute-start(f32[4,8]{1,0:T(4,128)S(1)} %get-tuple-element.24), channel_id=1, source_target_pairs={{4,0},{8,4},{12,8},{0,12},{5,1},{9,5},{13,9},{1,13},{6,2},{10,6},{... | collective-permute-start | bytes 392 | tf_op jit(solution)/shard_map/ppermute | solution.py:19
  6.0 3.6 %collective-permute-start.2 = (f32[4,128]{1,0:T(4,128)S(1)}, f32[4,128]{1,0:T(4,128)S(1)}, u32[]{:S(2)}, u32[]{:S(2)}) collective-permute-start(f32[4,128]{1,0:T(4,128)S(1)} %get-tuple-element.12), channel_id=1, source_target_pairs={{0,2},{1,3},{4,6},{5,7},{8,10},{9,11},{12,14},{13,15},{16,18},{17,... | collective-permute-start | bytes 6152 | tf_op jit(solution)/shard_map/ppermute | solution.py:29
  9.6 1.3 %collective-permute-start.5 = (f32[4,128]{1,0:T(4,128)S(1)}, f32[4,128]{1,0:T(4,128)S(1)}, u32[]{:S(2)}, u32[]{:S(2)}) collective-permute-start(f32[4,128]{1,0:T(4,128)S(1)} %get-tuple-element.11), channel_id=1, source_target_pairs={{0,2},{1,3},{4,6},{5,7},{8,10},{9,11},{12,14},{13,15},{16,18},{17,... | collective-permute-start | bytes 6152 | tf_op jit(solution)/shard_map/ppermute | solution.py:29
  10.9 1.3 %collective-permute-start.8 = (f32[4,128]{1,0:T(4,128)S(1)}, f32[4,128]{1,0:T(4,128)S(1)}, u32[]{:S(2)}, u32[]{:S(2)}) collective-permute-start(f32[4,128]{1,0:T(4,128)S(1)} %get-tuple-element.14), channel_id=1, source_target_pairs={{0,2},{1,3},{4,6},{5,7},{8,10},{9,11},{12,14},{13,15},{16,18},{17,... | collective-permute-start | bytes 6152 | tf_op jit(solution)/shard_map/ppermute | solution.py:29
  12.3 0.6 copy-done.2
  12.9 0.7 copy-done.6
  13.7 9.6 %all_gather.15 = bf16[8,4,512]{2,1,0:T(4,128)(2,1)S(1)} all-gather(bf16[8,4,128]{2,1,0:T(4,128)(2,1)S(1)} %convert_element_type.38), channel_id=1, replica_groups=mesh['groups'=2,'elem'=4,'lag'=2,'gust'=2] {'elem'}, dimensions={2}, use_global_device_ids=true | all-gather | bytes 40960 | tf_op jit(solution)/shard_map/all_gather | solution.py:46
  23.3 0.3 fusion
  23.6 1.3 %collective-permute-start.11 = (f32[4,128]{1,0:T(4,128)S(1)}, f32[4,128]{1,0:T(4,128)S(1)}, u32[]{:S(2)}, u32[]{:S(2)}) collective-permute-start(f32[4,128]{1,0:T(4,128)S(1)} %get-tuple-element.10), channel_id=1, source_target_pairs={{0,2},{1,3},{4,6},{5,7},{8,10},{9,11},{12,14},{13,15},{16,18},{17,... | collective-permute-start | bytes 6152 | tf_op jit(solution)/shard_map/ppermute | solution.py:29
  25.1 1.0 gather_fusion
  26.2 0.7 copy-done.4
  26.8 0.2 fusion.17
  27.1 0.6 copy-done.5
  27.7 0.4 fusion.7
  28.1 4.9 %psum.35 = f32[4,128]{1,0:T(4,128)S(1)} all-reduce(f32[4,128]{1,0:T(4,128)S(1)} %fusion.7), channel_id=1, replica_groups=mesh['groups'=2,'elem'=4,'lag'=2,'gust'=2] {'lag'}, use_global_device_ids=true, to_apply=%region_1.3 | all-reduce | flops 512 | bytes 4096 | tf_op jit(solution)/shard_map/psum | solution.py:62
  33.4 0.2 collective-permute-start.3
  33.6 3.7 %collective-permute-start.4 = (f32[4,8]{1,0:T(4,128)S(1)}, f32[4,8]{1,0:T(4,128)S(1)}, u32[]{:S(2)}, u32[]{:S(2)}) collective-permute-start(f32[4,8]{1,0:T(4,128)S(1)} %get-tuple-element.22), channel_id=1, source_target_pairs={{4,0},{8,4},{12,8},{0,12},{5,1},{9,5},{13,9},{1,13},{6,2},{10,6},{... | collective-permute-start | bytes 392 | tf_op jit(solution)/shard_map/ppermute | solution.py:19
  37.3 7.8 %all_gather.16 = bf16[8,4,512]{2,1,0:T(4,128)(2,1)S(1)} all-gather(bf16[8,4,128]{2,1,0:T(4,128)(2,1)S(1)} %fusion.25), channel_id=1, replica_groups=mesh['groups'=2,'elem'=4,'lag'=2,'gust'=2] {'elem'}, dimensions={2}, use_global_device_ids=true | all-gather | bytes 40960 | tf_op jit(solution)/shard_map/all_gather | solution.py:46
  45.4 1.0 gather_fusion.1
  46.4 0.2 fusion.15
  46.7 0.4 fusion.6
  47.1 4.9 %psum.36 = f32[4,128]{1,0:T(4,128)S(1)} all-reduce(f32[4,128]{1,0:T(4,128)S(1)} %fusion.6), channel_id=1, replica_groups=mesh['groups'=2,'elem'=4,'lag'=2,'gust'=2] {'lag'}, use_global_device_ids=true, to_apply=%region_3.5 | all-reduce | flops 512 | bytes 4096 | tf_op jit(solution)/shard_map/psum | solution.py:62
  52.4 2.0 %collective-permute-start.6 = (f32[4,8]{1,0:T(4,128)S(1)}, f32[4,8]{1,0:T(4,128)S(1)}, u32[]{:S(2)}, u32[]{:S(2)}) collective-permute-start(f32[4,8]{1,0:T(4,128)S(1)} %get-tuple-element.19), channel_id=1, source_target_pairs={{0,4},{4,8},{8,12},{12,0},{1,5},{5,9},{9,13},{13,1},{2,6},{6,10},{... | collective-permute-start | bytes 392 | tf_op jit(solution)/shard_map/ppermute | solution.py:17
  54.3 1.9 %collective-permute-start.7 = (f32[4,8]{1,0:T(4,128)S(1)}, f32[4,8]{1,0:T(4,128)S(1)}, u32[]{:S(2)}, u32[]{:S(2)}) collective-permute-start(f32[4,8]{1,0:T(4,128)S(1)} %get-tuple-element.20), channel_id=1, source_target_pairs={{4,0},{8,4},{12,8},{0,12},{5,1},{9,5},{13,9},{1,13},{6,2},{10,6},{... | collective-permute-start | bytes 392 | tf_op jit(solution)/shard_map/ppermute | solution.py:19
  56.3 8.0 %all_gather.17 = bf16[8,4,512]{2,1,0:T(4,128)(2,1)S(1)} all-gather(bf16[8,4,128]{2,1,0:T(4,128)(2,1)S(1)} %fusion.24), channel_id=1, replica_groups=mesh['groups'=2,'elem'=4,'lag'=2,'gust'=2] {'elem'}, dimensions={2}, use_global_device_ids=true | all-gather | bytes 40960 | tf_op jit(solution)/shard_map/all_gather | solution.py:46
  64.6 1.0 gather_fusion.2
  65.6 0.2 fusion.13
  65.9 0.4 fusion.5
  66.3 4.9 %psum.37 = f32[4,128]{1,0:T(4,128)S(1)} all-reduce(f32[4,128]{1,0:T(4,128)S(1)} %fusion.5), channel_id=1, replica_groups=mesh['groups'=2,'elem'=4,'lag'=2,'gust'=2] {'lag'}, use_global_device_ids=true, to_apply=%region_5.7 | all-reduce | flops 512 | bytes 4096 | tf_op jit(solution)/shard_map/psum | solution.py:62
  71.6 1.9 %collective-permute-start.10 = (f32[4,8]{1,0:T(4,128)S(1)}, f32[4,8]{1,0:T(4,128)S(1)}, u32[]{:S(2)}, u32[]{:S(2)}) collective-permute-start(f32[4,8]{1,0:T(4,128)S(1)} %get-tuple-element.18), channel_id=1, source_target_pairs={{4,0},{8,4},{12,8},{0,12},{5,1},{9,5},{13,9},{1,13},{6,2},{10,6},{... | collective-permute-start | bytes 392 | tf_op jit(solution)/shard_map/ppermute | solution.py:19
  73.5 8.0 %all_gather.18 = bf16[8,4,512]{2,1,0:T(4,128)(2,1)S(1)} all-gather(bf16[8,4,128]{2,1,0:T(4,128)(2,1)S(1)} %maximum_convert_fusion), channel_id=1, replica_groups=mesh['groups'=2,'elem'=4,'lag'=2,'gust'=2] {'elem'}, dimensions={2}, use_global_device_ids=true | all-gather | bytes 40960 | tf_op jit(solution)/shard_map/all_gather | solution.py:46
  81.5 1.7 %collective-permute-start.9 = (f32[4,8]{1,0:T(4,128)S(1)}, f32[4,8]{1,0:T(4,128)S(1)}, u32[]{:S(2)}, u32[]{:S(2)}) collective-permute-start(f32[4,8]{1,0:T(4,128)S(1)} %get-tuple-element.17), channel_id=1, source_target_pairs={{0,4},{4,8},{8,12},{12,0},{1,5},{5,9},{9,13},{13,1},{2,6},{6,10},{... | collective-permute-start | bytes 392 | tf_op jit(solution)/shard_map/ppermute | solution.py:17
  83.3 3.7 %collective-permute-done.9 = f32[4,8]{1,0:T(4,128)S(1)} collective-permute-done((f32[4,8]{1,0:T(4,128)S(1)}, f32[4,8]{1,0:T(4,128)S(1)}, u32[]{:S(2)}, u32[]{:S(2)}) %collective-permute-start.9) | collective-permute-done | bytes 160 | tf_op jit(solution)/shard_map/ppermute | solution.py:17
  87.1 1.0 gather_fusion.3
  88.2 0.2 fusion.11
  88.4 0.4 fusion.4
  88.8 4.9 %psum.38 = f32[4,128]{1,0:T(4,128)S(1)} all-reduce(f32[4,128]{1,0:T(4,128)S(1)} %fusion.4), channel_id=1, replica_groups=mesh['groups'=2,'elem'=4,'lag'=2,'gust'=2] {'lag'}, use_global_device_ids=true, to_apply=%region_7.9 | all-reduce | flops 512 | bytes 4096 | tf_op jit(solution)/shard_map/psum | solution.py:62
  93.8 0.2 constant_dynamic-update-slice_fusion
  94.1 0.5 copy-done.7
  94.6 3.8 %collective-permute-start.13 = (f32[4,8]{1,0:T(4,128)S(1)}, f32[4,8]{1,0:T(4,128)S(1)}, u32[]{:S(2)}, u32[]{:S(2)}) collective-permute-start(f32[4,8]{1,0:T(4,128)S(1)} %get-tuple-element.16), channel_id=1, source_target_pairs={{4,0},{8,4},{12,8},{0,12},{5,1},{9,5},{13,9},{1,13},{6,2},{10,6},{... | collective-permute-start | bytes 392 | tf_op jit(solution)/shard_map/ppermute | solution.py:19
  98.4 7.8 %all_gather.19 = bf16[8,4,512]{2,1,0:T(4,128)(2,1)S(1)} all-gather(bf16[8,4,128]{2,1,0:T(4,128)(2,1)S(1)} %pad_maximum_fusion.2), channel_id=1, replica_groups=mesh['groups'=2,'elem'=4,'lag'=2,'gust'=2] {'elem'}, dimensions={2}, use_global_device_ids=true | all-gather | bytes 40960 | tf_op jit(solution)/shard_map/all_gather | solution.py:46
  106.6 1.0 gather_fusion.4
  107.6 0.2 fusion.9
  107.9 0.4 fusion.3
  108.3 4.9 %psum.39 = f32[4,128]{1,0:T(4,128)S(1)} all-reduce(f32[4,128]{1,0:T(4,128)S(1)} %fusion.3), channel_id=1, replica_groups=mesh['groups'=2,'elem'=4,'lag'=2,'gust'=2] {'lag'}, use_global_device_ids=true, to_apply=%region_9.11 | all-reduce | flops 512 | bytes 4096 | tf_op jit(solution)/shard_map/psum | solution.py:62
  113.2 0.8 fusion.2
  (72 shorter events, 3.0 us)
Async XLA Ops:
  0.0 27.1 %copy-start = (bf16[8,128,512]{2,1,0:T(8,128)(2,1)S(1)}, bf16[8,128,512]{2,1,0:T(8,128)(2,1)}, u32[]{:S(2)}) copy-start(bf16[8,128,512]{2,1,0:T(8,128)(2,1)} %param.11) | copy-start | bytes 3145732
  0.9 22.7 %collective-permute-start = (f32[4,8]{1,0:T(4,128)S(1)}, f32[4,8]{1,0:T(4,128)S(1)}, u32[]{:S(2)}, u32[]{:S(2)}) collective-permute-start(f32[4,8]{1,0:T(4,128)S(1)} %get-tuple-element.23), channel_id=1, source_target_pairs={{0,4},{4,8},{8,12},{12,0},{1,5},{5,9},{9,13},{13,1},{2,6},{6,10},{... | collective-permute-start | bytes 392 | tf_op jit(solution)/shard_map/ppermute | solution.py:17
  3.9 21.0 %collective-permute-start.1 = (f32[4,8]{1,0:T(4,128)S(1)}, f32[4,8]{1,0:T(4,128)S(1)}, u32[]{:S(2)}, u32[]{:S(2)}) collective-permute-start(f32[4,8]{1,0:T(4,128)S(1)} %get-tuple-element.24), channel_id=1, source_target_pairs={{4,0},{8,4},{12,8},{0,12},{5,1},{9,5},{13,9},{1,13},{6,2},{10,6},{... | collective-permute-start | bytes 392 | tf_op jit(solution)/shard_map/ppermute | solution.py:19
  6.0 27.0 %collective-permute-start.2 = (f32[4,128]{1,0:T(4,128)S(1)}, f32[4,128]{1,0:T(4,128)S(1)}, u32[]{:S(2)}, u32[]{:S(2)}) collective-permute-start(f32[4,128]{1,0:T(4,128)S(1)} %get-tuple-element.12), channel_id=1, source_target_pairs={{0,2},{1,3},{4,6},{5,7},{8,10},{9,11},{12,14},{13,15},{16,18},{17,... | collective-permute-start | bytes 6152 | tf_op jit(solution)/shard_map/ppermute | solution.py:29
  9.6 42.5 %collective-permute-start.5 = (f32[4,128]{1,0:T(4,128)S(1)}, f32[4,128]{1,0:T(4,128)S(1)}, u32[]{:S(2)}, u32[]{:S(2)}) collective-permute-start(f32[4,128]{1,0:T(4,128)S(1)} %get-tuple-element.11), channel_id=1, source_target_pairs={{0,2},{1,3},{4,6},{5,7},{8,10},{9,11},{12,14},{13,15},{16,18},{17,... | collective-permute-start | bytes 6152 | tf_op jit(solution)/shard_map/ppermute | solution.py:29
  10.9 60.3 %collective-permute-start.8 = (f32[4,128]{1,0:T(4,128)S(1)}, f32[4,128]{1,0:T(4,128)S(1)}, u32[]{:S(2)}, u32[]{:S(2)}) collective-permute-start(f32[4,128]{1,0:T(4,128)S(1)} %get-tuple-element.14), channel_id=1, source_target_pairs={{0,2},{1,3},{4,6},{5,7},{8,10},{9,11},{12,14},{13,15},{16,18},{17,... | collective-permute-start | bytes 6152 | tf_op jit(solution)/shard_map/ppermute | solution.py:29
  12.2 0.7 copy-start.2
  12.9 0.7 copy-start.6
  13.6 9.6 %copy-start.8 = (s32[8,1,4]{0,2,1:T(4,128)S(1)}, s32[8,1,4]{0,2,1:T(4,128)}, u32[]{:S(2)}) copy-start(s32[8,1,4]{0,2,1:T(4,128)} %param.12) | copy-start | bytes 388
  23.6 70.4 %collective-permute-start.11 = (f32[4,128]{1,0:T(4,128)S(1)}, f32[4,128]{1,0:T(4,128)S(1)}, u32[]{:S(2)}, u32[]{:S(2)}) collective-permute-start(f32[4,128]{1,0:T(4,128)S(1)} %get-tuple-element.10), channel_id=1, source_target_pairs={{0,2},{1,3},{4,6},{5,7},{8,10},{9,11},{12,14},{13,15},{16,18},{17,... | collective-permute-start | bytes 6152 | tf_op jit(solution)/shard_map/ppermute | solution.py:29
  26.1 0.7 copy-start.4
  27.0 0.7 copy-start.5
  27.7 5.3 %copy-start.1 = (f32[128,128]{1,0:T(8,128)S(1)}, f32[128,128]{1,0:T(8,128)}, u32[]{:S(2)}) copy-start(f32[128,128]{1,0:T(8,128)} %param.13) | copy-start | bytes 196612
  33.4 11.8 %collective-permute-start.3 = (f32[4,8]{1,0:T(4,128)S(1)}, f32[4,8]{1,0:T(4,128)S(1)}, u32[]{:S(2)}, u32[]{:S(2)}) collective-permute-start(f32[4,8]{1,0:T(4,128)S(1)} %get-tuple-element.21), channel_id=1, source_target_pairs={{0,4},{4,8},{8,12},{12,0},{1,5},{5,9},{9,13},{13,1},{2,6},{6,10},{... | collective-permute-start | bytes 392 | tf_op jit(solution)/shard_map/ppermute | solution.py:17
  33.6 11.6 %collective-permute-start.4 = (f32[4,8]{1,0:T(4,128)S(1)}, f32[4,8]{1,0:T(4,128)S(1)}, u32[]{:S(2)}, u32[]{:S(2)}) collective-permute-start(f32[4,8]{1,0:T(4,128)S(1)} %get-tuple-element.22), channel_id=1, source_target_pairs={{4,0},{8,4},{12,8},{0,12},{5,1},{9,5},{13,9},{1,13},{6,2},{10,6},{... | collective-permute-start | bytes 392 | tf_op jit(solution)/shard_map/ppermute | solution.py:19
  52.4 12.0 %collective-permute-start.6 = (f32[4,8]{1,0:T(4,128)S(1)}, f32[4,8]{1,0:T(4,128)S(1)}, u32[]{:S(2)}, u32[]{:S(2)}) collective-permute-start(f32[4,8]{1,0:T(4,128)S(1)} %get-tuple-element.19), channel_id=1, source_target_pairs={{0,4},{4,8},{8,12},{12,0},{1,5},{5,9},{9,13},{13,1},{2,6},{6,10},{... | collective-permute-start | bytes 392 | tf_op jit(solution)/shard_map/ppermute | solution.py:17
  54.3 10.0 %collective-permute-start.7 = (f32[4,8]{1,0:T(4,128)S(1)}, f32[4,8]{1,0:T(4,128)S(1)}, u32[]{:S(2)}, u32[]{:S(2)}) collective-permute-start(f32[4,8]{1,0:T(4,128)S(1)} %get-tuple-element.20), channel_id=1, source_target_pairs={{4,0},{8,4},{12,8},{0,12},{5,1},{9,5},{13,9},{1,13},{6,2},{10,6},{... | collective-permute-start | bytes 392 | tf_op jit(solution)/shard_map/ppermute | solution.py:19
  71.6 11.6 %collective-permute-start.10 = (f32[4,8]{1,0:T(4,128)S(1)}, f32[4,8]{1,0:T(4,128)S(1)}, u32[]{:S(2)}, u32[]{:S(2)}) collective-permute-start(f32[4,8]{1,0:T(4,128)S(1)} %get-tuple-element.18), channel_id=1, source_target_pairs={{4,0},{8,4},{12,8},{0,12},{5,1},{9,5},{13,9},{1,13},{6,2},{10,6},{... | collective-permute-start | bytes 392 | tf_op jit(solution)/shard_map/ppermute | solution.py:19
  73.5 9.8 %copy-start.3 = (bf16[8,4,128]{2,1,0:T(4,128)(2,1)}, bf16[8,4,128]{2,1,0:T(4,128)(2,1)S(1)}, u32[]{:S(2)}) copy-start(bf16[8,4,128]{2,1,0:T(4,128)(2,1)S(1)} %maximum_convert_fusion) | copy-start | bytes 24580
  81.5 5.4 %collective-permute-start.9 = (f32[4,8]{1,0:T(4,128)S(1)}, f32[4,8]{1,0:T(4,128)S(1)}, u32[]{:S(2)}, u32[]{:S(2)}) collective-permute-start(f32[4,8]{1,0:T(4,128)S(1)} %get-tuple-element.17), channel_id=1, source_target_pairs={{0,4},{4,8},{8,12},{12,0},{1,5},{5,9},{9,13},{13,1},{2,6},{6,10},{... | collective-permute-start | bytes 392 | tf_op jit(solution)/shard_map/ppermute | solution.py:17
  93.9 0.7 copy-start.7
  94.0 4.4 %slice-start = ((bf16[8,4,128]{2,1,0:T(4,128)(2,1)}), bf16[7,4,128]{2,1,0:T(4,128)(2,1)S(1)}, s32[]{:S(2)}) async-start(bf16[8,4,128]{2,1,0:T(4,128)(2,1)} %copy-done.3), calls=%async_computation | async-start | bytes 14336 | tf_op jit(solution)/shard_map/slice | solution.py:68
  94.6 11.8 %collective-permute-start.12 = (f32[4,8]{1,0:T(4,128)S(1)}, f32[4,8]{1,0:T(4,128)S(1)}, u32[]{:S(2)}, u32[]{:S(2)}) collective-permute-start(f32[4,8]{1,0:T(4,128)S(1)} %get-tuple-element.15), channel_id=1, source_target_pairs={{0,4},{4,8},{8,12},{12,0},{1,5},{5,9},{9,13},{13,1},{2,6},{6,10},{... | collective-permute-start | bytes 392 | tf_op jit(solution)/shard_map/ppermute | solution.py:17
  94.6 11.8 %collective-permute-start.13 = (f32[4,8]{1,0:T(4,128)S(1)}, f32[4,8]{1,0:T(4,128)S(1)}, u32[]{:S(2)}, u32[]{:S(2)}) collective-permute-start(f32[4,8]{1,0:T(4,128)S(1)} %get-tuple-element.16), channel_id=1, source_target_pairs={{4,0},{8,4},{12,8},{0,12},{5,1},{9,5},{13,9},{1,13},{6,2},{10,6},{... | collective-permute-start | bytes 392 | tf_op jit(solution)/shard_map/ppermute | solution.py:19
where the time goes:
time: 115 us; the launch traced here: 114 us
  blocking collectives  66 us (57%)
  starting transfers between devices  27.7 us (24%)
  local copies, waits for them, and re-layouts  11 us (10%)
  matrix products  3.74 us (3%)
  waiting for transfers between devices  3.73 us (3%)
  other arithmetic  1.56 us (1%)
    all_gather x5, blocking collectives, on_device(): piece = lax.all_gather(rounded, 'elem', axis=2, tiled=True)  41.3 us
    psum x5, blocking collectives, on_device(): drive = lax.psum(first_flag * (forcing[step] + gradient) - retarded, 'lag')  24.7 us
    ppermute x5, starting transfers between devices, with_halo(): lax.ppermute(head, axis, [((i + 1) % count, i) for i in range(count)])  13.3 us
    ppermute x4, starting transfers between devices, from_behind(): lax.ppermute(value, axis, [(source, source + steps) for source in range(f...  7.45 us
    ppermute x5, starting transfers between devices, with_halo(): lax.ppermute(tail, axis, [(i, (i + 1) % count) for i in range(count)])  6.92 us
    gather x5, local copies, waits for them, and re-layouts, on_device(): across = jnp.take(padded, local_index, axis=1)  5.18 us
    ppermute x5, waiting for transfers between devices, with_halo(): lax.ppermute(tail, axis, [(i, (i + 1) % count) for i in range(count)])  3.66 us
    unnamed x21, local copies, waits for them, and re-layouts  3.12 us
  transfers between devices with their start and end apart: 14, of which 1 were waited for; matrix products, arithmetic and copies ran while one was open for 8% of the time, Pallas kernels for 0%

commit v1 on v0

v1 whole, which is shorter than its diff:
```python
import jax
import jax.numpy as jnp
from jax import lax
from jax.sharding import PartitionSpec as P

RIM = 8
STEPS = 5
FEW = 4


def gathered(value, dim):
    count = lax.axis_size("elem")
    if count > FEW or count & (count - 1):
        return lax.all_gather(value, "elem", axis=dim, tiled=True)
    place = lax.axis_index("elem")
    pieces = [value] + [
        lax.ppermute(value, "elem", [(i, i ^ flip) for i in range(count)])
        for flip in range(1, count)
    ]
    ordered = []
    for block in range(count):
        chosen = pieces[0]
        for flip in range(1, count):
            chosen = jnp.where(place ^ flip == block, pieces[flip], chosen)
        ordered.append(chosen)
    return jnp.concatenate(ordered, axis=dim)


def on_device(history, forcing, interaction, block_mask, correction, neighbours, edge_coef):
    precise = lax.Precision.HIGHEST
    rows = correction.shape[0]
    blocks = lax.axis_size("elem")
    total = rows * blocks
    lags, gusts, _ = history.shape
    lag_count = lax.axis_size("lag")
    lag_place = lax.axis_index("lag")
    own_start = lax.axis_index("elem") * rows
    late = STEPS - 1
    assert lags >= late

    live = jnp.repeat(block_mask[:, 0, :].astype(jnp.bfloat16), rows, axis=1)
    masked = interaction * live[:, None, :]

    own_places = own_start + jnp.arange(rows, dtype=jnp.int32)
    offsets = (neighbours - own_places[None, :] + RIM) % total
    spread = [
        jnp.sum(jnp.where(offsets == d, edge_coef, 0.0), axis=0) for d in range(2 * RIM + 1)
    ]

    def gradient_of(full):
        wide = jnp.concatenate([full[:, total - RIM :], full, full[:, :RIM]], axis=1)
        window = lax.dynamic_slice(wide, (0, own_start), (gusts, rows + 2 * RIM))
        own = window[:, RIM : RIM + rows]
        out = jnp.zeros_like(own)
        for d in range(2 * RIM + 1):
            if d != RIM:
                out += spread[d][None] * (window[:, d : d + rows] - own)
        return out

    hist = gathered(history.astype(jnp.bfloat16), 2)
    newest = gathered(history[0], 1)
    before = lax.ppermute(
        hist[lags - late :], "lag", [(i, (i + 1) % lag_count) for i in range(lag_count)]
    )
    before = jnp.where(lag_place == 0, jnp.zeros_like(before), before)
    longer = jnp.concatenate([before, hist], axis=0)
    stacked = jnp.stack(
        [longer[late - step : late - step + lags] for step in range(STEPS)], axis=1
    ).reshape(lags, STEPS * gusts, total)
    partial = jnp.einsum("lmc,lrc->mr", stacked, masked, preferred_element_type=jnp.float32)
    known = lax.psum(partial.reshape(STEPS, gusts, rows), "lag")
    base = forcing - known

    fresh_b = []
    results = []
    for step in range(STEPS):
        drive = base[step] + gradient_of(newest)
        if step:
            past = jnp.stack(fresh_b[::-1], axis=0)
            drive -= jnp.einsum(
                "lgc,lrc->gr", past, masked[:step], preferred_element_type=jnp.float32
            )
        fresh = drive + jnp.dot(drive, correction.T, precision=precise)
        results.append(fresh)
        if step < late:
            newest = gathered(fresh, 1)
            fresh_b.append(newest.astype(jnp.bfloat16))
    mine = jnp.stack(results, 0)
    return lax.psum(jnp.where(lag_place == 0, mine, 0.0), "lag")


def solution(mesh):
    placed = (
        P("lag", ("groups", "gust"), "elem"),
        P(None, ("groups", "gust"), "elem"),
        P("lag", "elem", None),
        P("lag", "elem", None),
        P("elem", None),
        P(None, "elem"),
        P(None, "elem"),
    )
    return jax.shard_map(
        on_device,
        mesh=mesh,
        in_specs=placed,
        out_specs=P(None, ("groups", "gust"), "elem"),
        check_vma=False,
    )
```

time: 115 us -> 65.9 us (0.57)
  blocking collectives: 66 us -> 15.9 us
  waiting for transfers between devices: 3.73 us -> 13.6 us
  local copies, waits for them, and re-layouts: 11 us -> 2.49 us
  starting transfers between devices: 27.7 us -> 29.4 us
  matrix products: 3.74 us -> 2.46 us
    all_gather x5 -> x0, blocking collectives: 41.3 us -> none  [on_device(): piece = lax.all_gather(rounded, 'elem', axis=2, tiled=True)]
    ppermute x14 -> x19, waiting for transfers between devices: 3.73 us -> 13.6 us  [the longest x18 11.4 us: gathered(): lax.ppermute(value, 'elem', [(i, i ^ flip) for i in range(count)])]
    psum x5 -> x2, blocking collectives: 24.7 us -> 15.9 us  [the longest x1 8.16 us: on_device(): known = lax.psum(partial.reshape(STEPS, gusts, rows), 'lag')]
    gather x5 -> x0, local copies, waits for them, and re-layouts: 5.18 us -> none  [on_device(): across = jnp.take(padded, local_index, axis=1)]
    ppermute x14 -> x19, starting transfers between devices: 27.7 us -> 29.4 us  [the longest x18 27.9 us: gathered(): lax.ppermute(value, 'elem', [(i, i ^ flip) for i in range(count)])]
    unnamed x21 -> x16, local copies, waits for them, and re-layouts: 3.12 us -> 1.54 us
    mul x0 -> x1, other arithmetic: none -> 1.33 us  [on_device(): masked = interaction * live[:, None, :]]
  transfers between devices with their start and end apart: 14 -> 19, of which waited for: 1 -> 12; matrix products, arithmetic and copies ran while one was open for 8% -> 2% of each run, Pallas kernels for 0% -> 0%
where the time goes in v1:
time: 65.9 us; the launch traced here: 65.7 us
  starting transfers between devices  29.4 us (45%)
  blocking collectives  15.9 us (24%)
  waiting for transfers between devices  13.6 us (21%)
  local copies, waits for them, and re-layouts  2.49 us (4%)
  matrix products  2.46 us (4%)
  other arithmetic  1.55 us (2%)
    ppermute x18, starting transfers between devices, gathered(): lax.ppermute(value, 'elem', [(i, i ^ flip) for i in range(count)])  27.9 us
    ppermute x18, waiting for transfers between devices, gathered(): lax.ppermute(value, 'elem', [(i, i ^ flip) for i in range(count)])  11.4 us
    psum x1, blocking collectives, on_device(): known = lax.psum(partial.reshape(STEPS, gusts, rows), 'lag')  8.16 us
    psum x1, blocking collectives, on_device(): return lax.psum(jnp.where(lag_place == 0, mine, 0.0), 'lag')  7.72 us
    ppermute x1, waiting for transfers between devices, on_device(): lax.ppermute(hist[lags - late:], 'lag', [(i, (i + 1) % lag_count) for i i...  2.24 us
    ppermute x1, starting transfers between devices, on_device(): lax.ppermute(hist[lags - late:], 'lag', [(i, (i + 1) % lag_count) for i i...  1.56 us
    unnamed x16, local copies, waits for them, and re-layouts  1.54 us
    mul x1, other arithmetic, on_device(): masked = interaction * live[:, None, :]  1.33 us
  transfers between devices with their start and end apart: 19, of which 12 were waited for; matrix products, arithmetic and copies ran while one was open for 2% of the time, Pallas kernels for 0%

profile of v1, /device:TPU:0, one launch (start us, length us, event | category | flops | bytes accessed | tf_op | source)
XLA Modules:
  0.0 65.7 jit_solution(3122565437625074362)
XLA Ops:
  0.0 0.8 %copy.29 = bf16[8,4,128]{2,0,1:T(8,128)(2,1)S(1)} copy(f32[8,4,128]{2,1,0:T(4,128)} %param.7) | data formatting | bytes 24576 | tf_op args[0]
  0.8 5.0 %collective-permute-start = (bf16[8,4,128]{2,0,1:T(8,128)(2,1)S(1)}, bf16[8,4,128]{2,0,1:T(8,128)(2,1)S(1)}, u32[]{:S(2)}, u32[]{:S(2)}) collective-permute-start(bf16[8,4,128]{2,0,1:T(8,128)(2,1)S(1)} %copy.29), channel_id=1, source_target_pairs={{0,12},{4,8},{8,4},{12,0},{1,13},{5,9},{9,5},{13,1},{2,14},{6,10},... | collective-permute-start | bytes 24584 | tf_op jit(solution)/shard_map/ppermute | solution.py:17
  5.9 1.9 %collective-permute-start.4 = (f32[4,128]{1,0:T(4,128)S(1)}, f32[4,128]{1,0:T(4,128)S(1)}, u32[]{:S(2)}, u32[]{:S(2)}) collective-permute-start(f32[4,128]{1,0:T(4,128)S(1)} %slice_bitcast_fusion.6), channel_id=1, source_target_pairs={{0,12},{4,8},{8,4},{12,0},{1,13},{5,9},{9,5},{13,1},{2,14},{6,10},... | collective-permute-start | bytes 6152 | tf_op jit(solution)/shard_map/ppermute | solution.py:17
  7.8 1.1 %collective-permute-start.5 = (f32[4,128]{1,0:T(4,128)S(1)}, f32[4,128]{1,0:T(4,128)S(1)}, u32[]{:S(2)}, u32[]{:S(2)}) collective-permute-start(f32[4,128]{1,0:T(4,128)S(1)} %slice_bitcast_fusion.6), channel_id=1, source_target_pairs={{0,8},{4,12},{8,0},{12,4},{1,9},{5,13},{9,1},{13,5},{2,10},{6,14},... | collective-permute-start | bytes 6152 | tf_op jit(solution)/shard_map/ppermute | solution.py:17
  8.8 1.5 %collective-permute-start.6 = (f32[4,128]{1,0:T(4,128)S(1)}, f32[4,128]{1,0:T(4,128)S(1)}, u32[]{:S(2)}, u32[]{:S(2)}) collective-permute-start(f32[4,128]{1,0:T(4,128)S(1)} %slice_bitcast_fusion.6), channel_id=1, source_target_pairs={{0,4},{4,0},{8,12},{12,8},{1,5},{5,1},{9,13},{13,9},{2,6},{6,2},{1... | collective-permute-start | bytes 6152 | tf_op jit(solution)/shard_map/ppermute | solution.py:17
  10.3 0.7 %copy-done.5 = s32[8,1,4]{0,2,1:T(4,128)S(1)} copy-done((s32[8,1,4]{0,2,1:T(4,128)S(1)}, s32[8,1,4]{0,2,1:T(4,128)}, u32[]{:S(2)}) %copy-start.5) | copy-done | bytes 152
  11.1 1.3 %broadcast_multiply_fusion = bf16[8,128,512]{2,1,0:T(8,128)(2,1)S(1)} fusion(bf16[8,128,512]{2,1,0:T(8,128)(2,1)} %param.9, bf16[8,512]{1,0:T(8,128)(2,1)S(1)} %broadcast_bitcast_fusion), kind=kLoop, calls=%fused_computation.17 | loop fusion | flops 524288 | bytes 2105344 | tf_op jit(solution)/shard_map/mul | solution.py:42
  12.5 0.6 collective-permute-start.2
  13.2 0.1 concatenate.107
  13.4 2.9 %collective-permute-done.2 = bf16[8,4,128]{2,0,1:T(8,128)(2,1)S(1)} collective-permute-done((bf16[8,4,128]{2,0,1:T(8,128)(2,1)S(1)}, bf16[8,4,128]{2,0,1:T(8,128)(2,1)S(1)}, u32[]{:S(2)}, u32[]{:S(2)}) %collective-permute-start.2) | collective-permute-done | bytes 8224 | tf_op jit(solution)/shard_map/ppermute | solution.py:17
  16.3 1.6 %collective-permute-start.3 = (bf16[4,4,512]{2,0,1:T(4,128)(2,1)S(1)}, bf16[4,4,512]{2,0,1:T(4,128)(2,1)S(1)}, u32[]{:S(2)}, u32[]{:S(2)}) collective-permute-start(bf16[4,4,512]{2,0,1:T(4,128)(2,1)S(1)} %slice.440), channel_id=1, source_target_pairs={{0,2},{2,0},{1,3},{3,1},{4,6},{6,4},{5,7},{7,5},{8,10},{10,8},{9,1... | collective-permute-start | bytes 49160 | tf_op jit(solution)/shard_map/ppermute | solution.py:62
  17.9 2.2 %collective-permute-done.3 = bf16[4,4,512]{2,0,1:T(4,128)(2,1)S(1)} collective-permute-done((bf16[4,4,512]{2,0,1:T(4,128)(2,1)S(1)}, bf16[4,4,512]{2,0,1:T(4,128)(2,1)S(1)}, u32[]{:S(2)}, u32[]{:S(2)}) %collective-permute-start.3) | collective-permute-done | bytes 16416 | tf_op jit(solution)/shard_map/ppermute | solution.py:62
  20.2 0.5 convolution_bitcast_fusion
  20.7 8.2 %psum.14 = f32[5,4,128]{2,0,1:T(8,128)S(1)} all-reduce(f32[5,4,128]{2,0,1:T(8,128)S(1)} %convolution_bitcast_fusion), channel_id=1, replica_groups=mesh['groups'=2,'elem'=4,'lag'=2,'gust'=2] {'lag'}, use_global_device_ids=true, to_apply=%region_0.1 | all-reduce | flops 2560 | bytes 20480 | tf_op jit(solution)/shard_map/psum | solution.py:71
  28.9 0.3 constant_dynamic-update-slice_fusion.3
  29.2 1.9 %collective-permute-start.7 = (f32[4,128]{1,0:T(4,128)S(1)}, f32[4,128]{1,0:T(4,128)S(1)}, u32[]{:S(2)}, u32[]{:S(2)}) collective-permute-start(f32[4,128]{1,0:T(4,128)S(1)} %get-tuple-element.91), channel_id=1, source_target_pairs={{0,12},{4,8},{8,4},{12,0},{1,13},{5,9},{9,5},{13,1},{2,14},{6,10},... | collective-permute-start | bytes 6152 | tf_op jit(solution)/shard_map/ppermute | solution.py:17
  31.1 0.2 collective-permute-start.8
  31.3 2.4 %collective-permute-start.9 = (f32[4,128]{1,0:T(4,128)S(1)}, f32[4,128]{1,0:T(4,128)S(1)}, u32[]{:S(2)}, u32[]{:S(2)}) collective-permute-start(f32[4,128]{1,0:T(4,128)S(1)} %get-tuple-element.91), channel_id=1, source_target_pairs={{0,4},{4,0},{8,12},{12,8},{1,5},{5,1},{9,13},{13,9},{2,6},{6,2},{1... | collective-permute-start | bytes 6152 | tf_op jit(solution)/shard_map/ppermute | solution.py:17
  33.7 1.0 %collective-permute-done.7 = f32[4,128]{1,0:T(4,128)S(1)} collective-permute-done((f32[4,128]{1,0:T(4,128)S(1)}, f32[4,128]{1,0:T(4,128)S(1)}, u32[]{:S(2)}, u32[]{:S(2)}) %collective-permute-start.7) | collective-permute-done | bytes 2080 | tf_op jit(solution)/shard_map/ppermute | solution.py:17
  34.7 1.0 %collective-permute-done.8 = f32[4,128]{1,0:T(4,128)S(1)} collective-permute-done((f32[4,128]{1,0:T(4,128)S(1)}, f32[4,128]{1,0:T(4,128)S(1)}, u32[]{:S(2)}, u32[]{:S(2)}) %collective-permute-start.8) | collective-permute-done | bytes 2080 | tf_op jit(solution)/shard_map/ppermute | solution.py:17
  35.7 0.1 concatenate.108
  35.8 0.2 convolution_subtract_fusion
  36.0 0.2 constant_dynamic-update-slice_fusion.2
  36.2 2.2 %collective-permute-start.10 = (f32[4,128]{1,0:T(4,128)S(1)}, f32[4,128]{1,0:T(4,128)S(1)}, u32[]{:S(2)}, u32[]{:S(2)}) collective-permute-start(f32[4,128]{1,0:T(4,128)S(1)} %get-tuple-element.93), channel_id=1, source_target_pairs={{0,12},{4,8},{8,4},{12,0},{1,13},{5,9},{9,5},{13,1},{2,14},{6,10},... | collective-permute-start | bytes 6152 | tf_op jit(solution)/shard_map/ppermute | solution.py:17
  38.4 1.0 %collective-permute-start.11 = (f32[4,128]{1,0:T(4,128)S(1)}, f32[4,128]{1,0:T(4,128)S(1)}, u32[]{:S(2)}, u32[]{:S(2)}) collective-permute-start(f32[4,128]{1,0:T(4,128)S(1)} %get-tuple-element.93), channel_id=1, source_target_pairs={{0,8},{4,12},{8,0},{12,4},{1,9},{5,13},{9,1},{13,5},{2,10},{6,14},... | collective-permute-start | bytes 6152 | tf_op jit(solution)/shard_map/ppermute | solution.py:17
  39.3 1.3 %collective-permute-start.12 = (f32[4,128]{1,0:T(4,128)S(1)}, f32[4,128]{1,0:T(4,128)S(1)}, u32[]{:S(2)}, u32[]{:S(2)}) collective-permute-start(f32[4,128]{1,0:T(4,128)S(1)} %get-tuple-element.93), channel_id=1, source_target_pairs={{0,4},{4,0},{8,12},{12,8},{1,5},{5,1},{9,13},{13,9},{2,6},{6,2},{1... | collective-permute-start | bytes 6152 | tf_op jit(solution)/shard_map/ppermute | solution.py:17
  40.6 1.0 %collective-permute-done.10 = f32[4,128]{1,0:T(4,128)S(1)} collective-permute-done((f32[4,128]{1,0:T(4,128)S(1)}, f32[4,128]{1,0:T(4,128)S(1)}, u32[]{:S(2)}, u32[]{:S(2)}) %collective-permute-start.10) | collective-permute-done | bytes 2080 | tf_op jit(solution)/shard_map/ppermute | solution.py:17
  41.6 1.2 %collective-permute-done.11 = f32[4,128]{1,0:T(4,128)S(1)} collective-permute-done((f32[4,128]{1,0:T(4,128)S(1)}, f32[4,128]{1,0:T(4,128)S(1)}, u32[]{:S(2)}, u32[]{:S(2)}) %collective-permute-start.11) | collective-permute-done | bytes 2080 | tf_op jit(solution)/shard_map/ppermute | solution.py:17
  43.0 0.1 concatenate.110
  43.1 0.2 fusion.4
  43.3 0.2 constant_dynamic-update-slice_fusion.1
  43.5 1.9 %collective-permute-start.13 = (f32[4,128]{1,0:T(4,128)S(1)}, f32[4,128]{1,0:T(4,128)S(1)}, u32[]{:S(2)}, u32[]{:S(2)}) collective-permute-start(f32[4,128]{1,0:T(4,128)S(1)} %get-tuple-element.95), channel_id=1, source_target_pairs={{0,12},{4,8},{8,4},{12,0},{1,13},{5,9},{9,5},{13,1},{2,14},{6,10},... | collective-permute-start | bytes 6152 | tf_op jit(solution)/shard_map/ppermute | solution.py:17
  45.4 0.9 %collective-permute-start.14 = (f32[4,128]{1,0:T(4,128)S(1)}, f32[4,128]{1,0:T(4,128)S(1)}, u32[]{:S(2)}, u32[]{:S(2)}) collective-permute-start(f32[4,128]{1,0:T(4,128)S(1)} %get-tuple-element.95), channel_id=1, source_target_pairs={{0,8},{4,12},{8,0},{12,4},{1,9},{5,13},{9,1},{13,5},{2,10},{6,14},... | collective-permute-start | bytes 6152 | tf_op jit(solution)/shard_map/ppermute | solution.py:17
  46.3 1.6 %collective-permute-start.15 = (f32[4,128]{1,0:T(4,128)S(1)}, f32[4,128]{1,0:T(4,128)S(1)}, u32[]{:S(2)}, u32[]{:S(2)}) collective-permute-start(f32[4,128]{1,0:T(4,128)S(1)} %get-tuple-element.95), channel_id=1, source_target_pairs={{0,4},{4,0},{8,12},{12,8},{1,5},{5,1},{9,13},{13,9},{2,6},{6,2},{1... | collective-permute-start | bytes 6152 | tf_op jit(solution)/shard_map/ppermute | solution.py:17
  47.9 1.0 %collective-permute-done.13 = f32[4,128]{1,0:T(4,128)S(1)} collective-permute-done((f32[4,128]{1,0:T(4,128)S(1)}, f32[4,128]{1,0:T(4,128)S(1)}, u32[]{:S(2)}, u32[]{:S(2)}) %collective-permute-start.13) | collective-permute-done | bytes 2080 | tf_op jit(solution)/shard_map/ppermute | solution.py:17
  48.9 1.0 %collective-permute-done.14 = f32[4,128]{1,0:T(4,128)S(1)} collective-permute-done((f32[4,128]{1,0:T(4,128)S(1)}, f32[4,128]{1,0:T(4,128)S(1)}, u32[]{:S(2)}, u32[]{:S(2)}) %collective-permute-start.14) | collective-permute-done | bytes 2080 | tf_op jit(solution)/shard_map/ppermute | solution.py:17
  50.0 0.1 concatenate.121
  50.1 0.2 fusion
  50.3 0.2 constant_dynamic-update-slice_fusion
  50.5 2.2 %collective-permute-start.16 = (f32[4,128]{1,0:T(4,128)S(1)}, f32[4,128]{1,0:T(4,128)S(1)}, u32[]{:S(2)}, u32[]{:S(2)}) collective-permute-start(f32[4,128]{1,0:T(4,128)S(1)} %get-tuple-element.97), channel_id=1, source_target_pairs={{0,12},{4,8},{8,4},{12,0},{1,13},{5,9},{9,5},{13,1},{2,14},{6,10},... | collective-permute-start | bytes 6152 | tf_op jit(solution)/shard_map/ppermute | solution.py:17
  52.7 1.0 %collective-permute-start.17 = (f32[4,128]{1,0:T(4,128)S(1)}, f32[4,128]{1,0:T(4,128)S(1)}, u32[]{:S(2)}, u32[]{:S(2)}) collective-permute-start(f32[4,128]{1,0:T(4,128)S(1)} %get-tuple-element.97), channel_id=1, source_target_pairs={{0,8},{4,12},{8,0},{12,4},{1,9},{5,13},{9,1},{13,5},{2,10},{6,14},... | collective-permute-start | bytes 6152 | tf_op jit(solution)/shard_map/ppermute | solution.py:17
  53.6 1.3 %collective-permute-start.18 = (f32[4,128]{1,0:T(4,128)S(1)}, f32[4,128]{1,0:T(4,128)S(1)}, u32[]{:S(2)}, u32[]{:S(2)}) collective-permute-start(f32[4,128]{1,0:T(4,128)S(1)} %get-tuple-element.97), channel_id=1, source_target_pairs={{0,4},{4,0},{8,12},{12,8},{1,5},{5,1},{9,13},{13,9},{2,6},{6,2},{1... | collective-permute-start | bytes 6152 | tf_op jit(solution)/shard_map/ppermute | solution.py:17
  54.9 1.0 %collective-permute-done.16 = f32[4,128]{1,0:T(4,128)S(1)} collective-permute-done((f32[4,128]{1,0:T(4,128)S(1)}, f32[4,128]{1,0:T(4,128)S(1)}, u32[]{:S(2)}, u32[]{:S(2)}) %collective-permute-start.16) | collective-permute-done | bytes 2080 | tf_op jit(solution)/shard_map/ppermute | solution.py:17
  55.9 1.2 %collective-permute-done.17 = f32[4,128]{1,0:T(4,128)S(1)} collective-permute-done((f32[4,128]{1,0:T(4,128)S(1)}, f32[4,128]{1,0:T(4,128)S(1)}, u32[]{:S(2)}, u32[]{:S(2)}) %collective-permute-start.17) | collective-permute-done | bytes 2080 | tf_op jit(solution)/shard_map/ppermute | solution.py:17
  57.3 0.1 concatenate.127
  57.4 0.3 fusion.1
  57.7 0.2 fusion.3
  57.9 7.7 %psum.15 = f32[5,4,128]{2,1,0:T(4,128)} all-reduce(f32[5,4,128]{2,1,0:T(4,128)S(1)} %broadcast_select_fusion.1), channel_id=1, replica_groups=mesh['groups'=2,'elem'=4,'lag'=2,'gust'=2] {'lag'}, use_global_device_ids=true, to_apply=%region_17.18 | all-reduce | flops 2560 | bytes 20480 | tf_op jit(solution)/shard_map/psum | solution.py:89
  (49 shorter events, 0.9 us)
Async XLA Ops:
  0.0 28.9 %copy-start = (f32[128,128]{1,0:T(8,128)S(1)}, f32[128,128]{1,0:T(8,128)}, u32[]{:S(2)}) copy-start(f32[128,128]{1,0:T(8,128)} %param.11) | copy-start | bytes 196612
  0.0 5.8 %copy-start.1 = (f32[8,4,128]{2,1,0:T(4,128)S(1)}, f32[8,4,128]{2,1,0:T(4,128)}, u32[]{:S(2)}) copy-start(f32[8,4,128]{2,1,0:T(4,128)} %param.7) | copy-start | bytes 49156
  0.8 12.5 %collective-permute-start = (bf16[8,4,128]{2,0,1:T(8,128)(2,1)S(1)}, bf16[8,4,128]{2,0,1:T(8,128)(2,1)S(1)}, u32[]{:S(2)}, u32[]{:S(2)}) collective-permute-start(bf16[8,4,128]{2,0,1:T(8,128)(2,1)S(1)} %copy.29), channel_id=1, source_target_pairs={{0,12},{4,8},{8,4},{12,0},{1,13},{5,9},{9,5},{13,1},{2,14},{6,10},... | collective-permute-start | bytes 24584 | tf_op jit(solution)/shard_map/ppermute | solution.py:17
  5.8 7.5 %collective-permute-start.1 = (bf16[8,4,128]{2,0,1:T(8,128)(2,1)S(1)}, bf16[8,4,128]{2,0,1:T(8,128)(2,1)S(1)}, u32[]{:S(2)}, u32[]{:S(2)}) collective-permute-start(bf16[8,4,128]{2,0,1:T(8,128)(2,1)S(1)} %copy.29), channel_id=1, source_target_pairs={{0,8},{4,12},{8,0},{12,4},{1,9},{5,13},{9,1},{13,5},{2,10},{6,14},... | collective-permute-start | bytes 24584 | tf_op jit(solution)/shard_map/ppermute | solution.py:17
  5.9 6.7 %collective-permute-start.4 = (f32[4,128]{1,0:T(4,128)S(1)}, f32[4,128]{1,0:T(4,128)S(1)}, u32[]{:S(2)}, u32[]{:S(2)}) collective-permute-start(f32[4,128]{1,0:T(4,128)S(1)} %slice_bitcast_fusion.6), channel_id=1, source_target_pairs={{0,12},{4,8},{8,4},{12,0},{1,13},{5,9},{9,5},{13,1},{2,14},{6,10},... | collective-permute-start | bytes 6152 | tf_op jit(solution)/shard_map/ppermute | solution.py:17
  7.8 5.4 %collective-permute-start.5 = (f32[4,128]{1,0:T(4,128)S(1)}, f32[4,128]{1,0:T(4,128)S(1)}, u32[]{:S(2)}, u32[]{:S(2)}) collective-permute-start(f32[4,128]{1,0:T(4,128)S(1)} %slice_bitcast_fusion.6), channel_id=1, source_target_pairs={{0,8},{4,12},{8,0},{12,4},{1,9},{5,13},{9,1},{13,5},{2,10},{6,14},... | collective-permute-start | bytes 6152 | tf_op jit(solution)/shard_map/ppermute | solution.py:17
  8.8 4.3 %collective-permute-start.6 = (f32[4,128]{1,0:T(4,128)S(1)}, f32[4,128]{1,0:T(4,128)S(1)}, u32[]{:S(2)}, u32[]{:S(2)}) collective-permute-start(f32[4,128]{1,0:T(4,128)S(1)} %slice_bitcast_fusion.6), channel_id=1, source_target_pairs={{0,4},{4,0},{8,12},{12,8},{1,5},{5,1},{9,13},{13,9},{2,6},{6,2},{1... | collective-permute-start | bytes 6152 | tf_op jit(solution)/shard_map/ppermute | solution.py:17
  10.3 0.7 %copy-start.5 = (s32[8,1,4]{0,2,1:T(4,128)S(1)}, s32[8,1,4]{0,2,1:T(4,128)}, u32[]{:S(2)}) copy-start(s32[8,1,4]{0,2,1:T(4,128)} %param.10) | copy-start | bytes 388
  11.1 1.3 %copy-start.3 = (f32[4,128]{1,0:T(4,128)S(1)}, f32[4,128]{1,0:T(4,128)}, u32[]{:S(2)}) copy-start(f32[4,128]{1,0:T(4,128)} %param.13) | copy-start | bytes 6148
  11.1 1.3 %copy-start.4 = (s32[4,128]{1,0:T(4,128)S(1)}, s32[4,128]{1,0:T(4,128)}, u32[]{:S(2)}) copy-start(s32[4,128]{1,0:T(4,128)} %param.12) | copy-start | bytes 6148
  12.5 3.7 %collective-permute-start.2 = (bf16[8,4,128]{2,0,1:T(8,128)(2,1)S(1)}, bf16[8,4,128]{2,0,1:T(8,128)(2,1)S(1)}, u32[]{:S(2)}, u32[]{:S(2)}) collective-permute-start(bf16[8,4,128]{2,0,1:T(8,128)(2,1)S(1)} %copy.29), channel_id=1, source_target_pairs={{0,4},{4,0},{8,12},{12,8},{1,5},{5,1},{9,13},{13,9},{2,6},{6,2},{1... | collective-permute-start | bytes 24584 | tf_op jit(solution)/shard_map/ppermute | solution.py:17
  16.3 3.8 %collective-permute-start.3 = (bf16[4,4,512]{2,0,1:T(4,128)(2,1)S(1)}, bf16[4,4,512]{2,0,1:T(4,128)(2,1)S(1)}, u32[]{:S(2)}, u32[]{:S(2)}) collective-permute-start(bf16[4,4,512]{2,0,1:T(4,128)(2,1)S(1)} %slice.440), channel_id=1, source_target_pairs={{0,2},{2,0},{1,3},{3,1},{4,6},{6,4},{5,7},{7,5},{8,10},{10,8},{9,1... | collective-permute-start | bytes 49160 | tf_op jit(solution)/shard_map/ppermute | solution.py:62
  20.7 8.2 %copy-start.2 = (f32[5,4,128]{2,1,0:T(4,128)S(1)}, f32[5,4,128]{2,1,0:T(4,128)}, u32[]{:S(2)}) copy-start(f32[5,4,128]{2,1,0:T(4,128)} %param.8) | copy-start | bytes 30724
  29.2 5.4 %collective-permute-start.7 = (f32[4,128]{1,0:T(4,128)S(1)}, f32[4,128]{1,0:T(4,128)S(1)}, u32[]{:S(2)}, u32[]{:S(2)}) collective-permute-start(f32[4,128]{1,0:T(4,128)S(1)} %get-tuple-element.91), channel_id=1, source_target_pairs={{0,12},{4,8},{8,4},{12,0},{1,13},{5,9},{9,5},{13,1},{2,14},{6,10},... | collective-permute-start | bytes 6152 | tf_op jit(solution)/shard_map/ppermute | solution.py:17
  31.1 4.5 %collective-permute-start.8 = (f32[4,128]{1,0:T(4,128)S(1)}, f32[4,128]{1,0:T(4,128)S(1)}, u32[]{:S(2)}, u32[]{:S(2)}) collective-permute-start(f32[4,128]{1,0:T(4,128)S(1)} %get-tuple-element.91), channel_id=1, source_target_pairs={{0,8},{4,12},{8,0},{12,4},{1,9},{5,13},{9,1},{13,5},{2,10},{6,14},... | collective-permute-start | bytes 6152 | tf_op jit(solution)/shard_map/ppermute | solution.py:17
  31.3 4.3 %collective-permute-start.9 = (f32[4,128]{1,0:T(4,128)S(1)}, f32[4,128]{1,0:T(4,128)S(1)}, u32[]{:S(2)}, u32[]{:S(2)}) collective-permute-start(f32[4,128]{1,0:T(4,128)S(1)} %get-tuple-element.91), channel_id=1, source_target_pairs={{0,4},{4,0},{8,12},{12,8},{1,5},{5,1},{9,13},{13,9},{2,6},{6,2},{1... | collective-permute-start | bytes 6152 | tf_op jit(solution)/shard_map/ppermute | solution.py:17
  36.2 5.4 %collective-permute-start.10 = (f32[4,128]{1,0:T(4,128)S(1)}, f32[4,128]{1,0:T(4,128)S(1)}, u32[]{:S(2)}, u32[]{:S(2)}) collective-permute-start(f32[4,128]{1,0:T(4,128)S(1)} %get-tuple-element.93), channel_id=1, source_target_pairs={{0,12},{4,8},{8,4},{12,0},{1,13},{5,9},{9,5},{13,1},{2,14},{6,10},... | collective-permute-start | bytes 6152 | tf_op jit(solution)/shard_map/ppermute | solution.py:17
  38.4 4.5 %collective-permute-start.11 = (f32[4,128]{1,0:T(4,128)S(1)}, f32[4,128]{1,0:T(4,128)S(1)}, u32[]{:S(2)}, u32[]{:S(2)}) collective-permute-start(f32[4,128]{1,0:T(4,128)S(1)} %get-tuple-element.93), channel_id=1, source_target_pairs={{0,8},{4,12},{8,0},{12,4},{1,9},{5,13},{9,1},{13,5},{2,10},{6,14},... | collective-permute-start | bytes 6152 | tf_op jit(solution)/shard_map/ppermute | solution.py:17
  39.3 3.6 %collective-permute-start.12 = (f32[4,128]{1,0:T(4,128)S(1)}, f32[4,128]{1,0:T(4,128)S(1)}, u32[]{:S(2)}, u32[]{:S(2)}) collective-permute-start(f32[4,128]{1,0:T(4,128)S(1)} %get-tuple-element.93), channel_id=1, source_target_pairs={{0,4},{4,0},{8,12},{12,8},{1,5},{5,1},{9,13},{13,9},{2,6},{6,2},{1... | collective-permute-start | bytes 6152 | tf_op jit(solution)/shard_map/ppermute | solution.py:17
  43.5 5.4 %collective-permute-start.13 = (f32[4,128]{1,0:T(4,128)S(1)}, f32[4,128]{1,0:T(4,128)S(1)}, u32[]{:S(2)}, u32[]{:S(2)}) collective-permute-start(f32[4,128]{1,0:T(4,128)S(1)} %get-tuple-element.95), channel_id=1, source_target_pairs={{0,12},{4,8},{8,4},{12,0},{1,13},{5,9},{9,5},{13,1},{2,14},{6,10},... | collective-permute-start | bytes 6152 | tf_op jit(solution)/shard_map/ppermute | solution.py:17
  45.4 4.5 %collective-permute-start.14 = (f32[4,128]{1,0:T(4,128)S(1)}, f32[4,128]{1,0:T(4,128)S(1)}, u32[]{:S(2)}, u32[]{:S(2)}) collective-permute-start(f32[4,128]{1,0:T(4,128)S(1)} %get-tuple-element.95), channel_id=1, source_target_pairs={{0,8},{4,12},{8,0},{12,4},{1,9},{5,13},{9,1},{13,5},{2,10},{6,14},... | collective-permute-start | bytes 6152 | tf_op jit(solution)/shard_map/ppermute | solution.py:17
  46.3 3.6 %collective-permute-start.15 = (f32[4,128]{1,0:T(4,128)S(1)}, f32[4,128]{1,0:T(4,128)S(1)}, u32[]{:S(2)}, u32[]{:S(2)}) collective-permute-start(f32[4,128]{1,0:T(4,128)S(1)} %get-tuple-element.95), channel_id=1, source_target_pairs={{0,4},{4,0},{8,12},{12,8},{1,5},{5,1},{9,13},{13,9},{2,6},{6,2},{1... | collective-permute-start | bytes 6152 | tf_op jit(solution)/shard_map/ppermute | solution.py:17
  50.5 5.4 %collective-permute-start.16 = (f32[4,128]{1,0:T(4,128)S(1)}, f32[4,128]{1,0:T(4,128)S(1)}, u32[]{:S(2)}, u32[]{:S(2)}) collective-permute-start(f32[4,128]{1,0:T(4,128)S(1)} %get-tuple-element.97), channel_id=1, source_target_pairs={{0,12},{4,8},{8,4},{12,0},{1,13},{5,9},{9,5},{13,1},{2,14},{6,10},... | collective-permute-start | bytes 6152 | tf_op jit(solution)/shard_map/ppermute | solution.py:17
  52.7 4.5 %collective-permute-start.17 = (f32[4,128]{1,0:T(4,128)S(1)}, f32[4,128]{1,0:T(4,128)S(1)}, u32[]{:S(2)}, u32[]{:S(2)}) collective-permute-start(f32[4,128]{1,0:T(4,128)S(1)} %get-tuple-element.97), channel_id=1, source_target_pairs={{0,8},{4,12},{8,0},{12,4},{1,9},{5,13},{9,1},{13,5},{2,10},{6,14},... | collective-permute-start | bytes 6152 | tf_op jit(solution)/shard_map/ppermute | solution.py:17
  53.6 3.6 %collective-permute-start.18 = (f32[4,128]{1,0:T(4,128)S(1)}, f32[4,128]{1,0:T(4,128)S(1)}, u32[]{:S(2)}, u32[]{:S(2)}) collective-permute-start(f32[4,128]{1,0:T(4,128)S(1)} %get-tuple-element.97), channel_id=1, source_target_pairs={{0,4},{4,0},{8,12},{12,8},{1,5},{5,1},{9,13},{13,9},{2,6},{6,2},{1... | collective-permute-start | bytes 6152 | tf_op jit(solution)/shard_map/ppermute | solution.py:17

commit v2 on v1

v2 whole, which is shorter than its diff:
```python
import jax
import jax.numpy as jnp
from jax import lax
from jax.experimental import pallas as pl
from jax.experimental.pallas import tpu as pltpu
from jax.sharding import PartitionSpec as P

RIM = 8
STEPS = 5
LATE = STEPS - 1
WORDS = 3


def in_words(value):
    out = []
    for _ in range(WORDS):
        head = lax.reduce_precision(value, 8, 7)
        out.append(head.astype(jnp.bfloat16))
        value = value - head
    return out


def from_words(words):
    return words[0].astype(jnp.float32) + (
        words[1].astype(jnp.float32) + words[2].astype(jnp.float32)
    )


def flips(value, flipped=(1, 2, 3)):
    count = lax.axis_size("elem")
    return [value] + [
        lax.ppermute(value, "elem", [(i, i ^ flip) for i in range(count)]) for flip in flipped
    ]


def in_order(pieces, dim):
    place = lax.axis_index("elem")
    ordered = []
    for block in range(len(pieces)):
        chosen = pieces[0]
        for flip in range(1, len(pieces)):
            chosen = jnp.where(place ^ flip == block, pieces[flip], chosen)
        ordered.append(chosen)
    return jnp.concatenate(ordered, axis=dim)


def lag_behind(value):
    count = lax.axis_size("lag")
    moved = lax.ppermute(value, "lag", [(i, (i + 1) % count) for i in range(count)])
    return jnp.where(lax.axis_index("lag") == 0, jnp.zeros_like(moved), moved)


def by_offset(neighbours, edge_coef):
    rows = neighbours.shape[1]
    total = rows * lax.axis_size("elem")
    places = lax.axis_index("elem") * rows + jnp.arange(rows, dtype=jnp.int32)
    return (neighbours - places[None, :] + RIM) % total


def spread_weights(offsets, edge_coef):
    return [
        jnp.sum(jnp.where(offsets == d, edge_coef, 0.0), axis=0, keepdims=True)
        for d in range(2 * RIM + 1)
    ]


def own_gradient(newest, spread):
    rows = spread[0].shape[1]
    total = newest.shape[1]
    wide = jnp.concatenate([newest[:, total - RIM :], newest, newest[:, :RIM]], axis=1)
    start = lax.axis_index("elem") * rows
    window = lax.dynamic_slice(wide, (0, start), (newest.shape[0], rows + 2 * RIM))
    own = window[:, RIM : RIM + rows]
    out = jnp.zeros_like(own)
    for d in range(2 * RIM + 1):
        if d != RIM:
            out += spread[d] * (window[:, d : d + rows] - own)
    return out


def known_part(hist, masked):
    lags, gusts, total = hist.shape
    longer = jnp.concatenate([lag_behind(hist[lags - LATE :]), hist], axis=0)
    stacked = jnp.stack(
        [longer[LATE - step : LATE - step + lags] for step in range(STEPS)], axis=1
    ).reshape(lags, STEPS * gusts, total)
    part = jnp.einsum("lmc,lrc->mr", stacked, masked, preferred_element_type=jnp.float32)
    return part.reshape(STEPS, gusts, masked.shape[1])


def live_coefficients(interaction, block_mask, rows):
    live = jnp.repeat(block_mask[:, 0, :].astype(jnp.bfloat16), rows, axis=1)
    return interaction * live[:, None, :]


def exchange_each_step(
    history, forcing, interaction, block_mask, correction, neighbours, edge_coef
):
    rows = correction.shape[0]
    masked = live_coefficients(interaction, block_mask, rows)
    spread = spread_weights(by_offset(neighbours, edge_coef), edge_coef)

    def gathered(value, dim):
        return lax.all_gather(value, "elem", axis=dim, tiled=True)

    hist = gathered(history.astype(jnp.bfloat16), 2)
    newest = gathered(history[0], 1)
    base = forcing - lax.psum(known_part(hist, masked), "lag")
    fresh_b = []
    results = []
    for step in range(STEPS):
        drive = base[step] + own_gradient(newest, spread)
        if step:
            past = jnp.stack(fresh_b[::-1], axis=0)
            drive -= jnp.einsum(
                "lgc,lrc->gr", past, masked[:step], preferred_element_type=jnp.float32
            )
        fresh = drive + jnp.dot(drive, correction.T, precision=lax.Precision.HIGHEST)
        results.append(fresh)
        if step < LATE:
            newest = gathered(fresh, 1)
            fresh_b.append(newest.astype(jnp.bfloat16))
    first = lax.axis_index("lag") == 0
    return lax.psum(jnp.where(first, jnp.stack(results, 0), 0.0), "lag")


def march(
    own_w, near_w, mid_w, far_w, near_s, mid_s, far_s, own_c,
    base_0, base_1, base_2, base_3, spread_ref,
    own_out, other_out,
    w, c, base, sems,
):
    place = lax.axis_index("elem")
    half = lax.axis_index("gust")
    rows = own_w.shape[1]
    cut = rows // 2
    gusts = base_0.shape[1]
    total = w.shape[2]
    copies = []

    def fetch(source, target):
        copy = pltpu.make_async_copy(source, target, sems.at[len(copies)])
        copy.start()
        copies.append(copy)

    def bring(received, flip, side, lags):
        start = pl.multiple_of((place ^ flip) * rows + side * cut, cut)
        fetch(received.at[pl.ds(0, lags)], w.at[pl.ds(0, lags), pl.ds(start, cut)])
        fetch(received.at[lags], c.at[pl.ds(start, cut)])

    own_start = pl.multiple_of(place * rows, rows)
    fetch(own_w, w.at[:, pl.ds(own_start, rows)])
    fetch(own_c, c.at[pl.ds(own_start, rows)])
    for side, received in ((half, (near_w, mid_w, far_w)), (1 - half, (near_s, mid_s, far_s))):
        bring(received[0], 1, side, LATE)
        bring(received[1], 3, side, LATE - 1)
        bring(received[2], 2, side, LATE - 1)
    for flip, received in enumerate((base_0, base_1, base_2, base_3)):
        start = pl.multiple_of((place ^ flip) * rows, rows)
        base[:, :, pl.ds(start, rows)] = received[...]
    for copy in copies:
        copy.wait()

    pair_start = pl.multiple_of((place // 2) * (2 * rows), 2 * rows)

    def times(fresh_b, lag, start, count):
        return lax.dot_general(
            fresh_b, w[lag, pl.ds(start, count), :], (((1,), (1,)), ((), ())),
            preferred_element_type=jnp.float32,
        )

    def small(lhs, rhs):
        return lax.dot_general(
            lhs, rhs, (((1,), (1,)), ((), ())), preferred_element_type=jnp.float32
        )

    def corrected(drive, starts):
        out = []
        for at, start in enumerate(starts):
            part = drive[:, at * rows : (at + 1) * rows]
            d_hi = part.astype(jnp.bfloat16)
            rest = part - d_hi.astype(jnp.float32)
            d_mid = rest.astype(jnp.bfloat16)
            d_lo = (rest - d_mid.astype(jnp.float32)).astype(jnp.bfloat16)
            c_hi, c_mid, c_lo = (
                c[pl.ds(start, rows), word * rows : (word + 1) * rows] for word in range(WORDS)
            )
            added = small(d_hi, c_lo) + small(d_lo, c_hi) + small(d_mid, c_mid)
            added = added + (small(d_hi, c_mid) + small(d_mid, c_hi))
            out.append(part + (added + small(d_hi, c_hi)))
        return jnp.concatenate(out, axis=1)

    def gradient(newest):
        out = jnp.zeros_like(newest)
        for d in range(2 * RIM + 1):
            if d != RIM:
                moved = pltpu.roll(newest, (RIM - d) % total, 1)
                out += spread_ref[d : d + 1, :] * (moved - newest)
        return out

    def pair_of(value):
        return jnp.where(place < 2, value[:, : 2 * rows], value[:, 2 * rows :])

    def put(step, pair):
        left, right = pair[:, :rows], pair[:, rows:]
        odd = place % 2 == 1
        own_out[step] = jnp.where(odd, right, left)
        other_out[step] = jnp.where(odd, left, right)

    all_blocks = [block * rows for block in range(total // rows)]
    waiting = {step: base[step] for step in range(LATE)}
    waiting[LATE] = pair_of(base[LATE])
    for step in range(LATE):
        fresh = corrected(waiting[step], all_blocks)
        put(step, pair_of(fresh))
        fresh_b = fresh.astype(jnp.bfloat16)
        slope = gradient(fresh)
        for later in range(step + 1, STEPS):
            lag = later - step - 1
            if later < LATE:
                change = times(fresh_b, lag, 0, total)
                if lag == 0:
                    change = change - slope
            else:
                change = times(fresh_b, lag, pair_start, 2 * rows)
                if lag == 0:
                    change = change - pair_of(slope)
            waiting[later] = waiting[later] - change
    put(LATE, corrected(waiting[LATE], [pair_start, pair_start + rows]))


def middle_marches(history, forcing, interaction, block_mask, correction, neighbours, edge_coef):
    rows = correction.shape[0]
    lags, gusts, _ = history.shape
    count = lax.axis_size("elem")
    total = rows * count
    place = lax.axis_index("elem")
    lag_place = lax.axis_index("lag")
    half = lax.axis_index("gust")
    cut = rows // 2

    offsets = by_offset(neighbours, edge_coef).astype(jnp.bfloat16)
    newest_words = in_words(history[0])[1:]
    message = jnp.concatenate(
        [history.astype(jnp.bfloat16)]
        + [word[None] for word in newest_words + [offsets] + in_words(edge_coef)],
        axis=0,
    )
    everyone = in_order(flips(message), 2)
    hist = everyone[:lags]
    newest = from_words([everyone[0], everyone[lags], everyone[lags + 1]])
    all_offsets = everyone[lags + 2].astype(jnp.int32)
    all_coef = from_words([everyone[lags + 3 + word] for word in range(WORDS)])
    spread = spread_weights(all_offsets, all_coef)

    masked = live_coefficients(interaction, block_mask, rows)
    words_c = in_words(correction)
    own_c = jnp.concatenate(words_c + [jnp.zeros_like(words_c[0])], axis=1)
    half_w = lax.dynamic_slice(masked, (0, half * cut, 0), (LATE, cut, total))
    half_c = lax.dynamic_slice(own_c, (half * cut, 0), (cut, total))[None]
    long_load = jnp.concatenate([half_w, half_c], axis=0)
    short_load = jnp.concatenate([half_w[: LATE - 1], half_c], axis=0)

    def at(elem, lag):
        return elem * 2 + lag

    def bulk(load, pairs):
        return lax.ppermute(load, ("elem", "lag"), [(at(a, 0), at(b, 0)) for a, b in pairs])

    near = bulk(long_load, [(0, 1), (3, 2)])
    mid = bulk(short_load, [(1, 2), (2, 1)])
    far = bulk(short_load, [(0, 2), (3, 1)])
    swapped = [lax.ppermute(load, "gust", [(0, 1), (1, 0)]) for load in (near, mid, far)]

    part = known_part(hist, masked)
    known = part + lax.ppermute(part, "lag", [(0, 1), (1, 0)])
    own_spread = [
        lax.dynamic_slice(row, (0, place * rows), (1, rows)) for row in spread
    ]
    slope = own_gradient(newest, own_spread)
    base = jnp.concatenate([(forcing[0] - known[0] + slope)[None], forcing[1:] - known[1:]], 0)
    bases = flips(base)

    vmem = pl.BlockSpec(memory_space=pltpu.VMEM)
    anywhere = pl.BlockSpec(memory_space=pl.ANY)
    shape = jax.ShapeDtypeStruct((STEPS, gusts, rows), jnp.float32)
    own, other = pl.pallas_call(
        march,
        out_shape=(shape, shape),
        in_specs=[anywhere] * 8 + [vmem] * 5,
        out_specs=(vmem, vmem),
        scratch_shapes=[
            pltpu.VMEM((LATE, total, total), jnp.bfloat16),
            pltpu.VMEM((total, total), jnp.bfloat16),
            pltpu.VMEM((STEPS, gusts, total), jnp.float32),
            pltpu.SemaphoreType.DMA((14,)),
        ],
        name="march",
    )(masked[:LATE], near, mid, far, *swapped, own_c, *bases, jnp.concatenate(spread, axis=0))

    def swap(value, flip):
        return lax.ppermute(
            value, ("elem", "lag"), [(i, i ^ flip) for i in range(2 * count)]
        )

    to_lag, to_outer, to_both = swap(own, 1), swap(other, 2), swap(other, 3)
    middle = (place == 1) | (place == 2)
    first = lag_place == 0
    return jnp.where(
        middle, jnp.where(first, own, to_lag), jnp.where(first, to_outer, to_both)
    )


def solution(mesh):
    placed = (
        P("lag", ("groups", "gust"), "elem"),
        P(None, ("groups", "gust"), "elem"),
        P("lag", "elem", None),
        P("lag", "elem", None),
        P("elem", None),
        P(None, "elem"),
        P(None, "elem"),
    )
    small = mesh.shape["elem"] == 4 and mesh.shape["lag"] == 2 and mesh.shape["gust"] == 2
    return jax.shard_map(
        middle_marches if small else exchange_each_step,
        mesh=mesh,
        in_specs=placed,
        out_specs=P(None, ("groups", "gust"), "elem"),
        check_vma=False,
    )
```

time: 65.9 us -> 55.3 us (0.84)
  blocking collectives: 15.9 us -> 0 us
  starting transfers between devices: 29.4 us -> 20.3 us
  other arithmetic: 1.55 us -> 8.83 us
  Pallas kernels: 0 us -> 6.49 us
  local copies, waits for them, and re-layouts: 2.49 us -> 5.65 us
  matrix products: 2.46 us -> 0.47 us
  waiting for transfers between devices: 13.6 us -> 12.6 us
    psum x2 -> x0, blocking collectives: 15.9 us -> none  [the longest x1 8.16 us: on_device(): known = lax.psum(partial.reshape(STEPS, gusts, rows), 'lag')]
    ppermute x19 -> x17, starting transfers between devices: 29.4 us -> 20.3 us  [the longest x6 8.43 us: flips(): lax.ppermute(value, 'elem', [(i, i ^ flip) for i in range(count)])]
    pallas_call x0 -> x1, Pallas kernels: none -> 6.49 us  [middle_marches(): pl.pallas_call(march, out_shape=(shape, shape), in_specs=[anywhere] * 8 +...]
    unnamed x1 -> x9, other arithmetic: 0.01 us -> 4.29 us
    dot_general x10 -> x1, matrix products: 2.46 us -> 0.47 us  [known_part(): jnp.einsum('lmc,lrc->mr', stacked, masked, preferred_element_type=jnp.flo...]
    concatenate x5 -> x2, local copies, waits for them, and re-layouts: 0.49 us -> 1.87 us  [the longest x1 1.87 us: middle_marches(): jnp.concatenate(spread, axis=0)]
    select_n x4 -> x3, other arithmetic: 0.08 us -> 1.35 us  [the longest x1 1.31 us: middle_marches(): jnp.where(middle, jnp.where(first, own, to_lag), jnp.where(first, to_oute...]
    another operation x1 -> x16, local copies, waits for them, and re-layouts: 0.01 us -> 1.18 us  [on_device(): jnp.stack([longer[late - step:late - step + lags] for step in range(STEPS...]
  transfers between devices with their start and end apart: 19 -> 17, of which waited for: 12 -> 7; matrix products, arithmetic and copies ran while one was open for 2% -> 13% of each run, Pallas kernels for 0% -> 0%
where the time goes in v2:
time: 55.3 us; the launch traced here: 54.8 us
  starting transfers between devices  20.3 us (37%)
  waiting for transfers between devices  12.6 us (23%)
  other arithmetic  8.83 us (16%)
  Pallas kernels  6.49 us (12%)
  local copies, waits for them, and re-layouts  5.65 us (10%)
    ppermute x6, starting transfers between devices, flips(): lax.ppermute(value, 'elem', [(i, i ^ flip) for i in range(count)])  8.43 us
    ppermute x3, starting transfers between devices, bulk(): lax.ppermute(load, ('elem', 'lag'), [(at(a, 0), at(b, 0)) for a, b in pai...  7.6 us
    pallas_call x1, Pallas kernels, middle_marches(): pl.pallas_call(march, out_shape=(shape, shape), in_specs=[anywhere] * 8 +...  6.49 us
    unnamed x9, other arithmetic  4.29 us
    ppermute x6, waiting for transfers between devices, flips(): lax.ppermute(value, 'elem', [(i, i ^ flip) for i in range(count)])  3.68 us
    ppermute x1, waiting for transfers between devices, lag_behind(): lax.ppermute(value, 'lag', [(i, (i + 1) % count) for i in range(count)])  3.61 us
    ppermute x3, starting transfers between devices, swap(): lax.ppermute(value, ('elem', 'lag'), [(i, i ^ flip) for i in range(2 * co...  3.55 us
    ppermute x3, waiting for transfers between devices, swap(): lax.ppermute(value, ('elem', 'lag'), [(i, i ^ flip) for i in range(2 * co...  2.95 us
  transfers between devices with their start and end apart: 17, of which 7 were waited for; matrix products, arithmetic and copies ran while one was open for 13% of the time, Pallas kernels for 0%

profile of v2, /device:TPU:0, one launch (start us, length us, event | category | flops | bytes accessed | tf_op | source)
XLA Modules:
  0.0 54.8 jit_solution(1175828244155702183)
XLA Ops:
  0.0 0.8 %constant_dynamic-update-slice_fusion.6 = bf16[14,4,128]{2,1,0:T(4,128)(2,1)S(1)} fusion(f32[8,4,128]{2,1,0:T(4,128)} %param.7), kind=kLoop, calls=%fused_computation.58 | loop fusion | flops 4095 | bytes 24576
  0.8 0.7 %constant_dynamic-update-slice_fusion.5 = bf16[14,4,128]{2,1,0:T(4,128)(2,1)S(1)} fusion(bf16[14,4,128]{2,1,0:T(4,128)(2,1)S(1)} %constant_dynamic-update-slice_fusion.6, f32[8,4,128]{2,1,0:T(4,128)} %param.7), kind=kLoop, calls=%fused_computation.57 | loop fusion | flops 2048 | bytes 3072
  1.5 0.7 %constant_dynamic-update-slice_fusion.4 = bf16[14,4,128]{2,1,0:T(4,128)(2,1)S(1)} fusion(bf16[14,4,128]{2,1,0:T(4,128)(2,1)S(1)} %constant_dynamic-update-slice_fusion.5, f32[8,4,128]{2,1,0:T(4,128)} %param.7), kind=kLoop, calls=%fused_computation.56 | loop fusion | flops 3072 | bytes 3072
  2.1 0.7 %constant_dynamic-update-slice_fusion.3 = bf16[14,4,128]{2,1,0:T(4,128)(2,1)S(1)} fusion(bf16[14,4,128]{2,1,0:T(4,128)(2,1)S(1)} %constant_dynamic-update-slice_fusion.4, s32[4,128]{1,0:T(4,128)} %param.12, s32[128]{0:T(128)S(1)} %iota_add_fusion), kind=kLoop, calls=%fused_computation.55 | loop fusion | flops 7168 | bytes 3584
  2.8 0.7 %constant_dynamic-update-slice_fusion.2 = bf16[14,4,128]{2,1,0:T(4,128)(2,1)S(1)} fusion(bf16[14,4,128]{2,1,0:T(4,128)(2,1)S(1)} %constant_dynamic-update-slice_fusion.3, f32[4,128]{1,0:T(4,128)} %param.13), kind=kLoop, calls=%fused_computation.54 | loop fusion | flops 1024 | bytes 3072
  3.5 0.7 %constant_dynamic-update-slice_fusion.1 = bf16[14,4,128]{2,1,0:T(4,128)(2,1)S(1)} fusion(bf16[14,4,128]{2,1,0:T(4,128)(2,1)S(1)} %constant_dynamic-update-slice_fusion.2, f32[4,128]{1,0:T(4,128)} %param.13), kind=kLoop, calls=%fused_computation.53 | loop fusion | flops 2048 | bytes 3072
  4.2 0.7 %constant_dynamic-update-slice_fusion = bf16[14,4,128]{2,1,0:T(4,128)(2,1)S(1)} fusion(bf16[14,4,128]{2,1,0:T(4,128)(2,1)S(1)} %constant_dynamic-update-slice_fusion.1, f32[4,128]{1,0:T(4,128)} %param.13), kind=kLoop, calls=%fused_computation.52 | loop fusion | flops 3072 | bytes 3072 | tf_op jit(solution)/shard_map/concatenate | solution.py:244
  4.9 3.0 %collective-permute-start.8 = (bf16[14,4,128]{2,1,0:T(4,128)(2,1)S(1)}, bf16[14,4,128]{2,1,0:T(4,128)(2,1)S(1)}, u32[]{:S(2)}, u32[]{:S(2)}) collective-permute-start(bf16[14,4,128]{2,1,0:T(4,128)(2,1)S(1)} %constant_dynamic-update-slice_fusion), channel_id=1, source_target_pairs={{0,4},{4,0},{8,12},{12,8},{1,5},{5,1},{9,13},{13,9},{2,6},{6,2},{1... | collective-permute-start | bytes 43016 | tf_op jit(solution)/shard_map/ppermute | solution.py:32
  7.9 2.6 %collective-permute-start.7 = (bf16[14,4,128]{2,1,0:T(4,128)(2,1)S(1)}, bf16[14,4,128]{2,1,0:T(4,128)(2,1)S(1)}, u32[]{:S(2)}, u32[]{:S(2)}) collective-permute-start(bf16[14,4,128]{2,1,0:T(4,128)(2,1)S(1)} %constant_dynamic-update-slice_fusion), channel_id=1, source_target_pairs={{0,8},{4,12},{8,0},{12,4},{1,9},{5,13},{9,1},{13,5},{2,10},{6,14},... | collective-permute-start | bytes 43016 | tf_op jit(solution)/shard_map/ppermute | solution.py:32
  10.5 0.7 %convert_bitcast_fusion = bf16[8,4]{0,1:T(4,128)(2,1)S(1)} fusion(s32[8,1,4]{0,2,1:T(4,128)} %param.10), kind=kLoop, calls=%fused_computation.164 | loop fusion | flops 32 | bytes 192 | tf_op jit(solution)/shard_map/convert_element_type | solution.py:92
  11.4 1.3 %broadcast_multiply_fusion = bf16[8,128,512]{2,1,0:T(8,128)(2,1)S(1)} fusion(bf16[8,128,512]{2,1,0:T(8,128)(2,1)} %param.9, bf16[8,512]{1,0:T(8,128)(2,1)S(1)} %broadcast_bitcast_fusion), kind=kLoop, calls=%fused_computation.2 | loop fusion | flops 524288 | bytes 2105344 | tf_op jit(solution)/shard_map/mul | solution.py:93
  12.8 3.8 %collective-permute-start.2 = (bf16[4,64,512]{2,1,0:T(8,128)(2,1)S(1)}, bf16[4,64,512]{2,1,0:T(8,128)(2,1)S(1)}, u32[]{:S(2)}, u32[]{:S(2)}) collective-permute-start(bf16[4,64,512]{2,1,0:T(8,128)(2,1)S(1)} %pad_maximum_fusion.1), channel_id=1, source_target_pairs={{0,8},{12,4},{1,9},{13,5},{16,24},{28,20},{17,25},{29,21}} | collective-permute-start | bytes 786440 | tf_op jit(solution)/shard_map/ppermute | solution.py:268
  16.7 0.7 %collective-permute-start.1 = (bf16[4,64,512]{2,1,0:T(8,128)(2,1)S(1)}, bf16[4,64,512]{2,1,0:T(8,128)(2,1)S(1)}, u32[]{:S(2)}, u32[]{:S(2)}) collective-permute-start(bf16[4,64,512]{2,1,0:T(8,128)(2,1)S(1)} %pad_maximum_fusion.1), channel_id=1, source_target_pairs={{4,8},{8,4},{5,9},{9,5},{20,24},{24,20},{21,25},{25,21}} | collective-permute-start | bytes 786440 | tf_op jit(solution)/shard_map/ppermute | solution.py:268
  17.5 3.1 %collective-permute-start = (bf16[5,64,512]{2,1,0:T(8,128)(2,1)S(1)}, bf16[5,64,512]{2,1,0:T(8,128)(2,1)S(1)}, u32[]{:S(2)}, u32[]{:S(2)}) collective-permute-start(bf16[5,64,512]{2,1,0:T(8,128)(2,1)S(1)} %pad_maximum_fusion), channel_id=1, source_target_pairs={{0,4},{12,8},{1,5},{13,9},{16,20},{28,24},{17,21},{29,25}} | collective-permute-start | bytes 983048 | tf_op jit(solution)/shard_map/ppermute | solution.py:268
  20.8 0.1 fusion.17
  20.9 3.6 %collective-permute-done.9 = bf16[4,4,512]{2,1,0:T(4,128)(2,1)S(1)} collective-permute-done((bf16[4,4,512]{2,1,0:T(4,128)(2,1)S(1)}, bf16[4,4,512]{2,1,0:T(4,128)(2,1)S(1)}, u32[]{:S(2)}, u32[]{:S(2)}) %collective-permute-start.9) | collective-permute-done | bytes 16416 | tf_op jit(solution)/shard_map/ppermute | solution.py:49
  24.7 0.5 convolution_bitcast_fusion
  25.2 0.1 select_reduce_fusion
  25.4 0.1 dynamic-slice.63
  25.4 0.1 dynamic-slice.62
  25.5 0.1 dynamic-slice.61
  25.6 0.1 dynamic-slice.60
  25.7 0.1 dynamic-slice.59
  25.8 0.1 dynamic-slice.57
  26.0 0.1 dynamic-slice.55
  26.1 0.1 dynamic-slice.53
  26.6 2.3 %collective-permute-done.10 = f32[5,4,128]{2,1,0:T(4,128)S(1)} collective-permute-done((f32[5,4,128]{2,1,0:T(4,128)S(1)}, f32[5,4,128]{2,1,0:T(4,128)S(1)}, u32[]{:S(2)}, u32[]{:S(2)}) %collective-permute-start.10) | collective-permute-done | bytes 10272 | tf_op jit(solution)/shard_map/ppermute | solution.py:276
  29.0 0.5 collective-permute-start.4
  29.5 0.1 collective-permute-start.3
  29.6 0.1 fusion.27
  29.7 1.4 %collective-permute-start.13 = (f32[5,4,128]{2,1,0:T(4,128)S(1)}, f32[5,4,128]{2,1,0:T(4,128)S(1)}, u32[]{:S(2)}, u32[]{:S(2)}) collective-permute-start(f32[5,4,128]{2,1,0:T(4,128)S(1)} %pad_maximum_fusion.4.base_0), channel_id=1, source_target_pairs={{0,12},{4,8},{8,4},{12,0},{1,13},{5,9},{9,5},{13,1},{2,14},{6,10},... | collective-permute-start | bytes 30728 | tf_op jit(solution)/shard_map/ppermute | solution.py:32
  31.1 1.4 %collective-permute-start.12 = (f32[5,4,128]{2,1,0:T(4,128)S(1)}, f32[5,4,128]{2,1,0:T(4,128)S(1)}, u32[]{:S(2)}, u32[]{:S(2)}) collective-permute-start(f32[5,4,128]{2,1,0:T(4,128)S(1)} %pad_maximum_fusion.4.base_0), channel_id=1, source_target_pairs={{0,8},{4,12},{8,0},{12,4},{1,9},{5,13},{9,1},{13,5},{2,10},{6,14},... | collective-permute-start | bytes 30728 | tf_op jit(solution)/shard_map/ppermute | solution.py:32
  32.6 2.7 %collective-permute-done.13.base_3 = f32[5,4,128]{2,1,0:T(4,128)S(1)} collective-permute-done((f32[5,4,128]{2,1,0:T(4,128)S(1)}, f32[5,4,128]{2,1,0:T(4,128)S(1)}, u32[]{:S(2)}, u32[]{:S(2)}) %collective-permute-start.13) | collective-permute-done | bytes 10272 | tf_op jit(solution)/shard_map/ppermute | solution.py:32
  35.3 0.8 %slice.157.own_w = bf16[4,128,512]{2,1,0:T(8,128)(2,1)} slice(bf16[8,128,512]{2,1,0:T(8,128)(2,1)S(1)} %broadcast_multiply_fusion), slice={[0:4], [0:128], [0:512]} | slice | bytes 1048576 | tf_op jit(solution)/shard_map/slice | solution.py:299
  36.1 1.9 %concatenate.35.spread_ref = f32[17,512]{1,0:T(8,128)} concatenate(f32[1,512]{1,0:T(1,128)S(1)} %bitcast.113, f32[1,512]{1,0:T(1,128)S(1)} %bitcast.112, f32[1,512]{1,0:T(1,128)S(1)} %bitcast.111, f32[1,512]{1,0:T(1,128)S(1)} %bitcast.110, f32[1,512]{1,0:T(1,128)S(1)} %bitcast.109, f32[1,512]{1,0:T(1,128)S(1)} %bitcast.108, f32[1,512]{1,0:T(1,128)S(1)} %bitcast.107, ...), dimensions={0} | concatenate | bytes 69632 | tf_op jit(solution)/shard_map/concatenate | solution.py:299
  38.0 1.0 %collective-permute-done.11.base_1 = f32[5,4,128]{2,1,0:T(4,128)S(1)} collective-permute-done((f32[5,4,128]{2,1,0:T(4,128)S(1)}, f32[5,4,128]{2,1,0:T(4,128)S(1)}, u32[]{:S(2)}, u32[]{:S(2)}) %collective-permute-start.11) | collective-permute-done | bytes 10272 | tf_op jit(solution)/shard_map/ppermute | solution.py:32
  39.0 0.5 copy-done.11
  39.5 0.1 copy-done.5
  39.7 0.1 copy-done.6
  39.8 0.7 %copy-done.2 = bf16[5,64,512]{2,1,0:T(8,128)(2,1)} copy-done((bf16[5,64,512]{2,1,0:T(8,128)(2,1)}, bf16[5,64,512]{2,1,0:T(8,128)(2,1)S(1)}, u32[]{:S(2)}) %copy-start.2) | copy-done | bytes 327704
  40.5 6.5 %march.1 = (f32[5,4,128]{2,1,0:T(4,128)}, f32[5,4,128]{2,1,0:T(4,128)}) custom-call(bf16[4,128,512]{2,1,0:T(8,128)(2,1)} %slice.157.own_w, bf16[5,64,512]{2,1,0:T(8,128)(2,1)} %copy-done.1, bf16[4,64,512]{2,1,0:T(8,128)(2,1)} %copy-done.4, bf16[4,64,512]{2,1,0:T(8,128)(2,1)} %copy-done.3, bf16[5,64,512]{2,1,0:T(8,128)(2,1)} %copy-done.2, ...), custom_call_target="tpu_custom_call" | custom-call | tf_op jit(solution)/shard_map/march/pallas_call | solution.py:287
  47.0 0.4 collective-permute-start.14
  47.4 2.2 %collective-permute-start.16 = (f32[5,4,128]{2,1,0:T(4,128)}, f32[5,4,128]{2,1,0:T(4,128)S(1)}, u32[]{:S(2)}, u32[]{:S(2)}) collective-permute-start(f32[5,4,128]{2,1,0:T(4,128)} %get-tuple-element.8), channel_id=1, source_target_pairs={{0,6},{2,4},{4,2},{6,0},{8,14},{10,12},{12,10},{14,8},{1,7},{3,5},... | collective-permute-start | bytes 30728 | tf_op jit(solution)/shard_map/ppermute | solution.py:302
  49.6 0.9 %collective-permute-start.15 = (f32[5,4,128]{2,1,0:T(4,128)}, f32[5,4,128]{2,1,0:T(4,128)S(1)}, u32[]{:S(2)}, u32[]{:S(2)}) collective-permute-start(f32[5,4,128]{2,1,0:T(4,128)} %get-tuple-element.8), channel_id=1, source_target_pairs={{0,4},{2,6},{4,0},{6,2},{8,12},{10,14},{12,8},{14,10},{1,5},{3,7},... | collective-permute-start | bytes 30728 | tf_op jit(solution)/shard_map/ppermute | solution.py:302
  50.5 0.4 collective-permute-done.14
  50.9 1.2 %collective-permute-done.16 = f32[5,4,128]{2,1,0:T(4,128)S(1)} collective-permute-done((f32[5,4,128]{2,1,0:T(4,128)}, f32[5,4,128]{2,1,0:T(4,128)S(1)}, u32[]{:S(2)}, u32[]{:S(2)}) %collective-permute-start.16) | collective-permute-done | bytes 10272 | tf_op jit(solution)/shard_map/ppermute | solution.py:302
  52.2 1.3 %collective-permute-done.15 = f32[5,4,128]{2,1,0:T(4,128)S(1)} collective-permute-done((f32[5,4,128]{2,1,0:T(4,128)}, f32[5,4,128]{2,1,0:T(4,128)S(1)}, u32[]{:S(2)}, u32[]{:S(2)}) %collective-permute-start.15) | collective-permute-done | bytes 10272 | tf_op jit(solution)/shard_map/ppermute | solution.py:302
  53.5 1.3 %select_select_fusion.4 = f32[5,4,128]{2,1,0:T(4,128)} fusion(f32[5,4,128]{2,1,0:T(4,128)S(1)} %collective-permute-done.15, f32[5,4,128]{2,1,0:T(4,128)S(1)} %collective-permute-done.16, f32[5,4,128]{2,1,0:T(4,128)} %get-tuple-element.7, f32[5,4,128]{2,1,0:T(4,128)S(1)} %collective-permute-done.14, pred[]{:T(512)S(6)} %eq.169, pred[]{:T(512)S(6)} %or.3), kind=kLoop, calls=%fused_computation.68 | loop fusion | flops 7680 | bytes 51202 | tf_op jit(solution)/shard_map/jit(_where)/select_n | solution.py:309
  (72 shorter events, 1.4 us)
Async XLA Ops:
  0.0 11.3 %copy-start.7 = (f32[128,128]{1,0:T(8,128)S(1)}, f32[128,128]{1,0:T(8,128)}, u32[]{:S(2)}) copy-start(f32[128,128]{1,0:T(8,128)} %param.11) | copy-start | bytes 196612
  4.9 12.5 %collective-permute-start.8 = (bf16[14,4,128]{2,1,0:T(4,128)(2,1)S(1)}, bf16[14,4,128]{2,1,0:T(4,128)(2,1)S(1)}, u32[]{:S(2)}, u32[]{:S(2)}) collective-permute-start(bf16[14,4,128]{2,1,0:T(4,128)(2,1)S(1)} %constant_dynamic-update-slice_fusion), channel_id=1, source_target_pairs={{0,4},{4,0},{8,12},{12,8},{1,5},{5,1},{9,13},{13,9},{2,6},{6,2},{1... | collective-permute-start | bytes 43016 | tf_op jit(solution)/shard_map/ppermute | solution.py:32
  7.9 12.6 %collective-permute-start.7 = (bf16[14,4,128]{2,1,0:T(4,128)(2,1)S(1)}, bf16[14,4,128]{2,1,0:T(4,128)(2,1)S(1)}, u32[]{:S(2)}, u32[]{:S(2)}) collective-permute-start(bf16[14,4,128]{2,1,0:T(4,128)(2,1)S(1)} %constant_dynamic-update-slice_fusion), channel_id=1, source_target_pairs={{0,8},{4,12},{8,0},{12,4},{1,9},{5,13},{9,1},{13,5},{2,10},{6,14},... | collective-permute-start | bytes 43016 | tf_op jit(solution)/shard_map/ppermute | solution.py:32
  10.5 10.0 %collective-permute-start.6 = (bf16[14,4,128]{2,1,0:T(4,128)(2,1)S(1)}, bf16[14,4,128]{2,1,0:T(4,128)(2,1)S(1)}, u32[]{:S(2)}, u32[]{:S(2)}) collective-permute-start(bf16[14,4,128]{2,1,0:T(4,128)(2,1)S(1)} %constant_dynamic-update-slice_fusion), channel_id=1, source_target_pairs={{0,12},{4,8},{8,4},{12,0},{1,13},{5,9},{9,5},{13,1},{2,14},{6,10},... | collective-permute-start | bytes 43016 | tf_op jit(solution)/shard_map/ppermute | solution.py:32
  11.4 1.4 %copy-start = (bf16[128,512]{1,0:T(8,128)(2,1)}, bf16[128,512]{1,0:T(8,128)(2,1)S(1)}, u32[]{:S(2)}) copy-start(bf16[128,512]{1,0:T(8,128)(2,1)S(1)} %maximum_maximum_fusion.own_c) | copy-start | bytes 393220
  12.8 16.1 %collective-permute-start.2 = (bf16[4,64,512]{2,1,0:T(8,128)(2,1)S(1)}, bf16[4,64,512]{2,1,0:T(8,128)(2,1)S(1)}, u32[]{:S(2)}, u32[]{:S(2)}) collective-permute-start(bf16[4,64,512]{2,1,0:T(8,128)(2,1)S(1)} %pad_maximum_fusion.1), channel_id=1, source_target_pairs={{0,8},{12,4},{1,9},{13,5},{16,24},{28,20},{17,25},{29,21}} | collective-permute-start | bytes 786440 | tf_op jit(solution)/shard_map/ppermute | solution.py:268
  16.7 12.4 %collective-permute-start.1 = (bf16[4,64,512]{2,1,0:T(8,128)(2,1)S(1)}, bf16[4,64,512]{2,1,0:T(8,128)(2,1)S(1)}, u32[]{:S(2)}, u32[]{:S(2)}) collective-permute-start(bf16[4,64,512]{2,1,0:T(8,128)(2,1)S(1)} %pad_maximum_fusion.1), channel_id=1, source_target_pairs={{4,8},{8,4},{5,9},{9,5},{20,24},{24,20},{21,25},{25,21}} | collective-permute-start | bytes 786440 | tf_op jit(solution)/shard_map/ppermute | solution.py:268
  17.5 12.1 %collective-permute-start = (bf16[5,64,512]{2,1,0:T(8,128)(2,1)S(1)}, bf16[5,64,512]{2,1,0:T(8,128)(2,1)S(1)}, u32[]{:S(2)}, u32[]{:S(2)}) collective-permute-start(bf16[5,64,512]{2,1,0:T(8,128)(2,1)S(1)} %pad_maximum_fusion), channel_id=1, source_target_pairs={{0,4},{12,8},{1,5},{13,9},{16,20},{28,24},{17,21},{29,25}} | collective-permute-start | bytes 983048 | tf_op jit(solution)/shard_map/ppermute | solution.py:268
  20.8 3.7 %collective-permute-start.9 = (bf16[4,4,512]{2,1,0:T(4,128)(2,1)S(1)}, bf16[4,4,512]{2,1,0:T(4,128)(2,1)S(1)}, u32[]{:S(2)}, u32[]{:S(2)}) collective-permute-start(bf16[4,4,512]{2,1,0:T(4,128)(2,1)S(1)} %slice.159), channel_id=1, source_target_pairs={{0,2},{2,0},{1,3},{3,1},{4,6},{6,4},{5,7},{7,5},{8,10},{10,8},{9,1... | collective-permute-start | bytes 49160 | tf_op jit(solution)/shard_map/ppermute | solution.py:49
  25.2 3.7 %collective-permute-start.10 = (f32[5,4,128]{2,1,0:T(4,128)S(1)}, f32[5,4,128]{2,1,0:T(4,128)S(1)}, u32[]{:S(2)}, u32[]{:S(2)}) collective-permute-start(f32[5,4,128]{2,1,0:T(4,128)S(1)} %copy.13), channel_id=1, source_target_pairs={{0,2},{2,0},{1,3},{3,1},{4,6},{6,4},{5,7},{7,5},{8,10},{10,8},{9,1... | collective-permute-start | bytes 30728 | tf_op jit(solution)/shard_map/ppermute | solution.py:276
  26.6 2.3 %copy-start.12 = (f32[5,4,128]{2,1,0:T(4,128)S(1)}, f32[5,4,128]{2,1,0:T(4,128)}, u32[]{:S(2)}) copy-start(f32[5,4,128]{2,1,0:T(4,128)} %param.8) | copy-start | bytes 30724
  28.9 7.2 %copy-start.3 = (bf16[4,64,512]{2,1,0:T(8,128)(2,1)}, bf16[4,64,512]{2,1,0:T(8,128)(2,1)S(1)}, u32[]{:S(2)}) copy-start(bf16[4,64,512]{2,1,0:T(8,128)(2,1)S(1)} %collective-permute-done.2.far_w) | copy-start | bytes 786436
  28.9 10.0 %collective-permute-start.5 = (bf16[4,64,512]{2,1,0:T(8,128)(2,1)S(1)}, bf16[4,64,512]{2,1,0:T(8,128)(2,1)S(1)}, u32[]{:S(2)}, u32[]{:S(2)}) collective-permute-start(bf16[4,64,512]{2,1,0:T(8,128)(2,1)S(1)} %collective-permute-done.2.far_w), channel_id=1, source_target_pairs={{0,1},{1,0},{2,3},{3,2},{4,5},{5,4},{6,7},{7,6},{8,9},{9,8},{10,11... | collective-permute-start | bytes 786440 | tf_op jit(solution)/shard_map/ppermute | solution.py:273
  29.0 7.1 %copy-start.4 = (bf16[4,64,512]{2,1,0:T(8,128)(2,1)}, bf16[4,64,512]{2,1,0:T(8,128)(2,1)S(1)}, u32[]{:S(2)}) copy-start(bf16[4,64,512]{2,1,0:T(8,128)(2,1)S(1)} %collective-permute-done.1.mid_w) | copy-start | bytes 786436
  29.0 9.9 %collective-permute-start.4 = (bf16[4,64,512]{2,1,0:T(8,128)(2,1)S(1)}, bf16[4,64,512]{2,1,0:T(8,128)(2,1)S(1)}, u32[]{:S(2)}, u32[]{:S(2)}) collective-permute-start(bf16[4,64,512]{2,1,0:T(8,128)(2,1)S(1)} %collective-permute-done.1.mid_w), channel_id=1, source_target_pairs={{0,1},{1,0},{2,3},{3,2},{4,5},{5,4},{6,7},{7,6},{8,9},{9,8},{10,11... | collective-permute-start | bytes 786440 | tf_op jit(solution)/shard_map/ppermute | solution.py:273
  29.5 6.6 %copy-start.1 = (bf16[5,64,512]{2,1,0:T(8,128)(2,1)}, bf16[5,64,512]{2,1,0:T(8,128)(2,1)S(1)}, u32[]{:S(2)}) copy-start(bf16[5,64,512]{2,1,0:T(8,128)(2,1)S(1)} %collective-permute-done.near_w) | copy-start | bytes 983044
  29.5 9.4 %collective-permute-start.3 = (bf16[5,64,512]{2,1,0:T(8,128)(2,1)S(1)}, bf16[5,64,512]{2,1,0:T(8,128)(2,1)S(1)}, u32[]{:S(2)}, u32[]{:S(2)}) collective-permute-start(bf16[5,64,512]{2,1,0:T(8,128)(2,1)S(1)} %collective-permute-done.near_w), channel_id=1, source_target_pairs={{0,1},{1,0},{2,3},{3,2},{4,5},{5,4},{6,7},{7,6},{8,9},{9,8},{10,11... | collective-permute-start | bytes 983048 | tf_op jit(solution)/shard_map/ppermute | solution.py:273
  29.7 6.4 %copy-start.8 = (f32[5,4,128]{2,1,0:T(4,128)}, f32[5,4,128]{2,1,0:T(4,128)S(1)}, u32[]{:S(2)}) copy-start(f32[5,4,128]{2,1,0:T(4,128)S(1)} %pad_maximum_fusion.4.base_0) | copy-start | bytes 30724
  29.7 5.5 %collective-permute-start.13 = (f32[5,4,128]{2,1,0:T(4,128)S(1)}, f32[5,4,128]{2,1,0:T(4,128)S(1)}, u32[]{:S(2)}, u32[]{:S(2)}) collective-permute-start(f32[5,4,128]{2,1,0:T(4,128)S(1)} %pad_maximum_fusion.4.base_0), channel_id=1, source_target_pairs={{0,12},{4,8},{8,4},{12,0},{1,13},{5,9},{9,5},{13,1},{2,14},{6,10},... | collective-permute-start | bytes 30728 | tf_op jit(solution)/shard_map/ppermute | solution.py:32
  31.1 6.8 %collective-permute-start.12 = (f32[5,4,128]{2,1,0:T(4,128)S(1)}, f32[5,4,128]{2,1,0:T(4,128)S(1)}, u32[]{:S(2)}, u32[]{:S(2)}) collective-permute-start(f32[5,4,128]{2,1,0:T(4,128)S(1)} %pad_maximum_fusion.4.base_0), channel_id=1, source_target_pairs={{0,8},{4,12},{8,0},{12,4},{1,9},{5,13},{9,1},{13,5},{2,10},{6,14},... | collective-permute-start | bytes 30728 | tf_op jit(solution)/shard_map/ppermute | solution.py:32
  35.3 0.8 %copy-start.9 = (f32[5,4,128]{2,1,0:T(4,128)}, f32[5,4,128]{2,1,0:T(4,128)S(1)}, u32[]{:S(2)}) copy-start(f32[5,4,128]{2,1,0:T(4,128)S(1)} %collective-permute-done.13.base_3) | copy-start | bytes 30724
  35.3 3.7 %collective-permute-start.11 = (f32[5,4,128]{2,1,0:T(4,128)S(1)}, f32[5,4,128]{2,1,0:T(4,128)S(1)}, u32[]{:S(2)}, u32[]{:S(2)}) collective-permute-start(f32[5,4,128]{2,1,0:T(4,128)S(1)} %pad_maximum_fusion.4.base_0), channel_id=1, source_target_pairs={{0,4},{4,0},{8,12},{12,8},{1,5},{5,1},{9,13},{13,9},{2,6},{6,2},{1... | collective-permute-start | bytes 30728 | tf_op jit(solution)/shard_map/ppermute | solution.py:32
  38.0 1.0 %copy-start.10 = (f32[5,4,128]{2,1,0:T(4,128)}, f32[5,4,128]{2,1,0:T(4,128)S(1)}, u32[]{:S(2)}) copy-start(f32[5,4,128]{2,1,0:T(4,128)S(1)} %collective-permute-done.12.base_2) | copy-start | bytes 30724
  38.9 0.6 %copy-start.11 = (f32[5,4,128]{2,1,0:T(4,128)}, f32[5,4,128]{2,1,0:T(4,128)S(1)}, u32[]{:S(2)}) copy-start(f32[5,4,128]{2,1,0:T(4,128)S(1)} %collective-permute-done.11.base_1) | copy-start | bytes 30724
  39.0 0.7 %copy-start.5 = (bf16[4,64,512]{2,1,0:T(8,128)(2,1)}, bf16[4,64,512]{2,1,0:T(8,128)(2,1)S(1)}, u32[]{:S(2)}) copy-start(bf16[4,64,512]{2,1,0:T(8,128)(2,1)S(1)} %collective-permute-done.5.far_s) | copy-start | bytes 786436
  39.0 0.8 %copy-start.6 = (bf16[4,64,512]{2,1,0:T(8,128)(2,1)}, bf16[4,64,512]{2,1,0:T(8,128)(2,1)S(1)}, u32[]{:S(2)}) copy-start(bf16[4,64,512]{2,1,0:T(8,128)(2,1)S(1)} %collective-permute-done.4.mid_s) | copy-start | bytes 786436
  39.8 0.7 %copy-start.2 = (bf16[5,64,512]{2,1,0:T(8,128)(2,1)}, bf16[5,64,512]{2,1,0:T(8,128)(2,1)S(1)}, u32[]{:S(2)}) copy-start(bf16[5,64,512]{2,1,0:T(8,128)(2,1)S(1)} %collective-permute-done.3.near_s) | copy-start | bytes 983044
  47.0 3.9 %collective-permute-start.14 = (f32[5,4,128]{2,1,0:T(4,128)}, f32[5,4,128]{2,1,0:T(4,128)S(1)}, u32[]{:S(2)}, u32[]{:S(2)}) collective-permute-start(f32[5,4,128]{2,1,0:T(4,128)} %get-tuple-element.7), channel_id=1, source_target_pairs={{0,2},{2,0},{4,6},{6,4},{8,10},{10,8},{12,14},{14,12},{1,3},{3,1},... | collective-permute-start | bytes 30728 | tf_op jit(solution)/shard_map/ppermute | solution.py:302
  47.4 4.8 %collective-permute-start.16 = (f32[5,4,128]{2,1,0:T(4,128)}, f32[5,4,128]{2,1,0:T(4,128)S(1)}, u32[]{:S(2)}, u32[]{:S(2)}) collective-permute-start(f32[5,4,128]{2,1,0:T(4,128)} %get-tuple-element.8), channel_id=1, source_target_pairs={{0,6},{2,4},{4,2},{6,0},{8,14},{10,12},{12,10},{14,8},{1,7},{3,5},... | collective-permute-start | bytes 30728 | tf_op jit(solution)/shard_map/ppermute | solution.py:302
  49.6 3.9 %collective-permute-start.15 = (f32[5,4,128]{2,1,0:T(4,128)}, f32[5,4,128]{2,1,0:T(4,128)S(1)}, u32[]{:S(2)}, u32[]{:S(2)}) collective-permute-start(f32[5,4,128]{2,1,0:T(4,128)} %get-tuple-element.8), channel_id=1, source_target_pairs={{0,4},{2,6},{4,0},{6,2},{8,12},{10,14},{12,8},{14,10},{1,5},{3,7},... | collective-permute-start | bytes 30728 | tf_op jit(solution)/shard_map/ppermute | solution.py:302

commit v3 on v1

v3 whole, which is shorter than its diff:
```python
import jax
import jax.numpy as jnp
from jax import lax
from jax.experimental import pallas as pl
from jax.experimental.pallas import tpu as pltpu
from jax.sharding import PartitionSpec as P

RIM = 8
STEPS = 5
LATE = STEPS - 1
GUST_ROWS = 8


def flips(value, flipped=(1, 2, 3)):
    count = lax.axis_size("elem")
    return [value] + [
        lax.ppermute(value, "elem", [(i, i ^ flip) for i in range(count)]) for flip in flipped
    ]


def lag_behind(value):
    count = lax.axis_size("lag")
    moved = lax.ppermute(value, "lag", [(i, (i + 1) % count) for i in range(count)])
    return jnp.where(lax.axis_index("lag") == 0, jnp.zeros_like(moved), moved)


def by_offset(neighbours, edge_coef):
    rows = neighbours.shape[1]
    total = rows * lax.axis_size("elem")
    places = lax.axis_index("elem") * rows + jnp.arange(rows, dtype=jnp.int32)
    return (neighbours - places[None, :] + RIM) % total


def spread_weights(offsets, edge_coef):
    return [
        jnp.sum(jnp.where(offsets == d, edge_coef, 0.0), axis=0, keepdims=True)
        for d in range(2 * RIM + 1)
    ]


def own_gradient(newest, spread):
    rows = spread[0].shape[1]
    total = newest.shape[1]
    wide = jnp.concatenate([newest[:, total - RIM :], newest, newest[:, :RIM]], axis=1)
    start = lax.axis_index("elem") * rows
    window = lax.dynamic_slice(wide, (0, start), (newest.shape[0], rows + 2 * RIM))
    own = window[:, RIM : RIM + rows]
    out = jnp.zeros_like(own)
    for d in range(2 * RIM + 1):
        if d != RIM:
            out += spread[d] * (window[:, d : d + rows] - own)
    return out


def known_part(hist, masked):
    lags, gusts, total = hist.shape
    longer = jnp.concatenate([lag_behind(hist[lags - LATE :]), hist], axis=0)
    stacked = jnp.stack(
        [longer[LATE - step : LATE - step + lags] for step in range(STEPS)], axis=1
    ).reshape(lags, STEPS * gusts, total)
    part = jnp.einsum("lmc,lrc->mr", stacked, masked, preferred_element_type=jnp.float32)
    return part.reshape(STEPS, gusts, masked.shape[1])


def live_coefficients(interaction, block_mask, rows):
    live = jnp.repeat(block_mask[:, 0, :].astype(jnp.bfloat16), rows, axis=1)
    return interaction * live[:, None, :]


def exchange_each_step(
    history, forcing, interaction, block_mask, correction, neighbours, edge_coef
):
    rows = correction.shape[0]
    masked = live_coefficients(interaction, block_mask, rows)
    spread = spread_weights(by_offset(neighbours, edge_coef), edge_coef)

    def gathered(value, dim):
        return lax.all_gather(value, "elem", axis=dim, tiled=True)

    hist = gathered(history.astype(jnp.bfloat16), 2)
    newest = gathered(history[0], 1)
    base = forcing - lax.psum(known_part(hist, masked), "lag")
    fresh_b = []
    results = []
    for step in range(STEPS):
        drive = base[step] + own_gradient(newest, spread)
        if step:
            past = jnp.stack(fresh_b[::-1], axis=0)
            drive -= jnp.einsum(
                "lgc,lrc->gr", past, masked[:step], preferred_element_type=jnp.float32
            )
        fresh = drive + jnp.dot(drive, correction.T, precision=lax.Precision.HIGHEST)
        results.append(fresh)
        if step < LATE:
            newest = gathered(fresh, 1)
            fresh_b.append(newest.astype(jnp.bfloat16))
    first = lax.axis_index("lag") == 0
    return lax.psum(jnp.where(first, jnp.stack(results, 0), 0.0), "lag")


def dot_rows(lhs, rhs):
    return lax.dot_general(lhs, rhs, (((1,), (1,)), ((), ())), preferred_element_type=jnp.float32)


def words_of(value, count):
    out = []
    for _ in range(count):
        word = value.astype(jnp.bfloat16)
        out.append(word)
        value = value - word.astype(jnp.float32)
    return out


def pack(history, neighbours, edge_coef, message):
    lags, gusts, rows = history.shape
    total = rows * lax.axis_size("elem")
    places = lax.axis_index("elem") * rows + lax.broadcasted_iota(
        jnp.int32, neighbours.shape, 1
    )
    offsets = lax.rem(neighbours[...] - places + (RIM + total), total)
    pieces = [history[lag] for lag in range(lags)]
    _, mid, low = words_of(history[0], 3)
    pieces += [mid.astype(jnp.float32), low.astype(jnp.float32), offsets.astype(jnp.float32)]
    pieces += [word.astype(jnp.float32) for word in words_of(edge_coef[...], 3)]
    pieces += [jnp.zeros_like(pieces[0])] * (message.shape[0] // gusts - len(pieces))
    message[...] = jnp.concatenate(pieces, axis=0).astype(jnp.bfloat16)


def make_load(mask, interaction, correction, masked, own_c, load):
    lags, rows, total = interaction.shape
    blocks = total // rows
    cut = rows // 2
    for lag in range(lags):
        for block in range(blocks):
            columns = pl.ds(block * rows, rows)
            piece = interaction[lag, :, columns]
            live = mask[lag, block] != 0
            masked[lag, :, columns] = jnp.where(live, piece, jnp.zeros_like(piece))
    own_c[...] = jnp.concatenate(words_of(correction[...], 2), axis=1)
    start = pl.multiple_of(lax.axis_index("gust") * cut, cut)
    for lag in range(LATE - 1):
        load[:, pl.ds(lag * total, total)] = masked[lag, pl.ds(start, cut), :]
    load[:, pl.ds((LATE - 1) * total, 2 * rows)] = own_c[pl.ds(start, cut), :]


def order(piece_0, piece_1, piece_2, piece_3, everyone, late):
    place = lax.axis_index("elem")
    rows = piece_0.shape[1]
    for flip, piece in enumerate((piece_0, piece_1, piece_2, piece_3)):
        start = pl.multiple_of((place ^ flip) * rows, rows)
        everyone[:, pl.ds(start, rows)] = piece[...]
    late[...] = everyone[late.shape[0] : 2 * late.shape[0], :]


def slope_of(newest, spread_ref):
    total = newest.shape[1]
    out = jnp.zeros_like(newest)
    for d in range(2 * RIM):
        shift = d - RIM if d < RIM else d - RIM + 1
        moved = pltpu.roll(newest, (-shift) % total, 1)
        out += spread_ref[d : d + 1, :] * (moved - newest)
    return out


def main_part(everyone, masked, part, slope, spread, longer, slopes):
    lags, rows, total = masked.shape
    gusts = 4
    known = lags * gusts
    wide = everyone[...].astype(jnp.float32)
    longer[...] = jnp.zeros_like(longer)
    longer[LATE * gusts : LATE * gusts + known, :] = wide[:known]
    acc = jnp.zeros(part.shape, jnp.float32)
    for lag in range(lags):
        lhs = longer[lag * gusts : lag * gusts + part.shape[0], :].astype(jnp.bfloat16)
        acc += dot_rows(lhs, masked[lag])
    part[...] = acc

    def piece(index):
        return wide[known + index * gusts : known + (index + 1) * gusts]

    newest = wide[:gusts] + (piece(0) + piece(1))
    offsets = piece(2)
    coef = piece(3) + (piece(4) + piece(5))
    for d in range(2 * RIM):
        value = d if d < RIM else d + 1
        spread[d : d + 1, :] = jnp.sum(
            jnp.where(offsets == float(value), coef, 0.0), axis=0, keepdims=True
        )
    newest = jnp.concatenate([newest, jnp.zeros_like(newest)], axis=0)
    slopes[...] = slope_of(newest, spread)
    start = pl.multiple_of(lax.axis_index("elem") * rows, rows)
    slope[...] = slopes[:, pl.ds(start, rows)]


def late_part(late, masked, part, both, longer):
    gusts = late.shape[0] // LATE
    value = late[...].astype(jnp.float32)
    longer[...] = jnp.zeros_like(longer)
    longer[: late.shape[0], :] = jnp.where(lax.axis_index("lag") == 0, 0.0, value)
    acc = part[...]
    for lag in range(LATE):
        lhs = longer[lag * gusts : lag * gusts + part.shape[0], :].astype(jnp.bfloat16)
        acc += dot_rows(lhs, masked[lag])
    both[...] = acc


def make_base(part, other, forcing, slope, base):
    gusts = forcing.shape[1]
    known = part[...] + other[...]
    for step in range(STEPS):
        at = (STEPS - 1 - step) * gusts
        value = forcing[step] - known[at : at + gusts]
        if step == 0:
            value = value + slope[:gusts]
        base[step] = jnp.concatenate([value, jnp.zeros_like(value)], axis=0)


def march(
    masked, load_1, load_2, load_3, swap_1, swap_2, swap_3, own_c,
    base_0, base_1, base_2, base_3, spread, out,
):
    place = lax.axis_index("elem")
    second = lax.axis_index("gust") == 1
    _, rows, total = masked.shape
    cut = rows // 2
    flips_of = range(total // rows)
    loads = (None, load_1, load_2, load_3)
    swaps = (None, swap_1, swap_2, swap_3)

    def flipped(values):
        odd = place % 2 == 1
        high = place // 2 == 1
        near = [jnp.where(odd, values[i ^ 1], values[i]) for i in flips_of]
        return [jnp.where(high, near[i ^ 2], near[i]) for i in flips_of]

    def rows_right(value):
        return jnp.where(second, pltpu.roll(value, cut, 1), value)

    def received(flip, start, count):
        columns = pl.ds(start, count)
        return jnp.concatenate([loads[flip][:, columns], swaps[flip][:, columns]], axis=0)

    def times(fresh_b, lag, flip):
        if flip == 0:
            return dot_rows(fresh_b, masked[lag])
        return rows_right(dot_rows(fresh_b, received(flip, lag * total, total)))

    def corrected(drive, flip):
        lhs = jnp.concatenate(words_of(drive, 2), axis=0)
        added = 0.0
        for word in range(2):
            if flip == 0:
                rhs = own_c[:, word * rows : (word + 1) * rows]
            else:
                rhs = received(flip, (LATE - 1) * total + word * rows, rows)
            both = dot_rows(lhs, rhs)
            added = added + (both[:GUST_ROWS] + both[GUST_ROWS:])
        return drive + (added if flip == 0 else rows_right(added))

    waiting = [[base[step] for base in (base_0, base_1, base_2, base_3)] for step in range(STEPS)]
    waiting[LATE] = waiting[LATE][:1]
    for step in range(LATE):
        fresh = [corrected(waiting[step][flip], flip) for flip in flips_of]
        out[step] = fresh[0]
        whole = jnp.concatenate(flipped(fresh), axis=1)
        fresh_b = whole.astype(jnp.bfloat16)
        slope = slope_of(whole, spread)
        slope = flipped([slope[:, i * rows : (i + 1) * rows] for i in flips_of])
        for later in range(step + 1, STEPS):
            lag = later - step - 1
            for flip in range(len(waiting[later])):
                change = times(fresh_b, lag, flip)
                if lag == 0:
                    change = change - slope[flip]
                waiting[later][flip] = waiting[later][flip] - change
    out[LATE] = corrected(waiting[LATE][0], 0)


def on_core(body, shapes, operands, scratch=(), in_specs=None, cost=(0, 0), name=None):
    vmem = pl.BlockSpec(memory_space=pltpu.VMEM)
    return pl.pallas_call(
        body,
        out_shape=[jax.ShapeDtypeStruct(shape, dtype) for shape, dtype in shapes],
        in_specs=in_specs or [vmem] * len(operands),
        out_specs=[vmem] * len(shapes),
        scratch_shapes=list(scratch),
        cost_estimate=pl.CostEstimate(flops=cost[0], bytes_accessed=cost[1], transcendentals=0),
        compiler_params=pltpu.CompilerParams(vmem_limit_bytes=24 * 2**20),
        name=name,
    )(*operands)


def places_march(history, forcing, interaction, block_mask, correction, neighbours, edge_coef):
    f32, bf16 = jnp.float32, jnp.bfloat16
    rows = correction.shape[0]
    lags, gusts, _ = history.shape
    total = rows * lax.axis_size("elem")
    part_rows = 24
    vmem = pl.BlockSpec(memory_space=pltpu.VMEM)
    smem = pl.BlockSpec(memory_space=pltpu.SMEM)

    (message,) = on_core(
        pack, [((64, rows), bf16)], (history, neighbours, edge_coef), name="pack"
    )
    messages = flips(message)
    masked, own_c, load = on_core(
        make_load,
        [
            (interaction.shape, bf16),
            ((rows, 2 * rows), bf16),
            ((rows // 2, (LATE - 1) * total + 2 * rows), bf16),
        ],
        (block_mask[:, 0, :], interaction, correction),
        in_specs=[smem, vmem, vmem],
        cost=(10**6, 3 * 2**20),
        name="load",
    )
    loads = flips(load)[1:]
    swaps = [lax.ppermute(piece, "gust", [(0, 1), (1, 0)]) for piece in loads]

    everyone, late = on_core(
        order, [((64, total), bf16), ((LATE * gusts, total), bf16)], messages, name="order"
    )
    before = lax.ppermute(late, "lag", [(0, 1), (1, 0)])
    part, slope, spread = on_core(
        main_part,
        [((part_rows, rows), f32), ((GUST_ROWS, rows), f32), ((2 * RIM, total), f32)],
        (everyone, masked),
        scratch=[pltpu.VMEM((56, total), f32), pltpu.VMEM((GUST_ROWS, total), f32)],
        cost=(10**7, 2**20),
        name="main_part",
    )
    (part,) = on_core(
        late_part,
        [((part_rows, rows), f32)],
        (before, masked, part),
        scratch=[pltpu.VMEM((40, total), f32)],
        name="late_part",
    )
    other = lax.ppermute(part, "lag", [(0, 1), (1, 0)])
    (base,) = on_core(
        make_base,
        [((STEPS, GUST_ROWS, rows), f32)],
        (part, other, forcing, slope),
        name="base",
    )
    bases = flips(base)
    (own,) = on_core(
        march,
        [((STEPS, GUST_ROWS, rows), f32)],
        (masked, *loads, *swaps, own_c, *bases, spread),
        cost=(10**8, 4 * 2**20),
        name="march",
    )
    moved = lax.ppermute(own, "lag", [(0, 1), (1, 0)])
    return jnp.where(lax.axis_index("lag") == 0, own, moved)[:, :gusts]


def solution(mesh):
    placed = (
        P("lag", ("groups", "gust"), "elem"),
        P(None, ("groups", "gust"), "elem"),
        P("lag", "elem", None),
        P("lag", "elem", None),
        P("elem", None),
        P(None, "elem"),
        P(None, "elem"),
    )
    small = mesh.shape["elem"] == 4 and mesh.shape["lag"] == 2 and mesh.shape["gust"] == 2
    return jax.shard_map(
        places_march if small else exchange_each_step,
        mesh=mesh,
        in_specs=placed,
        out_specs=P(None, ("groups", "gust"), "elem"),
        check_vma=False,
    )
```

time: 65.9 us -> 61.8 us (0.938)
  waiting for transfers between devices: 13.6 us -> 30.5 us
  blocking collectives: 15.9 us -> 0 us
  starting transfers between devices: 29.4 us -> 23.6 us
  Pallas kernels: 0 us -> 4.09 us
  matrix products: 2.46 us -> 0 us
  other arithmetic: 1.55 us -> 0.6 us
    ppermute x19 -> x15, waiting for transfers between devices: 13.6 us -> 30.5 us  [the longest x9 24.2 us: flips(): lax.ppermute(value, 'elem', [(i, i ^ flip) for i in range(count)])]
    psum x2 -> x0, blocking collectives: 15.9 us -> none  [the longest x1 8.16 us: on_device(): known = lax.psum(partial.reshape(STEPS, gusts, rows), 'lag')]
    ppermute x19 -> x15, starting transfers between devices: 29.4 us -> 23.6 us  [the longest x9 18.5 us: flips(): lax.ppermute(value, 'elem', [(i, i ^ flip) for i in range(count)])]
    pallas_call x0 -> x7, Pallas kernels: none -> 4.09 us  [on_core(): pl.pallas_call(body, out_shape=[jax.ShapeDtypeStruct(shape, dtype) for sh...]
    dot_general x10 -> x0, matrix products: 2.46 us -> none  [the longest x5 1.05 us: on_device(): fresh = drive + jnp.dot(drive, correction.T, precision=precise)]
    mul x1 -> x0, other arithmetic: 1.33 us -> none  [on_device(): masked = interaction * live[:, None, :]]
    squeeze x1, local copies, waits for them, and re-layouts: 0.01 us -> 0.76 us  [places_march(): block_mask[:, 0, :]]
    unnamed x16 -> x12, local copies, waits for them, and re-layouts: 1.54 us -> 2.08 us
  transfers between devices with their start and end apart: 19 -> 15, of which waited for: 12 -> 10; matrix products, arithmetic and copies ran while one was open for 2% -> 0% of each run, Pallas kernels for 0% -> 1%
where the time goes in v3:
time: 61.8 us; the launch traced here: 61.6 us
  waiting for transfers between devices  30.5 us (49%)
  starting transfers between devices  23.6 us (38%)
  Pallas kernels  4.09 us (7%)
  local copies, waits for them, and re-layouts  2.83 us (5%)
    ppermute x9, waiting for transfers between devices, flips(): lax.ppermute(value, 'elem', [(i, i ^ flip) for i in range(count)])  24.2 us
    ppermute x9, starting transfers between devices, flips(): lax.ppermute(value, 'elem', [(i, i ^ flip) for i in range(count)])  18.5 us
    pallas_call x7, Pallas kernels, on_core(): pl.pallas_call(body, out_shape=[jax.ShapeDtypeStruct(shape, dtype) for sh...  4.09 us
    ppermute x1, waiting for transfers between devices, places_march(): moved = lax.ppermute(own, 'lag', [(0, 1), (1, 0)])  2.29 us
    ppermute x1, waiting for transfers between devices, places_march(): other = lax.ppermute(part, 'lag', [(0, 1), (1, 0)])  2.2 us
    unnamed x12, local copies, waits for them, and re-layouts  2.08 us
    ppermute x1, waiting for transfers between devices, places_march(): before = lax.ppermute(late, 'lag', [(0, 1), (1, 0)])  1.78 us
    ppermute x1, starting transfers between devices, places_march(): before = lax.ppermute(late, 'lag', [(0, 1), (1, 0)])  1.55 us
  transfers between devices with their start and end apart: 15, of which 10 were waited for; matrix products, arithmetic and copies ran while one was open for 0% of the time, Pallas kernels for 1%

profile of v3, /device:TPU:0, one launch (start us, length us, event | category | flops | bytes accessed | tf_op | source)
XLA Modules:
  0.0 61.6 jit_solution(15625308213848572309)
XLA Ops:
  0.0 0.8 %copy.8.mask = s32[8,4]{1,0:T(8,128)S(1)} copy(s32[8,4]{0,1:T(4,128)} %bitcast.1) | data formatting | bytes 256 | tf_op jit(solution)/shard_map/squeeze | solution.py:313
  0.8 0.0 copy-start
  0.8 1.2 %copy-done = bf16[8,128,512]{2,1,0:T(8,128)(2,1)S(1)} copy-done((bf16[8,128,512]{2,1,0:T(8,128)(2,1)S(1)}, bf16[8,128,512]{2,1,0:T(8,128)(2,1)}, u32[]{:S(2)}) %copy-start) | copy-done | bytes 1048600
  2.0 0.0 copy-start.1
  2.0 0.8 %copy-done.1 = f32[128,128]{1,0:T(8,128)S(1)} copy-done((f32[128,128]{1,0:T(8,128)S(1)}, f32[128,128]{1,0:T(8,128)}, u32[]{:S(2)}) %copy-start.1) | copy-done | bytes 65560
  2.8 0.0 copy-start.2
  2.8 0.0 copy-start.4
  2.8 0.0 copy-start.5
  2.8 0.9 %load.1 = (bf16[8,128,512]{2,1,0:T(8,128)(2,1)S(1)}, bf16[128,256]{1,0:T(8,128)(2,1)S(1)}, bf16[64,1792]{1,0:T(8,128)(2,1)S(1)}) custom-call(s32[8,4]{1,0:T(8,128)S(1)} %copy.8.mask, bf16[8,128,512]{2,1,0:T(8,128)(2,1)S(1)} %copy-done, f32[128,128]{1,0:T(8,128)S(1)} %copy-done.1), custom_call_target="tpu_custom_call" | custom-call | flops 1000000 | bytes 3145728 | tf_op jit(solution)/shard_map/load/pallas_call | solution.py:281
  3.7 3.1 %collective-permute-start = (bf16[64,1792]{1,0:T(8,128)(2,1)S(1)}, bf16[64,1792]{1,0:T(8,128)(2,1)S(1)}, u32[]{:S(2)}, u32[]{:S(2)}) collective-permute-start(bf16[64,1792]{1,0:T(8,128)(2,1)S(1)} %get-tuple-element.14), channel_id=1, source_target_pairs={{0,4},{4,0},{8,12},{12,8},{1,5},{5,1},{9,13},{13,9},{2,6},{6,2},{1... | collective-permute-start | bytes 688136 | tf_op jit(solution)/shard_map/ppermute | solution.py:17
  6.8 2.6 %collective-permute-start.1 = (bf16[64,1792]{1,0:T(8,128)(2,1)S(1)}, bf16[64,1792]{1,0:T(8,128)(2,1)S(1)}, u32[]{:S(2)}, u32[]{:S(2)}) collective-permute-start(bf16[64,1792]{1,0:T(8,128)(2,1)S(1)} %get-tuple-element.14), channel_id=1, source_target_pairs={{0,8},{4,12},{8,0},{12,4},{1,9},{5,13},{9,1},{13,5},{2,10},{6,14},... | collective-permute-start | bytes 688136 | tf_op jit(solution)/shard_map/ppermute | solution.py:17
  9.4 0.0 collective-permute-start.2
  9.4 7.2 %collective-permute-done.load_1 = bf16[64,1792]{1,0:T(8,128)(2,1)S(1)} collective-permute-done((bf16[64,1792]{1,0:T(8,128)(2,1)S(1)}, bf16[64,1792]{1,0:T(8,128)(2,1)S(1)}, u32[]{:S(2)}, u32[]{:S(2)}) %collective-permute-start) | collective-permute-done | bytes 229408 | tf_op jit(solution)/shard_map/ppermute | solution.py:17
  16.5 0.0 collective-permute-start.3
  16.5 9.5 %collective-permute-done.1.load_2 = bf16[64,1792]{1,0:T(8,128)(2,1)S(1)} collective-permute-done((bf16[64,1792]{1,0:T(8,128)(2,1)S(1)}, bf16[64,1792]{1,0:T(8,128)(2,1)S(1)}, u32[]{:S(2)}, u32[]{:S(2)}) %collective-permute-start.1) | collective-permute-done | bytes 229408 | tf_op jit(solution)/shard_map/ppermute | solution.py:17
  26.0 0.0 collective-permute-start.4
  26.0 0.0 collective-permute-done.2.load_3
  26.1 0.5 collective-permute-start.5
  26.6 0.0 copy-done.2
  26.6 0.0 copy-done.4
  26.6 0.0 copy-done.5
  26.6 3.6 %collective-permute-start.6 = (bf16[64,128]{1,0:T(8,128)(2,1)S(1)}, bf16[64,128]{1,0:T(8,128)(2,1)S(1)}, u32[]{:S(2)}, u32[]{:S(2)}) collective-permute-start(bf16[64,128]{1,0:T(8,128)(2,1)S(1)} %pack.1.piece_0), channel_id=1, source_target_pairs={{0,4},{4,0},{8,12},{12,8},{1,5},{5,1},{9,13},{13,9},{2,6},{6,2},{1... | collective-permute-start | bytes 49160 | tf_op jit(solution)/shard_map/ppermute | solution.py:17
  30.2 1.1 %collective-permute-start.7 = (bf16[64,128]{1,0:T(8,128)(2,1)S(1)}, bf16[64,128]{1,0:T(8,128)(2,1)S(1)}, u32[]{:S(2)}, u32[]{:S(2)}) collective-permute-start(bf16[64,128]{1,0:T(8,128)(2,1)S(1)} %pack.1.piece_0), channel_id=1, source_target_pairs={{0,8},{4,12},{8,0},{12,4},{1,9},{5,13},{9,1},{13,5},{2,10},{6,14},... | collective-permute-start | bytes 49160 | tf_op jit(solution)/shard_map/ppermute | solution.py:17
  31.3 0.6 %collective-permute-done.6.piece_1 = bf16[64,128]{1,0:T(8,128)(2,1)S(1)} collective-permute-done((bf16[64,128]{1,0:T(8,128)(2,1)S(1)}, bf16[64,128]{1,0:T(8,128)(2,1)S(1)}, u32[]{:S(2)}, u32[]{:S(2)}) %collective-permute-start.6) | collective-permute-done | bytes 16416 | tf_op jit(solution)/shard_map/ppermute | solution.py:17
  31.9 2.5 %collective-permute-start.8 = (bf16[64,128]{1,0:T(8,128)(2,1)S(1)}, bf16[64,128]{1,0:T(8,128)(2,1)S(1)}, u32[]{:S(2)}, u32[]{:S(2)}) collective-permute-start(bf16[64,128]{1,0:T(8,128)(2,1)S(1)} %pack.1.piece_0), channel_id=1, source_target_pairs={{0,12},{4,8},{8,4},{12,0},{1,13},{5,9},{9,5},{13,1},{2,14},{6,10},... | collective-permute-start | bytes 49160 | tf_op jit(solution)/shard_map/ppermute | solution.py:17
  34.4 0.4 collective-permute-done.7.piece_2
  34.9 2.6 %collective-permute-done.8.piece_3 = bf16[64,128]{1,0:T(8,128)(2,1)S(1)} collective-permute-done((bf16[64,128]{1,0:T(8,128)(2,1)S(1)}, bf16[64,128]{1,0:T(8,128)(2,1)S(1)}, u32[]{:S(2)}, u32[]{:S(2)}) %collective-permute-start.8) | collective-permute-done | bytes 16416 | tf_op jit(solution)/shard_map/ppermute | solution.py:17
  37.5 1.6 %collective-permute-start.9 = (bf16[16,512]{1,0:T(8,128)(2,1)S(1)}, bf16[16,512]{1,0:T(8,128)(2,1)S(1)}, u32[]{:S(2)}, u32[]{:S(2)}) collective-permute-start(bf16[16,512]{1,0:T(8,128)(2,1)S(1)} %get-tuple-element.16), channel_id=1, source_target_pairs={{0,2},{2,0},{1,3},{3,1},{4,6},{6,4},{5,7},{7,5},{8,10},{10,8},{9,1... | collective-permute-start | bytes 49160 | tf_op jit(solution)/shard_map/ppermute | solution.py:324
  39.1 0.5 main_part.1
  39.5 1.8 %collective-permute-done.9.late = bf16[16,512]{1,0:T(8,128)(2,1)S(1)} collective-permute-done((bf16[16,512]{1,0:T(8,128)(2,1)S(1)}, bf16[16,512]{1,0:T(8,128)(2,1)S(1)}, u32[]{:S(2)}, u32[]{:S(2)}) %collective-permute-start.9) | collective-permute-done | bytes 16416 | tf_op jit(solution)/shard_map/ppermute | solution.py:324
  41.3 0.0 copy-start.3
  41.3 0.3 late_part.1.part
  41.6 1.5 %collective-permute-start.10 = (f32[24,128]{1,0:T(8,128)S(1)}, f32[24,128]{1,0:T(8,128)S(1)}, u32[]{:S(2)}, u32[]{:S(2)}) collective-permute-start(f32[24,128]{1,0:T(8,128)S(1)} %late_part.1.part), channel_id=1, source_target_pairs={{0,2},{2,0},{1,3},{3,1},{4,6},{6,4},{5,7},{7,5},{8,10},{10,8},{9,1... | collective-permute-start | bytes 36872 | tf_op jit(solution)/shard_map/ppermute | solution.py:340
  43.1 2.2 %collective-permute-done.10.other = f32[24,128]{1,0:T(8,128)S(1)} collective-permute-done((f32[24,128]{1,0:T(8,128)S(1)}, f32[24,128]{1,0:T(8,128)S(1)}, u32[]{:S(2)}, u32[]{:S(2)}) %collective-permute-start.10) | collective-permute-done | bytes 12320 | tf_op jit(solution)/shard_map/ppermute | solution.py:340
  45.3 0.0 copy-done.3
  45.3 0.4 collective-permute-start.11
  45.7 2.7 %collective-permute-start.12 = (f32[5,8,128]{2,1,0:T(8,128)S(1)}, f32[5,8,128]{2,1,0:T(8,128)S(1)}, u32[]{:S(2)}, u32[]{:S(2)}) collective-permute-start(f32[5,8,128]{2,1,0:T(8,128)S(1)} %base.1.base_0), channel_id=1, source_target_pairs={{0,8},{4,12},{8,0},{12,4},{1,9},{5,13},{9,1},{13,5},{2,10},{6,14},... | collective-permute-start | bytes 61448 | tf_op jit(solution)/shard_map/ppermute | solution.py:17
  48.4 0.7 %collective-permute-done.11.base_1 = f32[5,8,128]{2,1,0:T(8,128)S(1)} collective-permute-done((f32[5,8,128]{2,1,0:T(8,128)S(1)}, f32[5,8,128]{2,1,0:T(8,128)S(1)}, u32[]{:S(2)}, u32[]{:S(2)}) %collective-permute-start.11) | collective-permute-done | bytes 20512 | tf_op jit(solution)/shard_map/ppermute | solution.py:17
  49.1 2.5 %collective-permute-start.13 = (f32[5,8,128]{2,1,0:T(8,128)S(1)}, f32[5,8,128]{2,1,0:T(8,128)S(1)}, u32[]{:S(2)}, u32[]{:S(2)}) collective-permute-start(f32[5,8,128]{2,1,0:T(8,128)S(1)} %base.1.base_0), channel_id=1, source_target_pairs={{0,12},{4,8},{8,4},{12,0},{1,13},{5,9},{9,5},{13,1},{2,14},{6,10},... | collective-permute-start | bytes 61448 | tf_op jit(solution)/shard_map/ppermute | solution.py:17
  51.7 0.0 collective-permute-done.12.base_2
  51.7 3.1 %collective-permute-done.13.base_3 = f32[5,8,128]{2,1,0:T(8,128)S(1)} collective-permute-done((f32[5,8,128]{2,1,0:T(8,128)S(1)}, f32[5,8,128]{2,1,0:T(8,128)S(1)}, u32[]{:S(2)}, u32[]{:S(2)}) %collective-permute-start.13) | collective-permute-done | bytes 20512 | tf_op jit(solution)/shard_map/ppermute | solution.py:17
  54.7 0.0 collective-permute-done.3.swap_1
  54.7 0.0 collective-permute-done.4.swap_2
  54.7 0.0 collective-permute-done.5.swap_3
  54.7 2.4 %march.1 = f32[5,8,128]{2,1,0:T(8,128)S(1)} custom-call(bf16[8,128,512]{2,1,0:T(8,128)(2,1)S(1)} %get-tuple-element.13.masked, bf16[64,1792]{1,0:T(8,128)(2,1)S(1)} %collective-permute-done.load_1, bf16[64,1792]{1,0:T(8,128)(2,1)S(1)} %collective-permute-done.1.load_2, bf16[64,1792]{1,0:T(8,128)(2,1)S(1)} %collective-permute-done.2.load_3, ...), custom_call_target="tpu_custom_call" | custom-call | flops 100000000 | bytes 4194304 | tf_op jit(solution)/shard_map/march/pallas_call | solution.py:281
  57.2 1.5 %collective-permute-start.14 = (f32[5,8,128]{2,1,0:T(8,128)S(1)}, f32[5,8,128]{2,1,0:T(8,128)S(1)}, u32[]{:S(2)}, u32[]{:S(2)}) collective-permute-start(f32[5,8,128]{2,1,0:T(8,128)S(1)} %march.1), channel_id=1, source_target_pairs={{0,2},{2,0},{1,3},{3,1},{4,6},{6,4},{5,7},{7,5},{8,10},{10,8},{9,1... | collective-permute-start | bytes 61448 | tf_op jit(solution)/shard_map/ppermute | solution.py:355
  58.7 2.3 %collective-permute-done.14 = f32[5,8,128]{2,1,0:T(8,128)S(1)} collective-permute-done((f32[5,8,128]{2,1,0:T(8,128)S(1)}, f32[5,8,128]{2,1,0:T(8,128)S(1)}, u32[]{:S(2)}, u32[]{:S(2)}) %collective-permute-start.14) | collective-permute-done | bytes 20512 | tf_op jit(solution)/shard_map/ppermute | solution.py:355
  61.0 0.6 slice_select_fusion
  (3 shorter events, 0.1 us)
Async XLA Ops:
  0.8 1.2 %copy-start = (bf16[8,128,512]{2,1,0:T(8,128)(2,1)S(1)}, bf16[8,128,512]{2,1,0:T(8,128)(2,1)}, u32[]{:S(2)}) copy-start(bf16[8,128,512]{2,1,0:T(8,128)(2,1)} %interaction.1) | copy-start | bytes 3145732
  2.0 0.8 %copy-start.1 = (f32[128,128]{1,0:T(8,128)S(1)}, f32[128,128]{1,0:T(8,128)}, u32[]{:S(2)}) copy-start(f32[128,128]{1,0:T(8,128)} %correction.1) | copy-start | bytes 196612
  2.8 23.7 %copy-start.2 = (f32[8,4,128]{2,1,0:T(4,128)S(1)}, f32[8,4,128]{2,1,0:T(4,128)}, u32[]{:S(2)}) copy-start(f32[8,4,128]{2,1,0:T(4,128)} %history.1) | copy-start | bytes 49156
  2.8 23.7 %copy-start.4 = (s32[4,128]{1,0:T(4,128)S(1)}, s32[4,128]{1,0:T(4,128)}, u32[]{:S(2)}) copy-start(s32[4,128]{1,0:T(4,128)} %neighbours.1) | copy-start | bytes 6148
  2.8 23.7 %copy-start.5 = (f32[4,128]{1,0:T(4,128)S(1)}, f32[4,128]{1,0:T(4,128)}, u32[]{:S(2)}) copy-start(f32[4,128]{1,0:T(4,128)} %edge_coef.1) | copy-start | bytes 6148
  3.7 12.8 %collective-permute-start = (bf16[64,1792]{1,0:T(8,128)(2,1)S(1)}, bf16[64,1792]{1,0:T(8,128)(2,1)S(1)}, u32[]{:S(2)}, u32[]{:S(2)}) collective-permute-start(bf16[64,1792]{1,0:T(8,128)(2,1)S(1)} %get-tuple-element.14), channel_id=1, source_target_pairs={{0,4},{4,0},{8,12},{12,8},{1,5},{5,1},{9,13},{13,9},{2,6},{6,2},{1... | collective-permute-start | bytes 688136 | tf_op jit(solution)/shard_map/ppermute | solution.py:17
  6.8 19.3 %collective-permute-start.1 = (bf16[64,1792]{1,0:T(8,128)(2,1)S(1)}, bf16[64,1792]{1,0:T(8,128)(2,1)S(1)}, u32[]{:S(2)}, u32[]{:S(2)}) collective-permute-start(bf16[64,1792]{1,0:T(8,128)(2,1)S(1)} %get-tuple-element.14), channel_id=1, source_target_pairs={{0,8},{4,12},{8,0},{12,4},{1,9},{5,13},{9,1},{13,5},{2,10},{6,14},... | collective-permute-start | bytes 688136 | tf_op jit(solution)/shard_map/ppermute | solution.py:17
  9.4 16.7 %collective-permute-start.2 = (bf16[64,1792]{1,0:T(8,128)(2,1)S(1)}, bf16[64,1792]{1,0:T(8,128)(2,1)S(1)}, u32[]{:S(2)}, u32[]{:S(2)}) collective-permute-start(bf16[64,1792]{1,0:T(8,128)(2,1)S(1)} %get-tuple-element.14), channel_id=1, source_target_pairs={{0,12},{4,8},{8,4},{12,0},{1,13},{5,9},{9,5},{13,1},{2,14},{6,10},... | collective-permute-start | bytes 688136 | tf_op jit(solution)/shard_map/ppermute | solution.py:17
  16.5 38.2 %collective-permute-start.3 = (bf16[64,1792]{1,0:T(8,128)(2,1)S(1)}, bf16[64,1792]{1,0:T(8,128)(2,1)S(1)}, u32[]{:S(2)}, u32[]{:S(2)}) collective-permute-start(bf16[64,1792]{1,0:T(8,128)(2,1)S(1)} %collective-permute-done.load_1), channel_id=1, source_target_pairs={{0,1},{1,0},{2,3},{3,2},{4,5},{5,4},{6,7},{7,6},{8,9},{9,8},{10,11... | collective-permute-start | bytes 688136 | tf_op jit(solution)/shard_map/ppermute | solution.py:319
  26.0 28.7 %collective-permute-start.4 = (bf16[64,1792]{1,0:T(8,128)(2,1)S(1)}, bf16[64,1792]{1,0:T(8,128)(2,1)S(1)}, u32[]{:S(2)}, u32[]{:S(2)}) collective-permute-start(bf16[64,1792]{1,0:T(8,128)(2,1)S(1)} %collective-permute-done.1.load_2), channel_id=1, source_target_pairs={{0,1},{1,0},{2,3},{3,2},{4,5},{5,4},{6,7},{7,6},{8,9},{9,8},{10,11... | collective-permute-start | bytes 688136 | tf_op jit(solution)/shard_map/ppermute | solution.py:319
  26.1 28.7 %collective-permute-start.5 = (bf16[64,1792]{1,0:T(8,128)(2,1)S(1)}, bf16[64,1792]{1,0:T(8,128)(2,1)S(1)}, u32[]{:S(2)}, u32[]{:S(2)}) collective-permute-start(bf16[64,1792]{1,0:T(8,128)(2,1)S(1)} %collective-permute-done.2.load_3), channel_id=1, source_target_pairs={{0,1},{1,0},{2,3},{3,2},{4,5},{5,4},{6,7},{7,6},{8,9},{9,8},{10,11... | collective-permute-start | bytes 688136 | tf_op jit(solution)/shard_map/ppermute | solution.py:319
  26.6 5.3 %collective-permute-start.6 = (bf16[64,128]{1,0:T(8,128)(2,1)S(1)}, bf16[64,128]{1,0:T(8,128)(2,1)S(1)}, u32[]{:S(2)}, u32[]{:S(2)}) collective-permute-start(bf16[64,128]{1,0:T(8,128)(2,1)S(1)} %pack.1.piece_0), channel_id=1, source_target_pairs={{0,4},{4,0},{8,12},{12,8},{1,5},{5,1},{9,13},{13,9},{2,6},{6,2},{1... | collective-permute-start | bytes 49160 | tf_op jit(solution)/shard_map/ppermute | solution.py:17
  30.2 4.6 %collective-permute-start.7 = (bf16[64,128]{1,0:T(8,128)(2,1)S(1)}, bf16[64,128]{1,0:T(8,128)(2,1)S(1)}, u32[]{:S(2)}, u32[]{:S(2)}) collective-permute-start(bf16[64,128]{1,0:T(8,128)(2,1)S(1)} %pack.1.piece_0), channel_id=1, source_target_pairs={{0,8},{4,12},{8,0},{12,4},{1,9},{5,13},{9,1},{13,5},{2,10},{6,14},... | collective-permute-start | bytes 49160 | tf_op jit(solution)/shard_map/ppermute | solution.py:17
  31.9 5.5 %collective-permute-start.8 = (bf16[64,128]{1,0:T(8,128)(2,1)S(1)}, bf16[64,128]{1,0:T(8,128)(2,1)S(1)}, u32[]{:S(2)}, u32[]{:S(2)}) collective-permute-start(bf16[64,128]{1,0:T(8,128)(2,1)S(1)} %pack.1.piece_0), channel_id=1, source_target_pairs={{0,12},{4,8},{8,4},{12,0},{1,13},{5,9},{9,5},{13,1},{2,14},{6,10},... | collective-permute-start | bytes 49160 | tf_op jit(solution)/shard_map/ppermute | solution.py:17
  37.5 3.8 %collective-permute-start.9 = (bf16[16,512]{1,0:T(8,128)(2,1)S(1)}, bf16[16,512]{1,0:T(8,128)(2,1)S(1)}, u32[]{:S(2)}, u32[]{:S(2)}) collective-permute-start(bf16[16,512]{1,0:T(8,128)(2,1)S(1)} %get-tuple-element.16), channel_id=1, source_target_pairs={{0,2},{2,0},{1,3},{3,1},{4,6},{6,4},{5,7},{7,5},{8,10},{10,8},{9,1... | collective-permute-start | bytes 49160 | tf_op jit(solution)/shard_map/ppermute | solution.py:324
  41.3 4.0 %copy-start.3 = (f32[5,4,128]{2,1,0:T(4,128)S(1)}, f32[5,4,128]{2,1,0:T(4,128)}, u32[]{:S(2)}) copy-start(f32[5,4,128]{2,1,0:T(4,128)} %forcing.1) | copy-start | bytes 30724
  41.6 3.7 %collective-permute-start.10 = (f32[24,128]{1,0:T(8,128)S(1)}, f32[24,128]{1,0:T(8,128)S(1)}, u32[]{:S(2)}, u32[]{:S(2)}) collective-permute-start(f32[24,128]{1,0:T(8,128)S(1)} %late_part.1.part), channel_id=1, source_target_pairs={{0,2},{2,0},{1,3},{3,1},{4,6},{6,4},{5,7},{7,5},{8,10},{10,8},{9,1... | collective-permute-start | bytes 36872 | tf_op jit(solution)/shard_map/ppermute | solution.py:340
  45.3 3.8 %collective-permute-start.11 = (f32[5,8,128]{2,1,0:T(8,128)S(1)}, f32[5,8,128]{2,1,0:T(8,128)S(1)}, u32[]{:S(2)}, u32[]{:S(2)}) collective-permute-start(f32[5,8,128]{2,1,0:T(8,128)S(1)} %base.1.base_0), channel_id=1, source_target_pairs={{0,4},{4,0},{8,12},{12,8},{1,5},{5,1},{9,13},{13,9},{2,6},{6,2},{1... | collective-permute-start | bytes 61448 | tf_op jit(solution)/shard_map/ppermute | solution.py:17
  45.7 6.0 %collective-permute-start.12 = (f32[5,8,128]{2,1,0:T(8,128)S(1)}, f32[5,8,128]{2,1,0:T(8,128)S(1)}, u32[]{:S(2)}, u32[]{:S(2)}) collective-permute-start(f32[5,8,128]{2,1,0:T(8,128)S(1)} %base.1.base_0), channel_id=1, source_target_pairs={{0,8},{4,12},{8,0},{12,4},{1,9},{5,13},{9,1},{13,5},{2,10},{6,14},... | collective-permute-start | bytes 61448 | tf_op jit(solution)/shard_map/ppermute | solution.py:17
  49.1 5.6 %collective-permute-start.13 = (f32[5,8,128]{2,1,0:T(8,128)S(1)}, f32[5,8,128]{2,1,0:T(8,128)S(1)}, u32[]{:S(2)}, u32[]{:S(2)}) collective-permute-start(f32[5,8,128]{2,1,0:T(8,128)S(1)} %base.1.base_0), channel_id=1, source_target_pairs={{0,12},{4,8},{8,4},{12,0},{1,13},{5,9},{9,5},{13,1},{2,14},{6,10},... | collective-permute-start | bytes 61448 | tf_op jit(solution)/shard_map/ppermute | solution.py:17
  57.2 3.8 %collective-permute-start.14 = (f32[5,8,128]{2,1,0:T(8,128)S(1)}, f32[5,8,128]{2,1,0:T(8,128)S(1)}, u32[]{:S(2)}, u32[]{:S(2)}) collective-permute-start(f32[5,8,128]{2,1,0:T(8,128)S(1)} %march.1), channel_id=1, source_target_pairs={{0,2},{2,0},{1,3},{3,1},{4,6},{6,4},{5,7},{7,5},{8,10},{10,8},{9,1... | collective-permute-start | bytes 61448 | tf_op jit(solution)/shard_map/ppermute | solution.py:355

commit v4 on v3

--- a/solution.py
+++ b/solution.py
@@ -111,7 +111,21 @@
     return out
 
 
-def pack(history, neighbours, edge_coef, message):
+def fetched(copies, sems):
+    started = [
+        pltpu.make_async_copy(source, target, sems.at[index])
+        for index, (source, target) in enumerate(copies)
+    ]
+    for copy in started:
+        copy.start()
+    for copy in started:
+        copy.wait()
+
+
+def pack(history_in, neighbours_in, edge_coef_in, message, history, neighbours, edge_coef, sems):
+    fetched(
+        [(history_in, history), (neighbours_in, neighbours), (edge_coef_in, edge_coef)], sems
+    )
     lags, gusts, rows = history.shape
     total = rows * lax.axis_size("elem")
     places = lax.axis_index("elem") * rows + lax.broadcasted_iota(
@@ -126,7 +140,14 @@
     message[...] = jnp.concatenate(pieces, axis=0).astype(jnp.bfloat16)
 
 
-def make_load(mask, interaction, correction, masked, own_c, load):
+def make_load(
+    after, mask_in, interaction_in, correction_in, masked, own_c, near_load, mid_load,
+    mask, interaction, correction, sems,
+):
+    del after
+    fetched(
+        [(mask_in, mask), (interaction_in, interaction), (correction_in, correction)], sems
+    )
     lags, rows, total = interaction.shape
     blocks = total // rows
     cut = rows // 2
@@ -134,13 +155,38 @@
         for block in range(blocks):
             columns = pl.ds(block * rows, rows)
             piece = interaction[lag, :, columns]
-            live = mask[lag, block] != 0
+            live = mask[lag, 0, block] != 0
             masked[lag, :, columns] = jnp.where(live, piece, jnp.zeros_like(piece))
     own_c[...] = jnp.concatenate(words_of(correction[...], 2), axis=1)
     start = pl.multiple_of(lax.axis_index("gust") * cut, cut)
-    for lag in range(LATE - 1):
-        load[:, pl.ds(lag * total, total)] = masked[lag, pl.ds(start, cut), :]
-    load[:, pl.ds((LATE - 1) * total, 2 * rows)] = own_c[pl.ds(start, cut), :]
+    places = [lag * total for lag in range(LATE - 1)] + [(LATE - 1) * total + 2 * rows]
+    for lag, at in enumerate(places):
+        near_load[:, pl.ds(at, total)] = masked[lag, pl.ds(start, cut), :]
+    near_load[:, pl.ds((LATE - 1) * total, 2 * rows)] = own_c[pl.ds(start, cut), :]
+    mid_load[...] = near_load[:, : mid_load.shape[1]]
+
+
+def relay(after, near, load):
+    del after
+    load[...] = near[:, : load.shape[1]]
+
+
+def all_spread(after, everyone, spread):
+    del after
+    gusts = 4
+    known = everyone.shape[0] // 2
+
+    def piece(index):
+        at = known + index * gusts
+        return everyone[at : at + gusts, :].astype(jnp.float32)
+
+    offsets = piece(2)
+    coef = piece(3) + (piece(4) + piece(5))
+    for d in range(2 * RIM):
+        value = d if d < RIM else d + 1
+        spread[d : d + 1, :] = jnp.sum(
+            jnp.where(offsets == float(value), coef, 0.0), axis=0, keepdims=True
+        )
 
 
 def order(piece_0, piece_1, piece_2, piece_3, everyone, late):
@@ -162,7 +208,7 @@
     return out
 
 
-def main_part(everyone, masked, part, slope, spread, longer, slopes):
+def main_part(everyone, masked, part, slope, longer, spread, slopes):
     lags, rows, total = masked.shape
     gusts = 4
     known = lags * gusts
@@ -204,20 +250,27 @@
     both[...] = acc
 
 
-def make_base(part, other, forcing, slope, base):
+def known_base(part, forcing, slope, ahead):
     gusts = forcing.shape[1]
-    known = part[...] + other[...]
     for step in range(STEPS):
         at = (STEPS - 1 - step) * gusts
-        value = forcing[step] - known[at : at + gusts]
+        value = forcing[step] - part[at : at + gusts, :]
         if step == 0:
-            value = value + slope[:gusts]
-        base[step] = jnp.concatenate([value, jnp.zeros_like(value)], axis=0)
+            value = value + slope[:gusts, :]
+        ahead[step] = jnp.concatenate([value, jnp.zeros_like(value)], axis=0)
+
+
+def make_base(ahead, other, base):
+    gusts = 4
+    for step in range(STEPS):
+        at = (STEPS - 1 - step) * gusts
+        value = other[at : at + gusts, :]
+        base[step] = ahead[step] - jnp.concatenate([value, jnp.zeros_like(value)], axis=0)
 
 
 def march(
     masked, load_1, load_2, load_3, swap_1, swap_2, swap_3, own_c,
-    base_0, base_1, base_2, base_3, spread, out,
+    base_0, base_1, base_2, base_3, spread, out, near_out,
 ):
     place = lax.axis_index("elem")
     second = lax.axis_index("gust") == 1
@@ -243,7 +296,8 @@
     def times(fresh_b, lag, flip):
         if flip == 0:
             return dot_rows(fresh_b, masked[lag])
-        return rows_right(dot_rows(fresh_b, received(flip, lag * total, total)))
+        at = lag * total + (2 * rows if lag == LATE - 1 else 0)
+        return rows_right(dot_rows(fresh_b, received(flip, at, total)))
 
     def corrected(drive, flip):
         lhs = jnp.concatenate(words_of(drive, 2), axis=0)
@@ -258,10 +312,10 @@
         return drive + (added if flip == 0 else rows_right(added))
 
     waiting = [[base[step] for base in (base_0, base_1, base_2, base_3)] for step in range(STEPS)]
-    waiting[LATE] = waiting[LATE][:1]
+    waiting[LATE] = waiting[LATE][:2]
     for step in range(LATE):
         fresh = [corrected(waiting[step][flip], flip) for flip in flips_of]
-        out[step] = fresh[0]
+        out[step], near_out[step] = fresh[:2]
         whole = jnp.concatenate(flipped(fresh), axis=1)
         fresh_b = whole.astype(jnp.bfloat16)
         slope = slope_of(whole, spread)
@@ -273,10 +327,10 @@
                 if lag == 0:
                     change = change - slope[flip]
                 waiting[later][flip] = waiting[later][flip] - change
-    out[LATE] = corrected(waiting[LATE][0], 0)
-
-
-def on_core(body, shapes, operands, scratch=(), in_specs=None, cost=(0, 0), name=None):
+    out[LATE], near_out[LATE] = (corrected(waiting[LATE][flip], flip) for flip in (0, 1))
+
+
+def on_core(body, shapes, operands, scratch=(), in_specs=None, limit=24, name=None):
     vmem = pl.BlockSpec(memory_space=pltpu.VMEM)
     return pl.pallas_call(
         body,
@@ -284,8 +338,8 @@
         in_specs=in_specs or [vmem] * len(operands),
         out_specs=[vmem] * len(shapes),
         scratch_shapes=list(scratch),
-        cost_estimate=pl.CostEstimate(flops=cost[0], bytes_accessed=cost[1], transcendentals=0),
-        compiler_params=pltpu.CompilerParams(vmem_limit_bytes=24 * 2**20),
+        cost_estimate=pl.CostEstimate(flops=0, bytes_accessed=2**26, transcendentals=0),
+        compiler_params=pltpu.CompilerParams(vmem_limit_bytes=limit * 2**20 if limit else None),
         name=name,
     )(*operands)
 
@@ -294,42 +348,71 @@
     f32, bf16 = jnp.float32, jnp.bfloat16
     rows = correction.shape[0]
     lags, gusts, _ = history.shape
-    total = rows * lax.axis_size("elem")
+    count = lax.axis_size("elem")
+    total = rows * count
     part_rows = 24
+    width = (LATE - 1) * total + 2 * rows
+    anywhere = pl.BlockSpec(memory_space=pl.ANY)
     vmem = pl.BlockSpec(memory_space=pltpu.VMEM)
-    smem = pl.BlockSpec(memory_space=pltpu.SMEM)
+
+    def like(value):
+        return pltpu.VMEM(value.shape, value.dtype)
+
+    def crossed(value, axis):
+        return lax.ppermute(value, axis, [(0, 1), (1, 0)])
 
     (message,) = on_core(
-        pack, [((64, rows), bf16)], (history, neighbours, edge_coef), name="pack"
+        pack,
+        [((64, rows), bf16)],
+        (history, neighbours, edge_coef),
+        scratch=[like(history), like(neighbours), like(edge_coef), pltpu.SemaphoreType.DMA((3,))],
+        in_specs=[anywhere] * 3,
+        limit=None,
+        name="pack",
     )
     messages = flips(message)
-    masked, own_c, load = on_core(
+    masked, own_c, near_load, mid_load = on_core(
         make_load,
         [
             (interaction.shape, bf16),
             ((rows, 2 * rows), bf16),
-            ((rows // 2, (LATE - 1) * total + 2 * rows), bf16),
+            ((rows // 2, width + total), bf16),
+            ((rows // 2, width), bf16),
         ],
-        (block_mask[:, 0, :], interaction, correction),
-        in_specs=[smem, vmem, vmem],
-        cost=(10**6, 3 * 2**20),
+        (message, block_mask, interaction, correction),
+        scratch=[
+            pltpu.SMEM(block_mask.shape, block_mask.dtype),
+            like(interaction),
+            like(correction),
+            pltpu.SemaphoreType.DMA((3,)),
+        ],
+        in_specs=[anywhere] * 4,
         name="load",
     )
-    loads = flips(load)[1:]
-    swaps = [lax.ppermute(piece, "gust", [(0, 1), (1, 0)]) for piece in loads]
-
     everyone, late = on_core(
         order, [((64, total), bf16), ((LATE * gusts, total), bf16)], messages, name="order"
     )
-    before = lax.ppermute(late, "lag", [(0, 1), (1, 0)])
-    part, slope, spread = on_core(
+    before = crossed(late, "lag")
+    part, slope = on_core(
         main_part,
-        [((part_rows, rows), f32), ((GUST_ROWS, rows), f32), ((2 * RIM, total), f32)],
+        [((part_rows, rows), f32), ((GUST_ROWS, rows), f32)],
         (everyone, masked),
-        scratch=[pltpu.VMEM((56, total), f32), pltpu.VMEM((GUST_ROWS, total), f32)],
-        cost=(10**7, 2**20),
+        scratch=[
+            pltpu.VMEM((56, total), f32),
+            pltpu.VMEM((2 * RIM, total), f32),
+            pltpu.VMEM((GUST_ROWS, total), f32),
+        ],
         name="main_part",
     )
+
+    near_load, mid_load, _ = lax.optimization_barrier((near_load, mid_load, slope))
+
+    def bulk(value, pairs):
+        return lax.ppermute(value, ("elem", "lag"), [(2 * a, 2 * b) for a, b in pairs])
+
+    near = bulk(near_load, [(i, i ^ 1) for i in range(count)])
+    mid = bulk(mid_load, [(1, 2), (2, 1)])
+
     (part,) = on_core(
         late_part,
         [((part_rows, rows), f32)],
@@ -337,23 +420,48 @@
         scratch=[pltpu.VMEM((40, total), f32)],
         name="late_part",
     )
-    other = lax.ppermute(part, "lag", [(0, 1), (1, 0)])
+    other = crossed(part, "lag")
+    (ahead,) = on_core(
+        known_base,
+        [((STEPS, GUST_ROWS, rows), f32)],
+        (part, forcing, slope),
+        name="known_base",
+    )
+    (far_load,) = on_core(
+        relay, [((rows // 2, width), bf16)], (ahead, near), in_specs=[anywhere, vmem], name="relay"
+    )
+    far = bulk(far_load, [(1, 2), (2, 1)])
     (base,) = on_core(
-        make_base,
-        [((STEPS, GUST_ROWS, rows), f32)],
-        (part, other, forcing, slope),
-        name="base",
+        make_base, [((STEPS, GUST_ROWS, rows), f32)], (ahead, other), name="base"
     )
     bases = flips(base)
-    (own,) = on_core(
+    (spread,) = on_core(
+        all_spread,
+        [((2 * RIM, total), f32)],
+        (base, everyone),
+        in_specs=[anywhere, vmem],
+        name="spread",
+    )
+    loads, _ = lax.optimization_barrier(((near, far, mid), spread))
+    swaps = [crossed(piece, "gust") for piece in loads]
+    own, outer = on_core(
         march,
-        [((STEPS, GUST_ROWS, rows), f32)],
+        [((STEPS, GUST_ROWS, rows), f32)] * 2,
         (masked, *loads, *swaps, own_c, *bases, spread),
-        cost=(10**8, 4 * 2**20),
         name="march",
     )
-    moved = lax.ppermute(own, "lag", [(0, 1), (1, 0)])
-    return jnp.where(lax.axis_index("lag") == 0, own, moved)[:, :gusts]
+
+    def swap(value, flip):
+        return lax.ppermute(value, ("elem", "lag"), [(i, i ^ flip) for i in range(2 * count)])
+
+    to_lag, to_outer, to_both = swap(own, 1), swap(outer, 2), swap(outer, 3)
+    place = lax.axis_index("elem")
+    middle = (place == 1) | (place == 2)
+    first = lax.axis_index("lag") == 0
+    result = jnp.where(
+        middle, jnp.where(first, own, to_lag), jnp.where(first, to_outer, to_both)
+    )
+    return result[:, :gusts]
 
 
 def solution(mesh):

time: 61.8 us -> 47.5 us (0.77)
  waiting for transfers between devices: 30.5 us -> 16.2 us
  starting transfers between devices: 23.6 us -> 21.1 us
  Pallas kernels: 4.09 us -> 5.78 us
    ppermute x9 -> x6, waiting for transfers between devices: 24.2 us -> 5.24 us  [flips(): lax.ppermute(value, 'elem', [(i, i ^ flip) for i in range(count)])]
    ppermute x9 -> x6, starting transfers between devices: 18.5 us -> 13.3 us  [flips(): lax.ppermute(value, 'elem', [(i, i ^ flip) for i in range(count)])]
    ppermute x6 -> x11, waiting for transfers between devices: 6.28 us -> 11 us  [the longest x5 6.51 us: crossed(): return lax.ppermute(value, axis, [(0, 1), (1, 0)])]
    ppermute x6 -> x11, starting transfers between devices: 5.11 us -> 7.8 us  [the longest x3 3.52 us: swap(): lax.ppermute(value, ('elem', 'lag'), [(i, i ^ flip) for i in range(2 * co...]
    pallas_call x7 -> x10, Pallas kernels: 4.09 us -> 5.78 us  [on_core(): pl.pallas_call(body, out_shape=[jax.ShapeDtypeStruct(shape, dtype) for sh...]
    unnamed x12 -> x11, local copies, waits for them, and re-layouts: 2.08 us -> 3.31 us
    squeeze x1 -> x0, local copies, waits for them, and re-layouts: 0.76 us -> none  [places_march(): block_mask[:, 0, :]]
  transfers between devices with their start and end apart: 15 -> 17, of which waited for: 10 -> 9; matrix products, arithmetic and copies ran while one was open for 0% -> 0% of each run, Pallas kernels for 1% -> 3%
where the time goes in v4:
time: 47.5 us; the launch traced here: 47.1 us
  starting transfers between devices  21.1 us (44%)
  waiting for transfers between devices  16.2 us (34%)
  Pallas kernels  5.78 us (12%)
  local copies, waits for them, and re-layouts  3.31 us (7%)
  other arithmetic  0.61 us (1%)
    ppermute x6, starting transfers between devices, flips(): lax.ppermute(value, 'elem', [(i, i ^ flip) for i in range(count)])  13.3 us
    ppermute x5, waiting for transfers between devices, crossed(): return lax.ppermute(value, axis, [(0, 1), (1, 0)])  6.51 us
    pallas_call x10, Pallas kernels, on_core(): pl.pallas_call(body, out_shape=[jax.ShapeDtypeStruct(shape, dtype) for sh...  5.78 us
    ppermute x6, waiting for transfers between devices, flips(): lax.ppermute(value, 'elem', [(i, i ^ flip) for i in range(count)])  5.24 us
    ppermute x3, starting transfers between devices, swap(): lax.ppermute(value, ('elem', 'lag'), [(i, i ^ flip) for i in range(2 * co...  3.52 us
    unnamed x11, local copies, waits for them, and re-layouts  3.31 us
    ppermute x3, starting transfers between devices, bulk(): lax.ppermute(value, ('elem', 'lag'), [(2 * a, 2 * b) for a, b in pairs])  3.25 us
    ppermute x3, waiting for transfers between devices, bulk(): lax.ppermute(value, ('elem', 'lag'), [(2 * a, 2 * b) for a, b in pairs])  2.49 us
  transfers between devices with their start and end apart: 17, of which 9 were waited for; matrix products, arithmetic and copies ran while one was open for 0% of the time, Pallas kernels for 3%

profile of v4, /device:TPU:0, one launch (start us, length us, event | category | flops | bytes accessed | tf_op | source)
XLA Modules:
  0.0 47.1 jit_solution(673452529021059337)
XLA Ops:
  0.0 0.0 copy-start.4
  0.0 1.4 %pack.1.after.piece_0 = bf16[64,128]{1,0:T(8,128)(2,1)} custom-call(f32[8,4,128]{2,1,0:T(4,128)} %history_in.1, s32[4,128]{1,0:T(4,128)} %neighbours_in.1, f32[4,128]{1,0:T(4,128)} %edge_coef_in.1), custom_call_target="tpu_custom_call" | custom-call | bytes 67108864 | tf_op jit(solution)/shard_map/pack/pallas_call | solution.py:335
  1.4 3.1 %collective-permute-start = (bf16[64,128]{1,0:T(8,128)(2,1)}, bf16[64,128]{1,0:T(8,128)(2,1)S(1)}, u32[]{:S(2)}, u32[]{:S(2)}) collective-permute-start(bf16[64,128]{1,0:T(8,128)(2,1)} %pack.1.after.piece_0), channel_id=1, source_target_pairs={{0,4},{4,0},{8,12},{12,8},{1,5},{5,1},{9,13},{13,9},{2,6},{6,2},{1... | collective-permute-start | bytes 49160 | tf_op jit(solution)/shard_map/ppermute | solution.py:17
  4.5 2.6 %collective-permute-start.1 = (bf16[64,128]{1,0:T(8,128)(2,1)}, bf16[64,128]{1,0:T(8,128)(2,1)S(1)}, u32[]{:S(2)}, u32[]{:S(2)}) collective-permute-start(bf16[64,128]{1,0:T(8,128)(2,1)} %pack.1.after.piece_0), channel_id=1, source_target_pairs={{0,8},{4,12},{8,0},{12,4},{1,9},{5,13},{9,1},{13,5},{2,10},{6,14},... | collective-permute-start | bytes 49160 | tf_op jit(solution)/shard_map/ppermute | solution.py:17
  7.1 0.0 collective-permute-start.2
  7.1 0.0 copy-done.4
  7.1 0.1 copy.8.mask_in
  7.2 1.2 %copy-done = bf16[8,128,512]{2,1,0:T(8,128)(2,1)S(1)} copy-done((bf16[8,128,512]{2,1,0:T(8,128)(2,1)S(1)}, bf16[8,128,512]{2,1,0:T(8,128)(2,1)}, u32[]{:S(2)}) %copy-start) | copy-done | bytes 1048600
  8.4 0.7 %copy-done.1 = bf16[64,128]{1,0:T(8,128)(2,1)S(1)} copy-done((bf16[64,128]{1,0:T(8,128)(2,1)S(1)}, bf16[64,128]{1,0:T(8,128)(2,1)}, u32[]{:S(2)}) %copy-start.1) | copy-done | bytes 16408
  9.1 0.8 %copy-done.2 = f32[128,128]{1,0:T(8,128)S(1)} copy-done((f32[128,128]{1,0:T(8,128)S(1)}, f32[128,128]{1,0:T(8,128)}, u32[]{:S(2)}) %copy-start.2) | copy-done | bytes 65560
  9.9 0.9 %load.1 = (bf16[8,128,512]{2,1,0:T(8,128)(2,1)S(1)}, bf16[128,256]{1,0:T(8,128)(2,1)S(1)}, bf16[64,2304]{1,0:T(8,128)(2,1)S(1)}, bf16[64,1792]{1,0:T(8,128)(2,1)S(1)}) custom-call(bf16[64,128]{1,0:T(8,128)(2,1)S(1)} %copy-done.1, s32[8,1,4]{2,1,0:T(1,128)S(1)} %copy.8.mask_in, bf16[8,128,512]{2,1,0:T(8,128)(2,1)S(1)} %copy-done, f32[128,128]{1,0:T(8,128)S(1)} %copy-done.2), custom_call_target="tpu_custom_call" | custom-call | bytes 67108864 | tf_op jit(solution)/shard_map/load/pallas_call | solution.py:335
  10.9 0.0 collective-permute-done.piece_1
  10.9 0.0 collective-permute-done.1.piece_2
  10.9 1.9 %collective-permute-done.2.piece_3 = bf16[64,128]{1,0:T(8,128)(2,1)S(1)} collective-permute-done((bf16[64,128]{1,0:T(8,128)(2,1)}, bf16[64,128]{1,0:T(8,128)(2,1)S(1)}, u32[]{:S(2)}, u32[]{:S(2)}) %collective-permute-start.2) | collective-permute-done | bytes 16416 | tf_op jit(solution)/shard_map/ppermute | solution.py:17
  12.8 0.5 main_part.1
  13.3 1.9 %collective-permute-start.3 = (bf16[64,2304]{1,0:T(8,128)(2,1)S(1)}, bf16[64,2304]{1,0:T(8,128)(2,1)S(1)}, u32[]{:S(2)}, u32[]{:S(2)}) collective-permute-start(bf16[64,2304]{1,0:T(8,128)(2,1)S(1)} %get-tuple-element.25), channel_id=1, source_target_pairs={{0,4},{4,0},{8,12},{12,8},{1,5},{5,1},{9,13},{13,9},{16,20},{20,16... | collective-permute-start | bytes 884744 | tf_op jit(solution)/shard_map/ppermute | solution.py:411
  15.2 0.3 collective-permute-start.4
  15.5 0.7 %collective-permute-start.6 = (bf16[64,1792]{1,0:T(8,128)(2,1)S(1)}, bf16[64,1792]{1,0:T(8,128)(2,1)S(1)}, u32[]{:S(2)}, u32[]{:S(2)}) collective-permute-start(bf16[64,1792]{1,0:T(8,128)(2,1)S(1)} %get-tuple-element.28), channel_id=1, source_target_pairs={{4,8},{8,4},{5,9},{9,5},{20,24},{24,20},{21,25},{25,21}} | collective-permute-start | bytes 688136 | tf_op jit(solution)/shard_map/ppermute | solution.py:411
  16.2 2.8 %collective-permute-done.4.late = bf16[16,512]{1,0:T(8,128)(2,1)S(1)} collective-permute-done((bf16[16,512]{1,0:T(8,128)(2,1)S(1)}, bf16[16,512]{1,0:T(8,128)(2,1)S(1)}, u32[]{:S(2)}, u32[]{:S(2)}) %collective-permute-start.4) | collective-permute-done | bytes 16416 | tf_op jit(solution)/shard_map/ppermute | solution.py:362
  19.0 0.3 late_part.1.part
  19.3 0.4 copy-done.3
  19.7 2.5 %collective-permute-done.3.near.load_1 = bf16[64,2304]{1,0:T(8,128)(2,1)S(1)} collective-permute-done((bf16[64,2304]{1,0:T(8,128)(2,1)S(1)}, bf16[64,2304]{1,0:T(8,128)(2,1)S(1)}, u32[]{:S(2)}, u32[]{:S(2)}) %collective-permute-start.3) | collective-permute-done | bytes 294944 | tf_op jit(solution)/shard_map/ppermute | solution.py:411
  22.3 0.7 %collective-permute-start.5 = (bf16[64,1792]{1,0:T(8,128)(2,1)S(1)}, bf16[64,1792]{1,0:T(8,128)(2,1)S(1)}, u32[]{:S(2)}, u32[]{:S(2)}) collective-permute-start(bf16[64,1792]{1,0:T(8,128)(2,1)S(1)} %relay.1), channel_id=1, source_target_pairs={{4,8},{8,4},{5,9},{9,5},{20,24},{24,20},{21,25},{25,21}} | collective-permute-start | bytes 688136 | tf_op jit(solution)/shard_map/ppermute | solution.py:411
  22.9 0.1 collective-permute-start.7
  23.0 3.7 %collective-permute-done.7.other = f32[24,128]{1,0:T(8,128)S(1)} collective-permute-done((f32[24,128]{1,0:T(8,128)S(1)}, f32[24,128]{1,0:T(8,128)S(1)}, u32[]{:S(2)}, u32[]{:S(2)}) %collective-permute-start.7) | collective-permute-done | bytes 12320 | tf_op jit(solution)/shard_map/ppermute | solution.py:362
  26.7 0.1 spread.1
  26.8 0.0 collective-permute-done.6.load_3
  26.8 0.0 collective-permute-done.5.load_2
  26.8 0.1 collective-permute-start.8
  26.9 0.5 %collective-permute-start.10 = (bf16[64,1792]{1,0:T(8,128)(2,1)S(1)}, bf16[64,1792]{1,0:T(8,128)(2,1)S(1)}, u32[]{:S(2)}, u32[]{:S(2)}) collective-permute-start(bf16[64,1792]{1,0:T(8,128)(2,1)S(1)} %collective-permute-done.6.load_3), channel_id=1, source_target_pairs={{0,1},{1,0},{2,3},{3,2},{4,5},{5,4},{6,7},{7,6},{8,9},{9,8},{10,11... | collective-permute-start | bytes 688136 | tf_op jit(solution)/shard_map/ppermute | solution.py:362
  27.4 0.1 collective-permute-start.9
  27.5 3.5 %collective-permute-start.11 = (f32[5,8,128]{2,1,0:T(8,128)S(1)}, f32[5,8,128]{2,1,0:T(8,128)S(1)}, u32[]{:S(2)}, u32[]{:S(2)}) collective-permute-start(f32[5,8,128]{2,1,0:T(8,128)S(1)} %base.1.after.base_0), channel_id=1, source_target_pairs={{0,4},{4,0},{8,12},{12,8},{1,5},{5,1},{9,13},{13,9},{2,6},{6,2},{1... | collective-permute-start | bytes 61448 | tf_op jit(solution)/shard_map/ppermute | solution.py:17
  31.0 1.3 %collective-permute-start.12 = (f32[5,8,128]{2,1,0:T(8,128)S(1)}, f32[5,8,128]{2,1,0:T(8,128)S(1)}, u32[]{:S(2)}, u32[]{:S(2)}) collective-permute-start(f32[5,8,128]{2,1,0:T(8,128)S(1)} %base.1.after.base_0), channel_id=1, source_target_pairs={{0,8},{4,12},{8,0},{12,4},{1,9},{5,13},{9,1},{13,5},{2,10},{6,14},... | collective-permute-start | bytes 61448 | tf_op jit(solution)/shard_map/ppermute | solution.py:17
  32.3 0.5 %collective-permute-done.11.base_1 = f32[5,8,128]{2,1,0:T(8,128)S(1)} collective-permute-done((f32[5,8,128]{2,1,0:T(8,128)S(1)}, f32[5,8,128]{2,1,0:T(8,128)S(1)}, u32[]{:S(2)}, u32[]{:S(2)}) %collective-permute-start.11) | collective-permute-done | bytes 20512 | tf_op jit(solution)/shard_map/ppermute | solution.py:17
  32.8 2.8 %collective-permute-start.13 = (f32[5,8,128]{2,1,0:T(8,128)S(1)}, f32[5,8,128]{2,1,0:T(8,128)S(1)}, u32[]{:S(2)}, u32[]{:S(2)}) collective-permute-start(f32[5,8,128]{2,1,0:T(8,128)S(1)} %base.1.after.base_0), channel_id=1, source_target_pairs={{0,12},{4,8},{8,4},{12,0},{1,13},{5,9},{9,5},{13,1},{2,14},{6,10},... | collective-permute-start | bytes 61448 | tf_op jit(solution)/shard_map/ppermute | solution.py:17
  35.5 0.3 collective-permute-done.12.base_2
  35.9 2.5 %collective-permute-done.13.base_3 = f32[5,8,128]{2,1,0:T(8,128)S(1)} collective-permute-done((f32[5,8,128]{2,1,0:T(8,128)S(1)}, f32[5,8,128]{2,1,0:T(8,128)S(1)}, u32[]{:S(2)}, u32[]{:S(2)}) %collective-permute-start.13) | collective-permute-done | bytes 20512 | tf_op jit(solution)/shard_map/ppermute | solution.py:17
  38.4 0.0 collective-permute-done.10.swap_3
  38.4 0.0 collective-permute-done.9.swap_2
  38.4 0.0 collective-permute-done.8.swap_1
  38.4 2.6 %march.1 = (f32[5,8,128]{2,1,0:T(8,128)S(1)}, f32[5,8,128]{2,1,0:T(8,128)S(1)}) custom-call(bf16[8,128,512]{2,1,0:T(8,128)(2,1)S(1)} %get-tuple-element.20.masked, bf16[64,2304]{1,0:T(8,128)(2,1)S(1)} %collective-permute-done.3.near.load_1, bf16[64,1792]{1,0:T(8,128)(2,1)S(1)} %collective-permute-done.5.load_2, ...), custom_call_target="tpu_custom_call" | custom-call | bytes 67108864 | tf_op jit(solution)/shard_map/march/pallas_call | solution.py:335
  41.0 0.0 collective-permute-start.14
  41.0 0.2 collective-permute-start.15
  41.2 3.3 %collective-permute-start.16 = (f32[5,8,128]{2,1,0:T(8,128)S(1)}, f32[5,8,128]{2,1,0:T(8,128)S(1)}, u32[]{:S(2)}, u32[]{:S(2)}) collective-permute-start(f32[5,8,128]{2,1,0:T(8,128)S(1)} %get-tuple-element.34), channel_id=1, source_target_pairs={{0,6},{2,4},{4,2},{6,0},{8,14},{10,12},{12,10},{14,8},{1,7},{3,5},... | collective-permute-start | bytes 61448 | tf_op jit(solution)/shard_map/ppermute | solution.py:455
  44.5 0.3 collective-permute-done.14
  44.8 0.0 collective-permute-done.15
  44.8 1.7 %collective-permute-done.16 = f32[5,8,128]{2,1,0:T(8,128)S(1)} collective-permute-done((f32[5,8,128]{2,1,0:T(8,128)S(1)}, f32[5,8,128]{2,1,0:T(8,128)S(1)}, u32[]{:S(2)}, u32[]{:S(2)}) %collective-permute-start.16) | collective-permute-done | bytes 20512 | tf_op jit(solution)/shard_map/ppermute | solution.py:455
  46.5 0.6 %fusion = f32[5,4,128]{2,1,0:T(4,128)} fusion(f32[5,8,128]{2,1,0:T(8,128)S(1)} %collective-permute-done.16, f32[5,8,128]{2,1,0:T(8,128)S(1)} %collective-permute-done.15, f32[5,8,128]{2,1,0:T(8,128)S(1)} %collective-permute-done.14, f32[5,8,128]{2,1,0:T(8,128)S(1)} %get-tuple-element.33, pred[]{:T(512)S(6)} %or.3, pred[]{:T(512)S(6)} %eq.11), kind=kLoop, calls=%fused_computation.1 | loop fusion | flops 7680 | bytes 51202 | tf_op jit(solution)/shard_map/jit(_where)/select_n | solution.py:461
  (8 shorter events, 0.1 us)
Async XLA Ops:
  0.0 7.1 %copy-start.4 = (s32[8,1,4]{0,2,1:T(4,128)S(1)}, s32[8,1,4]{0,2,1:T(4,128)}, u32[]{:S(2)}) copy-start(s32[8,1,4]{0,2,1:T(4,128)} %param.10) | copy-start | bytes 388
  1.4 9.5 %collective-permute-start = (bf16[64,128]{1,0:T(8,128)(2,1)}, bf16[64,128]{1,0:T(8,128)(2,1)S(1)}, u32[]{:S(2)}, u32[]{:S(2)}) collective-permute-start(bf16[64,128]{1,0:T(8,128)(2,1)} %pack.1.after.piece_0), channel_id=1, source_target_pairs={{0,4},{4,0},{8,12},{12,8},{1,5},{5,1},{9,13},{13,9},{2,6},{6,2},{1... | collective-permute-start | bytes 49160 | tf_op jit(solution)/shard_map/ppermute | solution.py:17
  4.5 6.4 %collective-permute-start.1 = (bf16[64,128]{1,0:T(8,128)(2,1)}, bf16[64,128]{1,0:T(8,128)(2,1)S(1)}, u32[]{:S(2)}, u32[]{:S(2)}) collective-permute-start(bf16[64,128]{1,0:T(8,128)(2,1)} %pack.1.after.piece_0), channel_id=1, source_target_pairs={{0,8},{4,12},{8,0},{12,4},{1,9},{5,13},{9,1},{13,5},{2,10},{6,14},... | collective-permute-start | bytes 49160 | tf_op jit(solution)/shard_map/ppermute | solution.py:17
  7.1 5.7 %collective-permute-start.2 = (bf16[64,128]{1,0:T(8,128)(2,1)}, bf16[64,128]{1,0:T(8,128)(2,1)S(1)}, u32[]{:S(2)}, u32[]{:S(2)}) collective-permute-start(bf16[64,128]{1,0:T(8,128)(2,1)} %pack.1.after.piece_0), channel_id=1, source_target_pairs={{0,12},{4,8},{8,4},{12,0},{1,13},{5,9},{9,5},{13,1},{2,14},{6,10},... | collective-permute-start | bytes 49160 | tf_op jit(solution)/shard_map/ppermute | solution.py:17
  7.2 1.2 %copy-start = (bf16[8,128,512]{2,1,0:T(8,128)(2,1)S(1)}, bf16[8,128,512]{2,1,0:T(8,128)(2,1)}, u32[]{:S(2)}) copy-start(bf16[8,128,512]{2,1,0:T(8,128)(2,1)} %interaction_in.1) | copy-start | bytes 3145732
  8.4 0.7 %copy-start.1 = (bf16[64,128]{1,0:T(8,128)(2,1)S(1)}, bf16[64,128]{1,0:T(8,128)(2,1)}, u32[]{:S(2)}) copy-start(bf16[64,128]{1,0:T(8,128)(2,1)} %pack.1.after.piece_0) | copy-start | bytes 49156
  9.1 0.8 %copy-start.2 = (f32[128,128]{1,0:T(8,128)S(1)}, f32[128,128]{1,0:T(8,128)}, u32[]{:S(2)}) copy-start(f32[128,128]{1,0:T(8,128)} %correction_in.1) | copy-start | bytes 196612
  13.3 8.9 %collective-permute-start.3 = (bf16[64,2304]{1,0:T(8,128)(2,1)S(1)}, bf16[64,2304]{1,0:T(8,128)(2,1)S(1)}, u32[]{:S(2)}, u32[]{:S(2)}) collective-permute-start(bf16[64,2304]{1,0:T(8,128)(2,1)S(1)} %get-tuple-element.25), channel_id=1, source_target_pairs={{0,4},{4,0},{8,12},{12,8},{1,5},{5,1},{9,13},{13,9},{16,20},{20,16... | collective-permute-start | bytes 884744 | tf_op jit(solution)/shard_map/ppermute | solution.py:411
  15.2 3.8 %collective-permute-start.4 = (bf16[16,512]{1,0:T(8,128)(2,1)S(1)}, bf16[16,512]{1,0:T(8,128)(2,1)S(1)}, u32[]{:S(2)}, u32[]{:S(2)}) collective-permute-start(bf16[16,512]{1,0:T(8,128)(2,1)S(1)} %get-tuple-element.26), channel_id=1, source_target_pairs={{0,2},{2,0},{1,3},{3,1},{4,6},{6,4},{5,7},{7,5},{8,10},{10,8},{9,1... | collective-permute-start | bytes 49160 | tf_op jit(solution)/shard_map/ppermute | solution.py:362
  15.5 11.3 %collective-permute-start.6 = (bf16[64,1792]{1,0:T(8,128)(2,1)S(1)}, bf16[64,1792]{1,0:T(8,128)(2,1)S(1)}, u32[]{:S(2)}, u32[]{:S(2)}) collective-permute-start(bf16[64,1792]{1,0:T(8,128)(2,1)S(1)} %get-tuple-element.28), channel_id=1, source_target_pairs={{4,8},{8,4},{5,9},{9,5},{20,24},{24,20},{21,25},{25,21}} | collective-permute-start | bytes 688136 | tf_op jit(solution)/shard_map/ppermute | solution.py:411
  19.0 0.7 %copy-start.3 = (f32[5,4,128]{2,1,0:T(4,128)S(1)}, f32[5,4,128]{2,1,0:T(4,128)}, u32[]{:S(2)}) copy-start(f32[5,4,128]{2,1,0:T(4,128)} %forcing.1) | copy-start | bytes 30724
  22.3 4.6 %collective-permute-start.5 = (bf16[64,1792]{1,0:T(8,128)(2,1)S(1)}, bf16[64,1792]{1,0:T(8,128)(2,1)S(1)}, u32[]{:S(2)}, u32[]{:S(2)}) collective-permute-start(bf16[64,1792]{1,0:T(8,128)(2,1)S(1)} %relay.1), channel_id=1, source_target_pairs={{4,8},{8,4},{5,9},{9,5},{20,24},{24,20},{21,25},{25,21}} | collective-permute-start | bytes 688136 | tf_op jit(solution)/shard_map/ppermute | solution.py:411
  22.9 3.8 %collective-permute-start.7 = (f32[24,128]{1,0:T(8,128)S(1)}, f32[24,128]{1,0:T(8,128)S(1)}, u32[]{:S(2)}, u32[]{:S(2)}) collective-permute-start(f32[24,128]{1,0:T(8,128)S(1)} %late_part.1.part), channel_id=1, source_target_pairs={{0,2},{2,0},{1,3},{3,1},{4,6},{6,4},{5,7},{7,5},{8,10},{10,8},{9,1... | collective-permute-start | bytes 36872 | tf_op jit(solution)/shard_map/ppermute | solution.py:362
  26.8 11.5 %collective-permute-start.8 = (bf16[64,2304]{1,0:T(8,128)(2,1)S(1)}, bf16[64,2304]{1,0:T(8,128)(2,1)S(1)}, u32[]{:S(2)}, u32[]{:S(2)}) collective-permute-start(bf16[64,2304]{1,0:T(8,128)(2,1)S(1)} %collective-permute-done.3.near.load_1), channel_id=1, source_target_pairs={{0,1},{1,0},{2,3},{3,2},{4,5},{5,4},{6,7},{7,6},{8,9},{9,8},{10,11... | collective-permute-start | bytes 884744 | tf_op jit(solution)/shard_map/ppermute | solution.py:362
  26.9 11.4 %collective-permute-start.10 = (bf16[64,1792]{1,0:T(8,128)(2,1)S(1)}, bf16[64,1792]{1,0:T(8,128)(2,1)S(1)}, u32[]{:S(2)}, u32[]{:S(2)}) collective-permute-start(bf16[64,1792]{1,0:T(8,128)(2,1)S(1)} %collective-permute-done.6.load_3), channel_id=1, source_target_pairs={{0,1},{1,0},{2,3},{3,2},{4,5},{5,4},{6,7},{7,6},{8,9},{9,8},{10,11... | collective-permute-start | bytes 688136 | tf_op jit(solution)/shard_map/ppermute | solution.py:362
  27.4 11.0 %collective-permute-start.9 = (bf16[64,1792]{1,0:T(8,128)(2,1)S(1)}, bf16[64,1792]{1,0:T(8,128)(2,1)S(1)}, u32[]{:S(2)}, u32[]{:S(2)}) collective-permute-start(bf16[64,1792]{1,0:T(8,128)(2,1)S(1)} %collective-permute-done.5.load_2), channel_id=1, source_target_pairs={{0,1},{1,0},{2,3},{3,2},{4,5},{5,4},{6,7},{7,6},{8,9},{9,8},{10,11... | collective-permute-start | bytes 688136 | tf_op jit(solution)/shard_map/ppermute | solution.py:362
  27.5 5.3 %collective-permute-start.11 = (f32[5,8,128]{2,1,0:T(8,128)S(1)}, f32[5,8,128]{2,1,0:T(8,128)S(1)}, u32[]{:S(2)}, u32[]{:S(2)}) collective-permute-start(f32[5,8,128]{2,1,0:T(8,128)S(1)} %base.1.after.base_0), channel_id=1, source_target_pairs={{0,4},{4,0},{8,12},{12,8},{1,5},{5,1},{9,13},{13,9},{2,6},{6,2},{1... | collective-permute-start | bytes 61448 | tf_op jit(solution)/shard_map/ppermute | solution.py:17
  31.0 4.9 %collective-permute-start.12 = (f32[5,8,128]{2,1,0:T(8,128)S(1)}, f32[5,8,128]{2,1,0:T(8,128)S(1)}, u32[]{:S(2)}, u32[]{:S(2)}) collective-permute-start(f32[5,8,128]{2,1,0:T(8,128)S(1)} %base.1.after.base_0), channel_id=1, source_target_pairs={{0,8},{4,12},{8,0},{12,4},{1,9},{5,13},{9,1},{13,5},{2,10},{6,14},... | collective-permute-start | bytes 61448 | tf_op jit(solution)/shard_map/ppermute | solution.py:17
  32.8 5.6 %collective-permute-start.13 = (f32[5,8,128]{2,1,0:T(8,128)S(1)}, f32[5,8,128]{2,1,0:T(8,128)S(1)}, u32[]{:S(2)}, u32[]{:S(2)}) collective-permute-start(f32[5,8,128]{2,1,0:T(8,128)S(1)} %base.1.after.base_0), channel_id=1, source_target_pairs={{0,12},{4,8},{8,4},{12,0},{1,13},{5,9},{9,5},{13,1},{2,14},{6,10},... | collective-permute-start | bytes 61448 | tf_op jit(solution)/shard_map/ppermute | solution.py:17
  41.0 3.8 %collective-permute-start.14 = (f32[5,8,128]{2,1,0:T(8,128)S(1)}, f32[5,8,128]{2,1,0:T(8,128)S(1)}, u32[]{:S(2)}, u32[]{:S(2)}) collective-permute-start(f32[5,8,128]{2,1,0:T(8,128)S(1)} %get-tuple-element.33), channel_id=1, source_target_pairs={{0,2},{2,0},{4,6},{6,4},{8,10},{10,8},{12,14},{14,12},{1,3},{3,1},... | collective-permute-start | bytes 61448 | tf_op jit(solution)/shard_map/ppermute | solution.py:455
  41.0 3.8 %collective-permute-start.15 = (f32[5,8,128]{2,1,0:T(8,128)S(1)}, f32[5,8,128]{2,1,0:T(8,128)S(1)}, u32[]{:S(2)}, u32[]{:S(2)}) collective-permute-start(f32[5,8,128]{2,1,0:T(8,128)S(1)} %get-tuple-element.34), channel_id=1, source_target_pairs={{0,4},{2,6},{4,0},{6,2},{8,12},{10,14},{12,8},{14,10},{1,5},{3,7},... | collective-permute-start | bytes 61448 | tf_op jit(solution)/shard_map/ppermute | solution.py:455
  41.2 5.3 %collective-permute-start.16 = (f32[5,8,128]{2,1,0:T(8,128)S(1)}, f32[5,8,128]{2,1,0:T(8,128)S(1)}, u32[]{:S(2)}, u32[]{:S(2)}) collective-permute-start(f32[5,8,128]{2,1,0:T(8,128)S(1)} %get-tuple-element.34), channel_id=1, source_target_pairs={{0,6},{2,4},{4,2},{6,0},{8,14},{10,12},{12,10},{14,8},{1,7},{3,5},... | collective-permute-start | bytes 61448 | tf_op jit(solution)/shard_map/ppermute | solution.py:455

commit v5 on v4

--- a/solution.py
+++ b/solution.py
@@ -260,7 +260,8 @@
         ahead[step] = jnp.concatenate([value, jnp.zeros_like(value)], axis=0)
 
 
-def make_base(ahead, other, base):
+def make_base(after, ahead, other, base):
+    del after
     gusts = 4
     for step in range(STEPS):
         at = (STEPS - 1 - step) * gusts
@@ -338,7 +339,7 @@
         in_specs=in_specs or [vmem] * len(operands),
         out_specs=[vmem] * len(shapes),
         scratch_shapes=list(scratch),
-        cost_estimate=pl.CostEstimate(flops=0, bytes_accessed=2**26, transcendentals=0),
+        cost_estimate=pl.CostEstimate(flops=10**10, bytes_accessed=2**20, transcendentals=0),
         compiler_params=pltpu.CompilerParams(vmem_limit_bytes=limit * 2**20 if limit else None),
         name=name,
     )(*operands)
@@ -405,7 +406,7 @@
         name="main_part",
     )
 
-    near_load, mid_load, _ = lax.optimization_barrier((near_load, mid_load, slope))
+    mid_load, _ = lax.optimization_barrier((mid_load, slope))
 
     def bulk(value, pairs):
         return lax.ppermute(value, ("elem", "lag"), [(2 * a, 2 * b) for a, b in pairs])
@@ -431,8 +432,14 @@
         relay, [((rows // 2, width), bf16)], (ahead, near), in_specs=[anywhere, vmem], name="relay"
     )
     far = bulk(far_load, [(1, 2), (2, 1)])
+    early, _ = lax.optimization_barrier(((near, mid), ahead))
+    near_swap, mid_swap = (crossed(piece, "gust") for piece in early)
     (base,) = on_core(
-        make_base, [((STEPS, GUST_ROWS, rows), f32)], (ahead, other), name="base"
+        make_base,
+        [((STEPS, GUST_ROWS, rows), f32)],
+        (far_load, ahead, other),
+        in_specs=[anywhere, vmem, vmem],
+        name="base",
     )
     bases = flips(base)
     (spread,) = on_core(
@@ -442,12 +449,12 @@
         in_specs=[anywhere, vmem],
         name="spread",
     )
-    loads, _ = lax.optimization_barrier(((near, far, mid), spread))
-    swaps = [crossed(piece, "gust") for piece in loads]
+    far, _ = lax.optimization_barrier((far, bases[3]))
+    far_swap = crossed(far, "gust")
     own, outer = on_core(
         march,
         [((STEPS, GUST_ROWS, rows), f32)] * 2,
-        (masked, *loads, *swaps, own_c, *bases, spread),
+        (masked, near, far, mid, near_swap, far_swap, mid_swap, own_c, *bases, spread),
         name="march",
     )
 

time: 47.5 us -> 39.4 us (0.83)
  waiting for transfers between devices: 16.2 us -> 10.2 us
  local copies, waits for them, and re-layouts: 3.31 us -> 0.83 us
    ppermute x5, waiting for transfers between devices: 6.51 us -> 2.3 us  [crossed(): return lax.ppermute(value, axis, [(0, 1), (1, 0)])]
    ppermute x6, starting transfers between devices: 13.3 us -> 10.2 us  [flips(): lax.ppermute(value, 'elem', [(i, i ^ flip) for i in range(count)])]
    unnamed x11 -> x13, local copies, waits for them, and re-layouts: 3.31 us -> 0.83 us
    ppermute x5, starting transfers between devices: 1.03 us -> 3.45 us  [crossed(): return lax.ppermute(value, axis, [(0, 1), (1, 0)])]
    ppermute x3, waiting for transfers between devices: 2.49 us -> 0.5 us  [bulk(): lax.ppermute(value, ('elem', 'lag'), [(2 * a, 2 * b) for a, b in pairs])]
    ppermute x3, waiting for transfers between devices: 1.97 us -> 3.22 us  [swap(): lax.ppermute(value, ('elem', 'lag'), [(i, i ^ flip) for i in range(2 * co...]
    ppermute x6, waiting for transfers between devices: 5.24 us -> 4.18 us  [flips(): lax.ppermute(value, 'elem', [(i, i ^ flip) for i in range(count)])]
    ppermute x3, starting transfers between devices: 3.25 us -> 4.14 us  [bulk(): lax.ppermute(value, ('elem', 'lag'), [(2 * a, 2 * b) for a, b in pairs])]
  transfers between devices with their start and end apart: 17 -> 17, of which waited for: 9 -> 9; matrix products, arithmetic and copies ran while one was open for 0% -> 0% of each run, Pallas kernels for 3% -> 5%
where the time goes in v5:
time: 39.4 us; the launch traced here: 39 us
  starting transfers between devices  21.4 us (54%)
  waiting for transfers between devices  10.2 us (26%)
  Pallas kernels  5.85 us (15%)
  local copies, waits for them, and re-layouts  0.83 us (2%)
  other arithmetic  0.61 us (2%)
    ppermute x6, starting transfers between devices, flips(): lax.ppermute(value, 'elem', [(i, i ^ flip) for i in range(count)])  10.2 us
    pallas_call x10, Pallas kernels, on_core(): pl.pallas_call(body, out_shape=[jax.ShapeDtypeStruct(shape, dtype) for sh...  5.85 us
    ppermute x6, waiting for transfers between devices, flips(): lax.ppermute(value, 'elem', [(i, i ^ flip) for i in range(count)])  4.18 us
    ppermute x3, starting transfers between devices, bulk(): lax.ppermute(value, ('elem', 'lag'), [(2 * a, 2 * b) for a, b in pairs])  4.14 us
    ppermute x3, starting transfers between devices, swap(): lax.ppermute(value, ('elem', 'lag'), [(i, i ^ flip) for i in range(2 * co...  3.64 us
    ppermute x5, starting transfers between devices, crossed(): return lax.ppermute(value, axis, [(0, 1), (1, 0)])  3.45 us
    ppermute x3, waiting for transfers between devices, swap(): lax.ppermute(value, ('elem', 'lag'), [(i, i ^ flip) for i in range(2 * co...  3.22 us
    ppermute x5, waiting for transfers between devices, crossed(): return lax.ppermute(value, axis, [(0, 1), (1, 0)])  2.3 us
  transfers between devices with their start and end apart: 17, of which 9 were waited for; matrix products, arithmetic and copies ran while one was open for 0% of the time, Pallas kernels for 5%

profile of v5, /device:TPU:0, one launch (start us, length us, event | category | flops | bytes accessed | tf_op | source)
XLA Modules:
  0.0 39.0 jit_solution(11682180710348782765)
XLA Ops:
  0.0 1.5 %pack.1.after.piece_0 = bf16[64,128]{1,0:T(8,128)(2,1)} custom-call(f32[8,4,128]{2,1,0:T(4,128)} %history_in.1, s32[4,128]{1,0:T(4,128)} %neighbours_in.1, f32[4,128]{1,0:T(4,128)} %edge_coef_in.1), custom_call_target="tpu_custom_call" | custom-call | flops 10000000000 | bytes 1048576 | tf_op jit(solution)/shard_map/pack/pallas_call | solution.py:336
  1.5 3.1 %collective-permute-start.1 = (bf16[64,128]{1,0:T(8,128)(2,1)}, bf16[64,128]{1,0:T(8,128)(2,1)S(1)}, u32[]{:S(2)}, u32[]{:S(2)}) collective-permute-start(bf16[64,128]{1,0:T(8,128)(2,1)} %pack.1.after.piece_0), channel_id=1, source_target_pairs={{0,4},{4,0},{8,12},{12,8},{1,5},{5,1},{9,13},{13,9},{2,6},{6,2},{1... | collective-permute-start | bytes 49160 | tf_op jit(solution)/shard_map/ppermute | solution.py:17
  4.6 2.6 %collective-permute-start.2 = (bf16[64,128]{1,0:T(8,128)(2,1)}, bf16[64,128]{1,0:T(8,128)(2,1)S(1)}, u32[]{:S(2)}, u32[]{:S(2)}) collective-permute-start(bf16[64,128]{1,0:T(8,128)(2,1)} %pack.1.after.piece_0), channel_id=1, source_target_pairs={{0,8},{4,12},{8,0},{12,4},{1,9},{5,13},{9,1},{13,5},{2,10},{6,14},... | collective-permute-start | bytes 49160 | tf_op jit(solution)/shard_map/ppermute | solution.py:17
  7.2 0.0 collective-permute-start.3
  7.2 0.0 copy-done.5
  7.2 0.1 copy.8.mask_in
  7.2 0.0 copy-done.1
  7.2 0.0 copy-done
  7.2 0.7 %copy-done.2 = bf16[64,128]{1,0:T(8,128)(2,1)S(1)} copy-done((bf16[64,128]{1,0:T(8,128)(2,1)S(1)}, bf16[64,128]{1,0:T(8,128)(2,1)}, u32[]{:S(2)}) %copy-start.2) | copy-done | bytes 16408
  8.0 0.9 %load.1 = (bf16[8,128,512]{2,1,0:T(8,128)(2,1)S(1)}, bf16[128,256]{1,0:T(8,128)(2,1)S(1)}, bf16[64,2304]{1,0:T(8,128)(2,1)S(1)}, bf16[64,1792]{1,0:T(8,128)(2,1)S(1)}) custom-call(bf16[64,128]{1,0:T(8,128)(2,1)S(1)} %copy-done.2, s32[8,1,4]{2,1,0:T(1,128)S(1)} %copy.8.mask_in, bf16[8,128,512]{2,1,0:T(8,128)(2,1)S(1)} %copy-done, f32[128,128]{1,0:T(8,128)S(1)} %copy-done.1), custom_call_target="tpu_custom_call" | custom-call | flops 10000000000 | bytes 1048576 | tf_op jit(solution)/shard_map/load/pallas_call | solution.py:336
  8.9 2.8 %collective-permute-start = (bf16[64,2304]{1,0:T(8,128)(2,1)S(1)}, bf16[64,2304]{1,0:T(8,128)(2,1)S(1)}, u32[]{:S(2)}, u32[]{:S(2)}) collective-permute-start(bf16[64,2304]{1,0:T(8,128)(2,1)S(1)} %get-tuple-element.20), channel_id=1, source_target_pairs={{0,4},{4,0},{8,12},{12,8},{1,5},{5,1},{9,13},{13,9},{16,20},{20,16... | collective-permute-start | bytes 884744 | tf_op jit(solution)/shard_map/ppermute | solution.py:412
  11.7 0.0 collective-permute-done.1.piece_1
  11.7 0.0 collective-permute-done.2.piece_2
  11.7 1.3 %collective-permute-done.3.piece_3 = bf16[64,128]{1,0:T(8,128)(2,1)S(1)} collective-permute-done((bf16[64,128]{1,0:T(8,128)(2,1)}, bf16[64,128]{1,0:T(8,128)(2,1)S(1)}, u32[]{:S(2)}, u32[]{:S(2)}) %collective-permute-start.3) | collective-permute-done | bytes 16416 | tf_op jit(solution)/shard_map/ppermute | solution.py:17
  13.0 0.0 copy-done.3
  13.0 1.4 %collective-permute-start.4 = (bf16[16,512]{1,0:T(8,128)(2,1)S(1)}, bf16[16,512]{1,0:T(8,128)(2,1)S(1)}, u32[]{:S(2)}, u32[]{:S(2)}) collective-permute-start(bf16[16,512]{1,0:T(8,128)(2,1)S(1)} %get-tuple-element.21), channel_id=1, source_target_pairs={{0,2},{2,0},{1,3},{3,1},{4,6},{6,4},{5,7},{7,5},{8,10},{10,8},{9,1... | collective-permute-start | bytes 49160 | tf_op jit(solution)/shard_map/ppermute | solution.py:363
  14.5 0.5 %main_part.1 = (f32[24,128]{1,0:T(8,128)S(1)}, f32[8,128]{1,0:T(8,128)S(1)}) custom-call(bf16[64,512]{1,0:T(8,128)(2,1)S(1)} %get-tuple-element.22.everyone, bf16[8,128,512]{2,1,0:T(8,128)(2,1)S(1)} %get-tuple-element.19.masked), custom_call_target="tpu_custom_call" | custom-call | flops 10000000000 | bytes 1048576 | tf_op jit(solution)/shard_map/main_part/pallas_call | solution.py:336
  15.0 0.7 %collective-permute-start.8 = (bf16[64,1792]{1,0:T(8,128)(2,1)S(1)}, bf16[64,1792]{1,0:T(8,128)(2,1)S(1)}, u32[]{:S(2)}, u32[]{:S(2)}) collective-permute-start(bf16[64,1792]{1,0:T(8,128)(2,1)S(1)} %get-tuple-element.27), channel_id=1, source_target_pairs={{4,8},{8,4},{5,9},{9,5},{20,24},{24,20},{21,25},{25,21}} | collective-permute-start | bytes 688136 | tf_op jit(solution)/shard_map/ppermute | solution.py:412
  15.6 1.3 %collective-permute-done.4.late = bf16[16,512]{1,0:T(8,128)(2,1)S(1)} collective-permute-done((bf16[16,512]{1,0:T(8,128)(2,1)S(1)}, bf16[16,512]{1,0:T(8,128)(2,1)S(1)}, u32[]{:S(2)}, u32[]{:S(2)}) %collective-permute-start.4) | collective-permute-done | bytes 16416 | tf_op jit(solution)/shard_map/ppermute | solution.py:363
  16.9 0.3 late_part.1.part
  17.2 1.5 %collective-permute-start.6 = (f32[24,128]{1,0:T(8,128)S(1)}, f32[24,128]{1,0:T(8,128)S(1)}, u32[]{:S(2)}, u32[]{:S(2)}) collective-permute-start(f32[24,128]{1,0:T(8,128)S(1)} %late_part.1.part), channel_id=1, source_target_pairs={{0,2},{2,0},{1,3},{3,1},{4,6},{6,4},{5,7},{7,5},{8,10},{10,8},{9,1... | collective-permute-start | bytes 36872 | tf_op jit(solution)/shard_map/ppermute | solution.py:363
  18.6 0.0 copy-done.4
  18.7 0.5 %collective-permute-done.near.load_1 = bf16[64,2304]{1,0:T(8,128)(2,1)S(1)} collective-permute-done((bf16[64,2304]{1,0:T(8,128)(2,1)S(1)}, bf16[64,2304]{1,0:T(8,128)(2,1)S(1)}, u32[]{:S(2)}, u32[]{:S(2)}) %collective-permute-start) | collective-permute-done | bytes 294944 | tf_op jit(solution)/shard_map/ppermute | solution.py:412
  19.2 0.7 %collective-permute-start.5 = (bf16[64,1792]{1,0:T(8,128)(2,1)S(1)}, bf16[64,1792]{1,0:T(8,128)(2,1)S(1)}, u32[]{:S(2)}, u32[]{:S(2)}) collective-permute-start(bf16[64,1792]{1,0:T(8,128)(2,1)S(1)} %relay.1.after), channel_id=1, source_target_pairs={{4,8},{8,4},{5,9},{9,5},{20,24},{24,20},{21,25},{25,21}} | collective-permute-start | bytes 688136 | tf_op jit(solution)/shard_map/ppermute | solution.py:412
  19.9 1.0 %collective-permute-done.6.other = f32[24,128]{1,0:T(8,128)S(1)} collective-permute-done((f32[24,128]{1,0:T(8,128)S(1)}, f32[24,128]{1,0:T(8,128)S(1)}, u32[]{:S(2)}, u32[]{:S(2)}) %collective-permute-start.6) | collective-permute-done | bytes 12320 | tf_op jit(solution)/shard_map/ppermute | solution.py:363
  20.9 2.4 %collective-permute-start.7 = (f32[5,8,128]{2,1,0:T(8,128)S(1)}, f32[5,8,128]{2,1,0:T(8,128)S(1)}, u32[]{:S(2)}, u32[]{:S(2)}) collective-permute-start(f32[5,8,128]{2,1,0:T(8,128)S(1)} %base.1.after.base_0), channel_id=1, source_target_pairs={{0,12},{4,8},{8,4},{12,0},{1,13},{5,9},{9,5},{13,1},{2,14},{6,10},... | collective-permute-start | bytes 61448 | tf_op jit(solution)/shard_map/ppermute | solution.py:17
  23.3 0.7 %collective-permute-start.12 = (f32[5,8,128]{2,1,0:T(8,128)S(1)}, f32[5,8,128]{2,1,0:T(8,128)S(1)}, u32[]{:S(2)}, u32[]{:S(2)}) collective-permute-start(f32[5,8,128]{2,1,0:T(8,128)S(1)} %base.1.after.base_0), channel_id=1, source_target_pairs={{0,4},{4,0},{8,12},{12,8},{1,5},{5,1},{9,13},{13,9},{2,6},{6,2},{1... | collective-permute-start | bytes 61448 | tf_op jit(solution)/shard_map/ppermute | solution.py:17
  24.0 1.4 %collective-permute-start.13 = (f32[5,8,128]{2,1,0:T(8,128)S(1)}, f32[5,8,128]{2,1,0:T(8,128)S(1)}, u32[]{:S(2)}, u32[]{:S(2)}) collective-permute-start(f32[5,8,128]{2,1,0:T(8,128)S(1)} %base.1.after.base_0), channel_id=1, source_target_pairs={{0,8},{4,12},{8,0},{12,4},{1,9},{5,13},{9,1},{13,5},{2,10},{6,14},... | collective-permute-start | bytes 61448 | tf_op jit(solution)/shard_map/ppermute | solution.py:17
  25.4 0.0 collective-permute-done.8.load_3
  25.4 0.0 collective-permute-start.9
  25.4 1.1 %collective-permute-done.7.base_3 = f32[5,8,128]{2,1,0:T(8,128)S(1)} collective-permute-done((f32[5,8,128]{2,1,0:T(8,128)S(1)}, f32[5,8,128]{2,1,0:T(8,128)S(1)}, u32[]{:S(2)}, u32[]{:S(2)}) %collective-permute-start.7) | collective-permute-done | bytes 20512 | tf_op jit(solution)/shard_map/ppermute | solution.py:17
  26.5 0.0 collective-permute-start.11
  26.5 0.0 collective-permute-done.5.load_2
  26.5 0.5 %collective-permute-start.10 = (bf16[64,1792]{1,0:T(8,128)(2,1)S(1)}, bf16[64,1792]{1,0:T(8,128)(2,1)S(1)}, u32[]{:S(2)}, u32[]{:S(2)}) collective-permute-start(bf16[64,1792]{1,0:T(8,128)(2,1)S(1)} %collective-permute-done.5.load_2), channel_id=1, source_target_pairs={{0,1},{1,0},{2,3},{3,2},{4,5},{5,4},{6,7},{7,6},{8,9},{9,8},{10,11... | collective-permute-start | bytes 688136 | tf_op jit(solution)/shard_map/ppermute | solution.py:363
  27.0 0.1 spread.1
  27.1 0.0 collective-permute-done.12.base_1
  27.1 1.8 %collective-permute-done.13.base_2 = f32[5,8,128]{2,1,0:T(8,128)S(1)} collective-permute-done((f32[5,8,128]{2,1,0:T(8,128)S(1)}, f32[5,8,128]{2,1,0:T(8,128)S(1)}, u32[]{:S(2)}, u32[]{:S(2)}) %collective-permute-start.13) | collective-permute-done | bytes 20512 | tf_op jit(solution)/shard_map/ppermute | solution.py:17
  28.9 0.0 collective-permute-done.11.swap_3
  28.9 0.0 collective-permute-done.9.swap_1
  28.9 0.0 collective-permute-done.10.swap_2
  28.9 2.6 %march.1 = (f32[5,8,128]{2,1,0:T(8,128)S(1)}, f32[5,8,128]{2,1,0:T(8,128)S(1)}) custom-call(bf16[8,128,512]{2,1,0:T(8,128)(2,1)S(1)} %get-tuple-element.19.masked, bf16[64,2304]{1,0:T(8,128)(2,1)S(1)} %collective-permute-done.near.load_1, bf16[64,1792]{1,0:T(8,128)(2,1)S(1)} %collective-permute-done.5.load_2, ...), custom_call_target="tpu_custom_call" | custom-call | flops 10000000000 | bytes 1048576 | tf_op jit(solution)/shard_map/march/pallas_call | solution.py:336
  31.5 0.8 %collective-permute-start.14 = (f32[5,8,128]{2,1,0:T(8,128)S(1)}, f32[5,8,128]{2,1,0:T(8,128)S(1)}, u32[]{:S(2)}, u32[]{:S(2)}) collective-permute-start(f32[5,8,128]{2,1,0:T(8,128)S(1)} %get-tuple-element.31), channel_id=1, source_target_pairs={{0,2},{2,0},{4,6},{6,4},{8,10},{10,8},{12,14},{14,12},{1,3},{3,1},... | collective-permute-start | bytes 61448 | tf_op jit(solution)/shard_map/ppermute | solution.py:462
  32.4 1.3 %collective-permute-start.15 = (f32[5,8,128]{2,1,0:T(8,128)S(1)}, f32[5,8,128]{2,1,0:T(8,128)S(1)}, u32[]{:S(2)}, u32[]{:S(2)}) collective-permute-start(f32[5,8,128]{2,1,0:T(8,128)S(1)} %get-tuple-element.32), channel_id=1, source_target_pairs={{0,4},{2,6},{4,0},{6,2},{8,12},{10,14},{12,8},{14,10},{1,5},{3,7},... | collective-permute-start | bytes 61448 | tf_op jit(solution)/shard_map/ppermute | solution.py:462
  33.7 1.5 %collective-permute-start.16 = (f32[5,8,128]{2,1,0:T(8,128)S(1)}, f32[5,8,128]{2,1,0:T(8,128)S(1)}, u32[]{:S(2)}, u32[]{:S(2)}) collective-permute-start(f32[5,8,128]{2,1,0:T(8,128)S(1)} %get-tuple-element.32), channel_id=1, source_target_pairs={{0,6},{2,4},{4,2},{6,0},{8,14},{10,12},{12,10},{14,8},{1,7},{3,5},... | collective-permute-start | bytes 61448 | tf_op jit(solution)/shard_map/ppermute | solution.py:462
  35.2 0.2 collective-permute-done.14
  35.3 0.8 %collective-permute-done.15 = f32[5,8,128]{2,1,0:T(8,128)S(1)} collective-permute-done((f32[5,8,128]{2,1,0:T(8,128)S(1)}, f32[5,8,128]{2,1,0:T(8,128)S(1)}, u32[]{:S(2)}, u32[]{:S(2)}) %collective-permute-start.15) | collective-permute-done | bytes 20512 | tf_op jit(solution)/shard_map/ppermute | solution.py:462
  36.2 2.2 %collective-permute-done.16 = f32[5,8,128]{2,1,0:T(8,128)S(1)} collective-permute-done((f32[5,8,128]{2,1,0:T(8,128)S(1)}, f32[5,8,128]{2,1,0:T(8,128)S(1)}, u32[]{:S(2)}, u32[]{:S(2)}) %collective-permute-start.16) | collective-permute-done | bytes 20512 | tf_op jit(solution)/shard_map/ppermute | solution.py:462
  38.4 0.6 %fusion = f32[5,4,128]{2,1,0:T(4,128)} fusion(f32[5,8,128]{2,1,0:T(8,128)S(1)} %collective-permute-done.16, f32[5,8,128]{2,1,0:T(8,128)S(1)} %collective-permute-done.15, f32[5,8,128]{2,1,0:T(8,128)S(1)} %collective-permute-done.14, f32[5,8,128]{2,1,0:T(8,128)S(1)} %get-tuple-element.31, pred[]{:T(512)S(6)} %or.3, pred[]{:T(512)S(6)} %eq.11), kind=kLoop, calls=%fused_computation.1 | loop fusion | flops 7680 | bytes 51202 | tf_op jit(solution)/shard_map/jit(_where)/select_n | solution.py:468
  (10 shorter events, 0.1 us)
Async XLA Ops:
  0.0 7.2 %copy-start.5 = (s32[8,1,4]{0,2,1:T(4,128)S(1)}, s32[8,1,4]{0,2,1:T(4,128)}, u32[]{:S(2)}) copy-start(s32[8,1,4]{0,2,1:T(4,128)} %param.10) | copy-start | bytes 388
  0.0 7.2 %copy-start.1 = (f32[128,128]{1,0:T(8,128)S(1)}, f32[128,128]{1,0:T(8,128)}, u32[]{:S(2)}) copy-start(f32[128,128]{1,0:T(8,128)} %correction_in.1) | copy-start | bytes 196612
  0.0 7.2 %copy-start = (bf16[8,128,512]{2,1,0:T(8,128)(2,1)S(1)}, bf16[8,128,512]{2,1,0:T(8,128)(2,1)}, u32[]{:S(2)}) copy-start(bf16[8,128,512]{2,1,0:T(8,128)(2,1)} %interaction_in.1) | copy-start | bytes 3145732
  1.5 10.2 %collective-permute-start.1 = (bf16[64,128]{1,0:T(8,128)(2,1)}, bf16[64,128]{1,0:T(8,128)(2,1)S(1)}, u32[]{:S(2)}, u32[]{:S(2)}) collective-permute-start(bf16[64,128]{1,0:T(8,128)(2,1)} %pack.1.after.piece_0), channel_id=1, source_target_pairs={{0,4},{4,0},{8,12},{12,8},{1,5},{5,1},{9,13},{13,9},{2,6},{6,2},{1... | collective-permute-start | bytes 49160 | tf_op jit(solution)/shard_map/ppermute | solution.py:17
  4.6 7.1 %collective-permute-start.2 = (bf16[64,128]{1,0:T(8,128)(2,1)}, bf16[64,128]{1,0:T(8,128)(2,1)S(1)}, u32[]{:S(2)}, u32[]{:S(2)}) collective-permute-start(bf16[64,128]{1,0:T(8,128)(2,1)} %pack.1.after.piece_0), channel_id=1, source_target_pairs={{0,8},{4,12},{8,0},{12,4},{1,9},{5,13},{9,1},{13,5},{2,10},{6,14},... | collective-permute-start | bytes 49160 | tf_op jit(solution)/shard_map/ppermute | solution.py:17
  7.2 5.9 %collective-permute-start.3 = (bf16[64,128]{1,0:T(8,128)(2,1)}, bf16[64,128]{1,0:T(8,128)(2,1)S(1)}, u32[]{:S(2)}, u32[]{:S(2)}) collective-permute-start(bf16[64,128]{1,0:T(8,128)(2,1)} %pack.1.after.piece_0), channel_id=1, source_target_pairs={{0,12},{4,8},{8,4},{12,0},{1,13},{5,9},{9,5},{13,1},{2,14},{6,10},... | collective-permute-start | bytes 49160 | tf_op jit(solution)/shard_map/ppermute | solution.py:17
  7.2 0.7 %copy-start.2 = (bf16[64,128]{1,0:T(8,128)(2,1)S(1)}, bf16[64,128]{1,0:T(8,128)(2,1)}, u32[]{:S(2)}) copy-start(bf16[64,128]{1,0:T(8,128)(2,1)} %pack.1.after.piece_0) | copy-start | bytes 49156
  8.0 5.0 %copy-start.3 = (bf16[64,128]{1,0:T(8,128)(2,1)S(1)}, bf16[64,128]{1,0:T(8,128)(2,1)}, u32[]{:S(2)}) copy-start(bf16[64,128]{1,0:T(8,128)(2,1)} %pack.1.after.piece_0) | copy-start | bytes 49156
  8.9 10.3 %collective-permute-start = (bf16[64,2304]{1,0:T(8,128)(2,1)S(1)}, bf16[64,2304]{1,0:T(8,128)(2,1)S(1)}, u32[]{:S(2)}, u32[]{:S(2)}) collective-permute-start(bf16[64,2304]{1,0:T(8,128)(2,1)S(1)} %get-tuple-element.20), channel_id=1, source_target_pairs={{0,4},{4,0},{8,12},{12,8},{1,5},{5,1},{9,13},{13,9},{16,20},{20,16... | collective-permute-start | bytes 884744 | tf_op jit(solution)/shard_map/ppermute | solution.py:412
  13.0 3.9 %collective-permute-start.4 = (bf16[16,512]{1,0:T(8,128)(2,1)S(1)}, bf16[16,512]{1,0:T(8,128)(2,1)S(1)}, u32[]{:S(2)}, u32[]{:S(2)}) collective-permute-start(bf16[16,512]{1,0:T(8,128)(2,1)S(1)} %get-tuple-element.21), channel_id=1, source_target_pairs={{0,2},{2,0},{1,3},{3,1},{4,6},{6,4},{5,7},{7,5},{8,10},{10,8},{9,1... | collective-permute-start | bytes 49160 | tf_op jit(solution)/shard_map/ppermute | solution.py:363
  15.0 10.4 %collective-permute-start.8 = (bf16[64,1792]{1,0:T(8,128)(2,1)S(1)}, bf16[64,1792]{1,0:T(8,128)(2,1)S(1)}, u32[]{:S(2)}, u32[]{:S(2)}) collective-permute-start(bf16[64,1792]{1,0:T(8,128)(2,1)S(1)} %get-tuple-element.27), channel_id=1, source_target_pairs={{4,8},{8,4},{5,9},{9,5},{20,24},{24,20},{21,25},{25,21}} | collective-permute-start | bytes 688136 | tf_op jit(solution)/shard_map/ppermute | solution.py:412
  16.9 1.7 %copy-start.4 = (f32[5,4,128]{2,1,0:T(4,128)S(1)}, f32[5,4,128]{2,1,0:T(4,128)}, u32[]{:S(2)}) copy-start(f32[5,4,128]{2,1,0:T(4,128)} %forcing.1) | copy-start | bytes 30724
  17.2 3.7 %collective-permute-start.6 = (f32[24,128]{1,0:T(8,128)S(1)}, f32[24,128]{1,0:T(8,128)S(1)}, u32[]{:S(2)}, u32[]{:S(2)}) collective-permute-start(f32[24,128]{1,0:T(8,128)S(1)} %late_part.1.part), channel_id=1, source_target_pairs={{0,2},{2,0},{1,3},{3,1},{4,6},{6,4},{5,7},{7,5},{8,10},{10,8},{9,1... | collective-permute-start | bytes 36872 | tf_op jit(solution)/shard_map/ppermute | solution.py:363
  19.2 7.3 %collective-permute-start.5 = (bf16[64,1792]{1,0:T(8,128)(2,1)S(1)}, bf16[64,1792]{1,0:T(8,128)(2,1)S(1)}, u32[]{:S(2)}, u32[]{:S(2)}) collective-permute-start(bf16[64,1792]{1,0:T(8,128)(2,1)S(1)} %relay.1.after), channel_id=1, source_target_pairs={{4,8},{8,4},{5,9},{9,5},{20,24},{24,20},{21,25},{25,21}} | collective-permute-start | bytes 688136 | tf_op jit(solution)/shard_map/ppermute | solution.py:412
  20.9 5.6 %collective-permute-start.7 = (f32[5,8,128]{2,1,0:T(8,128)S(1)}, f32[5,8,128]{2,1,0:T(8,128)S(1)}, u32[]{:S(2)}, u32[]{:S(2)}) collective-permute-start(f32[5,8,128]{2,1,0:T(8,128)S(1)} %base.1.after.base_0), channel_id=1, source_target_pairs={{0,12},{4,8},{8,4},{12,0},{1,13},{5,9},{9,5},{13,1},{2,14},{6,10},... | collective-permute-start | bytes 61448 | tf_op jit(solution)/shard_map/ppermute | solution.py:17
  23.3 3.8 %collective-permute-start.12 = (f32[5,8,128]{2,1,0:T(8,128)S(1)}, f32[5,8,128]{2,1,0:T(8,128)S(1)}, u32[]{:S(2)}, u32[]{:S(2)}) collective-permute-start(f32[5,8,128]{2,1,0:T(8,128)S(1)} %base.1.after.base_0), channel_id=1, source_target_pairs={{0,4},{4,0},{8,12},{12,8},{1,5},{5,1},{9,13},{13,9},{2,6},{6,2},{1... | collective-permute-start | bytes 61448 | tf_op jit(solution)/shard_map/ppermute | solution.py:17
  24.0 4.9 %collective-permute-start.13 = (f32[5,8,128]{2,1,0:T(8,128)S(1)}, f32[5,8,128]{2,1,0:T(8,128)S(1)}, u32[]{:S(2)}, u32[]{:S(2)}) collective-permute-start(f32[5,8,128]{2,1,0:T(8,128)S(1)} %base.1.after.base_0), channel_id=1, source_target_pairs={{0,8},{4,12},{8,0},{12,4},{1,9},{5,13},{9,1},{13,5},{2,10},{6,14},... | collective-permute-start | bytes 61448 | tf_op jit(solution)/shard_map/ppermute | solution.py:17
  25.4 3.5 %collective-permute-start.9 = (bf16[64,2304]{1,0:T(8,128)(2,1)S(1)}, bf16[64,2304]{1,0:T(8,128)(2,1)S(1)}, u32[]{:S(2)}, u32[]{:S(2)}) collective-permute-start(bf16[64,2304]{1,0:T(8,128)(2,1)S(1)} %collective-permute-done.near.load_1), channel_id=1, source_target_pairs={{0,1},{1,0},{2,3},{3,2},{4,5},{5,4},{6,7},{7,6},{8,9},{9,8},{10,11... | collective-permute-start | bytes 884744 | tf_op jit(solution)/shard_map/ppermute | solution.py:363
  26.5 2.4 %collective-permute-start.11 = (bf16[64,1792]{1,0:T(8,128)(2,1)S(1)}, bf16[64,1792]{1,0:T(8,128)(2,1)S(1)}, u32[]{:S(2)}, u32[]{:S(2)}) collective-permute-start(bf16[64,1792]{1,0:T(8,128)(2,1)S(1)} %collective-permute-done.8.load_3), channel_id=1, source_target_pairs={{0,1},{1,0},{2,3},{3,2},{4,5},{5,4},{6,7},{7,6},{8,9},{9,8},{10,11... | collective-permute-start | bytes 688136 | tf_op jit(solution)/shard_map/ppermute | solution.py:363
  26.5 2.4 %collective-permute-start.10 = (bf16[64,1792]{1,0:T(8,128)(2,1)S(1)}, bf16[64,1792]{1,0:T(8,128)(2,1)S(1)}, u32[]{:S(2)}, u32[]{:S(2)}) collective-permute-start(bf16[64,1792]{1,0:T(8,128)(2,1)S(1)} %collective-permute-done.5.load_2), channel_id=1, source_target_pairs={{0,1},{1,0},{2,3},{3,2},{4,5},{5,4},{6,7},{7,6},{8,9},{9,8},{10,11... | collective-permute-start | bytes 688136 | tf_op jit(solution)/shard_map/ppermute | solution.py:363
  31.5 3.8 %collective-permute-start.14 = (f32[5,8,128]{2,1,0:T(8,128)S(1)}, f32[5,8,128]{2,1,0:T(8,128)S(1)}, u32[]{:S(2)}, u32[]{:S(2)}) collective-permute-start(f32[5,8,128]{2,1,0:T(8,128)S(1)} %get-tuple-element.31), channel_id=1, source_target_pairs={{0,2},{2,0},{4,6},{6,4},{8,10},{10,8},{12,14},{14,12},{1,3},{3,1},... | collective-permute-start | bytes 61448 | tf_op jit(solution)/shard_map/ppermute | solution.py:462
  32.4 3.8 %collective-permute-start.15 = (f32[5,8,128]{2,1,0:T(8,128)S(1)}, f32[5,8,128]{2,1,0:T(8,128)S(1)}, u32[]{:S(2)}, u32[]{:S(2)}) collective-permute-start(f32[5,8,128]{2,1,0:T(8,128)S(1)} %get-tuple-element.32), channel_id=1, source_target_pairs={{0,4},{2,6},{4,0},{6,2},{8,12},{10,14},{12,8},{14,10},{1,5},{3,7},... | collective-permute-start | bytes 61448 | tf_op jit(solution)/shard_map/ppermute | solution.py:462
  33.7 4.7 %collective-permute-start.16 = (f32[5,8,128]{2,1,0:T(8,128)S(1)}, f32[5,8,128]{2,1,0:T(8,128)S(1)}, u32[]{:S(2)}, u32[]{:S(2)}) collective-permute-start(f32[5,8,128]{2,1,0:T(8,128)S(1)} %get-tuple-element.32), channel_id=1, source_target_pairs={{0,6},{2,4},{4,2},{6,0},{8,14},{10,12},{12,10},{14,8},{1,7},{3,5},... | collective-permute-start | bytes 61448 | tf_op jit(solution)/shard_map/ppermute | solution.py:462

commit v6 on v5

--- a/solution.py
+++ b/solution.py
@@ -9,6 +9,9 @@
 STEPS = 5
 LATE = STEPS - 1
 GUST_ROWS = 8
+NEAR = ((0, 1), (1, 0), (2, 3), (3, 2))
+MID = ((1, 2), (2, 1))
+FAR = ((0, 2), (2, 0), (1, 3), (3, 1))
 
 
 def flips(value, flipped=(1, 2, 3)):
@@ -140,29 +143,44 @@
     message[...] = jnp.concatenate(pieces, axis=0).astype(jnp.bfloat16)
 
 
-def make_load(
-    after, mask_in, interaction_in, correction_in, masked, own_c, near_load, mid_load,
-    mask, interaction, correction, sems,
+def live_piece(interaction, mask, lag, block, columns, lines):
+    piece = interaction[lag, lines, columns]
+    return jnp.where(mask[0, block, lag] != 0, piece, jnp.zeros_like(piece))
+
+
+def make_near_load(
+    mask_in, interaction_in, correction_in, own_c, near_load, mask, interaction, correction, sems
 ):
-    del after
     fetched(
-        [(mask_in, mask), (interaction_in, interaction), (correction_in, correction)], sems
-    )
-    lags, rows, total = interaction.shape
-    blocks = total // rows
+        [
+            (mask_in, mask),
+            (interaction_in.at[pl.ds(0, LATE)], interaction),
+            (correction_in, correction),
+        ],
+        sems,
+    )
+    _, rows, total = interaction.shape
     cut = rows // 2
-    for lag in range(lags):
-        for block in range(blocks):
-            columns = pl.ds(block * rows, rows)
-            piece = interaction[lag, :, columns]
-            live = mask[lag, 0, block] != 0
-            masked[lag, :, columns] = jnp.where(live, piece, jnp.zeros_like(piece))
     own_c[...] = jnp.concatenate(words_of(correction[...], 2), axis=1)
     start = pl.multiple_of(lax.axis_index("gust") * cut, cut)
     places = [lag * total for lag in range(LATE - 1)] + [(LATE - 1) * total + 2 * rows]
     for lag, at in enumerate(places):
-        near_load[:, pl.ds(at, total)] = masked[lag, pl.ds(start, cut), :]
+        for block in range(total // rows):
+            near_load[:, pl.ds(at + block * rows, rows)] = live_piece(
+                interaction, mask, lag, block, pl.ds(block * rows, rows), pl.ds(start, cut)
+            )
     near_load[:, pl.ds((LATE - 1) * total, 2 * rows)] = own_c[pl.ds(start, cut), :]
+
+
+def make_masked(mask_in, interaction, near_load, masked, mid_load, mask, sems):
+    fetched([(mask_in, mask)], sems)
+    lags, rows, total = interaction.shape
+    for lag in range(lags):
+        for block in range(total // rows):
+            columns = pl.ds(block * rows, rows)
+            masked[lag, :, columns] = live_piece(
+                interaction, mask, lag, block, columns, pl.ds(0, rows)
+            )
     mid_load[...] = near_load[:, : mid_load.shape[1]]
 
 
@@ -345,6 +363,15 @@
     )(*operands)
 
 
+def exchanged(value, pairs, count):
+    named = {source for source, _ in pairs}
+    moves = [(2 * a + core, 2 * b + core) for a, b in pairs for core in (0, 1)]
+    moves += [
+        (2 * i + core, 2 * i + 1 - core) for i in range(count) if i not in named for core in (0, 1)
+    ]
+    return lax.ppermute(value, ("elem", "lag", "gust"), moves)
+
+
 def places_march(history, forcing, interaction, block_mask, correction, neighbours, edge_coef):
     f32, bf16 = jnp.float32, jnp.bfloat16
     rows = correction.shape[0]
@@ -372,23 +399,28 @@
         name="pack",
     )
     messages = flips(message)
-    masked, own_c, near_load, mid_load = on_core(
-        make_load,
-        [
-            (interaction.shape, bf16),
-            ((rows, 2 * rows), bf16),
-            ((rows // 2, width + total), bf16),
-            ((rows // 2, width), bf16),
-        ],
-        (message, block_mask, interaction, correction),
+    mask = jnp.transpose(block_mask, (1, 2, 0))
+    after_message, _ = lax.optimization_barrier((correction, message))
+    own_c, near_load = on_core(
+        make_near_load,
+        [((rows, 2 * rows), bf16), ((rows // 2, width + total), bf16)],
+        (mask, interaction, after_message),
         scratch=[
-            pltpu.SMEM(block_mask.shape, block_mask.dtype),
-            like(interaction),
+            pltpu.SMEM(mask.shape, mask.dtype),
+            pltpu.VMEM((LATE, rows, total), bf16),
             like(correction),
             pltpu.SemaphoreType.DMA((3,)),
         ],
-        in_specs=[anywhere] * 4,
-        name="load",
+        in_specs=[anywhere] * 3,
+        name="near_load",
+    )
+    masked, mid_load = on_core(
+        make_masked,
+        [(interaction.shape, bf16), ((rows // 2, width), bf16)],
+        (mask, interaction, near_load),
+        scratch=[pltpu.SMEM(mask.shape, mask.dtype), pltpu.SemaphoreType.DMA((1,))],
+        in_specs=[anywhere, vmem, vmem],
+        name="masked",
     )
     everyone, late = on_core(
         order, [((64, total), bf16), ((LATE * gusts, total), bf16)], messages, name="order"
@@ -409,10 +441,10 @@
     mid_load, _ = lax.optimization_barrier((mid_load, slope))
 
     def bulk(value, pairs):
-        return lax.ppermute(value, ("elem", "lag"), [(2 * a, 2 * b) for a, b in pairs])
-
-    near = bulk(near_load, [(i, i ^ 1) for i in range(count)])
-    mid = bulk(mid_load, [(1, 2), (2, 1)])
+        return exchanged(value, [(2 * a, 2 * b) for a, b in pairs], 2 * count)
+
+    near = bulk(near_load, NEAR)
+    mid = bulk(mid_load, MID)
 
     (part,) = on_core(
         late_part,
@@ -431,7 +463,7 @@
     (far_load,) = on_core(
         relay, [((rows // 2, width), bf16)], (ahead, near), in_specs=[anywhere, vmem], name="relay"
     )
-    far = bulk(far_load, [(1, 2), (2, 1)])
+    far = bulk(far_load, MID)
     early, _ = lax.optimization_barrier(((near, mid), ahead))
     near_swap, mid_swap = (crossed(piece, "gust") for piece in early)
     (base,) = on_core(
@@ -441,7 +473,7 @@
         in_specs=[anywhere, vmem, vmem],
         name="base",
     )
-    bases = flips(base)
+    bases = [base] + [bulk(base, pairs) for pairs in (NEAR, FAR, MID)]
     (spread,) = on_core(
         all_spread,
         [((2 * RIM, total), f32)],
@@ -458,10 +490,11 @@
         name="march",
     )
 
-    def swap(value, flip):
-        return lax.ppermute(value, ("elem", "lag"), [(i, i ^ flip) for i in range(2 * count)])
-
-    to_lag, to_outer, to_both = swap(own, 1), swap(outer, 2), swap(outer, 3)
+    def swap(value, to_elem, to_lag):
+        pairs = [(2 * a, 2 * (a ^ to_elem) + to_lag) for a in (1, 2)]
+        return exchanged(value, pairs + [(b, a) for a, b in pairs], 2 * count)
+
+    to_both, to_outer, to_lag = swap(outer, 1, 1), swap(outer, 1, 0), swap(own, 0, 1)
     place = lax.axis_index("elem")
     middle = (place == 1) | (place == 2)
     first = lax.axis_index("lag") == 0

time: 39.4 us -> 33.7 us (0.86)
  starting transfers between devices: 21.4 us -> 12.1 us
  waiting for transfers between devices: 10.2 us -> 14.2 us
  local copies, waits for them, and re-layouts: 0.83 us -> 0.02 us
  Pallas kernels: 5.85 us -> 6.44 us
    ppermute x6 -> x9, starting transfers between devices: 7.78 us -> 3.22 us  [exchanged(): return lax.ppermute(value, ('elem', 'lag', 'gust'), moves)]
    ppermute x6 -> x3, starting transfers between devices: 10.2 us -> 5.68 us  [flips(): lax.ppermute(value, 'elem', [(i, i ^ flip) for i in range(count)])]
    ppermute x6 -> x9, waiting for transfers between devices: 3.72 us -> 6.59 us  [exchanged(): return lax.ppermute(value, ('elem', 'lag', 'gust'), moves)]
    ppermute x5, waiting for transfers between devices: 2.3 us -> 4.2 us  [crossed(): return lax.ppermute(value, axis, [(0, 1), (1, 0)])]
    unnamed x13 -> x10, local copies, waits for them, and re-layouts: 0.83 us -> 0.02 us
    ppermute x6 -> x3, waiting for transfers between devices: 4.18 us -> 3.43 us  [flips(): lax.ppermute(value, 'elem', [(i, i ^ flip) for i in range(count)])]
    pallas_call x10 -> x11, Pallas kernels: 5.85 us -> 6.44 us  [on_core(): pl.pallas_call(body, out_shape=[jax.ShapeDtypeStruct(shape, dtype) for sh...]
  transfers between devices with their start and end apart: 17 -> 17, of which waited for: 9 -> 7; matrix products, arithmetic and copies ran while one was open for 0% -> 0% of each run, Pallas kernels for 5% -> 7%
where the time goes in v6:
time: 33.7 us; the launch traced here: 33.5 us
  waiting for transfers between devices  14.2 us (42%)
  starting transfers between devices  12.1 us (36%)
  Pallas kernels  6.44 us (19%)
  other arithmetic  0.61 us (2%)
    ppermute x9, waiting for transfers between devices, exchanged(): return lax.ppermute(value, ('elem', 'lag', 'gust'), moves)  6.59 us
    pallas_call x11, Pallas kernels, on_core(): pl.pallas_call(body, out_shape=[jax.ShapeDtypeStruct(shape, dtype) for sh...  6.44 us
    ppermute x3, starting transfers between devices, flips(): lax.ppermute(value, 'elem', [(i, i ^ flip) for i in range(count)])  5.68 us
    ppermute x5, waiting for transfers between devices, crossed(): return lax.ppermute(value, axis, [(0, 1), (1, 0)])  4.2 us
    ppermute x3, waiting for transfers between devices, flips(): lax.ppermute(value, 'elem', [(i, i ^ flip) for i in range(count)])  3.43 us
    ppermute x9, starting transfers between devices, exchanged(): return lax.ppermute(value, ('elem', 'lag', 'gust'), moves)  3.22 us
    ppermute x5, starting transfers between devices, crossed(): return lax.ppermute(value, axis, [(0, 1), (1, 0)])  3.2 us
  transfers between devices with their start and end apart: 17, of which 7 were waited for; matrix products, arithmetic and copies ran while one was open for 0% of the time, Pallas kernels for 7%

profile of v6, /device:TPU:0, one launch (start us, length us, event | category | flops | bytes accessed | tf_op | source)
XLA Modules:
  0.0 33.5 jit_solution(11965047646924772949)
XLA Ops:
  0.0 1.5 %pack.1.piece_0 = bf16[64,128]{1,0:T(8,128)(2,1)} custom-call(f32[8,4,128]{2,1,0:T(4,128)} %history_in.1, s32[4,128]{1,0:T(4,128)} %neighbours_in.1, f32[4,128]{1,0:T(4,128)} %edge_coef_in.1), custom_call_target="tpu_custom_call" | custom-call | flops 10000000000 | bytes 1048576 | tf_op jit(solution)/shard_map/pack/pallas_call | solution.py:354
  1.5 3.1 %collective-permute-start.1 = (bf16[64,128]{1,0:T(8,128)(2,1)}, bf16[64,128]{1,0:T(8,128)(2,1)S(1)}, u32[]{:S(2)}, u32[]{:S(2)}) collective-permute-start(bf16[64,128]{1,0:T(8,128)(2,1)} %pack.1.piece_0), channel_id=1, source_target_pairs={{0,4},{4,0},{8,12},{12,8},{1,5},{5,1},{9,13},{13,9},{2,6},{6,2},{1... | collective-permute-start | bytes 49160 | tf_op jit(solution)/shard_map/ppermute | solution.py:20
  4.6 2.6 %collective-permute-start.2 = (bf16[64,128]{1,0:T(8,128)(2,1)}, bf16[64,128]{1,0:T(8,128)(2,1)S(1)}, u32[]{:S(2)}, u32[]{:S(2)}) collective-permute-start(bf16[64,128]{1,0:T(8,128)(2,1)} %pack.1.piece_0), channel_id=1, source_target_pairs={{0,8},{4,12},{8,0},{12,4},{1,9},{5,13},{9,1},{13,5},{2,10},{6,14},... | collective-permute-start | bytes 49160 | tf_op jit(solution)/shard_map/ppermute | solution.py:20
  7.2 0.0 collective-permute-start.3
  7.2 0.0 copy-done.1
  7.2 0.0 copy-done.4
  7.2 0.0 copy-done
  7.2 0.7 %near_load.1 = (bf16[128,256]{1,0:T(8,128)(2,1)S(1)}, bf16[64,2304]{1,0:T(8,128)(2,1)S(1)}) custom-call(s32[1,4,8]{2,1,0:T(4,128)S(1)} %bitcast.1, bf16[8,128,512]{2,1,0:T(8,128)(2,1)S(1)} %copy-done, f32[128,128]{1,0:T(8,128)S(1)} %copy-done.1), custom_call_target="tpu_custom_call" | custom-call | flops 10000000000 | bytes 1048576 | tf_op jit(solution)/shard_map/near_load/pallas_call | solution.py:354
  7.9 0.0 copy-start.2
  7.9 0.9 %collective-permute-start = (bf16[64,2304]{1,0:T(8,128)(2,1)S(1)}, bf16[64,2304]{1,0:T(8,128)(2,1)S(1)}, u32[]{:S(2)}, u32[]{:S(2)}) collective-permute-start(bf16[64,2304]{1,0:T(8,128)(2,1)S(1)} %get-tuple-element.21.near_load), channel_id=1, source_target_pairs={{0,4},{1,5},{4,0},{5,1},{8,12},{9,13},{12,8},{13,9},{2,3},{3,2},{6... | collective-permute-start | bytes 884744 | tf_op jit(solution)/shard_map/ppermute | solution.py:372
  8.8 0.8 %masked.1 = (bf16[8,128,512]{2,1,0:T(8,128)(2,1)S(1)}, bf16[64,1792]{1,0:T(8,128)(2,1)S(1)}) custom-call(s32[1,4,8]{2,1,0:T(4,128)S(1)} %bitcast.2, bf16[8,128,512]{2,1,0:T(8,128)(2,1)S(1)} %copy-done, bf16[64,2304]{1,0:T(8,128)(2,1)S(1)} %get-tuple-element.21.near_load), custom_call_target="tpu_custom_call" | custom-call | flops 10000000000 | bytes 1048576 | tf_op jit(solution)/shard_map/masked/pallas_call | solution.py:354
  9.6 0.0 collective-permute-done.1.piece_1
  9.7 0.0 collective-permute-done.2.piece_2
  9.7 3.4 %collective-permute-done.3.piece_3 = bf16[64,128]{1,0:T(8,128)(2,1)S(1)} collective-permute-done((bf16[64,128]{1,0:T(8,128)(2,1)}, bf16[64,128]{1,0:T(8,128)(2,1)S(1)}, u32[]{:S(2)}, u32[]{:S(2)}) %collective-permute-start.3) | collective-permute-done | bytes 16416 | tf_op jit(solution)/shard_map/ppermute | solution.py:20
  13.1 0.0 copy-done.2
  13.1 1.4 %collective-permute-start.4 = (bf16[16,512]{1,0:T(8,128)(2,1)S(1)}, bf16[16,512]{1,0:T(8,128)(2,1)S(1)}, u32[]{:S(2)}, u32[]{:S(2)}) collective-permute-start(bf16[16,512]{1,0:T(8,128)(2,1)S(1)} %get-tuple-element.23), channel_id=1, source_target_pairs={{0,2},{2,0},{1,3},{3,1},{4,6},{6,4},{5,7},{7,5},{8,10},{10,8},{9,1... | collective-permute-start | bytes 49160 | tf_op jit(solution)/shard_map/ppermute | solution.py:390
  14.5 0.5 %main_part.1 = (f32[24,128]{1,0:T(8,128)S(1)}, f32[8,128]{1,0:T(8,128)S(1)}) custom-call(bf16[64,512]{1,0:T(8,128)(2,1)S(1)} %get-tuple-element.24.everyone, bf16[8,128,512]{2,1,0:T(8,128)(2,1)S(1)} %get-tuple-element.22.masked), custom_call_target="tpu_custom_call" | custom-call | flops 10000000000 | bytes 1048576 | tf_op jit(solution)/shard_map/main_part/pallas_call | solution.py:354
  15.0 0.0 collective-permute-start.8
  15.0 1.9 %collective-permute-done.4.late = bf16[16,512]{1,0:T(8,128)(2,1)S(1)} collective-permute-done((bf16[16,512]{1,0:T(8,128)(2,1)S(1)}, bf16[16,512]{1,0:T(8,128)(2,1)S(1)}, u32[]{:S(2)}, u32[]{:S(2)}) %collective-permute-start.4) | collective-permute-done | bytes 16416 | tf_op jit(solution)/shard_map/ppermute | solution.py:390
  16.9 0.3 late_part.1.part
  17.2 1.3 %collective-permute-start.6 = (f32[24,128]{1,0:T(8,128)S(1)}, f32[24,128]{1,0:T(8,128)S(1)}, u32[]{:S(2)}, u32[]{:S(2)}) collective-permute-start(f32[24,128]{1,0:T(8,128)S(1)} %late_part.1.part), channel_id=1, source_target_pairs={{0,2},{2,0},{1,3},{3,1},{4,6},{6,4},{5,7},{7,5},{8,10},{10,8},{9,1... | collective-permute-start | bytes 36872 | tf_op jit(solution)/shard_map/ppermute | solution.py:390
  18.5 0.0 copy-done.3
  18.5 0.0 collective-permute-done.near.load_1
  18.6 0.1 collective-permute-start.5
  18.6 2.3 %collective-permute-done.6.other = f32[24,128]{1,0:T(8,128)S(1)} collective-permute-done((f32[24,128]{1,0:T(8,128)S(1)}, f32[24,128]{1,0:T(8,128)S(1)}, u32[]{:S(2)}, u32[]{:S(2)}) %collective-permute-start.6) | collective-permute-done | bytes 12320 | tf_op jit(solution)/shard_map/ppermute | solution.py:390
  20.9 0.0 collective-permute-start.7
  20.9 0.6 %collective-permute-start.12 = (f32[5,8,128]{2,1,0:T(8,128)S(1)}, f32[5,8,128]{2,1,0:T(8,128)S(1)}, u32[]{:S(2)}, u32[]{:S(2)}) collective-permute-start(f32[5,8,128]{2,1,0:T(8,128)S(1)} %base.1.after.base_0), channel_id=1, source_target_pairs={{0,4},{1,5},{4,0},{5,1},{8,12},{9,13},{12,8},{13,9},{2,3},{3,2},{6... | collective-permute-start | bytes 61448 | tf_op jit(solution)/shard_map/ppermute | solution.py:372
  21.6 0.2 collective-permute-start.13
  21.8 0.0 collective-permute-done.8.load_3
  21.8 0.0 collective-permute-start.9
  21.8 0.3 collective-permute-done.7.base_3
  22.1 0.2 collective-permute-start.11
  22.3 0.0 collective-permute-done.5.load_2
  22.3 0.3 collective-permute-start.10
  22.6 0.1 spread.1
  22.7 2.0 %collective-permute-done.12.base_1 = f32[5,8,128]{2,1,0:T(8,128)S(1)} collective-permute-done((f32[5,8,128]{2,1,0:T(8,128)S(1)}, f32[5,8,128]{2,1,0:T(8,128)S(1)}, u32[]{:S(2)}, u32[]{:S(2)}) %collective-permute-start.12) | collective-permute-done | bytes 20512 | tf_op jit(solution)/shard_map/ppermute | solution.py:372
  24.8 1.7 %collective-permute-done.13.base_2 = f32[5,8,128]{2,1,0:T(8,128)S(1)} collective-permute-done((f32[5,8,128]{2,1,0:T(8,128)S(1)}, f32[5,8,128]{2,1,0:T(8,128)S(1)}, u32[]{:S(2)}, u32[]{:S(2)}) %collective-permute-start.13) | collective-permute-done | bytes 20512 | tf_op jit(solution)/shard_map/ppermute | solution.py:372
  26.5 0.0 collective-permute-done.11.swap_3
  26.5 0.0 collective-permute-done.9.swap_1
  26.5 0.0 collective-permute-done.10.swap_2
  26.5 2.6 %march.1 = (f32[5,8,128]{2,1,0:T(8,128)S(1)}, f32[5,8,128]{2,1,0:T(8,128)S(1)}) custom-call(bf16[8,128,512]{2,1,0:T(8,128)(2,1)S(1)} %get-tuple-element.22.masked, bf16[64,2304]{1,0:T(8,128)(2,1)S(1)} %collective-permute-done.near.load_1, bf16[64,1792]{1,0:T(8,128)(2,1)S(1)} %collective-permute-done.5.load_2, ...), custom_call_target="tpu_custom_call" | custom-call | flops 10000000000 | bytes 1048576 | tf_op jit(solution)/shard_map/march/pallas_call | solution.py:354
  29.1 0.0 collective-permute-start.14
  29.1 1.3 %collective-permute-start.15 = (f32[5,8,128]{2,1,0:T(8,128)S(1)}, f32[5,8,128]{2,1,0:T(8,128)S(1)}, u32[]{:S(2)}, u32[]{:S(2)}) collective-permute-start(f32[5,8,128]{2,1,0:T(8,128)S(1)} %get-tuple-element.34), channel_id=1, source_target_pairs={{4,0},{5,1},{8,12},{9,13},{0,4},{1,5},{12,8},{13,9},{2,3},{3,2},{6... | collective-permute-start | bytes 61448 | tf_op jit(solution)/shard_map/ppermute | solution.py:372
  30.4 0.0 collective-permute-start.16
  30.4 0.0 collective-permute-done.14
  30.4 2.5 %collective-permute-done.15 = f32[5,8,128]{2,1,0:T(8,128)S(1)} collective-permute-done((f32[5,8,128]{2,1,0:T(8,128)S(1)}, f32[5,8,128]{2,1,0:T(8,128)S(1)}, u32[]{:S(2)}, u32[]{:S(2)}) %collective-permute-start.15) | collective-permute-done | bytes 20512 | tf_op jit(solution)/shard_map/ppermute | solution.py:372
  32.9 0.0 collective-permute-done.16
  32.9 0.6 %fusion = f32[5,4,128]{2,1,0:T(4,128)} fusion(f32[5,8,128]{2,1,0:T(8,128)S(1)} %collective-permute-done.16, f32[5,8,128]{2,1,0:T(8,128)S(1)} %collective-permute-done.15, f32[5,8,128]{2,1,0:T(8,128)S(1)} %collective-permute-done.14, f32[5,8,128]{2,1,0:T(8,128)S(1)} %get-tuple-element.33, pred[]{:T(512)S(6)} %or.3, pred[]{:T(512)S(6)} %eq.11), kind=kLoop, calls=%fused_computation.1 | loop fusion | flops 7680 | bytes 51202 | tf_op jit(solution)/shard_map/jit(_where)/select_n | solution.py:501
  (8 shorter events, 0.1 us)
Async XLA Ops:
  0.0 7.2 %copy-start.1 = (f32[128,128]{1,0:T(8,128)S(1)}, f32[128,128]{1,0:T(8,128)}, u32[]{:S(2)}) copy-start(f32[128,128]{1,0:T(8,128)} %correction_in) | copy-start | bytes 196612
  0.0 7.2 %copy-start.4 = (s32[8,1,4]{0,2,1:T(4,128)S(1)}, s32[8,1,4]{0,2,1:T(4,128)}, u32[]{:S(2)}) copy-start(s32[8,1,4]{0,2,1:T(4,128)} %param.10) | copy-start | bytes 388
  0.0 7.2 %copy-start = (bf16[8,128,512]{2,1,0:T(8,128)(2,1)S(1)}, bf16[8,128,512]{2,1,0:T(8,128)(2,1)}, u32[]{:S(2)}) copy-start(bf16[8,128,512]{2,1,0:T(8,128)(2,1)} %interaction.1) | copy-start | bytes 3145732
  1.5 8.2 %collective-permute-start.1 = (bf16[64,128]{1,0:T(8,128)(2,1)}, bf16[64,128]{1,0:T(8,128)(2,1)S(1)}, u32[]{:S(2)}, u32[]{:S(2)}) collective-permute-start(bf16[64,128]{1,0:T(8,128)(2,1)} %pack.1.piece_0), channel_id=1, source_target_pairs={{0,4},{4,0},{8,12},{12,8},{1,5},{5,1},{9,13},{13,9},{2,6},{6,2},{1... | collective-permute-start | bytes 49160 | tf_op jit(solution)/shard_map/ppermute | solution.py:20
  4.6 5.1 %collective-permute-start.2 = (bf16[64,128]{1,0:T(8,128)(2,1)}, bf16[64,128]{1,0:T(8,128)(2,1)S(1)}, u32[]{:S(2)}, u32[]{:S(2)}) collective-permute-start(bf16[64,128]{1,0:T(8,128)(2,1)} %pack.1.piece_0), channel_id=1, source_target_pairs={{0,8},{4,12},{8,0},{12,4},{1,9},{5,13},{9,1},{13,5},{2,10},{6,14},... | collective-permute-start | bytes 49160 | tf_op jit(solution)/shard_map/ppermute | solution.py:20
  7.2 5.9 %collective-permute-start.3 = (bf16[64,128]{1,0:T(8,128)(2,1)}, bf16[64,128]{1,0:T(8,128)(2,1)S(1)}, u32[]{:S(2)}, u32[]{:S(2)}) collective-permute-start(bf16[64,128]{1,0:T(8,128)(2,1)} %pack.1.piece_0), channel_id=1, source_target_pairs={{0,12},{4,8},{8,4},{12,0},{1,13},{5,9},{9,5},{13,1},{2,14},{6,10},... | collective-permute-start | bytes 49160 | tf_op jit(solution)/shard_map/ppermute | solution.py:20
  7.9 5.2 %copy-start.2 = (bf16[64,128]{1,0:T(8,128)(2,1)S(1)}, bf16[64,128]{1,0:T(8,128)(2,1)}, u32[]{:S(2)}) copy-start(bf16[64,128]{1,0:T(8,128)(2,1)} %pack.1.piece_0) | copy-start | bytes 49156
  7.9 10.7 %collective-permute-start = (bf16[64,2304]{1,0:T(8,128)(2,1)S(1)}, bf16[64,2304]{1,0:T(8,128)(2,1)S(1)}, u32[]{:S(2)}, u32[]{:S(2)}) collective-permute-start(bf16[64,2304]{1,0:T(8,128)(2,1)S(1)} %get-tuple-element.21.near_load), channel_id=1, source_target_pairs={{0,4},{1,5},{4,0},{5,1},{8,12},{9,13},{12,8},{13,9},{2,3},{3,2},{6... | collective-permute-start | bytes 884744 | tf_op jit(solution)/shard_map/ppermute | solution.py:372
  13.1 3.8 %collective-permute-start.4 = (bf16[16,512]{1,0:T(8,128)(2,1)S(1)}, bf16[16,512]{1,0:T(8,128)(2,1)S(1)}, u32[]{:S(2)}, u32[]{:S(2)}) collective-permute-start(bf16[16,512]{1,0:T(8,128)(2,1)S(1)} %get-tuple-element.23), channel_id=1, source_target_pairs={{0,2},{2,0},{1,3},{3,1},{4,6},{6,4},{5,7},{7,5},{8,10},{10,8},{9,1... | collective-permute-start | bytes 49160 | tf_op jit(solution)/shard_map/ppermute | solution.py:390
  15.0 6.9 %collective-permute-start.8 = (bf16[64,1792]{1,0:T(8,128)(2,1)S(1)}, bf16[64,1792]{1,0:T(8,128)(2,1)S(1)}, u32[]{:S(2)}, u32[]{:S(2)}) collective-permute-start(bf16[64,1792]{1,0:T(8,128)(2,1)S(1)} %get-tuple-element.29), channel_id=1, source_target_pairs={{4,8},{5,9},{8,4},{9,5},{0,1},{1,0},{2,3},{3,2},{6,7},{7,6},{10,11... | collective-permute-start | bytes 688136 | tf_op jit(solution)/shard_map/ppermute | solution.py:372
  16.9 1.6 %copy-start.3 = (f32[5,4,128]{2,1,0:T(4,128)S(1)}, f32[5,4,128]{2,1,0:T(4,128)}, u32[]{:S(2)}) copy-start(f32[5,4,128]{2,1,0:T(4,128)} %forcing.1) | copy-start | bytes 30724
  17.2 3.7 %collective-permute-start.6 = (f32[24,128]{1,0:T(8,128)S(1)}, f32[24,128]{1,0:T(8,128)S(1)}, u32[]{:S(2)}, u32[]{:S(2)}) collective-permute-start(f32[24,128]{1,0:T(8,128)S(1)} %late_part.1.part), channel_id=1, source_target_pairs={{0,2},{2,0},{1,3},{3,1},{4,6},{6,4},{5,7},{7,5},{8,10},{10,8},{9,1... | collective-permute-start | bytes 36872 | tf_op jit(solution)/shard_map/ppermute | solution.py:390
  18.6 3.8 %collective-permute-start.5 = (bf16[64,1792]{1,0:T(8,128)(2,1)S(1)}, bf16[64,1792]{1,0:T(8,128)(2,1)S(1)}, u32[]{:S(2)}, u32[]{:S(2)}) collective-permute-start(bf16[64,1792]{1,0:T(8,128)(2,1)S(1)} %relay.1.after), channel_id=1, source_target_pairs={{4,8},{5,9},{8,4},{9,5},{0,1},{1,0},{2,3},{3,2},{6,7},{7,6},{10,11... | collective-permute-start | bytes 688136 | tf_op jit(solution)/shard_map/ppermute | solution.py:372
  20.9 1.2 %collective-permute-start.7 = (f32[5,8,128]{2,1,0:T(8,128)S(1)}, f32[5,8,128]{2,1,0:T(8,128)S(1)}, u32[]{:S(2)}, u32[]{:S(2)}) collective-permute-start(f32[5,8,128]{2,1,0:T(8,128)S(1)} %base.1.after.base_0), channel_id=1, source_target_pairs={{4,8},{5,9},{8,4},{9,5},{0,1},{1,0},{2,3},{3,2},{6,7},{7,6},{10,11... | collective-permute-start | bytes 61448 | tf_op jit(solution)/shard_map/ppermute | solution.py:372
  20.9 3.8 %collective-permute-start.12 = (f32[5,8,128]{2,1,0:T(8,128)S(1)}, f32[5,8,128]{2,1,0:T(8,128)S(1)}, u32[]{:S(2)}, u32[]{:S(2)}) collective-permute-start(f32[5,8,128]{2,1,0:T(8,128)S(1)} %base.1.after.base_0), channel_id=1, source_target_pairs={{0,4},{1,5},{4,0},{5,1},{8,12},{9,13},{12,8},{13,9},{2,3},{3,2},{6... | collective-permute-start | bytes 61448 | tf_op jit(solution)/shard_map/ppermute | solution.py:372
  21.6 4.9 %collective-permute-start.13 = (f32[5,8,128]{2,1,0:T(8,128)S(1)}, f32[5,8,128]{2,1,0:T(8,128)S(1)}, u32[]{:S(2)}, u32[]{:S(2)}) collective-permute-start(f32[5,8,128]{2,1,0:T(8,128)S(1)} %base.1.after.base_0), channel_id=1, source_target_pairs={{0,8},{1,9},{8,0},{9,1},{4,12},{5,13},{12,4},{13,5},{2,3},{3,2},{6... | collective-permute-start | bytes 61448 | tf_op jit(solution)/shard_map/ppermute | solution.py:372
  21.8 4.7 %collective-permute-start.9 = (bf16[64,2304]{1,0:T(8,128)(2,1)S(1)}, bf16[64,2304]{1,0:T(8,128)(2,1)S(1)}, u32[]{:S(2)}, u32[]{:S(2)}) collective-permute-start(bf16[64,2304]{1,0:T(8,128)(2,1)S(1)} %collective-permute-done.near.load_1), channel_id=1, source_target_pairs={{0,1},{1,0},{2,3},{3,2},{4,5},{5,4},{6,7},{7,6},{8,9},{9,8},{10,11... | collective-permute-start | bytes 884744 | tf_op jit(solution)/shard_map/ppermute | solution.py:390
  22.1 4.4 %collective-permute-start.11 = (bf16[64,1792]{1,0:T(8,128)(2,1)S(1)}, bf16[64,1792]{1,0:T(8,128)(2,1)S(1)}, u32[]{:S(2)}, u32[]{:S(2)}) collective-permute-start(bf16[64,1792]{1,0:T(8,128)(2,1)S(1)} %collective-permute-done.8.load_3), channel_id=1, source_target_pairs={{0,1},{1,0},{2,3},{3,2},{4,5},{5,4},{6,7},{7,6},{8,9},{9,8},{10,11... | collective-permute-start | bytes 688136 | tf_op jit(solution)/shard_map/ppermute | solution.py:390
  22.3 4.1 %collective-permute-start.10 = (bf16[64,1792]{1,0:T(8,128)(2,1)S(1)}, bf16[64,1792]{1,0:T(8,128)(2,1)S(1)}, u32[]{:S(2)}, u32[]{:S(2)}) collective-permute-start(bf16[64,1792]{1,0:T(8,128)(2,1)S(1)} %collective-permute-done.5.load_2), channel_id=1, source_target_pairs={{0,1},{1,0},{2,3},{3,2},{4,5},{5,4},{6,7},{7,6},{8,9},{9,8},{10,11... | collective-permute-start | bytes 688136 | tf_op jit(solution)/shard_map/ppermute | solution.py:390
  29.1 1.3 %collective-permute-start.14 = (f32[5,8,128]{2,1,0:T(8,128)S(1)}, f32[5,8,128]{2,1,0:T(8,128)S(1)}, u32[]{:S(2)}, u32[]{:S(2)}) collective-permute-start(f32[5,8,128]{2,1,0:T(8,128)S(1)} %get-tuple-element.33), channel_id=1, source_target_pairs={{4,6},{5,7},{8,10},{9,11},{6,4},{7,5},{10,8},{11,9},{0,1},{1,0},{2... | collective-permute-start | bytes 61448 | tf_op jit(solution)/shard_map/ppermute | solution.py:372
  29.1 3.8 %collective-permute-start.15 = (f32[5,8,128]{2,1,0:T(8,128)S(1)}, f32[5,8,128]{2,1,0:T(8,128)S(1)}, u32[]{:S(2)}, u32[]{:S(2)}) collective-permute-start(f32[5,8,128]{2,1,0:T(8,128)S(1)} %get-tuple-element.34), channel_id=1, source_target_pairs={{4,0},{5,1},{8,12},{9,13},{0,4},{1,5},{12,8},{13,9},{2,3},{3,2},{6... | collective-permute-start | bytes 61448 | tf_op jit(solution)/shard_map/ppermute | solution.py:372
  30.4 2.6 %collective-permute-start.16 = (f32[5,8,128]{2,1,0:T(8,128)S(1)}, f32[5,8,128]{2,1,0:T(8,128)S(1)}, u32[]{:S(2)}, u32[]{:S(2)}) collective-permute-start(f32[5,8,128]{2,1,0:T(8,128)S(1)} %get-tuple-element.34), channel_id=1, source_target_pairs={{4,2},{5,3},{8,14},{9,15},{2,4},{3,5},{14,8},{15,9},{0,1},{1,0},{6... | collective-permute-start | bytes 61448 | tf_op jit(solution)/shard_map/ppermute | solution.py:372

commit v7 on v6

--- a/solution.py
+++ b/solution.py
@@ -207,7 +207,7 @@
         )
 
 
-def order(piece_0, piece_1, piece_2, piece_3, everyone, late):
+def order(piece_0, piece_2, piece_3, piece_1, everyone, late):
     place = lax.axis_index("elem")
     rows = piece_0.shape[1]
     for flip, piece in enumerate((piece_0, piece_1, piece_2, piece_3)):
@@ -349,11 +349,14 @@
     out[LATE], near_out[LATE] = (corrected(waiting[LATE][flip], flip) for flip in (0, 1))
 
 
-def on_core(body, shapes, operands, scratch=(), in_specs=None, limit=24, name=None):
+def on_core(body, shapes, operands, scratch=(), in_specs=None, limit=24, name=None, force=False):
     vmem = pl.BlockSpec(memory_space=pltpu.VMEM)
     return pl.pallas_call(
         body,
-        out_shape=[jax.ShapeDtypeStruct(shape, dtype) for shape, dtype in shapes],
+        out_shape=[
+            pltpu.VMEM(shape, dtype) if force else jax.ShapeDtypeStruct(shape, dtype)
+            for shape, dtype in shapes
+        ],
         in_specs=in_specs or [vmem] * len(operands),
         out_specs=[vmem] * len(shapes),
         scratch_shapes=list(scratch),
@@ -396,6 +399,7 @@
         scratch=[like(history), like(neighbours), like(edge_coef), pltpu.SemaphoreType.DMA((3,))],
         in_specs=[anywhere] * 3,
         limit=None,
+        force=True,
         name="pack",
     )
     messages = flips(message)
@@ -423,7 +427,10 @@
         name="masked",
     )
     everyone, late = on_core(
-        order, [((64, total), bf16), ((LATE * gusts, total), bf16)], messages, name="order"
+        order,
+        [((64, total), bf16), ((LATE * gusts, total), bf16)],
+        [messages[flip] for flip in (0, 2, 3, 1)],
+        name="order",
     )
     before = crossed(late, "lag")
     part, slope = on_core(
@@ -490,16 +497,20 @@
         name="march",
     )
 
-    def swap(value, to_elem, to_lag):
-        pairs = [(2 * a, 2 * (a ^ to_elem) + to_lag) for a in (1, 2)]
-        return exchanged(value, pairs + [(b, a) for a, b in pairs], 2 * count)
-
-    to_both, to_outer, to_lag = swap(outer, 1, 1), swap(outer, 1, 0), swap(own, 0, 1)
+    def handed(value, *cycles):
+        moves = []
+        for cycle in cycles:
+            moves += zip(cycle, cycle[1:] + cycle[:1])
+        return exchanged(value, moves, 2 * count)
+
+    to_both = handed(outer, [2, 1, 3], [4, 7, 5])
+    to_outer = handed(outer, [2, 0], [4, 6])
+    to_lag = handed(own, [2, 3], [4, 5])
     place = lax.axis_index("elem")
-    middle = (place == 1) | (place == 2)
+    inside = (place == 1) | (place == 2)
     first = lax.axis_index("lag") == 0
     result = jnp.where(
-        middle, jnp.where(first, own, to_lag), jnp.where(first, to_outer, to_both)
+        inside, jnp.where(first, own, to_lag), jnp.where(first, to_outer, to_both)
     )
     return result[:, :gusts]
 

time: 33.7 us -> 32.8 us (0.973)
  waiting for transfers between devices: 14.2 us -> 10.2 us
  starting transfers between devices: 12.1 us -> 15.9 us
  Pallas kernels: 6.44 us -> 5.85 us
    ppermute x9, starting transfers between devices: 3.22 us -> 6.8 us  [exchanged(): return lax.ppermute(value, ('elem', 'lag', 'gust'), moves)]
    ppermute x3, waiting for transfers between devices: 3.43 us -> 0.68 us  [flips(): lax.ppermute(value, 'elem', [(i, i ^ flip) for i in range(count)])]
    ppermute x9, waiting for transfers between devices: 6.59 us -> 5.44 us  [exchanged(): return lax.ppermute(value, ('elem', 'lag', 'gust'), moves)]
    pallas_call x11, Pallas kernels: 6.44 us -> 5.85 us  [on_core(): pl.pallas_call(body, out_shape=[pltpu.VMEM(shape, dtype) if force else ja...]
  transfers between devices with their start and end apart: 17 -> 17, of which waited for: 7 -> 6; matrix products, arithmetic and copies ran while one was open for 0% -> 0% of each run, Pallas kernels for 7% -> 7%
where the time goes in v7:
time: 32.8 us; the launch traced here: 32.7 us
  starting transfers between devices  15.9 us (48%)
  waiting for transfers between devices  10.2 us (31%)
  Pallas kernels  5.85 us (18%)
  other arithmetic  0.61 us (2%)
    ppermute x9, starting transfers between devices, exchanged(): return lax.ppermute(value, ('elem', 'lag', 'gust'), moves)  6.8 us
    pallas_call x11, Pallas kernels, on_core(): pl.pallas_call(body, out_shape=[pltpu.VMEM(shape, dtype) if force else ja...  5.85 us
    ppermute x3, starting transfers between devices, flips(): lax.ppermute(value, 'elem', [(i, i ^ flip) for i in range(count)])  5.68 us
    ppermute x9, waiting for transfers between devices, exchanged(): return lax.ppermute(value, ('elem', 'lag', 'gust'), moves)  5.44 us
    ppermute x5, waiting for transfers between devices, crossed(): return lax.ppermute(value, axis, [(0, 1), (1, 0)])  4.03 us
    ppermute x5, starting transfers between devices, crossed(): return lax.ppermute(value, axis, [(0, 1), (1, 0)])  3.43 us
    ppermute x3, waiting for transfers between devices, flips(): lax.ppermute(value, 'elem', [(i, i ^ flip) for i in range(count)])  0.68 us
  transfers between devices with their start and end apart: 17, of which 6 were waited for; matrix products, arithmetic and copies ran while one was open for 0% of the time, Pallas kernels for 7%

profile of v7, /device:TPU:0, one launch (start us, length us, event | category | flops | bytes accessed | tf_op | source)
XLA Modules:
  0.0 32.7 jit_solution(9567249849646249786)
XLA Ops:
  0.0 0.0 copy-start.1
  0.0 0.0 copy-start.3
  0.0 0.9 %pack.1.piece_0 = bf16[64,128]{1,0:T(8,128)(2,1)S(1)} custom-call(f32[8,4,128]{2,1,0:T(4,128)} %history_in.1, s32[4,128]{1,0:T(4,128)} %neighbours_in.1, f32[4,128]{1,0:T(4,128)} %edge_coef_in.1), custom_call_target="tpu_custom_call" | custom-call | flops 10000000000 | bytes 1048576 | tf_op jit(solution)/shard_map/pack/pallas_call | solution.py:354
  0.9 4.1 %collective-permute-start.1 = (bf16[64,128]{1,0:T(8,128)(2,1)S(1)}, bf16[64,128]{1,0:T(8,128)(2,1)S(1)}, u32[]{:S(2)}, u32[]{:S(2)}) collective-permute-start(bf16[64,128]{1,0:T(8,128)(2,1)S(1)} %pack.1.piece_0), channel_id=1, source_target_pairs={{0,8},{4,12},{8,0},{12,4},{1,9},{5,13},{9,1},{13,5},{2,10},{6,14},... | collective-permute-start | bytes 49160 | tf_op jit(solution)/shard_map/ppermute | solution.py:20
  5.0 1.3 %collective-permute-start.2 = (bf16[64,128]{1,0:T(8,128)(2,1)S(1)}, bf16[64,128]{1,0:T(8,128)(2,1)S(1)}, u32[]{:S(2)}, u32[]{:S(2)}) collective-permute-start(bf16[64,128]{1,0:T(8,128)(2,1)S(1)} %pack.1.piece_0), channel_id=1, source_target_pairs={{0,12},{4,8},{8,4},{12,0},{1,13},{5,9},{9,5},{13,1},{2,14},{6,10},... | collective-permute-start | bytes 49160 | tf_op jit(solution)/shard_map/ppermute | solution.py:20
  6.3 0.2 collective-permute-start.3
  6.6 0.0 copy-done.1
  6.6 0.0 copy-done.3
  6.6 0.0 copy-done
  6.6 0.7 %near_load.1 = (bf16[128,256]{1,0:T(8,128)(2,1)S(1)}, bf16[64,2304]{1,0:T(8,128)(2,1)S(1)}) custom-call(s32[1,4,8]{2,1,0:T(4,128)S(1)} %bitcast.1, bf16[8,128,512]{2,1,0:T(8,128)(2,1)S(1)} %copy-done, f32[128,128]{1,0:T(8,128)S(1)} %copy-done.1), custom_call_target="tpu_custom_call" | custom-call | flops 10000000000 | bytes 1048576 | tf_op jit(solution)/shard_map/near_load/pallas_call | solution.py:354
  7.2 1.9 %collective-permute-start = (bf16[64,2304]{1,0:T(8,128)(2,1)S(1)}, bf16[64,2304]{1,0:T(8,128)(2,1)S(1)}, u32[]{:S(2)}, u32[]{:S(2)}) collective-permute-start(bf16[64,2304]{1,0:T(8,128)(2,1)S(1)} %get-tuple-element.21.near_load), channel_id=1, source_target_pairs={{0,4},{1,5},{4,0},{5,1},{8,12},{9,13},{12,8},{13,9},{2,3},{3,2},{6... | collective-permute-start | bytes 884744 | tf_op jit(solution)/shard_map/ppermute | solution.py:375
  9.1 0.8 %masked.1 = (bf16[8,128,512]{2,1,0:T(8,128)(2,1)S(1)}, bf16[64,1792]{1,0:T(8,128)(2,1)S(1)}) custom-call(s32[1,4,8]{2,1,0:T(4,128)S(1)} %bitcast.2, bf16[8,128,512]{2,1,0:T(8,128)(2,1)S(1)} %copy-done, bf16[64,2304]{1,0:T(8,128)(2,1)S(1)} %get-tuple-element.21.near_load), custom_call_target="tpu_custom_call" | custom-call | flops 10000000000 | bytes 1048576 | tf_op jit(solution)/shard_map/masked/pallas_call | solution.py:354
  9.9 0.0 collective-permute-done.1.piece_2
  9.9 0.7 %collective-permute-done.2.piece_3 = bf16[64,128]{1,0:T(8,128)(2,1)S(1)} collective-permute-done((bf16[64,128]{1,0:T(8,128)(2,1)S(1)}, bf16[64,128]{1,0:T(8,128)(2,1)S(1)}, u32[]{:S(2)}, u32[]{:S(2)}) %collective-permute-start.2) | collective-permute-done | bytes 16416 | tf_op jit(solution)/shard_map/ppermute | solution.py:20
  10.6 0.0 collective-permute-done.3.piece_1
  10.7 1.4 %collective-permute-start.4 = (bf16[16,512]{1,0:T(8,128)(2,1)S(1)}, bf16[16,512]{1,0:T(8,128)(2,1)S(1)}, u32[]{:S(2)}, u32[]{:S(2)}) collective-permute-start(bf16[16,512]{1,0:T(8,128)(2,1)S(1)} %get-tuple-element.23), channel_id=1, source_target_pairs={{0,2},{2,0},{1,3},{3,1},{4,6},{6,4},{5,7},{7,5},{8,10},{10,8},{9,1... | collective-permute-start | bytes 49160 | tf_op jit(solution)/shard_map/ppermute | solution.py:393
  12.1 0.5 %main_part.1 = (f32[24,128]{1,0:T(8,128)S(1)}, f32[8,128]{1,0:T(8,128)S(1)}) custom-call(bf16[64,512]{1,0:T(8,128)(2,1)S(1)} %get-tuple-element.24.everyone, bf16[8,128,512]{2,1,0:T(8,128)(2,1)S(1)} %get-tuple-element.22.masked), custom_call_target="tpu_custom_call" | custom-call | flops 10000000000 | bytes 1048576 | tf_op jit(solution)/shard_map/main_part/pallas_call | solution.py:354
  12.6 0.0 collective-permute-start.8
  12.6 1.8 %collective-permute-done.4.late = bf16[16,512]{1,0:T(8,128)(2,1)S(1)} collective-permute-done((bf16[16,512]{1,0:T(8,128)(2,1)S(1)}, bf16[16,512]{1,0:T(8,128)(2,1)S(1)}, u32[]{:S(2)}, u32[]{:S(2)}) %collective-permute-start.4) | collective-permute-done | bytes 16416 | tf_op jit(solution)/shard_map/ppermute | solution.py:393
  14.5 0.3 late_part.1.part
  14.7 1.4 %collective-permute-start.6 = (f32[24,128]{1,0:T(8,128)S(1)}, f32[24,128]{1,0:T(8,128)S(1)}, u32[]{:S(2)}, u32[]{:S(2)}) collective-permute-start(f32[24,128]{1,0:T(8,128)S(1)} %late_part.1.part), channel_id=1, source_target_pairs={{0,2},{2,0},{1,3},{3,1},{4,6},{6,4},{5,7},{7,5},{8,10},{10,8},{9,1... | collective-permute-start | bytes 36872 | tf_op jit(solution)/shard_map/ppermute | solution.py:393
  16.1 0.0 copy-done.2
  16.1 0.0 collective-permute-done.near.load_1
  16.2 0.1 collective-permute-start.5
  16.3 2.2 %collective-permute-done.6.other = f32[24,128]{1,0:T(8,128)S(1)} collective-permute-done((f32[24,128]{1,0:T(8,128)S(1)}, f32[24,128]{1,0:T(8,128)S(1)}, u32[]{:S(2)}, u32[]{:S(2)}) %collective-permute-start.6) | collective-permute-done | bytes 12320 | tf_op jit(solution)/shard_map/ppermute | solution.py:393
  18.4 0.0 collective-permute-start.7
  18.5 1.7 %collective-permute-start.12 = (f32[5,8,128]{2,1,0:T(8,128)S(1)}, f32[5,8,128]{2,1,0:T(8,128)S(1)}, u32[]{:S(2)}, u32[]{:S(2)}) collective-permute-start(f32[5,8,128]{2,1,0:T(8,128)S(1)} %base.1.after.base_0), channel_id=1, source_target_pairs={{0,4},{1,5},{4,0},{5,1},{8,12},{9,13},{12,8},{13,9},{2,3},{3,2},{6... | collective-permute-start | bytes 61448 | tf_op jit(solution)/shard_map/ppermute | solution.py:375
  20.2 0.9 %collective-permute-start.13 = (f32[5,8,128]{2,1,0:T(8,128)S(1)}, f32[5,8,128]{2,1,0:T(8,128)S(1)}, u32[]{:S(2)}, u32[]{:S(2)}) collective-permute-start(f32[5,8,128]{2,1,0:T(8,128)S(1)} %base.1.after.base_0), channel_id=1, source_target_pairs={{0,8},{1,9},{8,0},{9,1},{4,12},{5,13},{12,4},{13,5},{2,3},{3,2},{6... | collective-permute-start | bytes 61448 | tf_op jit(solution)/shard_map/ppermute | solution.py:375
  21.1 0.0 collective-permute-done.8.load_3
  21.1 0.0 collective-permute-start.9
  21.1 0.0 collective-permute-done.7.base_3
  21.1 0.5 %collective-permute-start.11 = (bf16[64,1792]{1,0:T(8,128)(2,1)S(1)}, bf16[64,1792]{1,0:T(8,128)(2,1)S(1)}, u32[]{:S(2)}, u32[]{:S(2)}) collective-permute-start(bf16[64,1792]{1,0:T(8,128)(2,1)S(1)} %collective-permute-done.8.load_3), channel_id=1, source_target_pairs={{0,1},{1,0},{2,3},{3,2},{4,5},{5,4},{6,7},{7,6},{8,9},{9,8},{10,11... | collective-permute-start | bytes 688136 | tf_op jit(solution)/shard_map/ppermute | solution.py:393
  21.6 0.0 collective-permute-done.5.load_2
  21.6 0.1 collective-permute-start.10
  21.7 0.1 spread.1
  21.8 0.5 %collective-permute-done.12.base_1 = f32[5,8,128]{2,1,0:T(8,128)S(1)} collective-permute-done((f32[5,8,128]{2,1,0:T(8,128)S(1)}, f32[5,8,128]{2,1,0:T(8,128)S(1)}, u32[]{:S(2)}, u32[]{:S(2)}) %collective-permute-start.12) | collective-permute-done | bytes 20512 | tf_op jit(solution)/shard_map/ppermute | solution.py:375
  22.3 3.2 %collective-permute-done.13.base_2 = f32[5,8,128]{2,1,0:T(8,128)S(1)} collective-permute-done((f32[5,8,128]{2,1,0:T(8,128)S(1)}, f32[5,8,128]{2,1,0:T(8,128)S(1)}, u32[]{:S(2)}, u32[]{:S(2)}) %collective-permute-start.13) | collective-permute-done | bytes 20512 | tf_op jit(solution)/shard_map/ppermute | solution.py:375
  25.5 0.0 collective-permute-done.11.swap_3
  25.5 0.0 collective-permute-done.9.swap_1
  25.5 0.0 collective-permute-done.10.swap_2
  25.5 2.6 %march.1 = (f32[5,8,128]{2,1,0:T(8,128)S(1)}, f32[5,8,128]{2,1,0:T(8,128)S(1)}) custom-call(bf16[8,128,512]{2,1,0:T(8,128)(2,1)S(1)} %get-tuple-element.22.masked, bf16[64,2304]{1,0:T(8,128)(2,1)S(1)} %collective-permute-done.near.load_1, bf16[64,1792]{1,0:T(8,128)(2,1)S(1)} %collective-permute-done.5.load_2, ...), custom_call_target="tpu_custom_call" | custom-call | flops 10000000000 | bytes 1048576 | tf_op jit(solution)/shard_map/march/pallas_call | solution.py:354
  28.1 0.0 collective-permute-start.14
  28.1 2.2 %collective-permute-start.15 = (f32[5,8,128]{2,1,0:T(8,128)S(1)}, f32[5,8,128]{2,1,0:T(8,128)S(1)}, u32[]{:S(2)}, u32[]{:S(2)}) collective-permute-start(f32[5,8,128]{2,1,0:T(8,128)S(1)} %get-tuple-element.34), channel_id=1, source_target_pairs={{4,0},{5,1},{0,4},{1,5},{8,12},{9,13},{12,8},{13,9},{2,3},{3,2},{6... | collective-permute-start | bytes 61448 | tf_op jit(solution)/shard_map/ppermute | solution.py:375
  30.3 0.0 collective-permute-start.16
  30.3 0.0 collective-permute-done.14
  30.3 1.8 %collective-permute-done.15 = f32[5,8,128]{2,1,0:T(8,128)S(1)} collective-permute-done((f32[5,8,128]{2,1,0:T(8,128)S(1)}, f32[5,8,128]{2,1,0:T(8,128)S(1)}, u32[]{:S(2)}, u32[]{:S(2)}) %collective-permute-start.15) | collective-permute-done | bytes 20512 | tf_op jit(solution)/shard_map/ppermute | solution.py:375
  32.0 0.0 collective-permute-done.16
  32.0 0.6 %fusion = f32[5,4,128]{2,1,0:T(4,128)} fusion(f32[5,8,128]{2,1,0:T(8,128)S(1)} %collective-permute-done.16, f32[5,8,128]{2,1,0:T(8,128)S(1)} %collective-permute-done.15, f32[5,8,128]{2,1,0:T(8,128)S(1)} %collective-permute-done.14, f32[5,8,128]{2,1,0:T(8,128)S(1)} %get-tuple-element.33, pred[]{:T(512)S(6)} %or.3, pred[]{:T(512)S(6)} %eq.11), kind=kLoop, calls=%fused_computation.1 | loop fusion | flops 7680 | bytes 51202 | tf_op jit(solution)/shard_map/jit(_where)/select_n | solution.py:512
  (6 shorter events, 0.1 us)
Async XLA Ops:
  0.0 6.6 %copy-start.1 = (f32[128,128]{1,0:T(8,128)S(1)}, f32[128,128]{1,0:T(8,128)}, u32[]{:S(2)}) copy-start(f32[128,128]{1,0:T(8,128)} %correction_in) | copy-start | bytes 196612
  0.0 6.6 %copy-start.3 = (s32[8,1,4]{0,2,1:T(4,128)S(1)}, s32[8,1,4]{0,2,1:T(4,128)}, u32[]{:S(2)}) copy-start(s32[8,1,4]{0,2,1:T(4,128)} %param.10) | copy-start | bytes 388
  0.0 6.6 %copy-start = (bf16[8,128,512]{2,1,0:T(8,128)(2,1)S(1)}, bf16[8,128,512]{2,1,0:T(8,128)(2,1)}, u32[]{:S(2)}) copy-start(bf16[8,128,512]{2,1,0:T(8,128)(2,1)} %interaction.1) | copy-start | bytes 3145732
  0.9 9.1 %collective-permute-start.1 = (bf16[64,128]{1,0:T(8,128)(2,1)S(1)}, bf16[64,128]{1,0:T(8,128)(2,1)S(1)}, u32[]{:S(2)}, u32[]{:S(2)}) collective-permute-start(bf16[64,128]{1,0:T(8,128)(2,1)S(1)} %pack.1.piece_0), channel_id=1, source_target_pairs={{0,8},{4,12},{8,0},{12,4},{1,9},{5,13},{9,1},{13,5},{2,10},{6,14},... | collective-permute-start | bytes 49160 | tf_op jit(solution)/shard_map/ppermute | solution.py:20
  5.0 5.6 %collective-permute-start.2 = (bf16[64,128]{1,0:T(8,128)(2,1)S(1)}, bf16[64,128]{1,0:T(8,128)(2,1)S(1)}, u32[]{:S(2)}, u32[]{:S(2)}) collective-permute-start(bf16[64,128]{1,0:T(8,128)(2,1)S(1)} %pack.1.piece_0), channel_id=1, source_target_pairs={{0,12},{4,8},{8,4},{12,0},{1,13},{5,9},{9,5},{13,1},{2,14},{6,10},... | collective-permute-start | bytes 49160 | tf_op jit(solution)/shard_map/ppermute | solution.py:20
  6.3 4.3 %collective-permute-start.3 = (bf16[64,128]{1,0:T(8,128)(2,1)S(1)}, bf16[64,128]{1,0:T(8,128)(2,1)S(1)}, u32[]{:S(2)}, u32[]{:S(2)}) collective-permute-start(bf16[64,128]{1,0:T(8,128)(2,1)S(1)} %pack.1.piece_0), channel_id=1, source_target_pairs={{0,4},{4,0},{8,12},{12,8},{1,5},{5,1},{9,13},{13,9},{2,6},{6,2},{1... | collective-permute-start | bytes 49160 | tf_op jit(solution)/shard_map/ppermute | solution.py:20
  7.2 8.9 %collective-permute-start = (bf16[64,2304]{1,0:T(8,128)(2,1)S(1)}, bf16[64,2304]{1,0:T(8,128)(2,1)S(1)}, u32[]{:S(2)}, u32[]{:S(2)}) collective-permute-start(bf16[64,2304]{1,0:T(8,128)(2,1)S(1)} %get-tuple-element.21.near_load), channel_id=1, source_target_pairs={{0,4},{1,5},{4,0},{5,1},{8,12},{9,13},{12,8},{13,9},{2,3},{3,2},{6... | collective-permute-start | bytes 884744 | tf_op jit(solution)/shard_map/ppermute | solution.py:375
  10.7 3.8 %collective-permute-start.4 = (bf16[16,512]{1,0:T(8,128)(2,1)S(1)}, bf16[16,512]{1,0:T(8,128)(2,1)S(1)}, u32[]{:S(2)}, u32[]{:S(2)}) collective-permute-start(bf16[16,512]{1,0:T(8,128)(2,1)S(1)} %get-tuple-element.23), channel_id=1, source_target_pairs={{0,2},{2,0},{1,3},{3,1},{4,6},{6,4},{5,7},{7,5},{8,10},{10,8},{9,1... | collective-permute-start | bytes 49160 | tf_op jit(solution)/shard_map/ppermute | solution.py:393
  12.6 8.5 %collective-permute-start.8 = (bf16[64,1792]{1,0:T(8,128)(2,1)S(1)}, bf16[64,1792]{1,0:T(8,128)(2,1)S(1)}, u32[]{:S(2)}, u32[]{:S(2)}) collective-permute-start(bf16[64,1792]{1,0:T(8,128)(2,1)S(1)} %get-tuple-element.29), channel_id=1, source_target_pairs={{4,8},{5,9},{8,4},{9,5},{0,1},{1,0},{2,3},{3,2},{6,7},{7,6},{10,11... | collective-permute-start | bytes 688136 | tf_op jit(solution)/shard_map/ppermute | solution.py:375
  14.5 1.7 %copy-start.2 = (f32[5,4,128]{2,1,0:T(4,128)S(1)}, f32[5,4,128]{2,1,0:T(4,128)}, u32[]{:S(2)}) copy-start(f32[5,4,128]{2,1,0:T(4,128)} %forcing.1) | copy-start | bytes 30724
  14.7 3.7 %collective-permute-start.6 = (f32[24,128]{1,0:T(8,128)S(1)}, f32[24,128]{1,0:T(8,128)S(1)}, u32[]{:S(2)}, u32[]{:S(2)}) collective-permute-start(f32[24,128]{1,0:T(8,128)S(1)} %late_part.1.part), channel_id=1, source_target_pairs={{0,2},{2,0},{1,3},{3,1},{4,6},{6,4},{5,7},{7,5},{8,10},{10,8},{9,1... | collective-permute-start | bytes 36872 | tf_op jit(solution)/shard_map/ppermute | solution.py:393
  16.2 5.4 %collective-permute-start.5 = (bf16[64,1792]{1,0:T(8,128)(2,1)S(1)}, bf16[64,1792]{1,0:T(8,128)(2,1)S(1)}, u32[]{:S(2)}, u32[]{:S(2)}) collective-permute-start(bf16[64,1792]{1,0:T(8,128)(2,1)S(1)} %relay.1.after), channel_id=1, source_target_pairs={{4,8},{5,9},{8,4},{9,5},{0,1},{1,0},{2,3},{3,2},{6,7},{7,6},{10,11... | collective-permute-start | bytes 688136 | tf_op jit(solution)/shard_map/ppermute | solution.py:375
  18.4 2.7 %collective-permute-start.7 = (f32[5,8,128]{2,1,0:T(8,128)S(1)}, f32[5,8,128]{2,1,0:T(8,128)S(1)}, u32[]{:S(2)}, u32[]{:S(2)}) collective-permute-start(f32[5,8,128]{2,1,0:T(8,128)S(1)} %base.1.after.base_0), channel_id=1, source_target_pairs={{4,8},{5,9},{8,4},{9,5},{0,1},{1,0},{2,3},{3,2},{6,7},{7,6},{10,11... | collective-permute-start | bytes 61448 | tf_op jit(solution)/shard_map/ppermute | solution.py:375
  18.5 3.8 %collective-permute-start.12 = (f32[5,8,128]{2,1,0:T(8,128)S(1)}, f32[5,8,128]{2,1,0:T(8,128)S(1)}, u32[]{:S(2)}, u32[]{:S(2)}) collective-permute-start(f32[5,8,128]{2,1,0:T(8,128)S(1)} %base.1.after.base_0), channel_id=1, source_target_pairs={{0,4},{1,5},{4,0},{5,1},{8,12},{9,13},{12,8},{13,9},{2,3},{3,2},{6... | collective-permute-start | bytes 61448 | tf_op jit(solution)/shard_map/ppermute | solution.py:375
  20.2 5.3 %collective-permute-start.13 = (f32[5,8,128]{2,1,0:T(8,128)S(1)}, f32[5,8,128]{2,1,0:T(8,128)S(1)}, u32[]{:S(2)}, u32[]{:S(2)}) collective-permute-start(f32[5,8,128]{2,1,0:T(8,128)S(1)} %base.1.after.base_0), channel_id=1, source_target_pairs={{0,8},{1,9},{8,0},{9,1},{4,12},{5,13},{12,4},{13,5},{2,3},{3,2},{6... | collective-permute-start | bytes 61448 | tf_op jit(solution)/shard_map/ppermute | solution.py:375
  21.1 4.4 %collective-permute-start.9 = (bf16[64,2304]{1,0:T(8,128)(2,1)S(1)}, bf16[64,2304]{1,0:T(8,128)(2,1)S(1)}, u32[]{:S(2)}, u32[]{:S(2)}) collective-permute-start(bf16[64,2304]{1,0:T(8,128)(2,1)S(1)} %collective-permute-done.near.load_1), channel_id=1, source_target_pairs={{0,1},{1,0},{2,3},{3,2},{4,5},{5,4},{6,7},{7,6},{8,9},{9,8},{10,11... | collective-permute-start | bytes 884744 | tf_op jit(solution)/shard_map/ppermute | solution.py:393
  21.1 4.4 %collective-permute-start.11 = (bf16[64,1792]{1,0:T(8,128)(2,1)S(1)}, bf16[64,1792]{1,0:T(8,128)(2,1)S(1)}, u32[]{:S(2)}, u32[]{:S(2)}) collective-permute-start(bf16[64,1792]{1,0:T(8,128)(2,1)S(1)} %collective-permute-done.8.load_3), channel_id=1, source_target_pairs={{0,1},{1,0},{2,3},{3,2},{4,5},{5,4},{6,7},{7,6},{8,9},{9,8},{10,11... | collective-permute-start | bytes 688136 | tf_op jit(solution)/shard_map/ppermute | solution.py:393
  21.6 3.9 %collective-permute-start.10 = (bf16[64,1792]{1,0:T(8,128)(2,1)S(1)}, bf16[64,1792]{1,0:T(8,128)(2,1)S(1)}, u32[]{:S(2)}, u32[]{:S(2)}) collective-permute-start(bf16[64,1792]{1,0:T(8,128)(2,1)S(1)} %collective-permute-done.5.load_2), channel_id=1, source_target_pairs={{0,1},{1,0},{2,3},{3,2},{4,5},{5,4},{6,7},{7,6},{8,9},{9,8},{10,11... | collective-permute-start | bytes 688136 | tf_op jit(solution)/shard_map/ppermute | solution.py:393
  28.1 2.2 %collective-permute-start.14 = (f32[5,8,128]{2,1,0:T(8,128)S(1)}, f32[5,8,128]{2,1,0:T(8,128)S(1)}, u32[]{:S(2)}, u32[]{:S(2)}) collective-permute-start(f32[5,8,128]{2,1,0:T(8,128)S(1)} %get-tuple-element.33), channel_id=1, source_target_pairs={{4,6},{5,7},{6,4},{7,5},{8,10},{9,11},{10,8},{11,9},{0,1},{1,0},{2... | collective-permute-start | bytes 61448 | tf_op jit(solution)/shard_map/ppermute | solution.py:375
  28.1 3.9 %collective-permute-start.15 = (f32[5,8,128]{2,1,0:T(8,128)S(1)}, f32[5,8,128]{2,1,0:T(8,128)S(1)}, u32[]{:S(2)}, u32[]{:S(2)}) collective-permute-start(f32[5,8,128]{2,1,0:T(8,128)S(1)} %get-tuple-element.34), channel_id=1, source_target_pairs={{4,0},{5,1},{0,4},{1,5},{8,12},{9,13},{12,8},{13,9},{2,3},{3,2},{6... | collective-permute-start | bytes 61448 | tf_op jit(solution)/shard_map/ppermute | solution.py:375
  30.3 1.8 %collective-permute-start.16 = (f32[5,8,128]{2,1,0:T(8,128)S(1)}, f32[5,8,128]{2,1,0:T(8,128)S(1)}, u32[]{:S(2)}, u32[]{:S(2)}) collective-permute-start(f32[5,8,128]{2,1,0:T(8,128)S(1)} %get-tuple-element.34), channel_id=1, source_target_pairs={{4,2},{5,3},{2,6},{3,7},{6,4},{7,5},{8,14},{9,15},{14,10},{15,11},... | collective-permute-start | bytes 61448 | tf_op jit(solution)/shard_map/ppermute | solution.py:375

commit v8 on v7

--- a/solution.py
+++ b/solution.py
@@ -445,7 +445,7 @@
         name="main_part",
     )
 
-    mid_load, _ = lax.optimization_barrier((mid_load, slope))
+    mid_load, _ = lax.optimization_barrier((mid_load, own_c))
 
     def bulk(value, pairs):
         return exchanged(value, [(2 * a, 2 * b) for a, b in pairs], 2 * count)

time: 32.8 us -> 32.1 us (0.979)
  starting transfers between devices: 15.9 us -> 15.2 us
    ppermute x9, starting transfers between devices: 6.8 us -> 6.08 us  [exchanged(): return lax.ppermute(value, ('elem', 'lag', 'gust'), moves)]
where the time goes in v8:
time: 32.1 us; the launch traced here: 31.9 us
  starting transfers between devices  15.2 us (47%)
  waiting for transfers between devices  10.2 us (32%)
  Pallas kernels  5.85 us (18%)
  other arithmetic  0.61 us (2%)
    ppermute x9, starting transfers between devices, exchanged(): return lax.ppermute(value, ('elem', 'lag', 'gust'), moves)  6.08 us
    pallas_call x11, Pallas kernels, on_core(): pl.pallas_call(body, out_shape=[pltpu.VMEM(shape, dtype) if force else ja...  5.85 us
    ppermute x3, starting transfers between devices, flips(): lax.ppermute(value, 'elem', [(i, i ^ flip) for i in range(count)])  5.68 us
    ppermute x9, waiting for transfers between devices, exchanged(): return lax.ppermute(value, ('elem', 'lag', 'gust'), moves)  5.48 us
    ppermute x5, waiting for transfers between devices, crossed(): return lax.ppermute(value, axis, [(0, 1), (1, 0)])  4.09 us
    ppermute x5, starting transfers between devices, crossed(): return lax.ppermute(value, axis, [(0, 1), (1, 0)])  3.43 us
  transfers between devices with their start and end apart: 17, of which 6 were waited for; matrix products, arithmetic and copies ran while one was open for 0% of the time, Pallas kernels for 7%

profile of v8, /device:TPU:0, one launch (start us, length us, event | category | flops | bytes accessed | tf_op | source)
XLA Modules:
  0.0 31.9 jit_solution(11005401380084566299)
XLA Ops:
  0.0 0.0 copy-start.1
  0.0 0.0 copy-start.3
  0.0 0.9 %pack.1.piece_0 = bf16[64,128]{1,0:T(8,128)(2,1)S(1)} custom-call(f32[8,4,128]{2,1,0:T(4,128)} %history_in.1, s32[4,128]{1,0:T(4,128)} %neighbours_in.1, f32[4,128]{1,0:T(4,128)} %edge_coef_in.1), custom_call_target="tpu_custom_call" | custom-call | flops 10000000000 | bytes 1048576 | tf_op jit(solution)/shard_map/pack/pallas_call | solution.py:354
  0.9 4.1 %collective-permute-start.1 = (bf16[64,128]{1,0:T(8,128)(2,1)S(1)}, bf16[64,128]{1,0:T(8,128)(2,1)S(1)}, u32[]{:S(2)}, u32[]{:S(2)}) collective-permute-start(bf16[64,128]{1,0:T(8,128)(2,1)S(1)} %pack.1.piece_0), channel_id=1, source_target_pairs={{0,8},{4,12},{8,0},{12,4},{1,9},{5,13},{9,1},{13,5},{2,10},{6,14},... | collective-permute-start | bytes 49160 | tf_op jit(solution)/shard_map/ppermute | solution.py:20
  5.0 1.3 %collective-permute-start.2 = (bf16[64,128]{1,0:T(8,128)(2,1)S(1)}, bf16[64,128]{1,0:T(8,128)(2,1)S(1)}, u32[]{:S(2)}, u32[]{:S(2)}) collective-permute-start(bf16[64,128]{1,0:T(8,128)(2,1)S(1)} %pack.1.piece_0), channel_id=1, source_target_pairs={{0,12},{4,8},{8,4},{12,0},{1,13},{5,9},{9,5},{13,1},{2,14},{6,10},... | collective-permute-start | bytes 49160 | tf_op jit(solution)/shard_map/ppermute | solution.py:20
  6.3 0.2 collective-permute-start.3
  6.6 0.0 copy-done.1
  6.6 0.0 copy-done.3
  6.6 0.0 copy-done
  6.6 0.7 %near_load.1 = (bf16[128,256]{1,0:T(8,128)(2,1)S(1)}, bf16[64,2304]{1,0:T(8,128)(2,1)S(1)}) custom-call(s32[1,4,8]{2,1,0:T(4,128)S(1)} %bitcast.1, bf16[8,128,512]{2,1,0:T(8,128)(2,1)S(1)} %copy-done, f32[128,128]{1,0:T(8,128)S(1)} %copy-done.1), custom_call_target="tpu_custom_call" | custom-call | flops 10000000000 | bytes 1048576 | tf_op jit(solution)/shard_map/near_load/pallas_call | solution.py:354
  7.2 1.9 %collective-permute-start = (bf16[64,2304]{1,0:T(8,128)(2,1)S(1)}, bf16[64,2304]{1,0:T(8,128)(2,1)S(1)}, u32[]{:S(2)}, u32[]{:S(2)}) collective-permute-start(bf16[64,2304]{1,0:T(8,128)(2,1)S(1)} %get-tuple-element.21.near_load), channel_id=1, source_target_pairs={{0,4},{1,5},{4,0},{5,1},{8,12},{9,13},{12,8},{13,9},{2,3},{3,2},{6... | collective-permute-start | bytes 884744 | tf_op jit(solution)/shard_map/ppermute | solution.py:375
  9.1 0.8 %masked.1 = (bf16[8,128,512]{2,1,0:T(8,128)(2,1)S(1)}, bf16[64,1792]{1,0:T(8,128)(2,1)S(1)}) custom-call(s32[1,4,8]{2,1,0:T(4,128)S(1)} %bitcast.2, bf16[8,128,512]{2,1,0:T(8,128)(2,1)S(1)} %copy-done, bf16[64,2304]{1,0:T(8,128)(2,1)S(1)} %get-tuple-element.21.near_load), custom_call_target="tpu_custom_call" | custom-call | flops 10000000000 | bytes 1048576 | tf_op jit(solution)/shard_map/masked/pallas_call | solution.py:354
  9.9 0.1 collective-permute-start.8
  10.0 0.0 collective-permute-done.1.piece_2
  10.0 0.6 %collective-permute-done.2.piece_3 = bf16[64,128]{1,0:T(8,128)(2,1)S(1)} collective-permute-done((bf16[64,128]{1,0:T(8,128)(2,1)S(1)}, bf16[64,128]{1,0:T(8,128)(2,1)S(1)}, u32[]{:S(2)}, u32[]{:S(2)}) %collective-permute-start.2) | collective-permute-done | bytes 16416 | tf_op jit(solution)/shard_map/ppermute | solution.py:20
  10.6 0.0 collective-permute-done.3.piece_1
  10.7 1.4 %collective-permute-start.4 = (bf16[16,512]{1,0:T(8,128)(2,1)S(1)}, bf16[16,512]{1,0:T(8,128)(2,1)S(1)}, u32[]{:S(2)}, u32[]{:S(2)}) collective-permute-start(bf16[16,512]{1,0:T(8,128)(2,1)S(1)} %get-tuple-element.23), channel_id=1, source_target_pairs={{0,2},{2,0},{1,3},{3,1},{4,6},{6,4},{5,7},{7,5},{8,10},{10,8},{9,1... | collective-permute-start | bytes 49160 | tf_op jit(solution)/shard_map/ppermute | solution.py:393
  12.1 0.5 %main_part.1 = (f32[24,128]{1,0:T(8,128)S(1)}, f32[8,128]{1,0:T(8,128)S(1)}) custom-call(bf16[64,512]{1,0:T(8,128)(2,1)S(1)} %get-tuple-element.24.everyone, bf16[8,128,512]{2,1,0:T(8,128)(2,1)S(1)} %get-tuple-element.22.masked), custom_call_target="tpu_custom_call" | custom-call | flops 10000000000 | bytes 1048576 | tf_op jit(solution)/shard_map/main_part/pallas_call | solution.py:354
  12.6 1.9 %collective-permute-done.4.late = bf16[16,512]{1,0:T(8,128)(2,1)S(1)} collective-permute-done((bf16[16,512]{1,0:T(8,128)(2,1)S(1)}, bf16[16,512]{1,0:T(8,128)(2,1)S(1)}, u32[]{:S(2)}, u32[]{:S(2)}) %collective-permute-start.4) | collective-permute-done | bytes 16416 | tf_op jit(solution)/shard_map/ppermute | solution.py:393
  14.5 0.3 late_part.1.part
  14.7 1.4 %collective-permute-start.6 = (f32[24,128]{1,0:T(8,128)S(1)}, f32[24,128]{1,0:T(8,128)S(1)}, u32[]{:S(2)}, u32[]{:S(2)}) collective-permute-start(f32[24,128]{1,0:T(8,128)S(1)} %late_part.1.part), channel_id=1, source_target_pairs={{0,2},{2,0},{1,3},{3,1},{4,6},{6,4},{5,7},{7,5},{8,10},{10,8},{9,1... | collective-permute-start | bytes 36872 | tf_op jit(solution)/shard_map/ppermute | solution.py:393
  16.1 0.0 copy-done.2
  16.1 0.0 collective-permute-done.near.load_1
  16.2 0.1 collective-permute-start.5
  16.3 2.2 %collective-permute-done.6.other = f32[24,128]{1,0:T(8,128)S(1)} collective-permute-done((f32[24,128]{1,0:T(8,128)S(1)}, f32[24,128]{1,0:T(8,128)S(1)}, u32[]{:S(2)}, u32[]{:S(2)}) %collective-permute-start.6) | collective-permute-done | bytes 12320 | tf_op jit(solution)/shard_map/ppermute | solution.py:393
  18.4 0.0 collective-permute-start.7
  18.5 1.7 %collective-permute-start.12 = (f32[5,8,128]{2,1,0:T(8,128)S(1)}, f32[5,8,128]{2,1,0:T(8,128)S(1)}, u32[]{:S(2)}, u32[]{:S(2)}) collective-permute-start(f32[5,8,128]{2,1,0:T(8,128)S(1)} %base.1.after.base_0), channel_id=1, source_target_pairs={{0,4},{1,5},{4,0},{5,1},{8,12},{9,13},{12,8},{13,9},{2,3},{3,2},{6... | collective-permute-start | bytes 61448 | tf_op jit(solution)/shard_map/ppermute | solution.py:375
  20.2 1.4 %collective-permute-start.13 = (f32[5,8,128]{2,1,0:T(8,128)S(1)}, f32[5,8,128]{2,1,0:T(8,128)S(1)}, u32[]{:S(2)}, u32[]{:S(2)}) collective-permute-start(f32[5,8,128]{2,1,0:T(8,128)S(1)} %base.1.after.base_0), channel_id=1, source_target_pairs={{0,8},{1,9},{8,0},{9,1},{4,12},{5,13},{12,4},{13,5},{2,3},{3,2},{6... | collective-permute-start | bytes 61448 | tf_op jit(solution)/shard_map/ppermute | solution.py:375
  21.6 0.0 collective-permute-done.8.load_3
  21.6 0.0 collective-permute-start.9
  21.6 0.0 collective-permute-done.7.base_3
  21.6 0.5 %collective-permute-start.11 = (bf16[64,1792]{1,0:T(8,128)(2,1)S(1)}, bf16[64,1792]{1,0:T(8,128)(2,1)S(1)}, u32[]{:S(2)}, u32[]{:S(2)}) collective-permute-start(bf16[64,1792]{1,0:T(8,128)(2,1)S(1)} %collective-permute-done.8.load_3), channel_id=1, source_target_pairs={{0,1},{1,0},{2,3},{3,2},{4,5},{5,4},{6,7},{7,6},{8,9},{9,8},{10,11... | collective-permute-start | bytes 688136 | tf_op jit(solution)/shard_map/ppermute | solution.py:393
  22.1 0.0 collective-permute-done.5.load_2
  22.1 0.1 collective-permute-start.10
  22.2 0.1 spread.1
  22.3 0.0 collective-permute-done.12.base_1
  22.3 2.6 %collective-permute-done.13.base_2 = f32[5,8,128]{2,1,0:T(8,128)S(1)} collective-permute-done((f32[5,8,128]{2,1,0:T(8,128)S(1)}, f32[5,8,128]{2,1,0:T(8,128)S(1)}, u32[]{:S(2)}, u32[]{:S(2)}) %collective-permute-start.13) | collective-permute-done | bytes 20512 | tf_op jit(solution)/shard_map/ppermute | solution.py:375
  24.9 0.0 collective-permute-done.11.swap_3
  24.9 0.0 collective-permute-done.9.swap_1
  24.9 0.0 collective-permute-done.10.swap_2
  24.9 2.6 %march.1 = (f32[5,8,128]{2,1,0:T(8,128)S(1)}, f32[5,8,128]{2,1,0:T(8,128)S(1)}) custom-call(bf16[8,128,512]{2,1,0:T(8,128)(2,1)S(1)} %get-tuple-element.22.masked, bf16[64,2304]{1,0:T(8,128)(2,1)S(1)} %collective-permute-done.near.load_1, bf16[64,1792]{1,0:T(8,128)(2,1)S(1)} %collective-permute-done.5.load_2, ...), custom_call_target="tpu_custom_call" | custom-call | flops 10000000000 | bytes 1048576 | tf_op jit(solution)/shard_map/march/pallas_call | solution.py:354
  27.5 0.0 collective-permute-start.14
  27.5 1.0 %collective-permute-start.15 = (f32[5,8,128]{2,1,0:T(8,128)S(1)}, f32[5,8,128]{2,1,0:T(8,128)S(1)}, u32[]{:S(2)}, u32[]{:S(2)}) collective-permute-start(f32[5,8,128]{2,1,0:T(8,128)S(1)} %get-tuple-element.34), channel_id=1, source_target_pairs={{4,0},{5,1},{0,4},{1,5},{8,12},{9,13},{12,8},{13,9},{2,3},{3,2},{6... | collective-permute-start | bytes 61448 | tf_op jit(solution)/shard_map/ppermute | solution.py:375
  28.5 0.0 collective-permute-start.16
  28.5 0.3 collective-permute-done.14
  28.7 2.6 %collective-permute-done.15 = f32[5,8,128]{2,1,0:T(8,128)S(1)} collective-permute-done((f32[5,8,128]{2,1,0:T(8,128)S(1)}, f32[5,8,128]{2,1,0:T(8,128)S(1)}, u32[]{:S(2)}, u32[]{:S(2)}) %collective-permute-start.15) | collective-permute-done | bytes 20512 | tf_op jit(solution)/shard_map/ppermute | solution.py:375
  31.3 0.0 collective-permute-done.16
  31.3 0.6 %fusion = f32[5,4,128]{2,1,0:T(4,128)} fusion(f32[5,8,128]{2,1,0:T(8,128)S(1)} %collective-permute-done.16, f32[5,8,128]{2,1,0:T(8,128)S(1)} %collective-permute-done.15, f32[5,8,128]{2,1,0:T(8,128)S(1)} %collective-permute-done.14, f32[5,8,128]{2,1,0:T(8,128)S(1)} %get-tuple-element.33, pred[]{:T(512)S(6)} %or.3, pred[]{:T(512)S(6)} %eq.11), kind=kLoop, calls=%fused_computation.1 | loop fusion | flops 7680 | bytes 51202 | tf_op jit(solution)/shard_map/jit(_where)/select_n | solution.py:512
  (6 shorter events, 0.1 us)
Async XLA Ops:
  0.0 6.6 %copy-start.1 = (f32[128,128]{1,0:T(8,128)S(1)}, f32[128,128]{1,0:T(8,128)}, u32[]{:S(2)}) copy-start(f32[128,128]{1,0:T(8,128)} %correction_in) | copy-start | bytes 196612
  0.0 6.6 %copy-start.3 = (s32[8,1,4]{0,2,1:T(4,128)S(1)}, s32[8,1,4]{0,2,1:T(4,128)}, u32[]{:S(2)}) copy-start(s32[8,1,4]{0,2,1:T(4,128)} %param.10) | copy-start | bytes 388
  0.0 6.6 %copy-start = (bf16[8,128,512]{2,1,0:T(8,128)(2,1)S(1)}, bf16[8,128,512]{2,1,0:T(8,128)(2,1)}, u32[]{:S(2)}) copy-start(bf16[8,128,512]{2,1,0:T(8,128)(2,1)} %interaction.1) | copy-start | bytes 3145732
  0.9 9.1 %collective-permute-start.1 = (bf16[64,128]{1,0:T(8,128)(2,1)S(1)}, bf16[64,128]{1,0:T(8,128)(2,1)S(1)}, u32[]{:S(2)}, u32[]{:S(2)}) collective-permute-start(bf16[64,128]{1,0:T(8,128)(2,1)S(1)} %pack.1.piece_0), channel_id=1, source_target_pairs={{0,8},{4,12},{8,0},{12,4},{1,9},{5,13},{9,1},{13,5},{2,10},{6,14},... | collective-permute-start | bytes 49160 | tf_op jit(solution)/shard_map/ppermute | solution.py:20
  5.0 5.6 %collective-permute-start.2 = (bf16[64,128]{1,0:T(8,128)(2,1)S(1)}, bf16[64,128]{1,0:T(8,128)(2,1)S(1)}, u32[]{:S(2)}, u32[]{:S(2)}) collective-permute-start(bf16[64,128]{1,0:T(8,128)(2,1)S(1)} %pack.1.piece_0), channel_id=1, source_target_pairs={{0,12},{4,8},{8,4},{12,0},{1,13},{5,9},{9,5},{13,1},{2,14},{6,10},... | collective-permute-start | bytes 49160 | tf_op jit(solution)/shard_map/ppermute | solution.py:20
  6.3 4.3 %collective-permute-start.3 = (bf16[64,128]{1,0:T(8,128)(2,1)S(1)}, bf16[64,128]{1,0:T(8,128)(2,1)S(1)}, u32[]{:S(2)}, u32[]{:S(2)}) collective-permute-start(bf16[64,128]{1,0:T(8,128)(2,1)S(1)} %pack.1.piece_0), channel_id=1, source_target_pairs={{0,4},{4,0},{8,12},{12,8},{1,5},{5,1},{9,13},{13,9},{2,6},{6,2},{1... | collective-permute-start | bytes 49160 | tf_op jit(solution)/shard_map/ppermute | solution.py:20
  7.2 8.9 %collective-permute-start = (bf16[64,2304]{1,0:T(8,128)(2,1)S(1)}, bf16[64,2304]{1,0:T(8,128)(2,1)S(1)}, u32[]{:S(2)}, u32[]{:S(2)}) collective-permute-start(bf16[64,2304]{1,0:T(8,128)(2,1)S(1)} %get-tuple-element.21.near_load), channel_id=1, source_target_pairs={{0,4},{1,5},{4,0},{5,1},{8,12},{9,13},{12,8},{13,9},{2,3},{3,2},{6... | collective-permute-start | bytes 884744 | tf_op jit(solution)/shard_map/ppermute | solution.py:375
  9.9 11.6 %collective-permute-start.8 = (bf16[64,1792]{1,0:T(8,128)(2,1)S(1)}, bf16[64,1792]{1,0:T(8,128)(2,1)S(1)}, u32[]{:S(2)}, u32[]{:S(2)}) collective-permute-start(bf16[64,1792]{1,0:T(8,128)(2,1)S(1)} %get-tuple-element.30), channel_id=1, source_target_pairs={{4,8},{5,9},{8,4},{9,5},{0,1},{1,0},{2,3},{3,2},{6,7},{7,6},{10,11... | collective-permute-start | bytes 688136 | tf_op jit(solution)/shard_map/ppermute | solution.py:375
  10.7 3.8 %collective-permute-start.4 = (bf16[16,512]{1,0:T(8,128)(2,1)S(1)}, bf16[16,512]{1,0:T(8,128)(2,1)S(1)}, u32[]{:S(2)}, u32[]{:S(2)}) collective-permute-start(bf16[16,512]{1,0:T(8,128)(2,1)S(1)} %get-tuple-element.23), channel_id=1, source_target_pairs={{0,2},{2,0},{1,3},{3,1},{4,6},{6,4},{5,7},{7,5},{8,10},{10,8},{9,1... | collective-permute-start | bytes 49160 | tf_op jit(solution)/shard_map/ppermute | solution.py:393
  14.5 1.7 %copy-start.2 = (f32[5,4,128]{2,1,0:T(4,128)S(1)}, f32[5,4,128]{2,1,0:T(4,128)}, u32[]{:S(2)}) copy-start(f32[5,4,128]{2,1,0:T(4,128)} %forcing.1) | copy-start | bytes 30724
  14.7 3.7 %collective-permute-start.6 = (f32[24,128]{1,0:T(8,128)S(1)}, f32[24,128]{1,0:T(8,128)S(1)}, u32[]{:S(2)}, u32[]{:S(2)}) collective-permute-start(f32[24,128]{1,0:T(8,128)S(1)} %late_part.1.part), channel_id=1, source_target_pairs={{0,2},{2,0},{1,3},{3,1},{4,6},{6,4},{5,7},{7,5},{8,10},{10,8},{9,1... | collective-permute-start | bytes 36872 | tf_op jit(solution)/shard_map/ppermute | solution.py:393
  16.2 5.9 %collective-permute-start.5 = (bf16[64,1792]{1,0:T(8,128)(2,1)S(1)}, bf16[64,1792]{1,0:T(8,128)(2,1)S(1)}, u32[]{:S(2)}, u32[]{:S(2)}) collective-permute-start(bf16[64,1792]{1,0:T(8,128)(2,1)S(1)} %relay.1.after), channel_id=1, source_target_pairs={{4,8},{5,9},{8,4},{9,5},{0,1},{1,0},{2,3},{3,2},{6,7},{7,6},{10,11... | collective-permute-start | bytes 688136 | tf_op jit(solution)/shard_map/ppermute | solution.py:375
  18.4 3.1 %collective-permute-start.7 = (f32[5,8,128]{2,1,0:T(8,128)S(1)}, f32[5,8,128]{2,1,0:T(8,128)S(1)}, u32[]{:S(2)}, u32[]{:S(2)}) collective-permute-start(f32[5,8,128]{2,1,0:T(8,128)S(1)} %base.1.after.base_0), channel_id=1, source_target_pairs={{4,8},{5,9},{8,4},{9,5},{0,1},{1,0},{2,3},{3,2},{6,7},{7,6},{10,11... | collective-permute-start | bytes 61448 | tf_op jit(solution)/shard_map/ppermute | solution.py:375
  18.5 3.8 %collective-permute-start.12 = (f32[5,8,128]{2,1,0:T(8,128)S(1)}, f32[5,8,128]{2,1,0:T(8,128)S(1)}, u32[]{:S(2)}, u32[]{:S(2)}) collective-permute-start(f32[5,8,128]{2,1,0:T(8,128)S(1)} %base.1.after.base_0), channel_id=1, source_target_pairs={{0,4},{1,5},{4,0},{5,1},{8,12},{9,13},{12,8},{13,9},{2,3},{3,2},{6... | collective-permute-start | bytes 61448 | tf_op jit(solution)/shard_map/ppermute | solution.py:375
  20.2 4.7 %collective-permute-start.13 = (f32[5,8,128]{2,1,0:T(8,128)S(1)}, f32[5,8,128]{2,1,0:T(8,128)S(1)}, u32[]{:S(2)}, u32[]{:S(2)}) collective-permute-start(f32[5,8,128]{2,1,0:T(8,128)S(1)} %base.1.after.base_0), channel_id=1, source_target_pairs={{0,8},{1,9},{8,0},{9,1},{4,12},{5,13},{12,4},{13,5},{2,3},{3,2},{6... | collective-permute-start | bytes 61448 | tf_op jit(solution)/shard_map/ppermute | solution.py:375
  21.6 3.3 %collective-permute-start.9 = (bf16[64,2304]{1,0:T(8,128)(2,1)S(1)}, bf16[64,2304]{1,0:T(8,128)(2,1)S(1)}, u32[]{:S(2)}, u32[]{:S(2)}) collective-permute-start(bf16[64,2304]{1,0:T(8,128)(2,1)S(1)} %collective-permute-done.near.load_1), channel_id=1, source_target_pairs={{0,1},{1,0},{2,3},{3,2},{4,5},{5,4},{6,7},{7,6},{8,9},{9,8},{10,11... | collective-permute-start | bytes 884744 | tf_op jit(solution)/shard_map/ppermute | solution.py:393
  21.6 3.3 %collective-permute-start.11 = (bf16[64,1792]{1,0:T(8,128)(2,1)S(1)}, bf16[64,1792]{1,0:T(8,128)(2,1)S(1)}, u32[]{:S(2)}, u32[]{:S(2)}) collective-permute-start(bf16[64,1792]{1,0:T(8,128)(2,1)S(1)} %collective-permute-done.8.load_3), channel_id=1, source_target_pairs={{0,1},{1,0},{2,3},{3,2},{4,5},{5,4},{6,7},{7,6},{8,9},{9,8},{10,11... | collective-permute-start | bytes 688136 | tf_op jit(solution)/shard_map/ppermute | solution.py:393
  22.1 2.8 %collective-permute-start.10 = (bf16[64,1792]{1,0:T(8,128)(2,1)S(1)}, bf16[64,1792]{1,0:T(8,128)(2,1)S(1)}, u32[]{:S(2)}, u32[]{:S(2)}) collective-permute-start(bf16[64,1792]{1,0:T(8,128)(2,1)S(1)} %collective-permute-done.5.load_2), channel_id=1, source_target_pairs={{0,1},{1,0},{2,3},{3,2},{4,5},{5,4},{6,7},{7,6},{8,9},{9,8},{10,11... | collective-permute-start | bytes 688136 | tf_op jit(solution)/shard_map/ppermute | solution.py:393
  27.5 1.2 %collective-permute-start.14 = (f32[5,8,128]{2,1,0:T(8,128)S(1)}, f32[5,8,128]{2,1,0:T(8,128)S(1)}, u32[]{:S(2)}, u32[]{:S(2)}) collective-permute-start(f32[5,8,128]{2,1,0:T(8,128)S(1)} %get-tuple-element.33), channel_id=1, source_target_pairs={{4,6},{5,7},{6,4},{7,5},{8,10},{9,11},{10,8},{11,9},{0,1},{1,0},{2... | collective-permute-start | bytes 61448 | tf_op jit(solution)/shard_map/ppermute | solution.py:375
  27.5 3.8 %collective-permute-start.15 = (f32[5,8,128]{2,1,0:T(8,128)S(1)}, f32[5,8,128]{2,1,0:T(8,128)S(1)}, u32[]{:S(2)}, u32[]{:S(2)}) collective-permute-start(f32[5,8,128]{2,1,0:T(8,128)S(1)} %get-tuple-element.34), channel_id=1, source_target_pairs={{4,0},{5,1},{0,4},{1,5},{8,12},{9,13},{12,8},{13,9},{2,3},{3,2},{6... | collective-permute-start | bytes 61448 | tf_op jit(solution)/shard_map/ppermute | solution.py:375
  28.5 2.9 %collective-permute-start.16 = (f32[5,8,128]{2,1,0:T(8,128)S(1)}, f32[5,8,128]{2,1,0:T(8,128)S(1)}, u32[]{:S(2)}, u32[]{:S(2)}) collective-permute-start(f32[5,8,128]{2,1,0:T(8,128)S(1)} %get-tuple-element.34), channel_id=1, source_target_pairs={{4,2},{5,3},{2,6},{3,7},{6,4},{7,5},{8,14},{9,15},{14,10},{15,11},... | collective-permute-start | bytes 61448 | tf_op jit(solution)/shard_map/ppermute | solution.py:375

commit v9 on v8

--- a/solution.py
+++ b/solution.py
@@ -330,23 +330,32 @@
             added = added + (both[:GUST_ROWS] + both[GUST_ROWS:])
         return drive + (added if flip == 0 else rows_right(added))
 
-    waiting = [[base[step] for base in (base_0, base_1, base_2, base_3)] for step in range(STEPS)]
-    waiting[LATE] = waiting[LATE][:2]
-    for step in range(LATE):
-        fresh = [corrected(waiting[step][flip], flip) for flip in flips_of]
-        out[step], near_out[step] = fresh[:2]
-        whole = jnp.concatenate(flipped(fresh), axis=1)
-        fresh_b = whole.astype(jnp.bfloat16)
-        slope = slope_of(whole, spread)
-        slope = flipped([slope[:, i * rows : (i + 1) * rows] for i in flips_of])
-        for later in range(step + 1, STEPS):
-            lag = later - step - 1
-            for flip in range(len(waiting[later])):
-                change = times(fresh_b, lag, flip)
-                if lag == 0:
-                    change = change - slope[flip]
-                waiting[later][flip] = waiting[later][flip] - change
-    out[LATE], near_out[LATE] = (corrected(waiting[LATE][flip], flip) for flip in (0, 1))
+    marching = ((place == 1) | (place == 2)) & (lax.axis_index("lag") == 0)
+
+    @pl.when(jnp.logical_not(marching))
+    def _():
+        out[...] = jnp.zeros_like(out)
+        near_out[...] = jnp.zeros_like(near_out)
+
+    @pl.when(marching)
+    def _():
+        waiting = [[base[step] for base in (base_0, base_1, base_2, base_3)] for step in range(STEPS)]
+        waiting[LATE] = waiting[LATE][:2]
+        for step in range(LATE):
+            fresh = [corrected(waiting[step][flip], flip) for flip in flips_of]
+            out[step], near_out[step] = fresh[:2]
+            whole = jnp.concatenate(flipped(fresh), axis=1)
+            fresh_b = whole.astype(jnp.bfloat16)
+            slope = slope_of(whole, spread)
+            slope = flipped([slope[:, i * rows : (i + 1) * rows] for i in flips_of])
+            for later in range(step + 1, STEPS):
+                lag = later - step - 1
+                for flip in range(len(waiting[later])):
+                    change = times(fresh_b, lag, flip)
+                    if lag == 0:
+                        change = change - slope[flip]
+                    waiting[later][flip] = waiting[later][flip] - change
+        out[LATE], near_out[LATE] = (corrected(waiting[LATE][flip], flip) for flip in (0, 1))
 
 
 def on_core(body, shapes, operands, scratch=(), in_specs=None, limit=24, name=None, force=False):

time: 32.1 us -> 31 us (0.966)
  starting transfers between devices: 15.2 us -> 17.8 us
  Pallas kernels: 5.85 us -> 3.26 us
  waiting for transfers between devices: 10.2 us -> 9.08 us
    pallas_call x11, Pallas kernels: 5.85 us -> 3.26 us  [on_core(): pl.pallas_call(body, out_shape=[pltpu.VMEM(shape, dtype) if force else ja...]
    ppermute x9, starting transfers between devices: 6.08 us -> 8.66 us  [exchanged(): return lax.ppermute(value, ('elem', 'lag', 'gust'), moves)]
    ppermute x9, waiting for transfers between devices: 5.48 us -> 4.39 us  [exchanged(): return lax.ppermute(value, ('elem', 'lag', 'gust'), moves)]
  transfers between devices with their start and end apart: 17 -> 17, of which waited for: 6 -> 5; matrix products, arithmetic and copies ran while one was open for 0% -> 0% of each run, Pallas kernels for 7% -> 8%
where the time goes in v9:
time: 31 us; the launch traced here: 30.9 us
  starting transfers between devices  17.8 us (57%)
  waiting for transfers between devices  9.08 us (29%)
  Pallas kernels  3.26 us (11%)
  other arithmetic  0.61 us (2%)
    ppermute x9, starting transfers between devices, exchanged(): return lax.ppermute(value, ('elem', 'lag', 'gust'), moves)  8.66 us
    ppermute x3, starting transfers between devices, flips(): lax.ppermute(value, 'elem', [(i, i ^ flip) for i in range(count)])  5.68 us
    ppermute x9, waiting for transfers between devices, exchanged(): return lax.ppermute(value, ('elem', 'lag', 'gust'), moves)  4.39 us
    ppermute x5, waiting for transfers between devices, crossed(): return lax.ppermute(value, axis, [(0, 1), (1, 0)])  4.09 us
    ppermute x5, starting transfers between devices, crossed(): return lax.ppermute(value, axis, [(0, 1), (1, 0)])  3.43 us
    pallas_call x11, Pallas kernels, on_core(): pl.pallas_call(body, out_shape=[pltpu.VMEM(shape, dtype) if force else ja...  3.26 us
  transfers between devices with their start and end apart: 17, of which 5 were waited for; matrix products, arithmetic and copies ran while one was open for 0% of the time, Pallas kernels for 8%

profile of v9, /device:TPU:0, one launch (start us, length us, event | category | flops | bytes accessed | tf_op | source)
XLA Modules:
  0.0 30.9 jit_solution(12079399789642883561)
XLA Ops:
  0.0 0.0 copy-start.1
  0.0 0.0 copy-start.3
  0.0 0.0 copy-start
  0.0 0.9 %pack.1.piece_0 = bf16[64,128]{1,0:T(8,128)(2,1)S(1)} custom-call(f32[8,4,128]{2,1,0:T(4,128)} %history_in.1, s32[4,128]{1,0:T(4,128)} %neighbours_in.1, f32[4,128]{1,0:T(4,128)} %edge_coef_in.1), custom_call_target="tpu_custom_call" | custom-call | flops 10000000000 | bytes 1048576 | tf_op jit(solution)/shard_map/pack/pallas_call | solution.py:363
  0.9 4.1 %collective-permute-start.1 = (bf16[64,128]{1,0:T(8,128)(2,1)S(1)}, bf16[64,128]{1,0:T(8,128)(2,1)S(1)}, u32[]{:S(2)}, u32[]{:S(2)}) collective-permute-start(bf16[64,128]{1,0:T(8,128)(2,1)S(1)} %pack.1.piece_0), channel_id=1, source_target_pairs={{0,8},{4,12},{8,0},{12,4},{1,9},{5,13},{9,1},{13,5},{2,10},{6,14},... | collective-permute-start | bytes 49160 | tf_op jit(solution)/shard_map/ppermute | solution.py:20
  5.0 1.3 %collective-permute-start.2 = (bf16[64,128]{1,0:T(8,128)(2,1)S(1)}, bf16[64,128]{1,0:T(8,128)(2,1)S(1)}, u32[]{:S(2)}, u32[]{:S(2)}) collective-permute-start(bf16[64,128]{1,0:T(8,128)(2,1)S(1)} %pack.1.piece_0), channel_id=1, source_target_pairs={{0,12},{4,8},{8,4},{12,0},{1,13},{5,9},{9,5},{13,1},{2,14},{6,10},... | collective-permute-start | bytes 49160 | tf_op jit(solution)/shard_map/ppermute | solution.py:20
  6.3 0.2 collective-permute-start.3
  6.6 0.0 copy-done.1
  6.6 0.0 copy-done.3
  6.6 0.0 copy-done
  6.6 0.7 %near_load.1 = (bf16[128,256]{1,0:T(8,128)(2,1)S(1)}, bf16[64,2304]{1,0:T(8,128)(2,1)S(1)}) custom-call(s32[1,4,8]{2,1,0:T(4,128)S(1)} %bitcast.1, bf16[8,128,512]{2,1,0:T(8,128)(2,1)S(1)} %copy-done, f32[128,128]{1,0:T(8,128)S(1)} %copy-done.1), custom_call_target="tpu_custom_call" | custom-call | flops 10000000000 | bytes 1048576 | tf_op jit(solution)/shard_map/near_load/pallas_call | solution.py:363
  7.2 1.9 %collective-permute-start = (bf16[64,2304]{1,0:T(8,128)(2,1)S(1)}, bf16[64,2304]{1,0:T(8,128)(2,1)S(1)}, u32[]{:S(2)}, u32[]{:S(2)}) collective-permute-start(bf16[64,2304]{1,0:T(8,128)(2,1)S(1)} %get-tuple-element.21.near_load), channel_id=1, source_target_pairs={{0,4},{1,5},{4,0},{5,1},{8,12},{9,13},{12,8},{13,9},{2,3},{3,2},{6... | collective-permute-start | bytes 884744 | tf_op jit(solution)/shard_map/ppermute | solution.py:384
  9.1 0.8 %masked.1 = (bf16[8,128,512]{2,1,0:T(8,128)(2,1)S(1)}, bf16[64,1792]{1,0:T(8,128)(2,1)S(1)}) custom-call(s32[1,4,8]{2,1,0:T(4,128)S(1)} %bitcast.2, bf16[8,128,512]{2,1,0:T(8,128)(2,1)S(1)} %copy-done, bf16[64,2304]{1,0:T(8,128)(2,1)S(1)} %get-tuple-element.21.near_load), custom_call_target="tpu_custom_call" | custom-call | flops 10000000000 | bytes 1048576 | tf_op jit(solution)/shard_map/masked/pallas_call | solution.py:363
  9.9 0.1 collective-permute-start.8
  10.0 0.0 collective-permute-done.1.piece_2
  10.0 0.6 %collective-permute-done.2.piece_3 = bf16[64,128]{1,0:T(8,128)(2,1)S(1)} collective-permute-done((bf16[64,128]{1,0:T(8,128)(2,1)S(1)}, bf16[64,128]{1,0:T(8,128)(2,1)S(1)}, u32[]{:S(2)}, u32[]{:S(2)}) %collective-permute-start.2) | collective-permute-done | bytes 16416 | tf_op jit(solution)/shard_map/ppermute | solution.py:20
  10.6 0.0 collective-permute-done.3.piece_1
  10.7 1.4 %collective-permute-start.4 = (bf16[16,512]{1,0:T(8,128)(2,1)S(1)}, bf16[16,512]{1,0:T(8,128)(2,1)S(1)}, u32[]{:S(2)}, u32[]{:S(2)}) collective-permute-start(bf16[16,512]{1,0:T(8,128)(2,1)S(1)} %get-tuple-element.23), channel_id=1, source_target_pairs={{0,2},{2,0},{1,3},{3,1},{4,6},{6,4},{5,7},{7,5},{8,10},{10,8},{9,1... | collective-permute-start | bytes 49160 | tf_op jit(solution)/shard_map/ppermute | solution.py:402
  12.1 0.5 %main_part.1 = (f32[24,128]{1,0:T(8,128)S(1)}, f32[8,128]{1,0:T(8,128)S(1)}) custom-call(bf16[64,512]{1,0:T(8,128)(2,1)S(1)} %get-tuple-element.24.everyone, bf16[8,128,512]{2,1,0:T(8,128)(2,1)S(1)} %get-tuple-element.22.masked), custom_call_target="tpu_custom_call" | custom-call | flops 10000000000 | bytes 1048576 | tf_op jit(solution)/shard_map/main_part/pallas_call | solution.py:363
  12.6 1.9 %collective-permute-done.4.late = bf16[16,512]{1,0:T(8,128)(2,1)S(1)} collective-permute-done((bf16[16,512]{1,0:T(8,128)(2,1)S(1)}, bf16[16,512]{1,0:T(8,128)(2,1)S(1)}, u32[]{:S(2)}, u32[]{:S(2)}) %collective-permute-start.4) | collective-permute-done | bytes 16416 | tf_op jit(solution)/shard_map/ppermute | solution.py:402
  14.5 0.3 late_part.1.part
  14.7 1.4 %collective-permute-start.6 = (f32[24,128]{1,0:T(8,128)S(1)}, f32[24,128]{1,0:T(8,128)S(1)}, u32[]{:S(2)}, u32[]{:S(2)}) collective-permute-start(f32[24,128]{1,0:T(8,128)S(1)} %late_part.1.part), channel_id=1, source_target_pairs={{0,2},{2,0},{1,3},{3,1},{4,6},{6,4},{5,7},{7,5},{8,10},{10,8},{9,1... | collective-permute-start | bytes 36872 | tf_op jit(solution)/shard_map/ppermute | solution.py:402
  16.1 0.0 copy-done.2
  16.1 0.0 collective-permute-done.near.load_1
  16.2 0.1 collective-permute-start.5
  16.3 2.2 %collective-permute-done.6.other = f32[24,128]{1,0:T(8,128)S(1)} collective-permute-done((f32[24,128]{1,0:T(8,128)S(1)}, f32[24,128]{1,0:T(8,128)S(1)}, u32[]{:S(2)}, u32[]{:S(2)}) %collective-permute-start.6) | collective-permute-done | bytes 12320 | tf_op jit(solution)/shard_map/ppermute | solution.py:402
  18.4 0.0 collective-permute-start.7
  18.5 1.7 %collective-permute-start.12 = (f32[5,8,128]{2,1,0:T(8,128)S(1)}, f32[5,8,128]{2,1,0:T(8,128)S(1)}, u32[]{:S(2)}, u32[]{:S(2)}) collective-permute-start(f32[5,8,128]{2,1,0:T(8,128)S(1)} %base.1.after.base_0), channel_id=1, source_target_pairs={{0,4},{1,5},{4,0},{5,1},{8,12},{9,13},{12,8},{13,9},{2,3},{3,2},{6... | collective-permute-start | bytes 61448 | tf_op jit(solution)/shard_map/ppermute | solution.py:384
  20.2 1.4 %collective-permute-start.13 = (f32[5,8,128]{2,1,0:T(8,128)S(1)}, f32[5,8,128]{2,1,0:T(8,128)S(1)}, u32[]{:S(2)}, u32[]{:S(2)}) collective-permute-start(f32[5,8,128]{2,1,0:T(8,128)S(1)} %base.1.after.base_0), channel_id=1, source_target_pairs={{0,8},{1,9},{8,0},{9,1},{4,12},{5,13},{12,4},{13,5},{2,3},{3,2},{6... | collective-permute-start | bytes 61448 | tf_op jit(solution)/shard_map/ppermute | solution.py:384
  21.6 0.0 collective-permute-done.8.load_3
  21.6 0.0 collective-permute-start.9
  21.6 0.0 collective-permute-done.7.base_3
  21.6 0.5 %collective-permute-start.11 = (bf16[64,1792]{1,0:T(8,128)(2,1)S(1)}, bf16[64,1792]{1,0:T(8,128)(2,1)S(1)}, u32[]{:S(2)}, u32[]{:S(2)}) collective-permute-start(bf16[64,1792]{1,0:T(8,128)(2,1)S(1)} %collective-permute-done.8.load_3), channel_id=1, source_target_pairs={{0,1},{1,0},{2,3},{3,2},{4,5},{5,4},{6,7},{7,6},{8,9},{9,8},{10,11... | collective-permute-start | bytes 688136 | tf_op jit(solution)/shard_map/ppermute | solution.py:402
  22.1 0.0 collective-permute-done.5.load_2
  22.1 0.1 collective-permute-start.10
  22.2 0.1 spread.1
  22.3 0.0 collective-permute-done.12.base_1
  22.3 2.6 %collective-permute-done.13.base_2 = f32[5,8,128]{2,1,0:T(8,128)S(1)} collective-permute-done((f32[5,8,128]{2,1,0:T(8,128)S(1)}, f32[5,8,128]{2,1,0:T(8,128)S(1)}, u32[]{:S(2)}, u32[]{:S(2)}) %collective-permute-start.13) | collective-permute-done | bytes 20512 | tf_op jit(solution)/shard_map/ppermute | solution.py:384
  24.9 0.0 collective-permute-done.11.swap_3
  24.9 0.0 collective-permute-done.9.swap_1
  24.9 0.0 collective-permute-done.10.swap_2
  24.9 0.1 collective-permute-start.14
  25.0 3.5 %collective-permute-start.15 = (f32[5,8,128]{2,1,0:T(8,128)S(1)}, f32[5,8,128]{2,1,0:T(8,128)S(1)}, u32[]{:S(2)}, u32[]{:S(2)}) collective-permute-start(f32[5,8,128]{2,1,0:T(8,128)S(1)} %get-tuple-element.34), channel_id=1, source_target_pairs={{4,0},{5,1},{0,4},{1,5},{8,12},{9,13},{12,8},{13,9},{2,3},{3,2},{6... | collective-permute-start | bytes 61448 | tf_op jit(solution)/shard_map/ppermute | solution.py:384
  28.5 0.0 collective-permute-start.16
  28.5 0.0 collective-permute-done.14
  28.5 1.8 %collective-permute-done.15 = f32[5,8,128]{2,1,0:T(8,128)S(1)} collective-permute-done((f32[5,8,128]{2,1,0:T(8,128)S(1)}, f32[5,8,128]{2,1,0:T(8,128)S(1)}, u32[]{:S(2)}, u32[]{:S(2)}) %collective-permute-start.15) | collective-permute-done | bytes 20512 | tf_op jit(solution)/shard_map/ppermute | solution.py:384
  30.2 0.0 collective-permute-done.16
  30.2 0.6 %fusion = f32[5,4,128]{2,1,0:T(4,128)} fusion(f32[5,8,128]{2,1,0:T(8,128)S(1)} %collective-permute-done.16, f32[5,8,128]{2,1,0:T(8,128)S(1)} %collective-permute-done.15, f32[5,8,128]{2,1,0:T(8,128)S(1)} %collective-permute-done.14, f32[5,8,128]{2,1,0:T(8,128)S(1)} %get-tuple-element.33, pred[]{:T(512)S(6)} %or.3, pred[]{:T(512)S(6)} %eq.11), kind=kLoop, calls=%fused_computation.1 | loop fusion | flops 7680 | bytes 51202 | tf_op jit(solution)/shard_map/jit(_where)/select_n | solution.py:521
  (6 shorter events, 0.1 us)
Async XLA Ops:
  0.0 6.6 %copy-start.1 = (f32[128,128]{1,0:T(8,128)S(1)}, f32[128,128]{1,0:T(8,128)}, u32[]{:S(2)}) copy-start(f32[128,128]{1,0:T(8,128)} %correction_in) | copy-start | bytes 196612
  0.0 6.6 %copy-start.3 = (s32[8,1,4]{0,2,1:T(4,128)S(1)}, s32[8,1,4]{0,2,1:T(4,128)}, u32[]{:S(2)}) copy-start(s32[8,1,4]{0,2,1:T(4,128)} %param.10) | copy-start | bytes 388
  0.0 6.6 %copy-start = (bf16[8,128,512]{2,1,0:T(8,128)(2,1)S(1)}, bf16[8,128,512]{2,1,0:T(8,128)(2,1)}, u32[]{:S(2)}) copy-start(bf16[8,128,512]{2,1,0:T(8,128)(2,1)} %interaction.1) | copy-start | bytes 3145732
  0.9 9.1 %collective-permute-start.1 = (bf16[64,128]{1,0:T(8,128)(2,1)S(1)}, bf16[64,128]{1,0:T(8,128)(2,1)S(1)}, u32[]{:S(2)}, u32[]{:S(2)}) collective-permute-start(bf16[64,128]{1,0:T(8,128)(2,1)S(1)} %pack.1.piece_0), channel_id=1, source_target_pairs={{0,8},{4,12},{8,0},{12,4},{1,9},{5,13},{9,1},{13,5},{2,10},{6,14},... | collective-permute-start | bytes 49160 | tf_op jit(solution)/shard_map/ppermute | solution.py:20
  5.0 5.6 %collective-permute-start.2 = (bf16[64,128]{1,0:T(8,128)(2,1)S(1)}, bf16[64,128]{1,0:T(8,128)(2,1)S(1)}, u32[]{:S(2)}, u32[]{:S(2)}) collective-permute-start(bf16[64,128]{1,0:T(8,128)(2,1)S(1)} %pack.1.piece_0), channel_id=1, source_target_pairs={{0,12},{4,8},{8,4},{12,0},{1,13},{5,9},{9,5},{13,1},{2,14},{6,10},... | collective-permute-start | bytes 49160 | tf_op jit(solution)/shard_map/ppermute | solution.py:20
  6.3 4.3 %collective-permute-start.3 = (bf16[64,128]{1,0:T(8,128)(2,1)S(1)}, bf16[64,128]{1,0:T(8,128)(2,1)S(1)}, u32[]{:S(2)}, u32[]{:S(2)}) collective-permute-start(bf16[64,128]{1,0:T(8,128)(2,1)S(1)} %pack.1.piece_0), channel_id=1, source_target_pairs={{0,4},{4,0},{8,12},{12,8},{1,5},{5,1},{9,13},{13,9},{2,6},{6,2},{1... | collective-permute-start | bytes 49160 | tf_op jit(solution)/shard_map/ppermute | solution.py:20
  7.2 8.9 %collective-permute-start = (bf16[64,2304]{1,0:T(8,128)(2,1)S(1)}, bf16[64,2304]{1,0:T(8,128)(2,1)S(1)}, u32[]{:S(2)}, u32[]{:S(2)}) collective-permute-start(bf16[64,2304]{1,0:T(8,128)(2,1)S(1)} %get-tuple-element.21.near_load), channel_id=1, source_target_pairs={{0,4},{1,5},{4,0},{5,1},{8,12},{9,13},{12,8},{13,9},{2,3},{3,2},{6... | collective-permute-start | bytes 884744 | tf_op jit(solution)/shard_map/ppermute | solution.py:384
  9.9 11.6 %collective-permute-start.8 = (bf16[64,1792]{1,0:T(8,128)(2,1)S(1)}, bf16[64,1792]{1,0:T(8,128)(2,1)S(1)}, u32[]{:S(2)}, u32[]{:S(2)}) collective-permute-start(bf16[64,1792]{1,0:T(8,128)(2,1)S(1)} %get-tuple-element.30), channel_id=1, source_target_pairs={{4,8},{5,9},{8,4},{9,5},{0,1},{1,0},{2,3},{3,2},{6,7},{7,6},{10,11... | collective-permute-start | bytes 688136 | tf_op jit(solution)/shard_map/ppermute | solution.py:384
  10.7 3.8 %collective-permute-start.4 = (bf16[16,512]{1,0:T(8,128)(2,1)S(1)}, bf16[16,512]{1,0:T(8,128)(2,1)S(1)}, u32[]{:S(2)}, u32[]{:S(2)}) collective-permute-start(bf16[16,512]{1,0:T(8,128)(2,1)S(1)} %get-tuple-element.23), channel_id=1, source_target_pairs={{0,2},{2,0},{1,3},{3,1},{4,6},{6,4},{5,7},{7,5},{8,10},{10,8},{9,1... | collective-permute-start | bytes 49160 | tf_op jit(solution)/shard_map/ppermute | solution.py:402
  14.5 1.7 %copy-start.2 = (f32[5,4,128]{2,1,0:T(4,128)S(1)}, f32[5,4,128]{2,1,0:T(4,128)}, u32[]{:S(2)}) copy-start(f32[5,4,128]{2,1,0:T(4,128)} %forcing.1) | copy-start | bytes 30724
  14.7 3.7 %collective-permute-start.6 = (f32[24,128]{1,0:T(8,128)S(1)}, f32[24,128]{1,0:T(8,128)S(1)}, u32[]{:S(2)}, u32[]{:S(2)}) collective-permute-start(f32[24,128]{1,0:T(8,128)S(1)} %late_part.1.part), channel_id=1, source_target_pairs={{0,2},{2,0},{1,3},{3,1},{4,6},{6,4},{5,7},{7,5},{8,10},{10,8},{9,1... | collective-permute-start | bytes 36872 | tf_op jit(solution)/shard_map/ppermute | solution.py:402
  16.2 5.9 %collective-permute-start.5 = (bf16[64,1792]{1,0:T(8,128)(2,1)S(1)}, bf16[64,1792]{1,0:T(8,128)(2,1)S(1)}, u32[]{:S(2)}, u32[]{:S(2)}) collective-permute-start(bf16[64,1792]{1,0:T(8,128)(2,1)S(1)} %relay.1.after), channel_id=1, source_target_pairs={{4,8},{5,9},{8,4},{9,5},{0,1},{1,0},{2,3},{3,2},{6,7},{7,6},{10,11... | collective-permute-start | bytes 688136 | tf_op jit(solution)/shard_map/ppermute | solution.py:384
  18.4 3.1 %collective-permute-start.7 = (f32[5,8,128]{2,1,0:T(8,128)S(1)}, f32[5,8,128]{2,1,0:T(8,128)S(1)}, u32[]{:S(2)}, u32[]{:S(2)}) collective-permute-start(f32[5,8,128]{2,1,0:T(8,128)S(1)} %base.1.after.base_0), channel_id=1, source_target_pairs={{4,8},{5,9},{8,4},{9,5},{0,1},{1,0},{2,3},{3,2},{6,7},{7,6},{10,11... | collective-permute-start | bytes 61448 | tf_op jit(solution)/shard_map/ppermute | solution.py:384
  18.5 3.8 %collective-permute-start.12 = (f32[5,8,128]{2,1,0:T(8,128)S(1)}, f32[5,8,128]{2,1,0:T(8,128)S(1)}, u32[]{:S(2)}, u32[]{:S(2)}) collective-permute-start(f32[5,8,128]{2,1,0:T(8,128)S(1)} %base.1.after.base_0), channel_id=1, source_target_pairs={{0,4},{1,5},{4,0},{5,1},{8,12},{9,13},{12,8},{13,9},{2,3},{3,2},{6... | collective-permute-start | bytes 61448 | tf_op jit(solution)/shard_map/ppermute | solution.py:384
  20.2 4.7 %collective-permute-start.13 = (f32[5,8,128]{2,1,0:T(8,128)S(1)}, f32[5,8,128]{2,1,0:T(8,128)S(1)}, u32[]{:S(2)}, u32[]{:S(2)}) collective-permute-start(f32[5,8,128]{2,1,0:T(8,128)S(1)} %base.1.after.base_0), channel_id=1, source_target_pairs={{0,8},{1,9},{8,0},{9,1},{4,12},{5,13},{12,4},{13,5},{2,3},{3,2},{6... | collective-permute-start | bytes 61448 | tf_op jit(solution)/shard_map/ppermute | solution.py:384
  21.6 3.3 %collective-permute-start.9 = (bf16[64,2304]{1,0:T(8,128)(2,1)S(1)}, bf16[64,2304]{1,0:T(8,128)(2,1)S(1)}, u32[]{:S(2)}, u32[]{:S(2)}) collective-permute-start(bf16[64,2304]{1,0:T(8,128)(2,1)S(1)} %collective-permute-done.near.load_1), channel_id=1, source_target_pairs={{0,1},{1,0},{2,3},{3,2},{4,5},{5,4},{6,7},{7,6},{8,9},{9,8},{10,11... | collective-permute-start | bytes 884744 | tf_op jit(solution)/shard_map/ppermute | solution.py:402
  21.6 3.3 %collective-permute-start.11 = (bf16[64,1792]{1,0:T(8,128)(2,1)S(1)}, bf16[64,1792]{1,0:T(8,128)(2,1)S(1)}, u32[]{:S(2)}, u32[]{:S(2)}) collective-permute-start(bf16[64,1792]{1,0:T(8,128)(2,1)S(1)} %collective-permute-done.8.load_3), channel_id=1, source_target_pairs={{0,1},{1,0},{2,3},{3,2},{4,5},{5,4},{6,7},{7,6},{8,9},{9,8},{10,11... | collective-permute-start | bytes 688136 | tf_op jit(solution)/shard_map/ppermute | solution.py:402
  22.1 2.8 %collective-permute-start.10 = (bf16[64,1792]{1,0:T(8,128)(2,1)S(1)}, bf16[64,1792]{1,0:T(8,128)(2,1)S(1)}, u32[]{:S(2)}, u32[]{:S(2)}) collective-permute-start(bf16[64,1792]{1,0:T(8,128)(2,1)S(1)} %collective-permute-done.5.load_2), channel_id=1, source_target_pairs={{0,1},{1,0},{2,3},{3,2},{4,5},{5,4},{6,7},{7,6},{8,9},{9,8},{10,11... | collective-permute-start | bytes 688136 | tf_op jit(solution)/shard_map/ppermute | solution.py:402
  24.9 3.6 %collective-permute-start.14 = (f32[5,8,128]{2,1,0:T(8,128)S(1)}, f32[5,8,128]{2,1,0:T(8,128)S(1)}, u32[]{:S(2)}, u32[]{:S(2)}) collective-permute-start(f32[5,8,128]{2,1,0:T(8,128)S(1)} %get-tuple-element.33), channel_id=1, source_target_pairs={{4,6},{5,7},{6,4},{7,5},{8,10},{9,11},{10,8},{11,9},{0,1},{1,0},{2... | collective-permute-start | bytes 61448 | tf_op jit(solution)/shard_map/ppermute | solution.py:384
  25.0 5.2 %collective-permute-start.15 = (f32[5,8,128]{2,1,0:T(8,128)S(1)}, f32[5,8,128]{2,1,0:T(8,128)S(1)}, u32[]{:S(2)}, u32[]{:S(2)}) collective-permute-start(f32[5,8,128]{2,1,0:T(8,128)S(1)} %get-tuple-element.34), channel_id=1, source_target_pairs={{4,0},{5,1},{0,4},{1,5},{8,12},{9,13},{12,8},{13,9},{2,3},{3,2},{6... | collective-permute-start | bytes 61448 | tf_op jit(solution)/shard_map/ppermute | solution.py:384
  28.5 1.8 %collective-permute-start.16 = (f32[5,8,128]{2,1,0:T(8,128)S(1)}, f32[5,8,128]{2,1,0:T(8,128)S(1)}, u32[]{:S(2)}, u32[]{:S(2)}) collective-permute-start(f32[5,8,128]{2,1,0:T(8,128)S(1)} %get-tuple-element.34), channel_id=1, source_target_pairs={{4,2},{5,3},{2,6},{3,7},{6,4},{7,5},{8,14},{9,15},{14,10},{15,11},... | collective-permute-start | bytes 61448 | tf_op jit(solution)/shard_map/ppermute | solution.py:384

commit v10 on v9

--- a/solution.py
+++ b/solution.py
@@ -258,33 +258,42 @@
 
 def late_part(late, masked, part, both, longer):
     gusts = late.shape[0] // LATE
-    value = late[...].astype(jnp.float32)
-    longer[...] = jnp.zeros_like(longer)
-    longer[: late.shape[0], :] = jnp.where(lax.axis_index("lag") == 0, 0.0, value)
-    acc = part[...]
-    for lag in range(LATE):
-        lhs = longer[lag * gusts : lag * gusts + part.shape[0], :].astype(jnp.bfloat16)
-        acc += dot_rows(lhs, masked[lag])
-    both[...] = acc
+    first = lax.axis_index("lag") == 0
+
+    @pl.when(first)
+    def _():
+        both[...] = part[...]
+
+    @pl.when(jnp.logical_not(first))
+    def _():
+        longer[...] = jnp.zeros_like(longer)
+        longer[: late.shape[0], :] = late[...].astype(jnp.float32)
+        acc = part[...]
+        for lag in range(LATE):
+            lhs = longer[lag * gusts : lag * gusts + part.shape[0], :].astype(jnp.bfloat16)
+            acc += dot_rows(lhs, masked[lag])
+        both[...] = acc
 
 
 def known_base(part, forcing, slope, ahead):
     gusts = forcing.shape[1]
+    values = []
     for step in range(STEPS):
         at = (STEPS - 1 - step) * gusts
         value = forcing[step] - part[at : at + gusts, :]
         if step == 0:
             value = value + slope[:gusts, :]
-        ahead[step] = jnp.concatenate([value, jnp.zeros_like(value)], axis=0)
+        values.append(value)
+    values.append(jnp.zeros_like(values[0]))
+    ahead[...] = jnp.concatenate(values, axis=0)
 
 
 def make_base(after, ahead, other, base):
     del after
     gusts = 4
-    for step in range(STEPS):
-        at = (STEPS - 1 - step) * gusts
-        value = other[at : at + gusts, :]
-        base[step] = ahead[step] - jnp.concatenate([value, jnp.zeros_like(value)], axis=0)
+    values = [other[at * gusts : (at + 1) * gusts, :] for at in reversed(range(STEPS))]
+    values.append(jnp.zeros_like(values[0]))
+    base[...] = ahead[...] - jnp.concatenate(values, axis=0)
 
 
 def march(
@@ -339,7 +348,10 @@
 
     @pl.when(marching)
     def _():
-        waiting = [[base[step] for base in (base_0, base_1, base_2, base_3)] for step in range(STEPS)]
+        waiting = [
+            [base[step * 4 : step * 4 + GUST_ROWS, :] for base in (base_0, base_1, base_2, base_3)]
+            for step in range(STEPS)
+        ]
         waiting[LATE] = waiting[LATE][:2]
         for step in range(LATE):
             fresh = [corrected(waiting[step][flip], flip) for flip in flips_of]
@@ -472,7 +484,7 @@
     other = crossed(part, "lag")
     (ahead,) = on_core(
         known_base,
-        [((STEPS, GUST_ROWS, rows), f32)],
+        [((part_rows, rows), f32)],
         (part, forcing, slope),
         name="known_base",
     )
@@ -484,7 +496,7 @@
     near_swap, mid_swap = (crossed(piece, "gust") for piece in early)
     (base,) = on_core(
         make_base,
-        [((STEPS, GUST_ROWS, rows), f32)],
+        [((part_rows, rows), f32)],
         (far_load, ahead, other),
         in_specs=[anywhere, vmem, vmem],
         name="base",

time: 31 us -> 30.7 us (level)
  waiting for transfers between devices: 9.08 us -> 8.7 us
  transfers between devices with their start and end apart: 17 -> 17, of which waited for: 5 -> 5; matrix products, arithmetic and copies ran while one was open for 0% -> 0% of each run, Pallas kernels for 8% -> 7%
where the time goes in v10:
time: 30.7 us; the launch traced here: 30.6 us
  starting transfers between devices  18.1 us (59%)
  waiting for transfers between devices  8.7 us (28%)
  Pallas kernels  3.01 us (10%)
  other arithmetic  0.61 us (2%)
    ppermute x9, starting transfers between devices, exchanged(): return lax.ppermute(value, ('elem', 'lag', 'gust'), moves)  8.75 us
    ppermute x3, starting transfers between devices, flips(): lax.ppermute(value, 'elem', [(i, i ^ flip) for i in range(count)])  5.68 us
    ppermute x9, waiting for transfers between devices, exchanged(): return lax.ppermute(value, ('elem', 'lag', 'gust'), moves)  4.3 us
    ppermute x5, waiting for transfers between devices, crossed(): return lax.ppermute(value, axis, [(0, 1), (1, 0)])  3.8 us
    ppermute x5, starting transfers between devices, crossed(): return lax.ppermute(value, axis, [(0, 1), (1, 0)])  3.69 us
    pallas_call x11, Pallas kernels, on_core(): pl.pallas_call(body, out_shape=[pltpu.VMEM(shape, dtype) if force else ja...  3.01 us
  transfers between devices with their start and end apart: 17, of which 5 were waited for; matrix products, arithmetic and copies ran while one was open for 0% of the time, Pallas kernels for 7%

profile of v10, /device:TPU:0, one launch (start us, length us, event | category | flops | bytes accessed | tf_op | source)
XLA Modules:
  0.0 30.6 jit_solution(2658177331118930902)
XLA Ops:
  0.0 0.0 copy-start.1
  0.0 0.0 copy-start.3
  0.0 0.0 copy-start
  0.0 0.9 %pack.1.piece_0 = bf16[64,128]{1,0:T(8,128)(2,1)S(1)} custom-call(f32[8,4,128]{2,1,0:T(4,128)} %history_in.1, s32[4,128]{1,0:T(4,128)} %neighbours_in.1, f32[4,128]{1,0:T(4,128)} %edge_coef_in.1), custom_call_target="tpu_custom_call" | custom-call | flops 10000000000 | bytes 1048576 | tf_op jit(solution)/shard_map/pack/pallas_call | solution.py:375
  0.9 4.1 %collective-permute-start.1 = (bf16[64,128]{1,0:T(8,128)(2,1)S(1)}, bf16[64,128]{1,0:T(8,128)(2,1)S(1)}, u32[]{:S(2)}, u32[]{:S(2)}) collective-permute-start(bf16[64,128]{1,0:T(8,128)(2,1)S(1)} %pack.1.piece_0), channel_id=1, source_target_pairs={{0,8},{4,12},{8,0},{12,4},{1,9},{5,13},{9,1},{13,5},{2,10},{6,14},... | collective-permute-start | bytes 49160 | tf_op jit(solution)/shard_map/ppermute | solution.py:20
  5.0 1.3 %collective-permute-start.2 = (bf16[64,128]{1,0:T(8,128)(2,1)S(1)}, bf16[64,128]{1,0:T(8,128)(2,1)S(1)}, u32[]{:S(2)}, u32[]{:S(2)}) collective-permute-start(bf16[64,128]{1,0:T(8,128)(2,1)S(1)} %pack.1.piece_0), channel_id=1, source_target_pairs={{0,12},{4,8},{8,4},{12,0},{1,13},{5,9},{9,5},{13,1},{2,14},{6,10},... | collective-permute-start | bytes 49160 | tf_op jit(solution)/shard_map/ppermute | solution.py:20
  6.3 0.2 collective-permute-start.3
  6.6 0.0 copy-done.1
  6.6 0.0 copy-done.3
  6.6 0.0 copy-done
  6.6 0.7 %near_load.1 = (bf16[128,256]{1,0:T(8,128)(2,1)S(1)}, bf16[64,2304]{1,0:T(8,128)(2,1)S(1)}) custom-call(s32[1,4,8]{2,1,0:T(4,128)S(1)} %bitcast.1, bf16[8,128,512]{2,1,0:T(8,128)(2,1)S(1)} %copy-done, f32[128,128]{1,0:T(8,128)S(1)} %copy-done.1), custom_call_target="tpu_custom_call" | custom-call | flops 10000000000 | bytes 1048576 | tf_op jit(solution)/shard_map/near_load/pallas_call | solution.py:375
  7.2 1.9 %collective-permute-start = (bf16[64,2304]{1,0:T(8,128)(2,1)S(1)}, bf16[64,2304]{1,0:T(8,128)(2,1)S(1)}, u32[]{:S(2)}, u32[]{:S(2)}) collective-permute-start(bf16[64,2304]{1,0:T(8,128)(2,1)S(1)} %get-tuple-element.21.near_load), channel_id=1, source_target_pairs={{0,4},{1,5},{4,0},{5,1},{8,12},{9,13},{12,8},{13,9},{2,3},{3,2},{6... | collective-permute-start | bytes 884744 | tf_op jit(solution)/shard_map/ppermute | solution.py:396
  9.1 0.8 %masked.1 = (bf16[8,128,512]{2,1,0:T(8,128)(2,1)S(1)}, bf16[64,1792]{1,0:T(8,128)(2,1)S(1)}) custom-call(s32[1,4,8]{2,1,0:T(4,128)S(1)} %bitcast.2, bf16[8,128,512]{2,1,0:T(8,128)(2,1)S(1)} %copy-done, bf16[64,2304]{1,0:T(8,128)(2,1)S(1)} %get-tuple-element.21.near_load), custom_call_target="tpu_custom_call" | custom-call | flops 10000000000 | bytes 1048576 | tf_op jit(solution)/shard_map/masked/pallas_call | solution.py:375
  9.9 0.1 collective-permute-start.8
  10.0 0.0 collective-permute-done.1.piece_2
  10.0 0.6 %collective-permute-done.2.piece_3 = bf16[64,128]{1,0:T(8,128)(2,1)S(1)} collective-permute-done((bf16[64,128]{1,0:T(8,128)(2,1)S(1)}, bf16[64,128]{1,0:T(8,128)(2,1)S(1)}, u32[]{:S(2)}, u32[]{:S(2)}) %collective-permute-start.2) | collective-permute-done | bytes 16416 | tf_op jit(solution)/shard_map/ppermute | solution.py:20
  10.6 0.0 collective-permute-done.3.piece_1
  10.7 1.4 %collective-permute-start.4 = (bf16[16,512]{1,0:T(8,128)(2,1)S(1)}, bf16[16,512]{1,0:T(8,128)(2,1)S(1)}, u32[]{:S(2)}, u32[]{:S(2)}) collective-permute-start(bf16[16,512]{1,0:T(8,128)(2,1)S(1)} %get-tuple-element.23), channel_id=1, source_target_pairs={{0,2},{2,0},{1,3},{3,1},{4,6},{6,4},{5,7},{7,5},{8,10},{10,8},{9,1... | collective-permute-start | bytes 49160 | tf_op jit(solution)/shard_map/ppermute | solution.py:414
  12.1 0.5 %main_part.1 = (f32[24,128]{1,0:T(8,128)S(1)}, f32[8,128]{1,0:T(8,128)S(1)}) custom-call(bf16[64,512]{1,0:T(8,128)(2,1)S(1)} %get-tuple-element.24.everyone, bf16[8,128,512]{2,1,0:T(8,128)(2,1)S(1)} %get-tuple-element.22.masked), custom_call_target="tpu_custom_call" | custom-call | flops 10000000000 | bytes 1048576 | tf_op jit(solution)/shard_map/main_part/pallas_call | solution.py:375
  12.6 1.9 %collective-permute-done.4.late = bf16[16,512]{1,0:T(8,128)(2,1)S(1)} collective-permute-done((bf16[16,512]{1,0:T(8,128)(2,1)S(1)}, bf16[16,512]{1,0:T(8,128)(2,1)S(1)}, u32[]{:S(2)}, u32[]{:S(2)}) %collective-permute-start.4) | collective-permute-done | bytes 16416 | tf_op jit(solution)/shard_map/ppermute | solution.py:414
  14.5 0.0 copy-start.2
  14.5 1.7 %collective-permute-start.6 = (f32[24,128]{1,0:T(8,128)S(1)}, f32[24,128]{1,0:T(8,128)S(1)}, u32[]{:S(2)}, u32[]{:S(2)}) collective-permute-start(f32[24,128]{1,0:T(8,128)S(1)} %late_part.1.part), channel_id=1, source_target_pairs={{0,2},{2,0},{1,3},{3,1},{4,6},{6,4},{5,7},{7,5},{8,10},{10,8},{9,1... | collective-permute-start | bytes 36872 | tf_op jit(solution)/shard_map/ppermute | solution.py:414
  16.1 0.0 copy-done.2
  16.1 0.0 collective-permute-done.near.load_1
  16.2 0.1 collective-permute-start.5
  16.3 1.9 %collective-permute-done.6.other = f32[24,128]{1,0:T(8,128)S(1)} collective-permute-done((f32[24,128]{1,0:T(8,128)S(1)}, f32[24,128]{1,0:T(8,128)S(1)}, u32[]{:S(2)}, u32[]{:S(2)}) %collective-permute-start.6) | collective-permute-done | bytes 12320 | tf_op jit(solution)/shard_map/ppermute | solution.py:414
  18.2 0.0 collective-permute-start.7
  18.2 1.7 %collective-permute-start.12 = (f32[24,128]{1,0:T(8,128)S(1)}, f32[24,128]{1,0:T(8,128)S(1)}, u32[]{:S(2)}, u32[]{:S(2)}) collective-permute-start(f32[24,128]{1,0:T(8,128)S(1)} %base.1.after.base_0), channel_id=1, source_target_pairs={{0,4},{1,5},{4,0},{5,1},{8,12},{9,13},{12,8},{13,9},{2,3},{3,2},{6... | collective-permute-start | bytes 36872 | tf_op jit(solution)/shard_map/ppermute | solution.py:396
  19.9 1.4 %collective-permute-start.13 = (f32[24,128]{1,0:T(8,128)S(1)}, f32[24,128]{1,0:T(8,128)S(1)}, u32[]{:S(2)}, u32[]{:S(2)}) collective-permute-start(f32[24,128]{1,0:T(8,128)S(1)} %base.1.after.base_0), channel_id=1, source_target_pairs={{0,8},{1,9},{8,0},{9,1},{4,12},{5,13},{12,4},{13,5},{2,3},{3,2},{6... | collective-permute-start | bytes 36872 | tf_op jit(solution)/shard_map/ppermute | solution.py:396
  21.3 0.0 collective-permute-done.8.load_3
  21.3 0.0 collective-permute-start.9
  21.3 0.0 collective-permute-done.7.base_3
  21.3 0.5 %collective-permute-start.11 = (bf16[64,1792]{1,0:T(8,128)(2,1)S(1)}, bf16[64,1792]{1,0:T(8,128)(2,1)S(1)}, u32[]{:S(2)}, u32[]{:S(2)}) collective-permute-start(bf16[64,1792]{1,0:T(8,128)(2,1)S(1)} %collective-permute-done.8.load_3), channel_id=1, source_target_pairs={{0,1},{1,0},{2,3},{3,2},{4,5},{5,4},{6,7},{7,6},{8,9},{9,8},{10,11... | collective-permute-start | bytes 688136 | tf_op jit(solution)/shard_map/ppermute | solution.py:414
  21.8 0.0 collective-permute-done.5.load_2
  21.8 0.1 collective-permute-start.10
  21.9 0.1 spread.1
  22.0 0.0 collective-permute-done.12.base_1
  22.0 2.5 %collective-permute-done.13.base_2 = f32[24,128]{1,0:T(8,128)S(1)} collective-permute-done((f32[24,128]{1,0:T(8,128)S(1)}, f32[24,128]{1,0:T(8,128)S(1)}, u32[]{:S(2)}, u32[]{:S(2)}) %collective-permute-start.13) | collective-permute-done | bytes 12320 | tf_op jit(solution)/shard_map/ppermute | solution.py:396
  24.5 0.0 collective-permute-done.11.swap_3
  24.5 0.0 collective-permute-done.9.swap_1
  24.5 0.0 collective-permute-done.10.swap_2
  24.6 0.1 collective-permute-start.14
  24.6 3.6 %collective-permute-start.15 = (f32[5,8,128]{2,1,0:T(8,128)S(1)}, f32[5,8,128]{2,1,0:T(8,128)S(1)}, u32[]{:S(2)}, u32[]{:S(2)}) collective-permute-start(f32[5,8,128]{2,1,0:T(8,128)S(1)} %get-tuple-element.34), channel_id=1, source_target_pairs={{4,0},{5,1},{0,4},{1,5},{8,12},{9,13},{12,8},{13,9},{2,3},{3,2},{6... | collective-permute-start | bytes 61448 | tf_op jit(solution)/shard_map/ppermute | solution.py:396
  28.2 0.0 collective-permute-start.16
  28.2 0.0 collective-permute-done.14
  28.2 1.8 %collective-permute-done.15 = f32[5,8,128]{2,1,0:T(8,128)S(1)} collective-permute-done((f32[5,8,128]{2,1,0:T(8,128)S(1)}, f32[5,8,128]{2,1,0:T(8,128)S(1)}, u32[]{:S(2)}, u32[]{:S(2)}) %collective-permute-start.15) | collective-permute-done | bytes 20512 | tf_op jit(solution)/shard_map/ppermute | solution.py:396
  30.0 0.0 collective-permute-done.16
  30.0 0.6 %fusion = f32[5,4,128]{2,1,0:T(4,128)} fusion(f32[5,8,128]{2,1,0:T(8,128)S(1)} %collective-permute-done.16, f32[5,8,128]{2,1,0:T(8,128)S(1)} %collective-permute-done.15, f32[5,8,128]{2,1,0:T(8,128)S(1)} %collective-permute-done.14, f32[5,8,128]{2,1,0:T(8,128)S(1)} %get-tuple-element.33, pred[]{:T(512)S(6)} %or.3, pred[]{:T(512)S(6)} %eq.11), kind=kLoop, calls=%fused_computation.1 | loop fusion | flops 7680 | bytes 51202 | tf_op jit(solution)/shard_map/jit(_where)/select_n | solution.py:533
  (6 shorter events, 0.1 us)
Async XLA Ops:
  0.0 6.6 %copy-start.1 = (f32[128,128]{1,0:T(8,128)S(1)}, f32[128,128]{1,0:T(8,128)}, u32[]{:S(2)}) copy-start(f32[128,128]{1,0:T(8,128)} %correction_in) | copy-start | bytes 196612
  0.0 6.6 %copy-start.3 = (s32[8,1,4]{0,2,1:T(4,128)S(1)}, s32[8,1,4]{0,2,1:T(4,128)}, u32[]{:S(2)}) copy-start(s32[8,1,4]{0,2,1:T(4,128)} %param.10) | copy-start | bytes 388
  0.0 6.6 %copy-start = (bf16[8,128,512]{2,1,0:T(8,128)(2,1)S(1)}, bf16[8,128,512]{2,1,0:T(8,128)(2,1)}, u32[]{:S(2)}) copy-start(bf16[8,128,512]{2,1,0:T(8,128)(2,1)} %interaction.1) | copy-start | bytes 3145732
  0.9 9.1 %collective-permute-start.1 = (bf16[64,128]{1,0:T(8,128)(2,1)S(1)}, bf16[64,128]{1,0:T(8,128)(2,1)S(1)}, u32[]{:S(2)}, u32[]{:S(2)}) collective-permute-start(bf16[64,128]{1,0:T(8,128)(2,1)S(1)} %pack.1.piece_0), channel_id=1, source_target_pairs={{0,8},{4,12},{8,0},{12,4},{1,9},{5,13},{9,1},{13,5},{2,10},{6,14},... | collective-permute-start | bytes 49160 | tf_op jit(solution)/shard_map/ppermute | solution.py:20
  5.0 5.6 %collective-permute-start.2 = (bf16[64,128]{1,0:T(8,128)(2,1)S(1)}, bf16[64,128]{1,0:T(8,128)(2,1)S(1)}, u32[]{:S(2)}, u32[]{:S(2)}) collective-permute-start(bf16[64,128]{1,0:T(8,128)(2,1)S(1)} %pack.1.piece_0), channel_id=1, source_target_pairs={{0,12},{4,8},{8,4},{12,0},{1,13},{5,9},{9,5},{13,1},{2,14},{6,10},... | collective-permute-start | bytes 49160 | tf_op jit(solution)/shard_map/ppermute | solution.py:20
  6.3 4.3 %collective-permute-start.3 = (bf16[64,128]{1,0:T(8,128)(2,1)S(1)}, bf16[64,128]{1,0:T(8,128)(2,1)S(1)}, u32[]{:S(2)}, u32[]{:S(2)}) collective-permute-start(bf16[64,128]{1,0:T(8,128)(2,1)S(1)} %pack.1.piece_0), channel_id=1, source_target_pairs={{0,4},{4,0},{8,12},{12,8},{1,5},{5,1},{9,13},{13,9},{2,6},{6,2},{1... | collective-permute-start | bytes 49160 | tf_op jit(solution)/shard_map/ppermute | solution.py:20
  7.2 8.9 %collective-permute-start = (bf16[64,2304]{1,0:T(8,128)(2,1)S(1)}, bf16[64,2304]{1,0:T(8,128)(2,1)S(1)}, u32[]{:S(2)}, u32[]{:S(2)}) collective-permute-start(bf16[64,2304]{1,0:T(8,128)(2,1)S(1)} %get-tuple-element.21.near_load), channel_id=1, source_target_pairs={{0,4},{1,5},{4,0},{5,1},{8,12},{9,13},{12,8},{13,9},{2,3},{3,2},{6... | collective-permute-start | bytes 884744 | tf_op jit(solution)/shard_map/ppermute | solution.py:396
  9.9 11.3 %collective-permute-start.8 = (bf16[64,1792]{1,0:T(8,128)(2,1)S(1)}, bf16[64,1792]{1,0:T(8,128)(2,1)S(1)}, u32[]{:S(2)}, u32[]{:S(2)}) collective-permute-start(bf16[64,1792]{1,0:T(8,128)(2,1)S(1)} %get-tuple-element.30), channel_id=1, source_target_pairs={{4,8},{5,9},{8,4},{9,5},{0,1},{1,0},{2,3},{3,2},{6,7},{7,6},{10,11... | collective-permute-start | bytes 688136 | tf_op jit(solution)/shard_map/ppermute | solution.py:396
  10.7 3.8 %collective-permute-start.4 = (bf16[16,512]{1,0:T(8,128)(2,1)S(1)}, bf16[16,512]{1,0:T(8,128)(2,1)S(1)}, u32[]{:S(2)}, u32[]{:S(2)}) collective-permute-start(bf16[16,512]{1,0:T(8,128)(2,1)S(1)} %get-tuple-element.23), channel_id=1, source_target_pairs={{0,2},{2,0},{1,3},{3,1},{4,6},{6,4},{5,7},{7,5},{8,10},{10,8},{9,1... | collective-permute-start | bytes 49160 | tf_op jit(solution)/shard_map/ppermute | solution.py:414
  14.5 1.7 %copy-start.2 = (f32[5,4,128]{2,1,0:T(4,128)S(1)}, f32[5,4,128]{2,1,0:T(4,128)}, u32[]{:S(2)}) copy-start(f32[5,4,128]{2,1,0:T(4,128)} %forcing.1) | copy-start | bytes 30724
  14.5 3.7 %collective-permute-start.6 = (f32[24,128]{1,0:T(8,128)S(1)}, f32[24,128]{1,0:T(8,128)S(1)}, u32[]{:S(2)}, u32[]{:S(2)}) collective-permute-start(f32[24,128]{1,0:T(8,128)S(1)} %late_part.1.part), channel_id=1, source_target_pairs={{0,2},{2,0},{1,3},{3,1},{4,6},{6,4},{5,7},{7,5},{8,10},{10,8},{9,1... | collective-permute-start | bytes 36872 | tf_op jit(solution)/shard_map/ppermute | solution.py:414
  16.2 5.6 %collective-permute-start.5 = (bf16[64,1792]{1,0:T(8,128)(2,1)S(1)}, bf16[64,1792]{1,0:T(8,128)(2,1)S(1)}, u32[]{:S(2)}, u32[]{:S(2)}) collective-permute-start(bf16[64,1792]{1,0:T(8,128)(2,1)S(1)} %relay.1.after), channel_id=1, source_target_pairs={{4,8},{5,9},{8,4},{9,5},{0,1},{1,0},{2,3},{3,2},{6,7},{7,6},{10,11... | collective-permute-start | bytes 688136 | tf_op jit(solution)/shard_map/ppermute | solution.py:396
  18.2 3.1 %collective-permute-start.7 = (f32[24,128]{1,0:T(8,128)S(1)}, f32[24,128]{1,0:T(8,128)S(1)}, u32[]{:S(2)}, u32[]{:S(2)}) collective-permute-start(f32[24,128]{1,0:T(8,128)S(1)} %base.1.after.base_0), channel_id=1, source_target_pairs={{4,8},{5,9},{8,4},{9,5},{0,1},{1,0},{2,3},{3,2},{6,7},{7,6},{10,11... | collective-permute-start | bytes 36872 | tf_op jit(solution)/shard_map/ppermute | solution.py:396
  18.2 3.8 %collective-permute-start.12 = (f32[24,128]{1,0:T(8,128)S(1)}, f32[24,128]{1,0:T(8,128)S(1)}, u32[]{:S(2)}, u32[]{:S(2)}) collective-permute-start(f32[24,128]{1,0:T(8,128)S(1)} %base.1.after.base_0), channel_id=1, source_target_pairs={{0,4},{1,5},{4,0},{5,1},{8,12},{9,13},{12,8},{13,9},{2,3},{3,2},{6... | collective-permute-start | bytes 36872 | tf_op jit(solution)/shard_map/ppermute | solution.py:396
  19.9 4.6 %collective-permute-start.13 = (f32[24,128]{1,0:T(8,128)S(1)}, f32[24,128]{1,0:T(8,128)S(1)}, u32[]{:S(2)}, u32[]{:S(2)}) collective-permute-start(f32[24,128]{1,0:T(8,128)S(1)} %base.1.after.base_0), channel_id=1, source_target_pairs={{0,8},{1,9},{8,0},{9,1},{4,12},{5,13},{12,4},{13,5},{2,3},{3,2},{6... | collective-permute-start | bytes 36872 | tf_op jit(solution)/shard_map/ppermute | solution.py:396
  21.3 3.2 %collective-permute-start.9 = (bf16[64,2304]{1,0:T(8,128)(2,1)S(1)}, bf16[64,2304]{1,0:T(8,128)(2,1)S(1)}, u32[]{:S(2)}, u32[]{:S(2)}) collective-permute-start(bf16[64,2304]{1,0:T(8,128)(2,1)S(1)} %collective-permute-done.near.load_1), channel_id=1, source_target_pairs={{0,1},{1,0},{2,3},{3,2},{4,5},{5,4},{6,7},{7,6},{8,9},{9,8},{10,11... | collective-permute-start | bytes 884744 | tf_op jit(solution)/shard_map/ppermute | solution.py:414
  21.3 3.2 %collective-permute-start.11 = (bf16[64,1792]{1,0:T(8,128)(2,1)S(1)}, bf16[64,1792]{1,0:T(8,128)(2,1)S(1)}, u32[]{:S(2)}, u32[]{:S(2)}) collective-permute-start(bf16[64,1792]{1,0:T(8,128)(2,1)S(1)} %collective-permute-done.8.load_3), channel_id=1, source_target_pairs={{0,1},{1,0},{2,3},{3,2},{4,5},{5,4},{6,7},{7,6},{8,9},{9,8},{10,11... | collective-permute-start | bytes 688136 | tf_op jit(solution)/shard_map/ppermute | solution.py:414
  21.8 2.7 %collective-permute-start.10 = (bf16[64,1792]{1,0:T(8,128)(2,1)S(1)}, bf16[64,1792]{1,0:T(8,128)(2,1)S(1)}, u32[]{:S(2)}, u32[]{:S(2)}) collective-permute-start(bf16[64,1792]{1,0:T(8,128)(2,1)S(1)} %collective-permute-done.5.load_2), channel_id=1, source_target_pairs={{0,1},{1,0},{2,3},{3,2},{4,5},{5,4},{6,7},{7,6},{8,9},{9,8},{10,11... | collective-permute-start | bytes 688136 | tf_op jit(solution)/shard_map/ppermute | solution.py:414
  24.6 3.7 %collective-permute-start.14 = (f32[5,8,128]{2,1,0:T(8,128)S(1)}, f32[5,8,128]{2,1,0:T(8,128)S(1)}, u32[]{:S(2)}, u32[]{:S(2)}) collective-permute-start(f32[5,8,128]{2,1,0:T(8,128)S(1)} %get-tuple-element.33), channel_id=1, source_target_pairs={{4,6},{5,7},{6,4},{7,5},{8,10},{9,11},{10,8},{11,9},{0,1},{1,0},{2... | collective-permute-start | bytes 61448 | tf_op jit(solution)/shard_map/ppermute | solution.py:396
  24.6 5.3 %collective-permute-start.15 = (f32[5,8,128]{2,1,0:T(8,128)S(1)}, f32[5,8,128]{2,1,0:T(8,128)S(1)}, u32[]{:S(2)}, u32[]{:S(2)}) collective-permute-start(f32[5,8,128]{2,1,0:T(8,128)S(1)} %get-tuple-element.34), channel_id=1, source_target_pairs={{4,0},{5,1},{0,4},{1,5},{8,12},{9,13},{12,8},{13,9},{2,3},{3,2},{6... | collective-permute-start | bytes 61448 | tf_op jit(solution)/shard_map/ppermute | solution.py:396
  28.2 1.8 %collective-permute-start.16 = (f32[5,8,128]{2,1,0:T(8,128)S(1)}, f32[5,8,128]{2,1,0:T(8,128)S(1)}, u32[]{:S(2)}, u32[]{:S(2)}) collective-permute-start(f32[5,8,128]{2,1,0:T(8,128)S(1)} %get-tuple-element.34), channel_id=1, source_target_pairs={{4,2},{5,3},{2,6},{3,7},{6,4},{7,5},{8,14},{9,15},{14,10},{15,11},... | collective-permute-start | bytes 61448 | tf_op jit(solution)/shard_map/ppermute | solution.py:396

commit v11 on v10

--- a/solution.py
+++ b/solution.py
@@ -193,10 +193,10 @@
     del after
     gusts = 4
     known = everyone.shape[0] // 2
+    extra = everyone[known : 2 * known, :].astype(jnp.float32)
 
     def piece(index):
-        at = known + index * gusts
-        return everyone[at : at + gusts, :].astype(jnp.float32)
+        return extra[index * gusts : (index + 1) * gusts]
 
     offsets = piece(2)
     coef = piece(3) + (piece(4) + piece(5))

time: 30.7 us -> 30.7 us (level)
  no operation moved by 1% of the time
where the time goes in v11:
time: 30.7 us; the launch traced here: 30.6 us
  starting transfers between devices  18.1 us (59%)
  waiting for transfers between devices  8.7 us (28%)
  Pallas kernels  3.01 us (10%)
  other arithmetic  0.61 us (2%)
    ppermute x9, starting transfers between devices, exchanged(): return lax.ppermute(value, ('elem', 'lag', 'gust'), moves)  8.75 us
    ppermute x3, starting transfers between devices, flips(): lax.ppermute(value, 'elem', [(i, i ^ flip) for i in range(count)])  5.68 us
    ppermute x9, waiting for transfers between devices, exchanged(): return lax.ppermute(value, ('elem', 'lag', 'gust'), moves)  4.3 us
    ppermute x5, waiting for transfers between devices, crossed(): return lax.ppermute(value, axis, [(0, 1), (1, 0)])  3.8 us
    ppermute x5, starting transfers between devices, crossed(): return lax.ppermute(value, axis, [(0, 1), (1, 0)])  3.69 us
    pallas_call x11, Pallas kernels, on_core(): pl.pallas_call(body, out_shape=[pltpu.VMEM(shape, dtype) if force else ja...  3.01 us
  transfers between devices with their start and end apart: 17, of which 5 were waited for; matrix products, arithmetic and copies ran while one was open for 0% of the time, Pallas kernels for 7%

profile of v11, /device:TPU:0, one launch (start us, length us, event | category | flops | bytes accessed | tf_op | source)
XLA Modules:
  0.0 30.6 jit_solution(4268914044879352449)
XLA Ops:
  0.0 0.0 copy-start.1
  0.0 0.0 copy-start.3
  0.0 0.0 copy-start
  0.0 0.9 %pack.1.piece_0 = bf16[64,128]{1,0:T(8,128)(2,1)S(1)} custom-call(f32[8,4,128]{2,1,0:T(4,128)} %history_in.1, s32[4,128]{1,0:T(4,128)} %neighbours_in.1, f32[4,128]{1,0:T(4,128)} %edge_coef_in.1), custom_call_target="tpu_custom_call" | custom-call | flops 10000000000 | bytes 1048576 | tf_op jit(solution)/shard_map/pack/pallas_call | solution.py:375
  0.9 4.1 %collective-permute-start.1 = (bf16[64,128]{1,0:T(8,128)(2,1)S(1)}, bf16[64,128]{1,0:T(8,128)(2,1)S(1)}, u32[]{:S(2)}, u32[]{:S(2)}) collective-permute-start(bf16[64,128]{1,0:T(8,128)(2,1)S(1)} %pack.1.piece_0), channel_id=1, source_target_pairs={{0,8},{4,12},{8,0},{12,4},{1,9},{5,13},{9,1},{13,5},{2,10},{6,14},... | collective-permute-start | bytes 49160 | tf_op jit(solution)/shard_map/ppermute | solution.py:20
  5.0 1.3 %collective-permute-start.2 = (bf16[64,128]{1,0:T(8,128)(2,1)S(1)}, bf16[64,128]{1,0:T(8,128)(2,1)S(1)}, u32[]{:S(2)}, u32[]{:S(2)}) collective-permute-start(bf16[64,128]{1,0:T(8,128)(2,1)S(1)} %pack.1.piece_0), channel_id=1, source_target_pairs={{0,12},{4,8},{8,4},{12,0},{1,13},{5,9},{9,5},{13,1},{2,14},{6,10},... | collective-permute-start | bytes 49160 | tf_op jit(solution)/shard_map/ppermute | solution.py:20
  6.3 0.2 collective-permute-start.3
  6.6 0.0 copy-done.1
  6.6 0.0 copy-done.3
  6.6 0.0 copy-done
  6.6 0.7 %near_load.1 = (bf16[128,256]{1,0:T(8,128)(2,1)S(1)}, bf16[64,2304]{1,0:T(8,128)(2,1)S(1)}) custom-call(s32[1,4,8]{2,1,0:T(4,128)S(1)} %bitcast.1, bf16[8,128,512]{2,1,0:T(8,128)(2,1)S(1)} %copy-done, f32[128,128]{1,0:T(8,128)S(1)} %copy-done.1), custom_call_target="tpu_custom_call" | custom-call | flops 10000000000 | bytes 1048576 | tf_op jit(solution)/shard_map/near_load/pallas_call | solution.py:375
  7.2 1.9 %collective-permute-start = (bf16[64,2304]{1,0:T(8,128)(2,1)S(1)}, bf16[64,2304]{1,0:T(8,128)(2,1)S(1)}, u32[]{:S(2)}, u32[]{:S(2)}) collective-permute-start(bf16[64,2304]{1,0:T(8,128)(2,1)S(1)} %get-tuple-element.21.near_load), channel_id=1, source_target_pairs={{0,4},{1,5},{4,0},{5,1},{8,12},{9,13},{12,8},{13,9},{2,3},{3,2},{6... | collective-permute-start | bytes 884744 | tf_op jit(solution)/shard_map/ppermute | solution.py:396
  9.1 0.8 %masked.1 = (bf16[8,128,512]{2,1,0:T(8,128)(2,1)S(1)}, bf16[64,1792]{1,0:T(8,128)(2,1)S(1)}) custom-call(s32[1,4,8]{2,1,0:T(4,128)S(1)} %bitcast.2, bf16[8,128,512]{2,1,0:T(8,128)(2,1)S(1)} %copy-done, bf16[64,2304]{1,0:T(8,128)(2,1)S(1)} %get-tuple-element.21.near_load), custom_call_target="tpu_custom_call" | custom-call | flops 10000000000 | bytes 1048576 | tf_op jit(solution)/shard_map/masked/pallas_call | solution.py:375
  9.9 0.1 collective-permute-start.8
  10.0 0.0 collective-permute-done.1.piece_2
  10.0 0.6 %collective-permute-done.2.piece_3 = bf16[64,128]{1,0:T(8,128)(2,1)S(1)} collective-permute-done((bf16[64,128]{1,0:T(8,128)(2,1)S(1)}, bf16[64,128]{1,0:T(8,128)(2,1)S(1)}, u32[]{:S(2)}, u32[]{:S(2)}) %collective-permute-start.2) | collective-permute-done | bytes 16416 | tf_op jit(solution)/shard_map/ppermute | solution.py:20
  10.6 0.0 collective-permute-done.3.piece_1
  10.7 1.4 %collective-permute-start.4 = (bf16[16,512]{1,0:T(8,128)(2,1)S(1)}, bf16[16,512]{1,0:T(8,128)(2,1)S(1)}, u32[]{:S(2)}, u32[]{:S(2)}) collective-permute-start(bf16[16,512]{1,0:T(8,128)(2,1)S(1)} %get-tuple-element.23), channel_id=1, source_target_pairs={{0,2},{2,0},{1,3},{3,1},{4,6},{6,4},{5,7},{7,5},{8,10},{10,8},{9,1... | collective-permute-start | bytes 49160 | tf_op jit(solution)/shard_map/ppermute | solution.py:414
  12.1 0.5 %main_part.1 = (f32[24,128]{1,0:T(8,128)S(1)}, f32[8,128]{1,0:T(8,128)S(1)}) custom-call(bf16[64,512]{1,0:T(8,128)(2,1)S(1)} %get-tuple-element.24.everyone, bf16[8,128,512]{2,1,0:T(8,128)(2,1)S(1)} %get-tuple-element.22.masked), custom_call_target="tpu_custom_call" | custom-call | flops 10000000000 | bytes 1048576 | tf_op jit(solution)/shard_map/main_part/pallas_call | solution.py:375
  12.6 1.9 %collective-permute-done.4.late = bf16[16,512]{1,0:T(8,128)(2,1)S(1)} collective-permute-done((bf16[16,512]{1,0:T(8,128)(2,1)S(1)}, bf16[16,512]{1,0:T(8,128)(2,1)S(1)}, u32[]{:S(2)}, u32[]{:S(2)}) %collective-permute-start.4) | collective-permute-done | bytes 16416 | tf_op jit(solution)/shard_map/ppermute | solution.py:414
  14.5 0.0 copy-start.2
  14.5 1.7 %collective-permute-start.6 = (f32[24,128]{1,0:T(8,128)S(1)}, f32[24,128]{1,0:T(8,128)S(1)}, u32[]{:S(2)}, u32[]{:S(2)}) collective-permute-start(f32[24,128]{1,0:T(8,128)S(1)} %late_part.1.part), channel_id=1, source_target_pairs={{0,2},{2,0},{1,3},{3,1},{4,6},{6,4},{5,7},{7,5},{8,10},{10,8},{9,1... | collective-permute-start | bytes 36872 | tf_op jit(solution)/shard_map/ppermute | solution.py:414
  16.1 0.0 copy-done.2
  16.1 0.0 collective-permute-done.near.load_1
  16.2 0.1 collective-permute-start.5
  16.3 1.9 %collective-permute-done.6.other = f32[24,128]{1,0:T(8,128)S(1)} collective-permute-done((f32[24,128]{1,0:T(8,128)S(1)}, f32[24,128]{1,0:T(8,128)S(1)}, u32[]{:S(2)}, u32[]{:S(2)}) %collective-permute-start.6) | collective-permute-done | bytes 12320 | tf_op jit(solution)/shard_map/ppermute | solution.py:414
  18.2 0.0 collective-permute-start.7
  18.2 1.7 %collective-permute-start.12 = (f32[24,128]{1,0:T(8,128)S(1)}, f32[24,128]{1,0:T(8,128)S(1)}, u32[]{:S(2)}, u32[]{:S(2)}) collective-permute-start(f32[24,128]{1,0:T(8,128)S(1)} %base.1.after.base_0), channel_id=1, source_target_pairs={{0,4},{1,5},{4,0},{5,1},{8,12},{9,13},{12,8},{13,9},{2,3},{3,2},{6... | collective-permute-start | bytes 36872 | tf_op jit(solution)/shard_map/ppermute | solution.py:396
  19.9 1.4 %collective-permute-start.13 = (f32[24,128]{1,0:T(8,128)S(1)}, f32[24,128]{1,0:T(8,128)S(1)}, u32[]{:S(2)}, u32[]{:S(2)}) collective-permute-start(f32[24,128]{1,0:T(8,128)S(1)} %base.1.after.base_0), channel_id=1, source_target_pairs={{0,8},{1,9},{8,0},{9,1},{4,12},{5,13},{12,4},{13,5},{2,3},{3,2},{6... | collective-permute-start | bytes 36872 | tf_op jit(solution)/shard_map/ppermute | solution.py:396
  21.3 0.0 collective-permute-done.8.load_3
  21.3 0.0 collective-permute-start.9
  21.3 0.0 collective-permute-done.7.base_3
  21.3 0.5 %collective-permute-start.11 = (bf16[64,1792]{1,0:T(8,128)(2,1)S(1)}, bf16[64,1792]{1,0:T(8,128)(2,1)S(1)}, u32[]{:S(2)}, u32[]{:S(2)}) collective-permute-start(bf16[64,1792]{1,0:T(8,128)(2,1)S(1)} %collective-permute-done.8.load_3), channel_id=1, source_target_pairs={{0,1},{1,0},{2,3},{3,2},{4,5},{5,4},{6,7},{7,6},{8,9},{9,8},{10,11... | collective-permute-start | bytes 688136 | tf_op jit(solution)/shard_map/ppermute | solution.py:414
  21.8 0.0 collective-permute-done.5.load_2
  21.8 0.1 collective-permute-start.10
  21.9 0.1 spread.1
  22.0 0.0 collective-permute-done.12.base_1
  22.0 2.5 %collective-permute-done.13.base_2 = f32[24,128]{1,0:T(8,128)S(1)} collective-permute-done((f32[24,128]{1,0:T(8,128)S(1)}, f32[24,128]{1,0:T(8,128)S(1)}, u32[]{:S(2)}, u32[]{:S(2)}) %collective-permute-start.13) | collective-permute-done | bytes 12320 | tf_op jit(solution)/shard_map/ppermute | solution.py:396
  24.5 0.0 collective-permute-done.11.swap_3
  24.5 0.0 collective-permute-done.9.swap_1
  24.5 0.0 collective-permute-done.10.swap_2
  24.6 0.1 collective-permute-start.14
  24.6 3.6 %collective-permute-start.15 = (f32[5,8,128]{2,1,0:T(8,128)S(1)}, f32[5,8,128]{2,1,0:T(8,128)S(1)}, u32[]{:S(2)}, u32[]{:S(2)}) collective-permute-start(f32[5,8,128]{2,1,0:T(8,128)S(1)} %get-tuple-element.34), channel_id=1, source_target_pairs={{4,0},{5,1},{0,4},{1,5},{8,12},{9,13},{12,8},{13,9},{2,3},{3,2},{6... | collective-permute-start | bytes 61448 | tf_op jit(solution)/shard_map/ppermute | solution.py:396
  28.2 0.0 collective-permute-start.16
  28.2 0.0 collective-permute-done.14
  28.2 1.8 %collective-permute-done.15 = f32[5,8,128]{2,1,0:T(8,128)S(1)} collective-permute-done((f32[5,8,128]{2,1,0:T(8,128)S(1)}, f32[5,8,128]{2,1,0:T(8,128)S(1)}, u32[]{:S(2)}, u32[]{:S(2)}) %collective-permute-start.15) | collective-permute-done | bytes 20512 | tf_op jit(solution)/shard_map/ppermute | solution.py:396
  30.0 0.0 collective-permute-done.16
  30.0 0.6 %fusion = f32[5,4,128]{2,1,0:T(4,128)} fusion(f32[5,8,128]{2,1,0:T(8,128)S(1)} %collective-permute-done.16, f32[5,8,128]{2,1,0:T(8,128)S(1)} %collective-permute-done.15, f32[5,8,128]{2,1,0:T(8,128)S(1)} %collective-permute-done.14, f32[5,8,128]{2,1,0:T(8,128)S(1)} %get-tuple-element.33, pred[]{:T(512)S(6)} %or.3, pred[]{:T(512)S(6)} %eq.11), kind=kLoop, calls=%fused_computation.1 | loop fusion | flops 7680 | bytes 51202 | tf_op jit(solution)/shard_map/jit(_where)/select_n | solution.py:533
  (6 shorter events, 0.1 us)
Async XLA Ops:
  0.0 6.6 %copy-start.1 = (f32[128,128]{1,0:T(8,128)S(1)}, f32[128,128]{1,0:T(8,128)}, u32[]{:S(2)}) copy-start(f32[128,128]{1,0:T(8,128)} %correction_in) | copy-start | bytes 196612
  0.0 6.6 %copy-start.3 = (s32[8,1,4]{0,2,1:T(4,128)S(1)}, s32[8,1,4]{0,2,1:T(4,128)}, u32[]{:S(2)}) copy-start(s32[8,1,4]{0,2,1:T(4,128)} %param.10) | copy-start | bytes 388
  0.0 6.6 %copy-start = (bf16[8,128,512]{2,1,0:T(8,128)(2,1)S(1)}, bf16[8,128,512]{2,1,0:T(8,128)(2,1)}, u32[]{:S(2)}) copy-start(bf16[8,128,512]{2,1,0:T(8,128)(2,1)} %interaction.1) | copy-start | bytes 3145732
  0.9 9.1 %collective-permute-start.1 = (bf16[64,128]{1,0:T(8,128)(2,1)S(1)}, bf16[64,128]{1,0:T(8,128)(2,1)S(1)}, u32[]{:S(2)}, u32[]{:S(2)}) collective-permute-start(bf16[64,128]{1,0:T(8,128)(2,1)S(1)} %pack.1.piece_0), channel_id=1, source_target_pairs={{0,8},{4,12},{8,0},{12,4},{1,9},{5,13},{9,1},{13,5},{2,10},{6,14},... | collective-permute-start | bytes 49160 | tf_op jit(solution)/shard_map/ppermute | solution.py:20
  5.0 5.6 %collective-permute-start.2 = (bf16[64,128]{1,0:T(8,128)(2,1)S(1)}, bf16[64,128]{1,0:T(8,128)(2,1)S(1)}, u32[]{:S(2)}, u32[]{:S(2)}) collective-permute-start(bf16[64,128]{1,0:T(8,128)(2,1)S(1)} %pack.1.piece_0), channel_id=1, source_target_pairs={{0,12},{4,8},{8,4},{12,0},{1,13},{5,9},{9,5},{13,1},{2,14},{6,10},... | collective-permute-start | bytes 49160 | tf_op jit(solution)/shard_map/ppermute | solution.py:20
  6.3 4.3 %collective-permute-start.3 = (bf16[64,128]{1,0:T(8,128)(2,1)S(1)}, bf16[64,128]{1,0:T(8,128)(2,1)S(1)}, u32[]{:S(2)}, u32[]{:S(2)}) collective-permute-start(bf16[64,128]{1,0:T(8,128)(2,1)S(1)} %pack.1.piece_0), channel_id=1, source_target_pairs={{0,4},{4,0},{8,12},{12,8},{1,5},{5,1},{9,13},{13,9},{2,6},{6,2},{1... | collective-permute-start | bytes 49160 | tf_op jit(solution)/shard_map/ppermute | solution.py:20
  7.2 8.9 %collective-permute-start = (bf16[64,2304]{1,0:T(8,128)(2,1)S(1)}, bf16[64,2304]{1,0:T(8,128)(2,1)S(1)}, u32[]{:S(2)}, u32[]{:S(2)}) collective-permute-start(bf16[64,2304]{1,0:T(8,128)(2,1)S(1)} %get-tuple-element.21.near_load), channel_id=1, source_target_pairs={{0,4},{1,5},{4,0},{5,1},{8,12},{9,13},{12,8},{13,9},{2,3},{3,2},{6... | collective-permute-start | bytes 884744 | tf_op jit(solution)/shard_map/ppermute | solution.py:396
  9.9 11.3 %collective-permute-start.8 = (bf16[64,1792]{1,0:T(8,128)(2,1)S(1)}, bf16[64,1792]{1,0:T(8,128)(2,1)S(1)}, u32[]{:S(2)}, u32[]{:S(2)}) collective-permute-start(bf16[64,1792]{1,0:T(8,128)(2,1)S(1)} %get-tuple-element.30), channel_id=1, source_target_pairs={{4,8},{5,9},{8,4},{9,5},{0,1},{1,0},{2,3},{3,2},{6,7},{7,6},{10,11... | collective-permute-start | bytes 688136 | tf_op jit(solution)/shard_map/ppermute | solution.py:396
  10.7 3.8 %collective-permute-start.4 = (bf16[16,512]{1,0:T(8,128)(2,1)S(1)}, bf16[16,512]{1,0:T(8,128)(2,1)S(1)}, u32[]{:S(2)}, u32[]{:S(2)}) collective-permute-start(bf16[16,512]{1,0:T(8,128)(2,1)S(1)} %get-tuple-element.23), channel_id=1, source_target_pairs={{0,2},{2,0},{1,3},{3,1},{4,6},{6,4},{5,7},{7,5},{8,10},{10,8},{9,1... | collective-permute-start | bytes 49160 | tf_op jit(solution)/shard_map/ppermute | solution.py:414
  14.5 1.7 %copy-start.2 = (f32[5,4,128]{2,1,0:T(4,128)S(1)}, f32[5,4,128]{2,1,0:T(4,128)}, u32[]{:S(2)}) copy-start(f32[5,4,128]{2,1,0:T(4,128)} %forcing.1) | copy-start | bytes 30724
  14.5 3.7 %collective-permute-start.6 = (f32[24,128]{1,0:T(8,128)S(1)}, f32[24,128]{1,0:T(8,128)S(1)}, u32[]{:S(2)}, u32[]{:S(2)}) collective-permute-start(f32[24,128]{1,0:T(8,128)S(1)} %late_part.1.part), channel_id=1, source_target_pairs={{0,2},{2,0},{1,3},{3,1},{4,6},{6,4},{5,7},{7,5},{8,10},{10,8},{9,1... | collective-permute-start | bytes 36872 | tf_op jit(solution)/shard_map/ppermute | solution.py:414
  16.2 5.6 %collective-permute-start.5 = (bf16[64,1792]{1,0:T(8,128)(2,1)S(1)}, bf16[64,1792]{1,0:T(8,128)(2,1)S(1)}, u32[]{:S(2)}, u32[]{:S(2)}) collective-permute-start(bf16[64,1792]{1,0:T(8,128)(2,1)S(1)} %relay.1.after), channel_id=1, source_target_pairs={{4,8},{5,9},{8,4},{9,5},{0,1},{1,0},{2,3},{3,2},{6,7},{7,6},{10,11... | collective-permute-start | bytes 688136 | tf_op jit(solution)/shard_map/ppermute | solution.py:396
  18.2 3.1 %collective-permute-start.7 = (f32[24,128]{1,0:T(8,128)S(1)}, f32[24,128]{1,0:T(8,128)S(1)}, u32[]{:S(2)}, u32[]{:S(2)}) collective-permute-start(f32[24,128]{1,0:T(8,128)S(1)} %base.1.after.base_0), channel_id=1, source_target_pairs={{4,8},{5,9},{8,4},{9,5},{0,1},{1,0},{2,3},{3,2},{6,7},{7,6},{10,11... | collective-permute-start | bytes 36872 | tf_op jit(solution)/shard_map/ppermute | solution.py:396
  18.2 3.8 %collective-permute-start.12 = (f32[24,128]{1,0:T(8,128)S(1)}, f32[24,128]{1,0:T(8,128)S(1)}, u32[]{:S(2)}, u32[]{:S(2)}) collective-permute-start(f32[24,128]{1,0:T(8,128)S(1)} %base.1.after.base_0), channel_id=1, source_target_pairs={{0,4},{1,5},{4,0},{5,1},{8,12},{9,13},{12,8},{13,9},{2,3},{3,2},{6... | collective-permute-start | bytes 36872 | tf_op jit(solution)/shard_map/ppermute | solution.py:396
  19.9 4.6 %collective-permute-start.13 = (f32[24,128]{1,0:T(8,128)S(1)}, f32[24,128]{1,0:T(8,128)S(1)}, u32[]{:S(2)}, u32[]{:S(2)}) collective-permute-start(f32[24,128]{1,0:T(8,128)S(1)} %base.1.after.base_0), channel_id=1, source_target_pairs={{0,8},{1,9},{8,0},{9,1},{4,12},{5,13},{12,4},{13,5},{2,3},{3,2},{6... | collective-permute-start | bytes 36872 | tf_op jit(solution)/shard_map/ppermute | solution.py:396
  21.3 3.2 %collective-permute-start.9 = (bf16[64,2304]{1,0:T(8,128)(2,1)S(1)}, bf16[64,2304]{1,0:T(8,128)(2,1)S(1)}, u32[]{:S(2)}, u32[]{:S(2)}) collective-permute-start(bf16[64,2304]{1,0:T(8,128)(2,1)S(1)} %collective-permute-done.near.load_1), channel_id=1, source_target_pairs={{0,1},{1,0},{2,3},{3,2},{4,5},{5,4},{6,7},{7,6},{8,9},{9,8},{10,11... | collective-permute-start | bytes 884744 | tf_op jit(solution)/shard_map/ppermute | solution.py:414
  21.3 3.2 %collective-permute-start.11 = (bf16[64,1792]{1,0:T(8,128)(2,1)S(1)}, bf16[64,1792]{1,0:T(8,128)(2,1)S(1)}, u32[]{:S(2)}, u32[]{:S(2)}) collective-permute-start(bf16[64,1792]{1,0:T(8,128)(2,1)S(1)} %collective-permute-done.8.load_3), channel_id=1, source_target_pairs={{0,1},{1,0},{2,3},{3,2},{4,5},{5,4},{6,7},{7,6},{8,9},{9,8},{10,11... | collective-permute-start | bytes 688136 | tf_op jit(solution)/shard_map/ppermute | solution.py:414
  21.8 2.7 %collective-permute-start.10 = (bf16[64,1792]{1,0:T(8,128)(2,1)S(1)}, bf16[64,1792]{1,0:T(8,128)(2,1)S(1)}, u32[]{:S(2)}, u32[]{:S(2)}) collective-permute-start(bf16[64,1792]{1,0:T(8,128)(2,1)S(1)} %collective-permute-done.5.load_2), channel_id=1, source_target_pairs={{0,1},{1,0},{2,3},{3,2},{4,5},{5,4},{6,7},{7,6},{8,9},{9,8},{10,11... | collective-permute-start | bytes 688136 | tf_op jit(solution)/shard_map/ppermute | solution.py:414
  24.6 3.7 %collective-permute-start.14 = (f32[5,8,128]{2,1,0:T(8,128)S(1)}, f32[5,8,128]{2,1,0:T(8,128)S(1)}, u32[]{:S(2)}, u32[]{:S(2)}) collective-permute-start(f32[5,8,128]{2,1,0:T(8,128)S(1)} %get-tuple-element.33), channel_id=1, source_target_pairs={{4,6},{5,7},{6,4},{7,5},{8,10},{9,11},{10,8},{11,9},{0,1},{1,0},{2... | collective-permute-start | bytes 61448 | tf_op jit(solution)/shard_map/ppermute | solution.py:396
  24.6 5.3 %collective-permute-start.15 = (f32[5,8,128]{2,1,0:T(8,128)S(1)}, f32[5,8,128]{2,1,0:T(8,128)S(1)}, u32[]{:S(2)}, u32[]{:S(2)}) collective-permute-start(f32[5,8,128]{2,1,0:T(8,128)S(1)} %get-tuple-element.34), channel_id=1, source_target_pairs={{4,0},{5,1},{0,4},{1,5},{8,12},{9,13},{12,8},{13,9},{2,3},{3,2},{6... | collective-permute-start | bytes 61448 | tf_op jit(solution)/shard_map/ppermute | solution.py:396
  28.2 1.8 %collective-permute-start.16 = (f32[5,8,128]{2,1,0:T(8,128)S(1)}, f32[5,8,128]{2,1,0:T(8,128)S(1)}, u32[]{:S(2)}, u32[]{:S(2)}) collective-permute-start(f32[5,8,128]{2,1,0:T(8,128)S(1)} %get-tuple-element.34), channel_id=1, source_target_pairs={{4,2},{5,3},{2,6},{3,7},{6,4},{7,5},{8,14},{9,15},{14,10},{15,11},... | collective-permute-start | bytes 61448 | tf_op jit(solution)/shard_map/ppermute | solution.py:396
